TPU v7x, 32 devices: a whole 2x2x4 slice. The times are simulated.
32 devices in a mesh: ctx: 4 (over z), fsdp: 8 (over y, x, core).
Axes of the slice: x: 2, y: 2, z: 4, core: 2. Of those that a mesh axis runs over, the one named last changes fastest.
Arguments:
- layer_input: bfloat16 [8, 1024, 2048], P('fsdp', 'ctx'), may hold values from -6 to 6
- cotangent: bfloat16 [8, 1024, 2048], P('fsdp', 'ctx'), may hold values from -6 to 6
- positions: int32 [8, 1024], replicated, may hold values from 0 to 1023, as said below
- w_attn: bfloat16 [4, 2048, 2048], P(None, 'ctx', 'fsdp'), may hold values from -0.24527766 to 0.24527766
- w_ffn: bfloat16 [3, 2048, 4, 2048], P(None, 'ctx', None, 'fsdp'), may hold values from -0.125 to 0.125
- gains: float32 [4, 2048], replicated, may hold values from 0.5 to 1.5
- mom_attn: float32 [4, 2048, 2048], P(None, 'ctx', 'fsdp'), may hold values from -160 to 160
- mom_ffn: float32 [3, 2048, 4, 2048], P(None, 'ctx', None, 'fsdp'), may hold values from -160 to 160
- gain_mom: float32 [4, 2048], replicated, may hold values from -160 to 160
Outputs:
- layer_output: bfloat16 [8, 1024, 2048], P('fsdp', 'ctx')
- grad_input: float32 [8, 1024, 2048], P('fsdp', 'ctx')
- grad_attn: float32 [4, 2048, 2048], P(None, 'ctx', 'fsdp')
- grad_ffn: float32 [3, 2048, 4, 2048], P(None, 'ctx', None, 'fsdp')
- grad_gains: float32 [4, 2048], replicated
- new_mom_attn: float32 [4, 2048, 2048], P(None, 'ctx', 'fsdp')
- new_mom_ffn: float32 [3, 2048, 4, 2048], P(None, 'ctx', None, 'fsdp')
- new_gain_mom: float32 [4, 2048], replicated
- step_attn: float32 [4, 2048, 2048], P(None, 'ctx', 'fsdp')
- step_ffn: float32 [3, 2048, 4, 2048], P(None, 'ctx', None, 'fsdp')
- step_gains: float32 [4, 2048], replicated
Inputs may be any that keep to these rules, and one draw needn't show every extreme that they name: Each position of a sequence stands in exactly one slot. The 256 slots that begin at slot c * 256 hold block j of 128 positions and then block 7 - j, in order; j differs from c to c.
All inputs are finite; a program needn't handle non-finite values.
Results may differ from a plain program's by a relative error of at most 0.03.
Values may be sent and summed in bfloat16 or wider, within the bound.
A program may use at most 320 MiB of HBM per device.

v0:
```python
import jax
import jax.numpy as jnp
from jax import lax
from jax.sharding import PartitionSpec as P

NS_STEPS = 3
HEAD_DIM = 128


epsilon = 1e-06
rope_theta = 500000.0
quintic_one = 3.4445
quintic_two = -4.775
quintic_three = 2.0315
momentum = 0.95
muon_rate = 1.0
gain_rate = 0.0005


def token_rows(operand):
    return lax.all_gather(operand, "fsdp", axis=0, tiled=True)


def token_sums(operand):
    return lax.psum_scatter(
        operand.astype(jnp.bfloat16), "fsdp", scatter_dimension=0, tiled=True
    ).astype(jnp.float32)


def norm_stats(first_sum, second_sum):
    return lax.psum((first_sum, second_sum), "fsdp")


def along_ctx(first_part, second_part):
    return (
        lax.all_gather(first_part, "ctx", axis=1, tiled=True),
        lax.all_gather(second_part, "ctx", axis=1, tiled=True),
    )


def rms_back(upstream, normed, inv_scale):
    return inv_scale * (upstream - normed * jnp.mean(upstream * normed, axis=-1, keepdims=True))


def rotary_tables(slot_order):
    half_dim = HEAD_DIM // 2
    inverse = rope_theta ** (-(jnp.arange(half_dim, dtype=jnp.float32) * 2.0) / HEAD_DIM)
    angles = slot_order.astype(jnp.float32)[..., None] * inverse
    angles = jnp.concatenate([angles, angles], axis=-1)
    return (jnp.cos(angles)[..., None, :], jnp.sin(angles)[..., None, :])


def rotate(operand, cosine_table, sine_table):
    half_dim = operand.shape[-1] // 2
    flipped = jnp.concatenate([-operand[..., half_dim:], operand[..., :half_dim]], axis=-1)
    return operand * cosine_table + flipped * sine_table


def unrotate(upstream, cosine_table, sine_table):
    half_dim = upstream.shape[-1] // 2
    shifted = upstream * sine_table
    flipped = jnp.concatenate([shifted[..., half_dim:], -shifted[..., :half_dim]], axis=-1)
    return upstream * cosine_table + flipped


def masked_scores(query_rows, key_rows, query_pos, key_pos):
    scores = jnp.einsum("gqhe,gkhe->ghqk", query_rows, key_rows, preferred_element_type=jnp.float32)
    causal = query_pos[:, None, :, None] >= key_pos[:, None, None, :]
    return jnp.where(causal, scores, -1e30)


def attend(operands):
    query_rows, key_rows, value_rows, query_pos, key_pos = operands
    scores = masked_scores(query_rows, key_rows, query_pos, key_pos)
    row_max = jnp.max(scores, axis=-1, keepdims=True)
    weights = jnp.exp(scores - row_max)
    row_total = jnp.sum(weights, axis=-1, keepdims=True)
    probabilities = (weights / row_total).astype(jnp.bfloat16)
    attn_mixed = jnp.einsum(
        "ghqk,gkhe->gqhe", probabilities, value_rows, preferred_element_type=jnp.float32
    )
    return (attn_mixed.astype(jnp.bfloat16), row_max + jnp.log(row_total))


def attend_back(operands):
    query_rows, key_rows, value_rows, query_pos, key_pos, grad_mixed, log_total = operands
    scores = masked_scores(query_rows, key_rows, query_pos, key_pos)
    probabilities = jnp.exp(scores - log_total)
    grad_probs = jnp.einsum(
        "gqhe,gkhe->ghqk", grad_mixed, value_rows, preferred_element_type=jnp.float32
    )
    grad_value = jnp.einsum(
        "ghqk,gqhe->gkhe",
        probabilities.astype(jnp.bfloat16),
        grad_mixed,
        preferred_element_type=jnp.float32,
    )
    inner_sum = jnp.sum(grad_probs * probabilities, axis=-1, keepdims=True)
    grad_scores = (probabilities * (grad_probs - inner_sum)).astype(jnp.bfloat16)
    grad_query = jnp.einsum(
        "ghqk,gkhe->gqhe", grad_scores, key_rows, preferred_element_type=jnp.float32
    )
    grad_key = jnp.einsum(
        "ghqk,gqhe->gkhe", grad_scores, query_rows, preferred_element_type=jnp.float32
    )
    return (grad_query, grad_key, grad_value)


def shards(layer_input, cotangent, positions, w_attn, w_ffn, gains, mom_attn, mom_ffn, gain_mom):
    ctx_place = lax.axis_index("ctx")
    fsdp_place = lax.axis_index("fsdp")
    local_rows = layer_input.shape[1]
    width = layer_input.shape[2]
    seq_total = positions.shape[0]
    seq_length = positions.shape[1]
    head_cols = w_attn.shape[2]
    local_heads = head_cols // HEAD_DIM
    block_count = w_ffn.shape[2]
    shard_rows = w_attn.shape[1]
    group_size = min(seq_total, max(1, 512 // local_rows))
    while seq_total % group_size:
        group_size -= 1
    rounds = seq_total // group_size

    def split_groups(operand):
        return operand.reshape((rounds, group_size) + operand.shape[1:])

    def join_groups(operand):
        return operand.reshape((seq_total,) + operand.shape[2:])

    own_pos = lax.dynamic_slice_in_dim(positions, ctx_place * local_rows, local_rows, 1)
    gain_query = lax.dynamic_slice_in_dim(gains[0], fsdp_place * head_cols, head_cols)
    gain_key = lax.dynamic_slice_in_dim(gains[1], fsdp_place * head_cols, head_cols)
    attn_full, ffn_full = along_ctx(w_attn, w_ffn)
    inputs = layer_input.astype(jnp.float32)
    input_all = token_rows(layer_input)
    projected = jnp.einsum(
        "std,jde->jste", input_all, attn_full[:3], preferred_element_type=jnp.float32
    )
    query_raw, key_raw, value_raw = (projected[0], projected[1], projected[2])
    query_total, key_total = norm_stats(
        jnp.sum(query_raw * query_raw, axis=-1), jnp.sum(key_raw * key_raw, axis=-1)
    )
    query_scale = lax.rsqrt(query_total / width + epsilon)[..., None]
    key_scale = lax.rsqrt(key_total / width + epsilon)[..., None]
    query_hat = query_raw * query_scale
    key_hat = key_raw * key_scale
    cosine_table, sine_table = rotary_tables(own_pos)
    head_shape = (seq_total, local_rows, local_heads, HEAD_DIM)
    query_rows = (
        rotate((query_hat * gain_query).reshape(head_shape), cosine_table, sine_table)
        * HEAD_DIM ** (-0.5)
    ).astype(jnp.bfloat16)
    key_own = rotate((key_hat * gain_key).reshape(head_shape), cosine_table, sine_table).astype(
        jnp.bfloat16
    )
    value_own = value_raw.astype(jnp.bfloat16)
    all_keys, all_values = along_ctx(key_own.reshape(seq_total, local_rows, head_cols), value_own)
    full_shape = (seq_total, seq_length, local_heads, HEAD_DIM)
    keys_heads = all_keys.reshape(full_shape)
    values_heads = all_values.reshape(full_shape)
    attn_mixed, log_total = lax.map(
        attend,
        (
            split_groups(query_rows),
            split_groups(keys_heads),
            split_groups(values_heads),
            split_groups(own_pos),
            split_groups(positions),
        ),
    )
    attn_mixed = join_groups(attn_mixed).reshape(seq_total, local_rows, head_cols)
    attn_part = jnp.einsum(
        "ste,de->std", attn_mixed, attn_full[3], preferred_element_type=jnp.float32
    )
    attn_out = token_sums(attn_part)
    attn_scale = lax.rsqrt(jnp.mean(attn_out * attn_out, axis=-1, keepdims=True) + epsilon)
    attn_hat = attn_out * attn_scale
    hidden_in = inputs + attn_hat * gains[2]
    mlp_all = token_rows(hidden_in.astype(jnp.bfloat16))
    gate_value = jnp.einsum(
        "std,dbj->stbj", mlp_all, ffn_full[0], preferred_element_type=jnp.float32
    )
    up_value = jnp.einsum("std,dbj->stbj", mlp_all, ffn_full[1], preferred_element_type=jnp.float32)
    gate_sigmoid = jax.nn.sigmoid(gate_value)
    gate_act = gate_value * gate_sigmoid
    hidden = (gate_act * up_value).astype(jnp.bfloat16)
    mlp_part = jnp.einsum("stbj,dbj->std", hidden, ffn_full[2], preferred_element_type=jnp.float32)
    mlp_out = token_sums(mlp_part)
    mlp_scale = lax.rsqrt(jnp.mean(mlp_out * mlp_out, axis=-1, keepdims=True) + epsilon)
    mlp_hat = mlp_out * mlp_scale
    result = hidden_in + mlp_hat * gains[3]
    grad_out = cotangent.astype(jnp.float32)
    grad_mlp_gain = jnp.sum(grad_out * mlp_hat, axis=(0, 1))
    grad_mlp = rms_back(grad_out * gains[3], mlp_hat, mlp_scale).astype(jnp.bfloat16)
    grad_mlp_all = token_rows(grad_mlp)
    grad_hidden = jnp.einsum(
        "std,dbj->stbj", grad_mlp_all, ffn_full[2], preferred_element_type=jnp.float32
    )
    grad_up = (grad_hidden * gate_act).astype(jnp.bfloat16)
    grad_gate = (
        grad_hidden * up_value * gate_sigmoid * (1.0 + gate_value * (1.0 - gate_sigmoid))
    ).astype(jnp.bfloat16)
    back_part = jnp.einsum(
        "stbj,dbj->std", grad_gate, ffn_full[0], preferred_element_type=jnp.float32
    )
    back_part = back_part + jnp.einsum(
        "stbj,dbj->std", grad_up, ffn_full[1], preferred_element_type=jnp.float32
    )
    grad_resid = grad_out + token_sums(back_part)
    grad_attn_gain = jnp.sum(grad_resid * attn_hat, axis=(0, 1))
    grad_attn_out = rms_back(grad_resid * gains[2], attn_hat, attn_scale).astype(jnp.bfloat16)
    grad_attn_all = token_rows(grad_attn_out)
    grad_mixed = jnp.einsum(
        "std,de->ste", grad_attn_all, attn_full[3], preferred_element_type=jnp.float32
    ).astype(jnp.bfloat16)
    grad_query, grad_keys, grad_values = lax.map(
        attend_back,
        (
            split_groups(query_rows),
            split_groups(keys_heads),
            split_groups(values_heads),
            split_groups(own_pos),
            split_groups(positions),
            split_groups(grad_mixed.reshape(head_shape)),
            log_total,
        ),
    )
    grad_query = join_groups(grad_query)
    grad_keys = join_groups(grad_keys).reshape(seq_total, seq_length, head_cols)
    grad_values = join_groups(grad_values).reshape(seq_total, seq_length, head_cols)
    key_grad, value_grad = (
        lax.psum_scatter(
            grad_keys.astype(jnp.bfloat16), "ctx", scatter_dimension=1, tiled=True
        ).astype(jnp.float32),
        lax.psum_scatter(
            grad_values.astype(jnp.bfloat16), "ctx", scatter_dimension=1, tiled=True
        ).astype(jnp.float32),
    )
    grad_query_norm = unrotate(grad_query * HEAD_DIM ** (-0.5), cosine_table, sine_table).reshape(
        seq_total, local_rows, head_cols
    )
    grad_key_norm = unrotate(key_grad.reshape(head_shape), cosine_table, sine_table).reshape(
        seq_total, local_rows, head_cols
    )
    query_gain_cols = jnp.sum(grad_query_norm * query_hat, axis=(0, 1))
    key_gain_cols = jnp.sum(grad_key_norm * key_hat, axis=(0, 1))
    query_weighted = grad_query_norm * gain_query
    key_weighted = grad_key_norm * gain_key
    query_inner, key_inner = norm_stats(
        jnp.sum(query_weighted * query_hat, axis=-1), jnp.sum(key_weighted * key_hat, axis=-1)
    )
    grad_query_raw = (
        query_scale * (query_weighted - query_hat * (query_inner / width)[..., None])
    ).astype(jnp.bfloat16)
    grad_key_raw = (key_scale * (key_weighted - key_hat * (key_inner / width)[..., None])).astype(
        jnp.bfloat16
    )
    grad_value_raw = value_grad.astype(jnp.bfloat16)
    grad_projected = jnp.stack([grad_query_raw, grad_key_raw, grad_value_raw])
    input_part = jnp.einsum(
        "jste,jde->std", grad_projected, attn_full[:3], preferred_element_type=jnp.float32
    )
    grad_input = grad_resid + token_sums(input_part)
    projections = jnp.einsum(
        "std,jste->dje", input_all, grad_projected, preferred_element_type=jnp.float32
    )
    output_rows = jnp.einsum(
        "std,ste->de", grad_attn_all, attn_mixed, preferred_element_type=jnp.float32
    )[:, None, :]
    gate_rows = jnp.einsum("std,stbj->dbj", mlp_all, grad_gate, preferred_element_type=jnp.float32)
    up_rows = jnp.einsum("std,stbj->dbj", mlp_all, grad_up, preferred_element_type=jnp.float32)
    down_rows = jnp.einsum(
        "std,stbj->dbj", grad_mlp_all, hidden, preferred_element_type=jnp.float32
    )
    weight_grads = lax.psum_scatter(
        jnp.concatenate([projections, output_rows, gate_rows, up_rows, down_rows], axis=1).astype(
            jnp.bfloat16
        ),
        "ctx",
        scatter_dimension=0,
        tiled=True,
    ).astype(jnp.float32)
    empty_row = jnp.zeros((width,), jnp.float32)
    gain_local = jnp.stack(
        [
            lax.dynamic_update_slice(empty_row, query_gain_cols, (fsdp_place * head_cols,)),
            lax.dynamic_update_slice(empty_row, key_gain_cols, (fsdp_place * head_cols,)),
            grad_attn_gain,
            grad_mlp_gain,
        ]
    )
    mom_units = jnp.concatenate(
        [
            jnp.transpose(mom_attn, (1, 0, 2)),
            jnp.transpose(mom_ffn, (1, 0, 2, 3)).reshape(shard_rows, 3 * block_count, head_cols),
        ],
        axis=1,
    )
    new_units = momentum * mom_units + weight_grads
    gain_total, unit_total = lax.psum(
        (gain_local, jnp.sum(new_units * new_units, axis=(0, 2))), ("ctx", "fsdp")
    )
    unit_start = (new_units / (jnp.sqrt(unit_total) + 1e-07)[None, :, None]).astype(jnp.bfloat16)
    unit_piece = lax.all_to_all(unit_start, "ctx", split_axis=1, concat_axis=0, tiled=True)
    for iteration in range(NS_STEPS):
        chosen = unit_piece
        gram_part = lax.psum_scatter(
            jnp.einsum(
                "rul,sul->rus", chosen, unit_piece, preferred_element_type=jnp.float32
            ).astype(jnp.bfloat16),
            "fsdp",
            scatter_dimension=0,
            tiled=True,
        )
        gram_full = lax.all_gather(gram_part, "fsdp", axis=0, tiled=True)
        product = jnp.einsum(
            "rus,sul->rul", gram_full, unit_piece, preferred_element_type=jnp.float32
        )
        product_two = jnp.einsum(
            "rus,sul->rul",
            gram_full,
            product.astype(jnp.bfloat16),
            preferred_element_type=jnp.float32,
        )
        unit_piece = (
            quintic_one * unit_piece.astype(jnp.float32)
            + quintic_two * product
            + quintic_three * product_two
        ).astype(jnp.bfloat16)
    final_units = lax.all_to_all(unit_piece, "ctx", split_axis=0, concat_axis=1, tiled=True)
    unit_steps = -muon_rate * final_units.astype(jnp.float32)

    def attn_layout(units):
        return jnp.transpose(units[:, :4], (1, 0, 2))

    def ffn_layout(units):
        return jnp.transpose(
            units[:, 4:].reshape(shard_rows, 3, block_count, head_cols), (1, 0, 2, 3)
        )

    new_gain_mom = momentum * gain_mom + gain_total
    return (
        result.astype(jnp.bfloat16),
        grad_input,
        attn_layout(weight_grads),
        ffn_layout(weight_grads),
        gain_total,
        attn_layout(new_units),
        ffn_layout(new_units),
        new_gain_mom,
        attn_layout(unit_steps),
        ffn_layout(unit_steps),
        -gain_rate * new_gain_mom,
    )


def solution(mesh):
    in_specs = (
        P("fsdp", "ctx", None),
        P("fsdp", "ctx", None),
        P(),
        P(None, "ctx", "fsdp"),
        P(None, "ctx", None, "fsdp"),
        P(),
        P(None, "ctx", "fsdp"),
        P(None, "ctx", None, "fsdp"),
        P(),
    )
    out_specs = (
        P("fsdp", "ctx", None),
        P("fsdp", "ctx", None),
        P(None, "ctx", "fsdp"),
        P(None, "ctx", None, "fsdp"),
        P(),
        P(None, "ctx", "fsdp"),
        P(None, "ctx", None, "fsdp"),
        P(),
        P(None, "ctx", "fsdp"),
        P(None, "ctx", None, "fsdp"),
        P(),
    )
    return jax.shard_map(shards, mesh=mesh, in_specs=in_specs, out_specs=out_specs, check_vma=False)
```

profile of v0, /device:TPU:0, one launch (start us, length us, event | category | flops | bytes accessed | tf_op | source)
XLA Modules:
  0.0 3257.5 jit_solution(9434199227795178104)
XLA Ops:
  15.3 78.4 %all-gather.13.cloned.1.call-done = bf16[4,2048,256]{1,2,0:T(8,128)(2,1)} async-done(((bf16[4,512,256]{1,2,0:T(8,128)(2,1)}), bf16[4,2048,256]{1,2,0:T(8,128)(2,1)}) %all-gather.13.cloned.1.call-update) | async-done | bytes 4194320 | tf_op jit(solution)/shard_map/all_gather | solution.py:36
  93.7 54.8 %all-gather.15.cloned.1.call-done = bf16[8,256,2048]{2,1,0:T(8,128)(2,1)} async-done(((bf16[1,256,2048]{2,1,0:T(8,128)(2,1)}), bf16[8,256,2048]{2,1,0:T(8,128)(2,1)}) %all-gather.15.cloned.1.call-update) | async-done | bytes 8388624 | tf_op jit(solution)/shard_map/all_gather | solution.py:21
  204.0 68.0 %all-gather.17.cloned.1.call-done = bf16[8,1024,256]{1,2,0:T(8,128)(2,1)} async-done(((bf16[8,256,256]{1,2,0:T(8,128)(2,1)}), bf16[8,1024,256]{1,2,0:T(8,128)(2,1)}) %all-gather.17.cloned.1.call-update) | async-done | bytes 4194320 | tf_op jit(solution)/shard_map/all_gather | solution.py:36
  278.2 74.5 %all-gather.33.cloned.1.call-done = bf16[1,8,1024,256]{2,3,1,0:T(8,128)(2,1)} async-done(((bf16[1,8,256,256]{2,3,1,0:T(8,128)(2,1)}), bf16[1,8,1024,256]{2,3,1,0:T(8,128)(2,1)}) %all-gather.33.cloned.1.call-update) | async-done | bytes 4194320 | tf_op jit(solution)/shard_map/all_gather | solution.py:37
  388.8 65.3 %reduce-scatter.11.cloned.1.call-done = bf16[1,256,2048]{2,1,0:T(8,128)(2,1)} async-done(((bf16[8,256,2048]{2,1,0:T(8,128)(2,1)}), bf16[1,256,2048]{2,1,0:T(8,128)(2,1)}) %reduce-scatter.11.cloned.1.call-update) | async-done | bytes 1048592 | tf_op jit(solution)/shard_map/reduce_scatter | solution.py:25
  458.5 215.9 %all-gather.21.cloned.1.call-done = bf16[3,2048,4,256]{3,1,2,0:T(8,128)(2,1)} async-done(((bf16[3,512,4,256]{3,1,2,0:T(8,128)(2,1)}), bf16[3,2048,4,256]{3,1,2,0:T(8,128)(2,1)}) %all-gather.21.cloned.1.call-update) | async-done | bytes 12582928 | tf_op jit(solution)/shard_map/all_gather | solution.py:37
  674.4 55.2 %all-gather.19.cloned.1.call-done = bf16[8,256,2048]{2,1,0:T(8,128)(2,1)} async-done(((bf16[1,256,2048]{2,1,0:T(8,128)(2,1)}), bf16[8,256,2048]{2,1,0:T(8,128)(2,1)}) %all-gather.19.cloned.1.call-update) | async-done | bytes 8388624 | tf_op jit(solution)/shard_map/all_gather | solution.py:21
  773.4 71.4 %reduce-scatter.13.cloned.1.call-done = bf16[1,256,2048]{2,1,0:T(8,128)(2,1)} async-done(((bf16[8,256,2048]{2,1,0:T(8,128)(2,1)}), bf16[1,256,2048]{2,1,0:T(8,128)(2,1)}) %reduce-scatter.13.cloned.1.call-update) | async-done | bytes 1048592 | tf_op jit(solution)/shard_map/reduce_scatter | solution.py:25
  852.1 54.3 %all-gather.23.cloned.1.call-done = bf16[8,256,2048]{2,1,0:T(8,128)(2,1)} async-done(((bf16[1,256,2048]{2,1,0:T(8,128)(2,1)}), bf16[8,256,2048]{2,1,0:T(8,128)(2,1)}) %all-gather.23.cloned.1.call-update) | async-done | bytes 8388624 | tf_op jit(solution)/shard_map/all_gather | solution.py:21
  960.6 71.4 %reduce-scatter.15.cloned.1.call-done = bf16[1,256,2048]{2,1,0:T(8,128)(2,1)} async-done(((bf16[8,256,2048]{2,1,0:T(8,128)(2,1)}), bf16[1,256,2048]{2,1,0:T(8,128)(2,1)}) %reduce-scatter.15.cloned.1.call-update) | async-done | bytes 1048592 | tf_op jit(solution)/shard_map/reduce_scatter | solution.py:25
  1039.2 54.5 %all-gather.25.cloned.1.call-done = bf16[8,256,2048]{2,1,0:T(8,128)(2,1)} async-done(((bf16[1,256,2048]{2,1,0:T(8,128)(2,1)}), bf16[8,256,2048]{2,1,0:T(8,128)(2,1)}) %all-gather.25.cloned.1.call-update) | async-done | bytes 8388624 | tf_op jit(solution)/shard_map/all_gather | solution.py:21
  1099.7 56.5 %while.27 = (s32[]{:T(128)}, f32[4,2,256,2,128]{2,4,3,1,0:T(8,128)}, bf16[4,2,1024,2,128]{2,4,3,1,0:T(8,128)(2,1)}, bf16[4,2,1024,2,128]{2,4,3,1,0:T(8,128)(2,1)...) while((s32[]{:T(128)}, ...), condition=%wide.region_17.18_spmd, body=%wide.region_15.17_spmd.sunk | while | flops 1355283456 | bytes 76086456 | solution.py:217
  1165.6 67.5 %reduce-scatter.17.cloned.1.call-done = bf16[8,256,256]{1,2,0:T(8,128)(2,1)} async-done(((bf16[8,1024,256]{1,2,0:T(8,128)(2,1)}), bf16[8,256,256]{1,2,0:T(8,128)(2,1)}) %reduce-scatter.17.cloned.1.call-update) | async-done | bytes 1048592 | tf_op jit(solution)/shard_map/reduce_scatter | solution.py:233
  1271.4 41.3 %reduce-scatter.19.cloned.1.call-done = bf16[8,256,256]{1,2,0:T(8,128)(2,1)} async-done(((bf16[8,1024,256]{1,2,0:T(8,128)(2,1)}), bf16[8,256,256]{1,2,0:T(8,128)(2,1)}) %reduce-scatter.19.cloned.1.call-update) | async-done | bytes 1048592 | tf_op jit(solution)/shard_map/reduce_scatter | solution.py:236
  1376.3 274.0 %reduce-scatter.23.cloned.1.call-done = bf16[512,16,256]{2,0,1:T(8,128)(2,1)} async-done(((bf16[2048,16,256]{2,0,1:T(8,128)(2,1)}), bf16[512,16,256]{2,0,1:T(8,128)(2,1)}) %reduce-scatter.23.cloned.1.call-update) | async-done | bytes 4194320 | tf_op jit(solution)/shard_map/reduce_scatter | solution.py:276
  1657.5 41.8 %all-reduce = (f32[4,2048]{1,0:T(4,128)}, f32[16]{0:T(128)S(1)}) all-reduce(f32[4,2048]{1,0:T(4,128)S(1)} %pad_maximum_fusion.7, f32[16]{0:T(128)S(1)} %get-tuple-element.251), channel_id=1, replica_groups=mesh['ctx'=4,'fsdp'=8] {'ctx','fsdp'}, use_global_device_ids=true, to_apply=%region_30.31 | all-reduce | flops 8208 | bytes 65664 | tf_op jit(solution)/shard_map/psum | solution.py:301
  1703.6 95.7 %all_to_all.27 = bf16[512,16,256]{2,0,1:T(8,128)(2,1)S(1)} all-to-all(bf16[512,16,256]{2,0,1:T(8,128)(2,1)S(1)} %divide_convert_fusion.8), channel_id=1, replica_groups=mesh['ctx'=4,'fsdp'=8] {'ctx'}, dimensions={1} | all-to-all | bytes 8388608 | tf_op jit(solution)/shard_map/all_to_all | solution.py:305
  1818.9 204.4 %reduce-scatter.25.cloned.1.call-done = bf16[256,4,2048]{0,2,1:T(8,128)(2,1)} async-done(((bf16[2048,4,2048]{0,2,1:T(8,128)(2,1)}), bf16[256,4,2048]{0,2,1:T(8,128)(2,1)}) %reduce-scatter.25.cloned.1.call-update) | async-done | bytes 4194320 | tf_op jit(solution)/shard_map/reduce_scatter | solution.py:308
  2023.3 169.3 %all-gather.27.cloned.1.call-done = bf16[2048,4,2048]{0,2,1:T(8,128)(2,1)} async-done(((bf16[256,4,2048]{0,2,1:T(8,128)(2,1)}), bf16[2048,4,2048]{0,2,1:T(8,128)(2,1)}) %all-gather.27.cloned.1.call-update) | async-done | bytes 33554448 | tf_op jit(solution)/shard_map/all_gather | solution.py:316
  2260.1 205.4 %reduce-scatter.27.cloned.1.call-done = bf16[256,4,2048]{0,2,1:T(8,128)(2,1)} async-done(((bf16[2048,4,2048]{0,2,1:T(8,128)(2,1)}), bf16[256,4,2048]{0,2,1:T(8,128)(2,1)}) %reduce-scatter.27.cloned.1.call-update) | async-done | bytes 4194320 | tf_op jit(solution)/shard_map/reduce_scatter | solution.py:308
  2465.5 169.1 %all-gather.29.cloned.1.call-done = bf16[2048,4,2048]{0,2,1:T(8,128)(2,1)} async-done(((bf16[256,4,2048]{0,2,1:T(8,128)(2,1)}), bf16[2048,4,2048]{0,2,1:T(8,128)(2,1)}) %all-gather.29.cloned.1.call-update) | async-done | bytes 33554448 | tf_op jit(solution)/shard_map/all_gather | solution.py:316
  2702.1 205.3 %reduce-scatter.29.cloned.1.call-done = bf16[256,4,2048]{0,2,1:T(8,128)(2,1)} async-done(((bf16[2048,4,2048]{0,2,1:T(8,128)(2,1)}), bf16[256,4,2048]{0,2,1:T(8,128)(2,1)}) %reduce-scatter.29.cloned.1.call-update) | async-done | bytes 4194320 | tf_op jit(solution)/shard_map/reduce_scatter | solution.py:308
  2919.4 157.4 %all-gather.31.cloned.1.call-done = bf16[2048,4,2048]{0,2,1:T(8,128)(2,1)} async-done(((bf16[256,4,2048]{0,2,1:T(8,128)(2,1)}), bf16[2048,4,2048]{0,2,1:T(8,128)(2,1)}) %all-gather.31.cloned.1.call-update) | async-done | bytes 33554448 | tf_op jit(solution)/shard_map/all_gather | solution.py:316
  3178.9 57.3 %all-to-all-done.1 = bf16[2048,4,256]{2,1,0:T(4,128)(2,1)} async-done(((bf16[2048,4,256]{2,1,0:T(4,128)(2,1)}), bf16[2048,4,256]{2,1,0:T(4,128)(2,1)}, u32[]{:S(2)}, u32[]{:S(2)}) %all-to-all-start.1) | async-done | bytes 4194336 | tf_op jit(solution)/shard_map/all_to_all | solution.py:331
  (361 shorter events, 713.7 us)
Async XLA Ops:
  7.2 86.5 %all-gather.13.cloned.1.call-start = ((), (), s32[]{:S(2)}) async-start(), calls=%async_computation.12 | async-start | bytes 5242880 | tf_op jit(solution)/shard_map/all_gather | solution.py:36
  9.5 139.0 %all-gather.15.cloned.1.call-start = ((), (), s32[]{:S(2)}) async-start(), calls=%async_computation.13 | async-start | bytes 9437184 | tf_op jit(solution)/shard_map/all_gather | solution.py:21
  10.3 261.6 %all-gather.17.cloned.1.call-start = ((), (), s32[]{:S(2)}) async-start(), calls=%async_computation.14 | async-start | bytes 5242880 | tf_op jit(solution)/shard_map/all_gather | solution.py:36
  191.2 161.5 %all-gather.33.cloned.1.call-start = ((), (), s32[]{:S(2)}) async-start(), calls=%async_computation.32 | async-start | bytes 5242880 | tf_op jit(solution)/shard_map/all_gather | solution.py:37
  194.0 260.1 %reduce-scatter.11.cloned.1.call-start = ((), (), s32[]{:S(2)}) async-start(), calls=%async_computation.15 | async-start | bytes 9437184 | tf_op jit(solution)/shard_map/reduce_scatter | solution.py:25
  384.5 289.9 %all-gather.21.cloned.1.call-start = ((), (), s32[]{:S(2)}) async-start(), calls=%async_computation.17 | async-start | bytes 15728640 | tf_op jit(solution)/shard_map/all_gather | solution.py:37
  388.7 340.9 %all-gather.19.cloned.1.call-start = ((), (), s32[]{:S(2)}) async-start(), calls=%async_computation.16 | async-start | bytes 9437184 | tf_op jit(solution)/shard_map/all_gather | solution.py:21
  458.3 386.6 %reduce-scatter.13.cloned.1.call-start = ((), (), s32[]{:S(2)}) async-start(), calls=%async_computation.18 | async-start | bytes 9437184 | tf_op jit(solution)/shard_map/reduce_scatter | solution.py:25
  773.4 133.0 %all-gather.23.cloned.1.call-start = ((), (), s32[]{:S(2)}) async-start(), calls=%async_computation.19 | async-start | bytes 9437184 | tf_op jit(solution)/shard_map/all_gather | solution.py:21
  851.8 180.1 %reduce-scatter.15.cloned.1.call-start = ((), (), s32[]{:S(2)}) async-start(), calls=%async_computation.20 | async-start | bytes 9437184 | tf_op jit(solution)/shard_map/reduce_scatter | solution.py:25
  960.5 133.1 %all-gather.25.cloned.1.call-start = ((), (), s32[]{:S(2)}) async-start(), calls=%async_computation.21 | async-start | bytes 9437184 | tf_op jit(solution)/shard_map/all_gather | solution.py:21
  1039.1 194.1 %reduce-scatter.17.cloned.1.call-start = ((), (), s32[]{:S(2)}) async-start(), calls=%async_computation.22 | async-start | bytes 5242880 | tf_op jit(solution)/shard_map/reduce_scatter | solution.py:233
  1156.2 156.5 %reduce-scatter.19.cloned.1.call-start = ((), (), s32[]{:S(2)}) async-start(), calls=%async_computation.23 | async-start | bytes 5242880 | tf_op jit(solution)/shard_map/reduce_scatter | solution.py:236
  1157.0 493.4 %reduce-scatter.23.cloned.1.call-start = ((), (), s32[]{:S(2)}) async-start(), calls=%async_computation.25 | async-start | bytes 20971520 | tf_op jit(solution)/shard_map/reduce_scatter | solution.py:276
  1369.4 653.9 %reduce-scatter.25.cloned.1.call-start = ((), (), s32[]{:S(2)}) async-start(), calls=%async_computation.26 | async-start | bytes 37748736 | tf_op jit(solution)/shard_map/reduce_scatter | solution.py:308
  1369.5 280.9 %copy-start.25 = (f32[4,512,256]{2,1,0:T(8,128)S(1)}, f32[4,512,256]{2,1,0:T(8,128)}, u32[]{:S(2)}) copy-start(f32[4,512,256]{2,1,0:T(8,128)} %param.19) | copy-start | bytes 6291460
  1818.9 373.7 %all-gather.27.cloned.1.call-start = ((), (), s32[]{:S(2)}) async-start(), calls=%async_computation.27 | async-start | bytes 37748736 | tf_op jit(solution)/shard_map/all_gather | solution.py:316
  2023.3 442.1 %reduce-scatter.27.cloned.1.call-start = ((), (), s32[]{:S(2)}) async-start(), calls=%async_computation.28 | async-start | bytes 37748736 | tf_op jit(solution)/shard_map/reduce_scatter | solution.py:308
  2260.0 374.6 %all-gather.29.cloned.1.call-start = ((), (), s32[]{:S(2)}) async-start(), calls=%async_computation.29 | async-start | bytes 37748736 | tf_op jit(solution)/shard_map/all_gather | solution.py:316
  2465.5 442.0 %reduce-scatter.29.cloned.1.call-start = ((), (), s32[]{:S(2)}) async-start(), calls=%async_computation.30 | async-start | bytes 37748736 | tf_op jit(solution)/shard_map/reduce_scatter | solution.py:308
  2702.1 205.5 %copy-start.27 = (bf16[1,8,256,256]{2,3,1,0:T(8,128)(2,1)S(1)}, bf16[1,8,256,256]{2,3,1,0:T(8,128)(2,1)}, u32[]{:S(2)}) copy-start(bf16[1,8,256,256]{2,3,1,0:T(8,128)(2,1)} %fusion.127) | copy-start | bytes 3145732
  2702.1 374.7 %all-gather.31.cloned.1.call-start = ((), (), s32[]{:S(2)}) async-start(), calls=%async_computation.31 | async-start | bytes 37748736 | tf_op jit(solution)/shard_map/all_gather | solution.py:316
  2907.5 244.5 %reduce-scatter.21.cloned.1.call-start = ((), (), s32[]{:S(2)}) async-start(), calls=%async_computation.24 | async-start | bytes 9437184 | tf_op jit(solution)/shard_map/reduce_scatter | solution.py:25
  3137.1 99.1 %all-to-all-start.1 = ((bf16[2048,4,256]{2,1,0:T(4,128)(2,1)}), bf16[2048,4,256]{2,1,0:T(4,128)(2,1)}, u32[]{:S(2)}, u32[]{:S(2)}) async-start(bf16[2048,4,256]{2,1,0:T(4,128)(2,1)} %copy.152), calls=%async_computation.11 | async-start | bytes 8388608 | tf_op jit(solution)/shard_map/all_to_all | solution.py:331
  (65 other events, 1541.0 us)
Sparse Core Ops, SparseCore 0:
  10.2 83.4 all-gather.12
  95.6 52.9 all-gather.14
  191.3 80.5 all-gather.16
  273.9 78.7 all-gather.32
  384.6 69.4 reduce-scatter.10
  456.2 218.1 all-gather.20
  677.0 52.5 all-gather.18
  773.5 71.3 reduce-scatter.12
  851.9 54.3 all-gather.22
  960.6 71.2 reduce-scatter.14
  1039.2 54.3 all-gather.24
  1156.3 76.7 reduce-scatter.16
  1235.4 77.2 reduce-scatter.18
  1369.5 280.7 reduce-scatter.22
  1819.0 204.2 reduce-scatter.24
  2025.1 167.4 all-gather.26
  2260.1 205.2 reduce-scatter.26
  2467.2 167.4 all-gather.28
  2702.2 205.2 reduce-scatter.28
  2909.3 167.4 all-gather.30
  3080.6 71.3 reduce-scatter.20
where the time goes:
time: 3270 us; the launch traced here: 3260 us
  waiting for transfers between devices  2430 us (74%)
  matrix products  425 us (13%)
  blocking collectives  185 us (6%)
  local copies, waits for them, and re-layouts  110 us (3%)
  other arithmetic  87.3 us (3%)
    reduce_scatter x3, waiting for transfers between devices, shards(): lax.psum_scatter(jnp.einsum('rul,sul->rus', chosen, unit_piece, preferred...  615 us
    all_gather x3, waiting for transfers between devices, shards(): gram_full = lax.all_gather(gram_part, 'fsdp', axis=0, tiled=True)  496 us
    all_gather x2, waiting for transfers between devices, along_ctx(): lax.all_gather(second_part, 'ctx', axis=1, tiled=True)  290 us
    reduce_scatter x1, waiting for transfers between devices, shards(): lax.psum_scatter(jnp.concatenate([projections, output_rows, gate_rows, up...  274 us
    all_gather x4, waiting for transfers between devices, token_rows(): return lax.all_gather(operand, 'fsdp', axis=0, tiled=True)  219 us
    reduce_scatter x4, waiting for transfers between devices, token_sums(): lax.psum_scatter(operand.astype(jnp.bfloat16), 'fsdp', scatter_dimension=...  218 us
    all_gather x2, waiting for transfers between devices, along_ctx(): lax.all_gather(first_part, 'ctx', axis=1, tiled=True)  146 us
    all_to_all x1, blocking collectives, shards(): lax.all_to_all(unit_start, 'ctx', split_axis=1, concat_axis=0, tiled=True)  95.7 us
  transfers between devices with their start and end apart: 22, of which 22 were waited for; matrix products, arithmetic and copies ran while one was open for 5% of the time, Pallas kernels for 0%

commit v1 on v0

v1 whole, which is shorter than its diff:
```python
import functools
import jax
import jax.numpy as jnp
from jax import lax
from jax.sharding import PartitionSpec as P

NS_STEPS = 3
HEAD_DIM = 128
UNITS_ATTN = 4

epsilon = 1e-06
rope_theta = 500000.0
quintic_one = 3.4445
quintic_two = -4.775
quintic_three = 2.0315
momentum = 0.95
muon_rate = 1.0
gain_rate = 0.0005
BOTH = ("ctx", "fsdp")
bf16 = jnp.bfloat16
f32 = jnp.float32


def dot(a, b, ca, cb):
    return lax.dot_general(a, b, (((ca,), (cb,)), ((), ())), preferred_element_type=f32)


def token_rows(operand):
    return lax.all_gather(operand, "fsdp", axis=0, tiled=True)


def token_sums(operand):
    return lax.psum_scatter(operand.astype(bf16), "fsdp", scatter_dimension=0, tiled=True).astype(f32)


def norm_stats(first_sum, second_sum):
    got = lax.all_gather(jnp.stack([first_sum, second_sum]), "fsdp", axis=0, tiled=False)
    total = jnp.sum(got, axis=0)
    return total[0], total[1]


def rms_back(upstream, normed, inv_scale):
    return inv_scale * (upstream - normed * jnp.mean(upstream * normed, axis=-1, keepdims=True))


def rotary_tables(slot_order):
    half_dim = HEAD_DIM // 2
    inverse = rope_theta ** (-(jnp.arange(half_dim, dtype=f32) * 2.0) / HEAD_DIM)
    angles = slot_order.astype(f32)[..., None] * inverse
    angles = jnp.concatenate([angles, angles], axis=-1)
    return (jnp.cos(angles)[..., None, :], jnp.sin(angles)[..., None, :])


def rotate(operand, cosine_table, sine_table):
    half_dim = operand.shape[-1] // 2
    flipped = jnp.concatenate([-operand[..., half_dim:], operand[..., :half_dim]], axis=-1)
    return operand * cosine_table + flipped * sine_table


def unrotate(upstream, cosine_table, sine_table):
    half_dim = upstream.shape[-1] // 2
    shifted = upstream * sine_table
    flipped = jnp.concatenate([shifted[..., half_dim:], -shifted[..., :half_dim]], axis=-1)
    return upstream * cosine_table + flipped


def masked_scores(query_rows, key_rows, pos):
    scores = jnp.einsum("gqhe,gkhe->ghqk", query_rows, key_rows, preferred_element_type=f32)
    causal = pos[:, None, :, None] >= pos[:, None, None, :]
    return jnp.where(causal, scores, -1e30)


def attend(query_rows, key_rows, value_rows, pos):
    scores = masked_scores(query_rows, key_rows, pos)
    row_max = jnp.max(scores, axis=-1, keepdims=True)
    weights = jnp.exp(scores - row_max)
    row_total = jnp.sum(weights, axis=-1, keepdims=True)
    probabilities = (weights / row_total).astype(bf16)
    attn_mixed = jnp.einsum("ghqk,gkhe->gqhe", probabilities, value_rows, preferred_element_type=f32)
    return attn_mixed.astype(bf16), row_max + jnp.log(row_total)


def attend_back(query_rows, key_rows, value_rows, pos, grad_mixed, log_total):
    scores = masked_scores(query_rows, key_rows, pos)
    probabilities = jnp.exp(scores - log_total)
    grad_probs = jnp.einsum("gqhe,gkhe->ghqk", grad_mixed, value_rows, preferred_element_type=f32)
    grad_value = jnp.einsum(
        "ghqk,gqhe->gkhe", probabilities.astype(bf16), grad_mixed, preferred_element_type=f32
    )
    inner_sum = jnp.sum(grad_probs * probabilities, axis=-1, keepdims=True)
    grad_scores = (probabilities * (grad_probs - inner_sum)).astype(bf16)
    grad_query = jnp.einsum("ghqk,gkhe->gqhe", grad_scores, key_rows, preferred_element_type=f32)
    grad_key = jnp.einsum("ghqk,gqhe->gkhe", grad_scores, query_rows, preferred_element_type=f32)
    return grad_query, grad_key, grad_value


def shards(C, F, layer_input, cotangent, positions, w_attn, w_ffn, gains, mom_attn, mom_ffn, gain_mom):
    z = lax.axis_index("ctx")
    f = lax.axis_index("fsdp")
    local_rows, width = layer_input.shape[1], layer_input.shape[2]
    seq_total, seq_length = positions.shape
    dz, head_cols = w_attn.shape[1], w_attn.shape[2]
    local_heads = head_cols // HEAD_DIM
    block_count = w_ffn.shape[2]
    per = seq_total // C
    hidden_cols = block_count * head_cols
    units = UNITS_ATTN + 3 * block_count
    parts = C * F // units
    ring = [(i, (i + 1) % C) for i in range(C)]
    out_pairs = [
        (zi * F + fi, (fi // per) * F + (fi % per) * C + zi) for zi in range(C) for fi in range(F)
    ]
    back_pairs = [(b, a) for a, b in out_pairs]

    def cyc(a):
        blocks = [
            lax.dynamic_slice_in_dim(a, lax.rem(z - k + C, C) * dz, dz, a.ndim - 1) for k in range(C)
        ]
        return jnp.concatenate(blocks, axis=-1)

    def to_layer(a):
        return cyc(lax.ppermute(a, BOTH, out_pairs))

    def from_layer(a):
        return lax.ppermute(cyc(a), BOTH, back_pairs)

    def ring_gather(shard):
        held = [shard]
        for _ in range(C - 1):
            held.append(lax.ppermute(held[-1], "ctx", ring))
        return jnp.concatenate(held, axis=0), held[-1]

    def after(a, b):
        return lax.optimization_barrier((a, b))[0]

    def ring_scatter(lhs, rhs):
        def part(k):
            return dot(lhs[:, k * dz : (k + 1) * dz], rhs, 0, 0)

        run = part(1).astype(bf16)
        for k in range(2, C + 1):
            got = lax.ppermute(run, "ctx", ring)
            total = got.astype(f32) + part(k % C)
            run = total.astype(bf16)
        return total

    own_input = to_layer(layer_input.reshape(local_rows, width))
    input_all = token_rows(own_input)
    wq = jnp.concatenate([w_attn[0], w_attn[1], w_attn[2]], axis=1)
    w_qkv, last = ring_gather(wq)
    w_out, last = ring_gather(after(w_attn[3], last))
    ffn_flat = w_ffn.reshape(3, dz, hidden_cols)
    w_gate, last = ring_gather(after(ffn_flat[0], last))
    w_up, last = ring_gather(after(ffn_flat[1], last))
    w_down, last = ring_gather(after(ffn_flat[2], last))
    own_grad = to_layer(after(cotangent.reshape(local_rows, width), last))

    gain_rows = cyc(gains[2:4])
    gain_attn, gain_mlp = gain_rows[0], gain_rows[1]
    gain_query = lax.dynamic_slice_in_dim(gains[0], f * head_cols, head_cols)
    gain_key = lax.dynamic_slice_in_dim(gains[1], f * head_cols, head_cols)
    pos = lax.dynamic_slice_in_dim(positions, z * per, per, 0)
    cosine_table, sine_table = rotary_tables(pos)

    projected = dot(input_all, w_qkv, 1, 0)
    query_raw = projected[:, :head_cols]
    key_raw = projected[:, head_cols : 2 * head_cols]
    value_raw = projected[:, 2 * head_cols :]
    query_total, key_total = norm_stats(
        jnp.sum(query_raw * query_raw, axis=-1), jnp.sum(key_raw * key_raw, axis=-1)
    )
    query_scale = lax.rsqrt(query_total / width + epsilon)[..., None]
    key_scale = lax.rsqrt(key_total / width + epsilon)[..., None]
    query_hat = query_raw * query_scale
    key_hat = key_raw * key_scale
    head_shape = (per, seq_length, local_heads, HEAD_DIM)
    query_rows = (
        rotate((query_hat * gain_query).reshape(head_shape), cosine_table, sine_table)
        * HEAD_DIM ** (-0.5)
    ).astype(bf16)
    key_rows = rotate((key_hat * gain_key).reshape(head_shape), cosine_table, sine_table).astype(bf16)
    value_rows = value_raw.astype(bf16).reshape(head_shape)
    attn_mixed, log_total = attend(query_rows, key_rows, value_rows, pos)
    attn_mixed = attn_mixed.reshape(per * seq_length, head_cols)
    attn_out = token_sums(dot(attn_mixed, w_out, 1, 1))
    attn_scale = lax.rsqrt(jnp.mean(attn_out * attn_out, axis=-1, keepdims=True) + epsilon)
    attn_hat = attn_out * attn_scale
    hidden_in = own_input.astype(f32) + attn_hat * gain_attn
    mlp_all = token_rows(hidden_in.astype(bf16))
    gate_value = dot(mlp_all, w_gate, 1, 0)
    up_value = dot(mlp_all, w_up, 1, 0)
    gate_sigmoid = jax.nn.sigmoid(gate_value)
    gate_act = gate_value * gate_sigmoid
    hidden = (gate_act * up_value).astype(bf16)
    mlp_out = token_sums(dot(hidden, w_down, 1, 1))
    mlp_scale = lax.rsqrt(jnp.mean(mlp_out * mlp_out, axis=-1, keepdims=True) + epsilon)
    mlp_hat = mlp_out * mlp_scale
    result = from_layer((hidden_in + mlp_hat * gain_mlp).astype(bf16))

    grad_out = own_grad.astype(f32)
    grad_mlp_gain = jnp.sum(grad_out * mlp_hat, axis=0)
    grad_mlp = rms_back(grad_out * gain_mlp, mlp_hat, mlp_scale).astype(bf16)
    grad_mlp_all = token_rows(grad_mlp)
    grad_hidden = dot(grad_mlp_all, w_down, 1, 0)
    grad_up = (grad_hidden * gate_act).astype(bf16)
    grad_gate = (
        grad_hidden * up_value * gate_sigmoid * (1.0 + gate_value * (1.0 - gate_sigmoid))
    ).astype(bf16)
    back_part = dot(grad_gate, w_gate, 1, 1) + dot(grad_up, w_up, 1, 1)
    g_down = ring_scatter(grad_mlp_all, hidden)
    g_gate = ring_scatter(mlp_all, grad_gate)
    g_up = ring_scatter(mlp_all, grad_up)
    grad_resid = grad_out + token_sums(back_part)
    grad_attn_gain = jnp.sum(grad_resid * attn_hat, axis=0)
    grad_attn_out = rms_back(grad_resid * gain_attn, attn_hat, attn_scale).astype(bf16)
    grad_attn_all = token_rows(grad_attn_out)
    grad_mixed = dot(grad_attn_all, w_out, 1, 0).astype(bf16)
    g_out = ring_scatter(grad_attn_all, attn_mixed)
    grad_query, grad_key, grad_value = attend_back(
        query_rows, key_rows, value_rows, pos, grad_mixed.reshape(head_shape), log_total
    )
    flat = (per * seq_length, head_cols)
    grad_query_norm = unrotate(grad_query * HEAD_DIM ** (-0.5), cosine_table, sine_table).reshape(flat)
    grad_key_norm = unrotate(grad_key, cosine_table, sine_table).reshape(flat)
    query_gain_cols = jnp.sum(grad_query_norm * query_hat, axis=0)
    key_gain_cols = jnp.sum(grad_key_norm * key_hat, axis=0)
    query_weighted = grad_query_norm * gain_query
    key_weighted = grad_key_norm * gain_key
    query_inner, key_inner = norm_stats(
        jnp.sum(query_weighted * query_hat, axis=-1), jnp.sum(key_weighted * key_hat, axis=-1)
    )
    grad_query_raw = query_scale * (query_weighted - query_hat * (query_inner / width)[..., None])
    grad_key_raw = key_scale * (key_weighted - key_hat * (key_inner / width)[..., None])
    grad_projected = jnp.concatenate(
        [grad_query_raw.astype(bf16), grad_key_raw.astype(bf16), grad_value.reshape(flat).astype(bf16)],
        axis=1,
    )
    g_qkv = ring_scatter(input_all, grad_projected)
    grad_input = grad_resid + token_sums(dot(grad_projected, w_qkv, 1, 1))
    grad_input = from_layer(grad_input.astype(bf16)).astype(f32)

    zero = jnp.zeros((width,), f32)
    natural = cyc(jnp.stack([grad_attn_gain, grad_mlp_gain]))
    gain_local = jnp.stack(
        [
            lax.dynamic_update_slice(zero, query_gain_cols, (f * head_cols,)),
            lax.dynamic_update_slice(zero, key_gain_cols, (f * head_cols,)),
            natural[0],
            natural[1],
        ]
    )
    gain_total = jnp.sum(lax.all_gather(gain_local, BOTH, axis=0, tiled=False), axis=0)

    grad_attn = jnp.stack(
        [g_qkv[:, :head_cols], g_qkv[:, head_cols : 2 * head_cols], g_qkv[:, 2 * head_cols :], g_out]
    )
    grad_ffn = jnp.stack([g_gate, g_up, g_down]).reshape(3, dz, block_count, head_cols)
    new_attn = momentum * mom_attn + grad_attn
    new_ffn = momentum * mom_ffn + grad_ffn
    send = jnp.concatenate(
        [
            new_attn.astype(bf16),
            jnp.transpose(new_ffn.astype(bf16), (0, 2, 1, 3)).reshape(3 * block_count, dz, head_cols),
        ],
        axis=0,
    ).reshape(C * F, dz // parts, head_cols)
    got = lax.all_to_all(send, BOTH, split_axis=0, concat_axis=0, tiled=True)
    own = jnp.transpose(got.reshape(C, F, dz // parts, head_cols), (0, 2, 1, 3)).reshape(
        C * dz // parts, F * head_cols
    )

    def peers(a):
        out = [a]
        for s in range(1, parts):
            pairs = [(i, i - i % parts + (i + parts - s) % parts) for i in range(C * F)]
            out.append(lax.ppermute(a, BOTH, pairs))
        return out

    own32 = own.astype(f32)
    square = jnp.sum(own32 * own32)
    total = sum(peers(square.reshape(1, 1)))
    inv = 1.0 / (jnp.sqrt(total) + 1e-07)
    for iteration in range(NS_STEPS):
        factor = inv if iteration == 0 else 1.0
        every = peers(own)
        gram = [(dot(own, b, 1, 1) * (factor * factor)).astype(bf16) for b in every]
        product = sum(dot(g, b, 1, 0) for g, b in zip(gram, every)) * factor
        product_all = peers(product.astype(bf16))
        product_two = sum(dot(g, b, 1, 0) for g, b in zip(gram, product_all))
        own = (
            quintic_one * factor * own.astype(f32) + quintic_two * product + quintic_three * product_two
        ).astype(bf16)
    home = jnp.transpose(own.reshape(C, dz // parts, F, head_cols), (0, 2, 1, 3)).reshape(
        C * F, dz // parts, head_cols
    )
    steps = lax.all_to_all(home, BOTH, split_axis=0, concat_axis=0, tiled=True)
    steps = -muon_rate * steps.astype(f32).reshape(units, dz, head_cols)
    step_attn = steps[:UNITS_ATTN]
    step_ffn = jnp.transpose(
        steps[UNITS_ATTN:].reshape(3, block_count, dz, head_cols), (0, 2, 1, 3)
    )
    new_gain_mom = momentum * gain_mom + gain_total
    return (
        result.reshape(layer_input.shape),
        grad_input.reshape(layer_input.shape),
        grad_attn,
        grad_ffn,
        gain_total,
        new_attn,
        new_ffn,
        new_gain_mom,
        step_attn,
        step_ffn,
        -gain_rate * new_gain_mom,
    )


def solution(mesh):
    tokens = P("fsdp", "ctx", None)
    attn = P(None, "ctx", "fsdp")
    ffn = P(None, "ctx", None, "fsdp")
    in_specs = (tokens, tokens, P(), attn, ffn, P(), attn, ffn, P())
    out_specs = (tokens, tokens, attn, ffn, P(), attn, ffn, P(), attn, ffn, P())
    body = functools.partial(shards, mesh.shape["ctx"], mesh.shape["fsdp"])
    return jax.shard_map(body, mesh=mesh, in_specs=in_specs, out_specs=out_specs, check_vma=False)
```

time: 3270 us -> 1750 us (0.54)
  waiting for transfers between devices: 2430 us -> 921 us
  starting transfers between devices: 6.94 us -> 102 us
  blocking collectives: 185 us -> 113 us
  matrix products: 425 us -> 362 us
    reduce_scatter x10 -> x4, waiting for transfers between devices: 1220 us -> 258 us  [token_sums(): lax.psum_scatter(operand.astype(bf16), 'fsdp', scatter_dimension=0, tiled...]
    all_gather x7 -> x1, waiting for transfers between devices: 932 us -> 101 us  [shards(): lax.all_gather(gain_local, BOTH, axis=0, tiled=False)]
    ppermute x0 -> x41, waiting for transfers between devices: none -> 507 us  [the longest x15 276 us: ring_gather(): held.append(lax.ppermute(held[-1], 'ctx', ring))]
    all_gather x4, waiting for transfers between devices: 219 us -> 54.5 us  [token_rows(): return lax.all_gather(operand, 'fsdp', axis=0, tiled=True)]
    ppermute x0 -> x41, starting transfers between devices: none -> 98.1 us  [the longest x15 84.9 us: ring_gather(): held.append(lax.ppermute(held[-1], 'ctx', ring))]
    psum x3 -> x0, blocking collectives: 89.8 us -> none  [the longest x2 48 us: norm_stats(): return lax.psum((first_sum, second_sum), 'fsdp')]
    all_to_all x1, waiting for transfers between devices: 57.3 us -> 0.01 us  [shards(): steps = lax.all_to_all(home, BOTH, split_axis=0, concat_axis=0, tiled=True)]
    unnamed x122 -> x240, local copies, waits for them, and re-layouts: 24.2 us -> 62.8 us
  transfers between devices with their start and end apart: 22 -> 51, of which waited for: 22 -> 36; matrix products, arithmetic and copies ran while one was open for 5% -> 13% of each run, Pallas kernels for 0% -> 0%
where the time goes in v1:
time: 1750 us; the launch traced here: 1720 us
  waiting for transfers between devices  921 us (53%)
  matrix products  362 us (21%)
  local copies, waits for them, and re-layouts  117 us (7%)
  blocking collectives  113 us (6%)
  starting transfers between devices  102 us (6%)
  other arithmetic  86.1 us (5%)
    dot_general x48, matrix products, dot(): lax.dot_general(a, b, (((ca,), (cb,)), ((), ())), preferred_element_type=...  328 us
    ppermute x15, waiting for transfers between devices, ring_gather(): held.append(lax.ppermute(held[-1], 'ctx', ring))  276 us
    reduce_scatter x4, waiting for transfers between devices, token_sums(): lax.psum_scatter(operand.astype(bf16), 'fsdp', scatter_dimension=0, tiled...  258 us
    ppermute x15, waiting for transfers between devices, ring_scatter(): got = lax.ppermute(run, 'ctx', ring)  226 us
    all_gather x1, waiting for transfers between devices, shards(): lax.all_gather(gain_local, BOTH, axis=0, tiled=False)  101 us
    all_to_all x1, blocking collectives, shards(): got = lax.all_to_all(send, BOTH, split_axis=0, concat_axis=0, tiled=True)  95.4 us
    ppermute x15, starting transfers between devices, ring_gather(): held.append(lax.ppermute(held[-1], 'ctx', ring))  84.9 us
    unnamed x240, local copies, waits for them, and re-layouts  62.8 us
  transfers between devices with their start and end apart: 51, of which 36 were waited for; matrix products, arithmetic and copies ran while one was open for 13% of the time, Pallas kernels for 0%

profile of v1, /device:TPU:0, one launch (start us, length us, event | category | flops | bytes accessed | tf_op | source)
XLA Modules:
  0.0 1718.4 jit_solution(11273401963727962453)
XLA Ops:
  11.6 80.1 %collective-permute-start.1 = (bf16[512,768]{1,0:T(8,128)(2,1)S(1)}, bf16[512,768]{1,0:T(8,128)(2,1)S(1)}, u32[]{:S(2)}, u32[]{:S(2)}) collective-permute-start(bf16[512,768]{1,0:T(8,128)(2,1)S(1)} %pad_maximum_fusion.9), channel_id=1, source_target_pairs={{0,8},{8,16},{16,24},{24,0},{1,9},{9,17},{17,25},{25,1},{2,10},{10... | collective-permute-start | bytes 2359304 | tf_op jit(solution)/shard_map/ppermute | solution.py:130
  257.1 68.4 %reduce-scatter.5.cloned.1.call-done = bf16[256,2048]{1,0:T(8,128)(2,1)} async-done(((bf16[2048,2048]{1,0:T(8,128)(2,1)}), bf16[256,2048]{1,0:T(8,128)(2,1)}) %reduce-scatter.5.cloned.1.call-update) | async-done | bytes 1048592 | tf_op jit(solution)/shard_map/reduce_scatter | solution.py:33
  334.4 25.2 %collective-permute-done.7 = bf16[512,1024]{1,0:T(8,128)(2,1)S(1)} collective-permute-done((bf16[512,1024]{1,0:T(8,128)(2,1)S(1)}, bf16[512,1024]{1,0:T(8,128)(2,1)S(1)}, u32[]{:S(2)}, u32[]{:S(2)}) %collective-permute-start.7) | collective-permute-done | bytes 1048608 | tf_op jit(solution)/shard_map/ppermute | solution.py:130
  359.6 25.8 %collective-permute-done.8 = bf16[512,1024]{1,0:T(8,128)(2,1)S(1)} collective-permute-done((bf16[512,1024]{1,0:T(8,128)(2,1)S(1)}, bf16[512,1024]{1,0:T(8,128)(2,1)S(1)}, u32[]{:S(2)}, u32[]{:S(2)}) %collective-permute-start.8) | collective-permute-done | bytes 1048608 | tf_op jit(solution)/shard_map/ppermute | solution.py:130
  385.7 24.7 %collective-permute-done.9 = bf16[512,1024]{1,0:T(8,128)(2,1)S(1)} collective-permute-done((bf16[512,1024]{1,0:T(8,128)(2,1)S(1)}, bf16[512,1024]{1,0:T(8,128)(2,1)S(1)}, u32[]{:S(2)}, u32[]{:S(2)}) %collective-permute-start.9) | collective-permute-done | bytes 1048608 | tf_op jit(solution)/shard_map/ppermute | solution.py:130
  410.4 24.0 %collective-permute-done.10 = bf16[512,1024]{1,0:T(8,128)(2,1)S(1)} collective-permute-done((bf16[512,1024]{1,0:T(8,128)(2,1)S(1)}, bf16[512,1024]{1,0:T(8,128)(2,1)S(1)}, u32[]{:S(2)}, u32[]{:S(2)}) %collective-permute-start.10) | collective-permute-done | bytes 1048608 | tf_op jit(solution)/shard_map/ppermute | solution.py:130
  434.4 23.3 %collective-permute-done.11 = bf16[512,1024]{1,0:T(8,128)(2,1)S(1)} collective-permute-done((bf16[512,1024]{1,0:T(8,128)(2,1)S(1)}, bf16[512,1024]{1,0:T(8,128)(2,1)S(1)}, u32[]{:S(2)}, u32[]{:S(2)}) %collective-permute-start.11) | collective-permute-done | bytes 1048608 | tf_op jit(solution)/shard_map/ppermute | solution.py:130
  457.9 23.1 %collective-permute-done.12 = bf16[512,1024]{1,0:T(8,128)(2,1)S(1)} collective-permute-done((bf16[512,1024]{1,0:T(8,128)(2,1)S(1)}, bf16[512,1024]{1,0:T(8,128)(2,1)S(1)}, u32[]{:S(2)}, u32[]{:S(2)}) %collective-permute-start.12) | collective-permute-done | bytes 1048608 | tf_op jit(solution)/shard_map/ppermute | solution.py:130
  481.0 23.3 %collective-permute-done.13 = bf16[512,1024]{1,0:T(8,128)(2,1)S(1)} collective-permute-done((bf16[512,1024]{1,0:T(8,128)(2,1)S(1)}, bf16[512,1024]{1,0:T(8,128)(2,1)S(1)}, u32[]{:S(2)}, u32[]{:S(2)}) %collective-permute-start.13) | collective-permute-done | bytes 1048608 | tf_op jit(solution)/shard_map/ppermute | solution.py:130
  504.6 23.1 %collective-permute-done.14 = bf16[512,1024]{1,0:T(8,128)(2,1)S(1)} collective-permute-done((bf16[512,1024]{1,0:T(8,128)(2,1)S(1)}, bf16[512,1024]{1,0:T(8,128)(2,1)S(1)}, u32[]{:S(2)}, u32[]{:S(2)}) %collective-permute-start.14) | collective-permute-done | bytes 1048608 | tf_op jit(solution)/shard_map/ppermute | solution.py:130
  593.7 84.4 %reduce-scatter.7.cloned.1.call-done = bf16[256,2048]{1,0:T(8,128)(2,1)} async-done(((bf16[2048,2048]{1,0:T(8,128)(2,1)}), bf16[256,2048]{1,0:T(8,128)(2,1)}) %reduce-scatter.7.cloned.1.call-update) | async-done | bytes 1048592 | tf_op jit(solution)/shard_map/reduce_scatter | solution.py:33
  685.1 54.5 %all-gather.16.cloned.1.call-done = bf16[2048,2048]{1,0:T(8,128)(2,1)} async-done(((bf16[256,2048]{1,0:T(8,128)(2,1)}), bf16[2048,2048]{1,0:T(8,128)(2,1)}) %all-gather.16.cloned.1.call-update) | async-done | bytes 8388624 | tf_op jit(solution)/shard_map/all_gather | solution.py:29
  739.6 20.6 %multiply_convert_fusion.2 = (bf16[2048,1024]{1,0:T(8,128)(2,1)}, bf16[2048,1024]{1,0:T(8,128)(2,1)}) fusion(f32[2048,1024]{1,0:T(8,128)} %fusion.148, f32[2048,1024]{1,0:T(8,128)} %get-tuple-element.131, bf16[2048,2048]{1,0:T(8,128)(2,1)} %all-gather.16.cloned.1.call-done, bf16[2048,1024]{1,0:T(8,128)(2,1)} %constant_dynamic-update-slice_fusion.12), kind=kOutput, calls=%fused_computation.18 | convolution fusion | flops 8617197568 | bytes 37748736 | tf_op jit(solution)/shard_map/dot_general | solution.py:25
  790.5 71.4 %reduce-scatter.9.cloned.1.call-done = bf16[256,2048]{1,0:T(8,128)(2,1)} async-done(((bf16[2048,2048]{1,0:T(8,128)(2,1)}), bf16[256,2048]{1,0:T(8,128)(2,1)}) %reduce-scatter.9.cloned.1.call-update) | async-done | bytes 1048592 | tf_op jit(solution)/shard_map/reduce_scatter | solution.py:33
  904.0 20.0 %collective-permute-done.28 = bf16[512,1024]{1,0:T(8,128)(2,1)S(1)} collective-permute-done((bf16[512,1024]{1,0:T(8,128)(2,1)S(1)}, bf16[512,1024]{1,0:T(8,128)(2,1)S(1)}, u32[]{:S(2)}, u32[]{:S(2)}) %collective-permute-start.28) | collective-permute-done | bytes 1048608 | tf_op jit(solution)/shard_map/ppermute | solution.py:142
  926.5 20.0 %collective-permute-done.25 = bf16[512,1024]{1,0:T(8,128)(2,1)S(1)} collective-permute-done((bf16[512,1024]{1,0:T(8,128)(2,1)S(1)}, bf16[512,1024]{1,0:T(8,128)(2,1)S(1)}, u32[]{:S(2)}, u32[]{:S(2)}) %collective-permute-start.25) | collective-permute-done | bytes 1048608 | tf_op jit(solution)/shard_map/ppermute | solution.py:142
  949.0 20.0 %collective-permute-done.32 = bf16[512,1024]{1,0:T(8,128)(2,1)S(1)} collective-permute-done((bf16[512,1024]{1,0:T(8,128)(2,1)S(1)}, bf16[512,1024]{1,0:T(8,128)(2,1)S(1)}, u32[]{:S(2)}, u32[]{:S(2)}) %collective-permute-start.32) | collective-permute-done | bytes 1048608 | tf_op jit(solution)/shard_map/ppermute | solution.py:142
  971.4 20.0 %collective-permute-done.29 = bf16[512,1024]{1,0:T(8,128)(2,1)S(1)} collective-permute-done((bf16[512,1024]{1,0:T(8,128)(2,1)S(1)}, bf16[512,1024]{1,0:T(8,128)(2,1)S(1)}, u32[]{:S(2)}, u32[]{:S(2)}) %collective-permute-start.29) | collective-permute-done | bytes 1048608 | tf_op jit(solution)/shard_map/ppermute | solution.py:142
  994.8 19.1 %collective-permute-done.26 = bf16[512,1024]{1,0:T(8,128)(2,1)S(1)} collective-permute-done((bf16[512,1024]{1,0:T(8,128)(2,1)S(1)}, bf16[512,1024]{1,0:T(8,128)(2,1)S(1)}, u32[]{:S(2)}, u32[]{:S(2)}) %collective-permute-start.26) | collective-permute-done | bytes 1048608 | tf_op jit(solution)/shard_map/ppermute | solution.py:142
  1207.1 21.2 %collective-permute-done.22 = bf16[512,256]{1,0:T(8,128)(2,1)S(1)} collective-permute-done((bf16[512,256]{1,0:T(8,128)(2,1)S(1)}, bf16[512,256]{1,0:T(8,128)(2,1)S(1)}, u32[]{:S(2)}, u32[]{:S(2)}) %collective-permute-start.22) | collective-permute-done | bytes 262176 | tf_op jit(solution)/shard_map/ppermute | solution.py:142
  1241.2 19.2 %collective-permute-done.24 = bf16[512,256]{1,0:T(8,128)(2,1)S(1)} collective-permute-done((bf16[512,256]{1,0:T(8,128)(2,1)S(1)}, bf16[512,256]{1,0:T(8,128)(2,1)S(1)}, u32[]{:S(2)}, u32[]{:S(2)}) %collective-permute-start.24) | collective-permute-done | bytes 262176 | tf_op jit(solution)/shard_map/ppermute | solution.py:142
  1266.9 95.4 %all_to_all.10 = bf16[32,256,256]{2,1,0:T(8,128)(2,1)S(1)} all-to-all(bf16[32,256,256]{2,1,0:T(8,128)(2,1)S(1)} %bitcast.213), channel_id=1, replica_groups=mesh['ctx'=4,'fsdp'=8] {'ctx','fsdp'}, dimensions={0} | all-to-all | bytes 8388608 | tf_op jit(solution)/shard_map/all_to_all | solution.py:267
  1539.9 34.3 %reduce-scatter.11.cloned.1.call-done = bf16[256,2048]{1,0:T(8,128)(2,1)} async-done(((bf16[2048,2048]{1,0:T(8,128)(2,1)}), bf16[256,2048]{1,0:T(8,128)(2,1)}) %reduce-scatter.11.cloned.1.call-update) | async-done | bytes 1048592 | tf_op jit(solution)/shard_map/reduce_scatter | solution.py:33
  1593.8 101.1 %all-gather.20.cloned.1.call-done = f32[32,4,2048]{2,1,0:T(4,128)} async-done(((f32[1,4,2048]{2,1,0:T(4,128)}), f32[32,4,2048]{2,1,0:T(4,128)}) %all-gather.20.cloned.1.call-update) | async-done | bytes 1048592 | tf_op jit(solution)/shard_map/all_gather | solution.py:252
  (486 shorter events, 758.8 us)
Async XLA Ops:
  7.2 169.6 %all-gather.12.cloned.1.call-start = ((), (), s32[]{:S(2)}) async-start(), calls=%async_computation.6 | async-start | bytes 9437184 | tf_op jit(solution)/shard_map/all_gather | solution.py:29
  11.4 314.1 %reduce-scatter.5.cloned.1.call-start = ((), (), s32[]{:S(2)}) async-start(), calls=%async_computation.7 | async-start | bytes 9437184 | tf_op jit(solution)/shard_map/reduce_scatter | solution.py:33
  11.6 97.5 %collective-permute-start.1 = (bf16[512,768]{1,0:T(8,128)(2,1)S(1)}, bf16[512,768]{1,0:T(8,128)(2,1)S(1)}, u32[]{:S(2)}, u32[]{:S(2)}) collective-permute-start(bf16[512,768]{1,0:T(8,128)(2,1)S(1)} %pad_maximum_fusion.9), channel_id=1, source_target_pairs={{0,8},{8,16},{16,24},{24,0},{1,9},{9,17},{17,25},{25,1},{2,10},{10... | collective-permute-start | bytes 2359304 | tf_op jit(solution)/shard_map/ppermute | solution.py:130
  256.3 292.1 %all-gather.14.cloned.1.call-start = ((), (), s32[]{:S(2)}) async-start(), calls=%async_computation.8 | async-start | bytes 9437184 | tf_op jit(solution)/shard_map/all_gather | solution.py:29
  329.7 348.5 %reduce-scatter.7.cloned.1.call-start = ((), (), s32[]{:S(2)}) async-start(), calls=%async_computation.9 | async-start | bytes 9437184 | tf_op jit(solution)/shard_map/reduce_scatter | solution.py:33
  591.6 148.0 %all-gather.16.cloned.1.call-start = ((), (), s32[]{:S(2)}) async-start(), calls=%async_computation.10 | async-start | bytes 9437184 | tf_op jit(solution)/shard_map/all_gather | solution.py:29
  685.1 176.8 %reduce-scatter.9.cloned.1.call-start = ((), (), s32[]{:S(2)}) async-start(), calls=%async_computation.11 | async-start | bytes 9437184 | tf_op jit(solution)/shard_map/reduce_scatter | solution.py:33
  790.4 304.8 %all-gather.18.cloned.1.call-start = ((), (), s32[]{:S(2)}) async-start(), calls=%async_computation.12 | async-start | bytes 9437184 | tf_op jit(solution)/shard_map/all_gather | solution.py:29
  868.2 706.0 %reduce-scatter.11.cloned.1.call-start = ((), (), s32[]{:S(2)}) async-start(), calls=%async_computation.13 | async-start | bytes 9437184 | tf_op jit(solution)/shard_map/reduce_scatter | solution.py:33
  873.7 27.9 %collective-permute-start.31 = (bf16[512,1024]{1,0:T(8,128)(2,1)S(1)}, bf16[512,1024]{1,0:T(8,128)(2,1)S(1)}, u32[]{:S(2)}, u32[]{:S(2)}) collective-permute-start(bf16[512,1024]{1,0:T(8,128)(2,1)S(1)} %fusion.88), channel_id=1, source_target_pairs={{0,8},{8,16},{16,24},{24,0},{1,9},{9,17},{17,25},{25,1},{2,10},{10... | collective-permute-start | bytes 3145736 | tf_op jit(solution)/shard_map/ppermute | solution.py:142
  880.4 43.6 %collective-permute-start.28 = (bf16[512,1024]{1,0:T(8,128)(2,1)S(1)}, bf16[512,1024]{1,0:T(8,128)(2,1)S(1)}, u32[]{:S(2)}, u32[]{:S(2)}) collective-permute-start(bf16[512,1024]{1,0:T(8,128)(2,1)S(1)} %fusion.85), channel_id=1, source_target_pairs={{0,8},{8,16},{16,24},{24,0},{1,9},{9,17},{17,25},{25,1},{2,10},{10... | collective-permute-start | bytes 3145736 | tf_op jit(solution)/shard_map/ppermute | solution.py:142
  884.4 62.2 %collective-permute-start.25 = (bf16[512,1024]{1,0:T(8,128)(2,1)S(1)}, bf16[512,1024]{1,0:T(8,128)(2,1)S(1)}, u32[]{:S(2)}, u32[]{:S(2)}) collective-permute-start(bf16[512,1024]{1,0:T(8,128)(2,1)S(1)} %fusion.82), channel_id=1, source_target_pairs={{0,8},{8,16},{16,24},{24,0},{1,9},{9,17},{17,25},{25,1},{2,10},{10... | collective-permute-start | bytes 3145736 | tf_op jit(solution)/shard_map/ppermute | solution.py:142
  904.0 65.0 %collective-permute-start.32 = (bf16[512,1024]{1,0:T(8,128)(2,1)S(1)}, bf16[512,1024]{1,0:T(8,128)(2,1)S(1)}, u32[]{:S(2)}, u32[]{:S(2)}) collective-permute-start(bf16[512,1024]{1,0:T(8,128)(2,1)S(1)} %add_convert_fusion.5), channel_id=1, source_target_pairs={{0,8},{8,16},{16,24},{24,0},{1,9},{9,17},{17,25},{25,1},{2,10},{10... | collective-permute-start | bytes 3145736 | tf_op jit(solution)/shard_map/ppermute | solution.py:142
  926.4 65.0 %collective-permute-start.29 = (bf16[512,1024]{1,0:T(8,128)(2,1)S(1)}, bf16[512,1024]{1,0:T(8,128)(2,1)S(1)}, u32[]{:S(2)}, u32[]{:S(2)}) collective-permute-start(bf16[512,1024]{1,0:T(8,128)(2,1)S(1)} %add_convert_fusion.7), channel_id=1, source_target_pairs={{0,8},{8,16},{16,24},{24,0},{1,9},{9,17},{17,25},{25,1},{2,10},{10... | collective-permute-start | bytes 3145736 | tf_op jit(solution)/shard_map/ppermute | solution.py:142
  948.9 65.0 %collective-permute-start.26 = (bf16[512,1024]{1,0:T(8,128)(2,1)S(1)}, bf16[512,1024]{1,0:T(8,128)(2,1)S(1)}, u32[]{:S(2)}, u32[]{:S(2)}) collective-permute-start(bf16[512,1024]{1,0:T(8,128)(2,1)S(1)} %add_convert_fusion.9), channel_id=1, source_target_pairs={{0,8},{8,16},{16,24},{24,0},{1,9},{9,17},{17,25},{25,1},{2,10},{10... | collective-permute-start | bytes 3145736 | tf_op jit(solution)/shard_map/ppermute | solution.py:142
  971.3 65.0 %collective-permute-start.33 = (bf16[512,1024]{1,0:T(8,128)(2,1)S(1)}, bf16[512,1024]{1,0:T(8,128)(2,1)S(1)}, u32[]{:S(2)}, u32[]{:S(2)}) collective-permute-start(bf16[512,1024]{1,0:T(8,128)(2,1)S(1)} %add_convert_fusion.4), channel_id=1, source_target_pairs={{0,8},{8,16},{16,24},{24,0},{1,9},{9,17},{17,25},{25,1},{2,10},{10... | collective-permute-start | bytes 3145736 | tf_op jit(solution)/shard_map/ppermute | solution.py:142
  994.8 64.2 %collective-permute-start.30 = (bf16[512,1024]{1,0:T(8,128)(2,1)}, bf16[512,1024]{1,0:T(8,128)(2,1)}, u32[]{:S(2)}, u32[]{:S(2)}) collective-permute-start(bf16[512,1024]{1,0:T(8,128)(2,1)} %add_convert_fusion.6), channel_id=1, source_target_pairs={{0,8},{8,16},{16,24},{24,0},{1,9},{9,17},{17,25},{25,1},{2,10},{10... | collective-permute-start | bytes 3145736 | tf_op jit(solution)/shard_map/ppermute | solution.py:142
  1017.3 63.0 %collective-permute-start.27 = (bf16[512,1024]{1,0:T(8,128)(2,1)}, bf16[512,1024]{1,0:T(8,128)(2,1)}, u32[]{:S(2)}, u32[]{:S(2)}) collective-permute-start(bf16[512,1024]{1,0:T(8,128)(2,1)} %add_convert_fusion.8), channel_id=1, source_target_pairs={{0,8},{8,16},{16,24},{24,0},{1,9},{9,17},{17,25},{25,1},{2,10},{10... | collective-permute-start | bytes 3145736 | tf_op jit(solution)/shard_map/ppermute | solution.py:142
  1231.3 29.2 %collective-permute-start.21 = (bf16[512,768]{1,0:T(8,128)(2,1)S(1)}, bf16[512,768]{1,0:T(8,128)(2,1)S(1)}, u32[]{:S(2)}, u32[]{:S(2)}) collective-permute-start(bf16[512,768]{1,0:T(8,128)(2,1)S(1)} %add_convert_fusion.11), channel_id=1, source_target_pairs={{0,8},{8,16},{16,24},{24,0},{1,9},{9,17},{17,25},{25,1},{2,10},{10... | collective-permute-start | bytes 2359304 | tf_op jit(solution)/shard_map/ppermute | solution.py:142
  1463.8 28.6 %collective-permute-start.39 = (bf16[1024,2048]{1,0:T(8,128)(2,1)}, bf16[1024,2048]{1,0:T(8,128)(2,1)}, u32[]{:S(2)}, u32[]{:S(2)}) collective-permute-start(bf16[1024,2048]{1,0:T(8,128)(2,1)} %add_convert_fusion.2), channel_id=1, source_target_pairs={{0,1},{1,0},{2,3},{3,2},{4,5},{5,4},{6,7},{7,6},{8,9},{9,8},{10,11... | collective-permute-start | bytes 12582920 | tf_op jit(solution)/shard_map/ppermute | solution.py:276
  1532.0 166.5 %all-to-all-start.1 = ((bf16[32,256,256]{2,1,0:T(8,128)(2,1)}), bf16[32,256,256]{2,1,0:T(8,128)(2,1)}, u32[]{:S(2)}, u32[]{:S(2)}) async-start(bf16[32,256,256]{2,1,0:T(8,128)(2,1)} %bitcast.212), calls=%async_computation.5 | async-start | bytes 8388608 | tf_op jit(solution)/shard_map/all_to_all | solution.py:296
  1535.9 159.0 %all-gather.20.cloned.1.call-start = ((), (), s32[]{:S(2)}) async-start(), calls=%async_computation.14 | async-start | bytes 1081344 | tf_op jit(solution)/shard_map/all_gather | solution.py:252
  1538.0 55.8 %collective-permute-start.16 = (bf16[256,2048]{1,0:T(8,128)(2,1)}, bf16[256,2048]{1,0:T(8,128)(2,1)S(1)}, u32[]{:S(2)}, u32[]{:S(2)}) collective-permute-start(bf16[256,2048]{1,0:T(8,128)(2,1)} %pad_maximum_fusion.6), channel_id=1, source_target_pairs={{0,0},{4,1},{8,2},{12,3},{16,4},{20,5},{24,6},{28,7},{1,8},{5,9},{... | collective-permute-start | bytes 3145736 | tf_op jit(solution)/shard_map/ppermute | solution.py:125
  1576.2 120.8 %collective-permute-start.18 = (bf16[256,2048]{1,0:T(8,128)(2,1)S(1)}, bf16[256,2048]{1,0:T(8,128)(2,1)S(1)}, u32[]{:S(2)}, u32[]{:S(2)}) collective-permute-start(bf16[256,2048]{1,0:T(8,128)(2,1)S(1)} %pad_maximum_fusion.8), channel_id=1, source_target_pairs={{0,0},{4,1},{8,2},{12,3},{16,4},{20,5},{24,6},{28,7},{1,8},{5,9},{... | collective-permute-start | bytes 3145736 | tf_op jit(solution)/shard_map/ppermute | solution.py:125
  (134 other events, 3782.8 us)
Sparse Core Ops, SparseCore 0:
  11.5 132.1 all-gather.11
  256.4 69.0 reduce-scatter.4
  329.8 54.3 all-gather.13
  591.7 86.3 reduce-scatter.6
  685.2 54.3 all-gather.15
  790.6 71.2 reduce-scatter.8
  868.3 54.3 all-gather.17
  1477.8 96.2 reduce-scatter.10
  1577.6 117.2 all-gather.19

commit v2 on v1

v2 whole, which is shorter than its diff:
```python
import functools
import jax
import jax.numpy as jnp
from jax import lax
from jax.experimental import pallas as pl
from jax.experimental.pallas import tpu as pltpu
from jax.sharding import PartitionSpec as P

NS_STEPS = 3
HEAD_DIM = 128
UNITS_ATTN = 4

epsilon = 1e-06
rope_theta = 500000.0
quintic_one = 3.4445
quintic_two = -4.775
quintic_three = 2.0315
momentum = 0.95
muon_rate = 1.0
gain_rate = 0.0005
BOTH = ("ctx", "fsdp")
bf16 = jnp.bfloat16
f32 = jnp.float32


def dot(a, b, ca, cb):
    return lax.dot_general(a, b, (((ca,), (cb,)), ((), ())), preferred_element_type=f32)


def token_rows(operand):
    return lax.all_gather(operand, "fsdp", axis=0, tiled=True)


def token_sums(operand):
    return lax.psum_scatter(operand.astype(bf16), "fsdp", scatter_dimension=0, tiled=True).astype(f32)


def norm_stats(first_sum, second_sum):
    got = lax.all_gather(jnp.stack([first_sum, second_sum]), "fsdp", axis=0, tiled=False)
    total = jnp.sum(got, axis=0)
    return total[0], total[1]


def rms_back(upstream, normed, inv_scale):
    return inv_scale * (upstream - normed * jnp.mean(upstream * normed, axis=-1, keepdims=True))


def rotary_tables(slot_order):
    half_dim = HEAD_DIM // 2
    inverse = rope_theta ** (-(jnp.arange(half_dim, dtype=f32) * 2.0) / HEAD_DIM)
    angles = slot_order.astype(f32)[..., None] * inverse
    angles = jnp.concatenate([angles, angles], axis=-1)
    return (jnp.cos(angles)[..., None, :], jnp.sin(angles)[..., None, :])


def rotate(operand, cosine_table, sine_table):
    half_dim = operand.shape[-1] // 2
    flipped = jnp.concatenate([-operand[..., half_dim:], operand[..., :half_dim]], axis=-1)
    return operand * cosine_table + flipped * sine_table


def unrotate(upstream, cosine_table, sine_table):
    half_dim = upstream.shape[-1] // 2
    shifted = upstream * sine_table
    flipped = jnp.concatenate([shifted[..., half_dim:], -shifted[..., :half_dim]], axis=-1)
    return upstream * cosine_table + flipped


def masked_scores(query_rows, key_rows, pos):
    scores = jnp.einsum("gqhe,gkhe->ghqk", query_rows, key_rows, preferred_element_type=f32)
    causal = pos[:, None, :, None] >= pos[:, None, None, :]
    return jnp.where(causal, scores, -1e30)


def attend(query_rows, key_rows, value_rows, pos):
    scores = masked_scores(query_rows, key_rows, pos)
    row_max = jnp.max(scores, axis=-1, keepdims=True)
    weights = jnp.exp(scores - row_max)
    row_total = jnp.sum(weights, axis=-1, keepdims=True)
    probabilities = (weights / row_total).astype(bf16)
    attn_mixed = jnp.einsum("ghqk,gkhe->gqhe", probabilities, value_rows, preferred_element_type=f32)
    return attn_mixed.astype(bf16), row_max + jnp.log(row_total)


def attend_back(query_rows, key_rows, value_rows, pos, grad_mixed, log_total):
    scores = masked_scores(query_rows, key_rows, pos)
    probabilities = jnp.exp(scores - log_total)
    grad_probs = jnp.einsum("gqhe,gkhe->ghqk", grad_mixed, value_rows, preferred_element_type=f32)
    grad_value = jnp.einsum(
        "ghqk,gqhe->gkhe", probabilities.astype(bf16), grad_mixed, preferred_element_type=f32
    )
    inner_sum = jnp.sum(grad_probs * probabilities, axis=-1, keepdims=True)
    grad_scores = (probabilities * (grad_probs - inner_sum)).astype(bf16)
    grad_query = jnp.einsum("ghqk,gkhe->gqhe", grad_scores, key_rows, preferred_element_type=f32)
    grad_key = jnp.einsum("ghqk,gqhe->gkhe", grad_scores, query_rows, preferred_element_type=f32)
    return grad_query, grad_key, grad_value


MESH = pl.DeviceIdType.MESH
VMEM_LIMIT = 60 * 1024 * 1024
ANY = pl.BlockSpec(memory_space=pl.ANY)


class Plane:
    def __init__(self):
        f = lax.axis_index("fsdp")
        self.f, self.c, self.chip = f, f % 2, f // 2
        x, y = self.chip % 2, self.chip // 2
        self.qx = self.chip + 1 - 2 * x
        self.qy = self.chip + 2 - 4 * y
        self.qd = self.qx + 2 - 4 * y
        self.fc = f + 1 - 2 * self.c
        self.fx = 2 * self.qx + self.c
        self.fy = 2 * self.qy + self.c
        self.fd = 2 * self.qd + self.c
        self.other = 1 - self.c

    def greet(self):
        barrier = pltpu.get_barrier_semaphore()
        for to in (self.fc, self.fx, self.fy):
            pl.semaphore_signal(barrier, inc=1, device_id={"fsdp": to}, device_id_type=MESH)
        pl.semaphore_wait(barrier, 3)


def remote(src, dst, send, recv, i, to, axis="fsdp"):
    return pltpu.make_async_remote_copy(
        src_ref=src, dst_ref=dst, send_sem=send.at[i], recv_sem=recv.at[i],
        device_id={axis: to}, device_id_type=MESH,
    )


def local(src, dst, sems, i):
    copy = pltpu.make_async_copy(src, dst, sems.at[i])
    copy.start()
    return copy


def nn(a, b):
    return lax.dot_general(a, b, (((1,), (0,)), ((), ())), preferred_element_type=f32)


def nt(a, b):
    return lax.dot_general(a, b, (((1,), (1,)), ((), ())), preferred_element_type=f32)


def gather_phase(at, rows, send, recv, base, on_rows):
    half = rows.shape[1] // 2
    A, B = pl.ds(0, half), pl.ds(half, half)

    def cp(i, slot, part, to):
        ref = rows.at[slot] if part is None else rows.at[slot, part]
        return remote(ref, ref, send, recv, base + i, to)

    fcx, fcy, fcd = 2 * at.qx + at.other, 2 * at.qy + at.other, 2 * at.qd + at.other
    sent = []

    def go(*a):
        c = cp(*a)
        c.start()
        sent.append(c)

    def arrived(i, slot, part, frm):
        cp(i, slot, part, frm).wait_recv()

    go(0, at.f, None, at.fc)
    go(1, at.f, A, at.fx)
    go(3, at.f, B, at.fy)
    go(2, at.f, B, at.fx)
    go(4, at.f, A, at.fy)
    arrived(0, at.fc, None, at.fc)
    on_rows(2 * at.chip, 2)
    arrived(1, at.fx, A, at.fx)
    go(5, at.fx, A, at.fy)
    go(7, at.fx, A, at.fc)
    arrived(3, at.fy, B, at.fy)
    go(6, at.fy, B, at.fx)
    go(8, at.fy, B, at.fc)
    arrived(2, at.fx, B, at.fx)
    go(9, at.fx, B, at.fc)
    arrived(4, at.fy, A, at.fy)
    go(10, at.fy, A, at.fc)
    arrived(7, fcx, A, at.fc)
    arrived(9, fcx, B, at.fc)
    on_rows(2 * at.qx, 2)
    arrived(8, fcy, B, at.fc)
    arrived(10, fcy, A, at.fc)
    on_rows(2 * at.qy, 2)
    arrived(5, at.fd, A, at.fy)
    go(11, at.fd, A, at.fc)
    arrived(6, at.fd, B, at.fx)
    go(12, at.fd, B, at.fc)
    on_rows(at.fd, 1)
    arrived(11, fcd, A, at.fc)
    arrived(12, fcd, B, at.fc)
    on_rows(fcd, 1)
    for c in sent:
        c.wait_send()


GATHER_COPIES = 13
SCATTER_COPIES = 10


def scatter_scratch(R, D):
    return [
        pltpu.VMEM((4, R, D), bf16),
        pltpu.VMEM((4, R, D), bf16),
        pltpu.VMEM((2, R, D), f32),
        pltpu.VMEM((3, R, D), bf16),
        pltpu.VMEM((3, R, D), bf16),
    ]


def scatter_phase(at, partial, bufs, send, recv, base):
    to_core, from_core, mine, out, inc = bufs
    R, D = to_core.shape[1], to_core.shape[2]
    half = R // 2
    A, B = pl.ds(0, half), pl.ds(half, half)
    tile = 512
    step = 16
    sent = []

    def go(i, src, dst, to):
        c = remote(src, dst, send, recv, base + i, to)
        c.start()
        sent.append(c)

    def arrived(i, dst, frm):
        remote(dst, dst, send, recv, base + i, frm).wait_recv()

    def compute(order, chip, slot):
        @pl.loop(0, D // tile)
        def _(n):
            cols = pl.ds(pl.multiple_of(n * tile, tile), tile)
            got = partial(chip, cols)
            lo, hi = got[:R], got[R:]
            first = at.c == 0
            mine[slot, :, cols] = jnp.where(first, lo, hi)
            to_core[order, :, cols] = jnp.where(first, hi, lo).astype(bf16)

        go(order, to_core.at[order], from_core.at[order], at.fc)

    def chip_sum(order, slot):
        arrived(order, from_core.at[order], at.fc)

        @pl.loop(0, R // step)
        def _(r):
            rows = pl.ds(pl.multiple_of(r * step, step), step)
            out[order, rows, :] = (mine[slot, rows, :] + from_core[order, rows, :].astype(f32)).astype(bf16)

    def relay(order, start, src):
        @pl.loop(0, half // step)
        def _(r):
            rows = pl.ds(pl.multiple_of(start + r * step, step), step)
            out[order, rows, :] = (out[order, rows, :].astype(f32) + inc[src, rows, :].astype(f32)).astype(bf16)

    compute(0, at.qd, 0)
    compute(1, at.qx, 1)
    chip_sum(0, 0)
    go(4, out.at[0, A], inc.at[0, A], at.fx)
    go(5, out.at[0, B], inc.at[0, B], at.fy)
    compute(2, at.qy, 0)
    chip_sum(1, 1)
    go(6, out.at[1, A], inc.at[1, A], at.fx)
    compute(3, at.chip, 1)
    chip_sum(2, 0)
    go(8, out.at[2, B], inc.at[2, B], at.fy)
    arrived(5, inc.at[0, B], at.fy)
    relay(1, half, 0)
    go(7, out.at[1, B], inc.at[1, B], at.fx)
    arrived(4, inc.at[0, A], at.fx)
    relay(2, 0, 0)
    go(9, out.at[2, A], inc.at[2, A], at.fy)
    arrived(3, from_core.at[3], at.fc)
    arrived(6, inc.at[1, A], at.fx)
    arrived(8, inc.at[2, B], at.fy)
    arrived(7, inc.at[1, B], at.fx)
    arrived(9, inc.at[2, A], at.fy)
    for c in sent:
        c.wait_send()

    def total(rows):
        return (
            mine[1, rows, :]
            + from_core[3, rows, :].astype(f32)
            + inc[1, rows, :].astype(f32)
            + inc[2, rows, :].astype(f32)
        )

    return total


def rms(v):
    return lax.rsqrt(jnp.mean(v * v, axis=-1, keepdims=True) + epsilon)


def back(weighted, normed, scale):
    return scale * (weighted - normed * jnp.mean(weighted * normed, axis=-1, keepdims=True))


def row_loop(R, body, step=16):
    @pl.loop(0, R // step)
    def _(r):
        body(pl.ds(pl.multiple_of(r * step, step), step))


def pair_loop(rows, w_cols, total_cols, body):
    @pl.loop(0, total_cols // w_cols)
    def _(t):
        body(pl.ds(pl.multiple_of(t * w_cols, w_cols), w_cols))


class Stores:
    def __init__(self, sems):
        self.sems, self.steps, self.n = sems, [], 0

    def slot(self):
        if len(self.steps) >= 2:
            for c in self.steps[-2]:
                c.wait()
            self.steps[-2] = []
        return len(self.steps) % 2

    def put(self, pairs):
        done = []
        for src, dst in pairs:
            done.append(local(src, dst, self.sems, self.n))
            self.n += 1
        self.steps.append(done)

    def finish(self):
        for step in self.steps:
            for c in step:
                c.wait()


def enter_kernel(C, x_ref, g_ref, own_ref, gown_ref, all_ref, stage, mine, rows, gown, lsem, osem, send, recv, tsend, trecv):
    at = Plane()
    z = lax.axis_index("ctx")
    F, R = rows.shape[0], rows.shape[1]
    piece = R // C
    barrier = pltpu.get_barrier_semaphore()
    for k in range(1, C):
        pl.semaphore_signal(barrier, inc=1, device_id={"ctx": (z + k) % C}, device_id_type=MESH)
        pl.semaphore_signal(
            barrier, inc=1, device_id={"fsdp": 2 * ((at.chip + k) % C) + at.c}, device_id_type=MESH
        )
    pl.semaphore_signal(barrier, inc=1, device_id={"fsdp": at.fc}, device_id_type=MESH)
    loads = [local(x_ref, mine.at[0], lsem, 0), local(g_ref, mine.at[1], lsem, 1)]
    pl.semaphore_wait(barrier, 2 * (C - 1) + 1)
    sent = []
    keep = []
    for a in range(2):
        loads[a].wait()
        for k in range(1, C):
            j = (at.chip + k) % C
            c = remote(
                mine.at[a, pl.ds(j * piece, piece)], stage.at[a, at.chip], tsend, trecv, 2 * C * a + k, 2 * j + at.c
            )
            c.start()
            sent.append(c)
        keep.append(local(mine.at[a, pl.ds(at.chip * piece, piece)], stage.at[a, at.chip], lsem, 2 + a))

    def landing(a, layer):
        r = pl.ds(layer * piece, piece)
        return rows.at[at.f, r] if a == 0 else gown.at[r]

    for a in range(2):
        keep[a].wait()
        for k in range(1, C):
            frm = (at.chip - k + C) % C
            remote(stage.at[a, frm], stage.at[a, frm], tsend, trecv, 2 * C * a + k, 2 * frm + at.c).wait_recv()
        for k in range(1, C):
            to = (z + k) % C
            c = remote(stage.at[a, to], landing(a, z), tsend, trecv, 2 * C * a + C + k, to, "ctx")
            c.start()
            sent.append(c)
        keep[a] = local(stage.at[a, z], landing(a, z), lsem, 4 + a)

    def arrive(a):
        keep[a].wait()
        for k in range(1, C):
            frm = (z - k + C) % C
            remote(landing(a, frm), landing(a, frm), tsend, trecv, 2 * C * a + C + k, frm, "ctx").wait_recv()

    arrive(0)
    save = local(rows.at[at.f], own_ref, lsem, 6)
    stores = []

    def on_rows(first, count):
        stores.append(local(rows.at[pl.ds(first, count)], all_ref.at[pl.ds(first, count)], osem, len(stores)))

    gather_phase(at, rows, send, recv, 0, on_rows)
    arrive(1)
    local(gown, gown_ref, lsem, 7).wait()
    for c in sent:
        c.wait_send()
    save.wait()
    for c in stores:
        c.wait()


def enter_call(C, F, x, g):
    R, D = x.shape
    one = jax.ShapeDtypeStruct((R, D), bf16)
    return pl.pallas_call(
        functools.partial(enter_kernel, C),
        out_shape=[one, one, jax.ShapeDtypeStruct((F, R, D), bf16)],
        in_specs=[ANY] * 2,
        out_specs=[ANY] * 3,
        scratch_shapes=[
            pltpu.VMEM((2, C, R // C, D), bf16),
            pltpu.VMEM((2, R, D), bf16),
            pltpu.VMEM((F, R, D), bf16),
            pltpu.VMEM((R, D), bf16),
            dma(8), dma(5), dma(GATHER_COPIES), dma(GATHER_COPIES), dma(4 * C), dma(4 * C),
        ],
        compiler_params=params(1),
        cost_estimate=cost(75),
    )(x, g)


def qkv_kernel(all_ref, w_ref, proj_ref, st_ref, rows, w, acc, st, lsem, osem, ssend, srecv):
    at = Plane()
    F, R = rows.shape[0], rows.shape[1]
    e = w.shape[1] // 3
    m = 2 * R
    loads = [local(w_ref, w, lsem, 0)] + [
        local(all_ref.at[pl.ds(2 * p, 2)], rows.at[pl.ds(2 * p, 2)], lsem, 1 + p) for p in range(F // 2)
    ]
    barrier = pltpu.get_barrier_semaphore()
    for k in range(1, F):
        pl.semaphore_signal(barrier, inc=1, device_id={"fsdp": (at.f + k) % F}, device_id_type=MESH)
    pl.semaphore_wait(barrier, F - 1)
    loads[0].wait()
    stores = Stores(osem)
    for p in range(F // 2):
        loads[1 + p].wait()
        s = stores.slot()

        def tile(c):
            acc[s, :, c] = nn(rows[pl.ds(2 * p, 2)].reshape(m, rows.shape[2]), w[:, c])

        pair_loop(m, 256, w.shape[1], tile)
        q, k = acc[s, :, :e], acc[s, :, e : 2 * e]
        st[at.f, :, pl.ds(p * m, m)] = row_sums(q * q, k * k)
        stores.put([(acc.at[s], proj_ref.at[pl.ds(p * m, m)])])
    share_stats(at, F, st, ssend, srecv, 0)
    local(st, st_ref, lsem, 1 + F // 2).wait()
    stores.finish()


def params(number):
    return pltpu.CompilerParams(
        collective_id=number, has_side_effects=True, vmem_limit_bytes=VMEM_LIMIT
    )


def cost(us):
    return pl.CostEstimate(flops=int(us * 1e9), bytes_accessed=2**20, transcendentals=0)


def dma(n):
    return pltpu.SemaphoreType.DMA((n,))


def qkv_call(F, rows, w):
    _, R, D = rows.shape
    n = w.shape[1]
    return pl.pallas_call(
        qkv_kernel,
        out_shape=[
            jax.ShapeDtypeStruct((F * R, n), f32),
            jax.ShapeDtypeStruct((F, 8, F * R), f32),
        ],
        in_specs=[ANY] * 2,
        out_specs=[ANY] * 2,
        scratch_shapes=[
            pltpu.VMEM((F, R, D), bf16),
            pltpu.VMEM((D, n), bf16),
            pltpu.VMEM((2, 2 * R, n), f32),
            pltpu.VMEM((F, 8, F * R), f32),
            dma(6), dma(4), dma(F), dma(F),
        ],
        compiler_params=params(7),
        cost_estimate=cost(22),
    )(rows, w)


def out_kernel(
    mixed_ref, wo_ref, x_ref, gain_ref, hid_ref, ao_ref, in_ref,
    mixed, wo, x, gain, hid, ao, inp, b0, b1, b2, b3, b4, lsem, send, recv,
):
    at = Plane()
    pairs = [(mixed_ref, mixed), (wo_ref, wo), (x_ref, x), (gain_ref, gain)]
    loads = [local(s, d, lsem, i) for i, (s, d) in enumerate(pairs)]
    at.greet()
    R = x.shape[0]
    loads[0].wait()
    loads[1].wait()

    def partial(chip, cols):
        return nt(mixed[pl.ds(pl.multiple_of(chip * 2 * R, 2 * R), 2 * R), :], wo[cols, :])

    total = scatter_phase(at, partial, (b0, b1, b2, b3, b4), send, recv, 0)
    loads[2].wait()
    loads[3].wait()

    def finish(r):
        out = total(r)
        ao[r, :] = out
        hidden_in = x[r, :].astype(f32) + out * rms(out) * gain[...]
        hid[r, :] = hidden_in
        inp[r, :] = hidden_in.astype(bf16)

    row_loop(R, finish)
    for c in [local(ao, ao_ref, lsem, 4), local(hid, hid_ref, lsem, 5), local(inp, in_ref, lsem, 6)]:
        c.wait()


def out_call(F, mixed, wo, x, gain):
    R, D = x.shape
    e = wo.shape[1]
    return pl.pallas_call(
        out_kernel,
        out_shape=[
            jax.ShapeDtypeStruct((R, D), f32),
            jax.ShapeDtypeStruct((R, D), f32),
            jax.ShapeDtypeStruct((R, D), bf16),
        ],
        in_specs=[ANY] * 4,
        out_specs=[ANY] * 3,
        scratch_shapes=[
            pltpu.VMEM((F * R, e), bf16),
            pltpu.VMEM((D, e), bf16),
            pltpu.VMEM((R, D), bf16),
            pltpu.VMEM((1, D), f32),
            pltpu.VMEM((R, D), f32),
            pltpu.VMEM((R, D), f32),
            pltpu.VMEM((R, D), bf16),
        ]
        + scatter_scratch(R, D)
        + [dma(7), dma(SCATTER_COPIES), dma(SCATTER_COPIES)],
        compiler_params=params(8),
        cost_estimate=cost(46),
    )(mixed, wo, x, gain)


def up_kernel(
    in_ref, wg_ref, wu_ref, all_ref, act_ref, der_ref, h_ref,
    wg, wu, rows, act, der, h, lsem, osem, send, recv,
):
    at = Plane()
    own = local(in_ref, rows.at[at.f], lsem, 0)
    loads = [local(wg_ref, wg, lsem, 1), local(wu_ref, wu, lsem, 2)]
    at.greet()
    R = rows.shape[1]
    own.wait()
    waited = []
    stores = Stores(osem)

    def on_rows(first, count):
        s = stores.slot()
        m = count * R
        if not waited:
            for c in loads:
                c.wait()
            waited.append(1)

        def tile(c):
            lhs = rows[pl.ds(first, count)].reshape(m, rows.shape[2])
            g = nn(lhs, wg[:, c])
            u = nn(lhs, wu[:, c])
            sig = jax.nn.sigmoid(g)
            a = g * sig
            act[s, pl.ds(0, m), c] = a.astype(bf16)
            der[s, pl.ds(0, m), c] = (u * (sig * (1.0 + g * (1.0 - sig)))).astype(bf16)
            h[s, pl.ds(0, m), c] = (a * u).astype(bf16)

        pair_loop(m, 256, wg.shape[1], tile)
        start = pl.multiple_of(first * R, R)
        stores.put(
            [
                (act.at[s, pl.ds(0, m)], act_ref.at[pl.ds(start, m)]),
                (der.at[s, pl.ds(0, m)], der_ref.at[pl.ds(start, m)]),
                (h.at[s, pl.ds(0, m)], h_ref.at[pl.ds(start, m)]),
                (rows.at[pl.ds(first, count)], all_ref.at[pl.ds(first, count)]),
            ]
        )

    gather_phase(at, rows, send, recv, 0, on_rows)
    stores.finish()


def up_call(F, inp, wg, wu):
    R, D = inp.shape
    n = wg.shape[1]
    T = F * R
    wide = jax.ShapeDtypeStruct((T, n), bf16)
    return pl.pallas_call(
        up_kernel,
        out_shape=[jax.ShapeDtypeStruct((F, R, D), bf16), wide, wide, wide],
        in_specs=[ANY] * 3,
        out_specs=[ANY] * 4,
        scratch_shapes=[
            pltpu.VMEM((D, n), bf16),
            pltpu.VMEM((D, n), bf16),
            pltpu.VMEM((F, R, D), bf16),
            pltpu.VMEM((2, 2 * R, n), bf16),
            pltpu.VMEM((2, 2 * R, n), bf16),
            pltpu.VMEM((2, 2 * R, n), bf16),
        ]
        + [dma(3), dma(20), dma(GATHER_COPIES), dma(GATHER_COPIES)],
        compiler_params=params(2),
        cost_estimate=cost(46),
    )(inp, wg, wu)


def down_kernel(
    h_ref, wd_ref, hid_ref, cot_ref, gain_ref, act_ref, der_ref,
    res_ref, gg_ref, all_ref, gate_ref, up_ref,
    h, wd, hid, cot, gain, act, der, res, gacc, rows, ggate, gup, b0, b1, b2, b3, b4,
    lsem, osem, asem, send, recv,
):
    at = Plane()
    loads = [
        local(s, d, lsem, i)
        for i, (s, d) in enumerate(
            [(h_ref, h), (wd_ref, wd), (hid_ref, hid), (cot_ref, cot), (gain_ref, gain)]
        )
    ]
    at.greet()
    R = rows.shape[1]
    loads[0].wait()
    loads[1].wait()

    def partial(chip, cols):
        return nt(h[pl.ds(pl.multiple_of(chip * 2 * R, 2 * R), 2 * R), :], wd[cols, :])

    total = scatter_phase(at, partial, (b0, b1, b2, b3, b4), send, recv, 0)
    for c in loads[2:]:
        c.wait()
    gacc[...] = jnp.zeros_like(gacc)

    def finish(r):
        out = total(r)
        scale = rms(out)
        hat = out * scale
        res[r, :] = (hid[r, :] + hat * gain[...]).astype(bf16)
        g = cot[r, :].astype(f32)
        gacc[...] += jnp.sum(g * hat, axis=0, keepdims=True)
        rows[at.f, r, :] = back(g * gain[...], hat, scale).astype(bf16)

    row_loop(R, finish)
    saves = [local(res, res_ref, lsem, 5), local(gacc, gg_ref, lsem, 6)]
    stores = Stores(osem)

    def on_rows(first, count):
        s = stores.slot()
        m = count * R
        start = pl.multiple_of(first * R, R)
        k = len(stores.steps)
        la = local(act_ref.at[pl.ds(start, m)], act.at[s, pl.ds(0, m)], asem, 2 * k)
        ld = local(der_ref.at[pl.ds(start, m)], der.at[s, pl.ds(0, m)], asem, 2 * k + 1)
        la.wait()
        ld.wait()

        def tile(c):
            gh = nn(rows[pl.ds(first, count)].reshape(m, rows.shape[2]), wd[:, c])
            gup[s, pl.ds(0, m), c] = (gh * act[s, pl.ds(0, m), c].astype(f32)).astype(bf16)
            ggate[s, pl.ds(0, m), c] = (gh * der[s, pl.ds(0, m), c].astype(f32)).astype(bf16)

        pair_loop(m, 256, wd.shape[1], tile)
        stores.put(
            [
                (ggate.at[s, pl.ds(0, m)], gate_ref.at[pl.ds(start, m)]),
                (gup.at[s, pl.ds(0, m)], up_ref.at[pl.ds(start, m)]),
                (rows.at[pl.ds(first, count)], all_ref.at[pl.ds(first, count)]),
            ]
        )

    gather_phase(at, rows, send, recv, SCATTER_COPIES, on_rows)
    for s in saves:
        s.wait()
    stores.finish()


def down_call(F, h, wd, hid, cot, gain, act, der):
    R, D = hid.shape
    n = wd.shape[1]
    T = F * R
    copies = SCATTER_COPIES + GATHER_COPIES
    return pl.pallas_call(
        down_kernel,
        out_shape=[
            jax.ShapeDtypeStruct((R, D), bf16),
            jax.ShapeDtypeStruct((1, D), f32),
            jax.ShapeDtypeStruct((F, R, D), bf16),
            jax.ShapeDtypeStruct((T, n), bf16),
            jax.ShapeDtypeStruct((T, n), bf16),
        ],
        in_specs=[ANY] * 7,
        out_specs=[ANY] * 5,
        scratch_shapes=[
            pltpu.VMEM((T, n), bf16),
            pltpu.VMEM((D, n), bf16),
            pltpu.VMEM((R, D), f32),
            pltpu.VMEM((R, D), bf16),
            pltpu.VMEM((1, D), f32),
            pltpu.VMEM((2, 2 * R, n), bf16),
            pltpu.VMEM((2, 2 * R, n), bf16),
            pltpu.VMEM((R, D), bf16),
            pltpu.VMEM((1, D), f32),
            pltpu.VMEM((F, R, D), bf16),
            pltpu.VMEM((2, 2 * R, n), bf16),
            pltpu.VMEM((2, 2 * R, n), bf16),
        ]
        + scatter_scratch(R, D)
        + [dma(7), dma(15), dma(10), dma(copies), dma(copies)],
        compiler_params=params(3),
        cost_estimate=cost(92),
    )(h, wd, hid, cot, gain, act, der)


def mid_kernel(
    gate_ref, up_ref, wg_ref, wu_ref, cot_ref, ao_ref, gain_ref, wo_ref,
    res_ref, gg_ref, all_ref, gm_ref,
    ggate, gup, wg, wu, cot, ao, gain, wo, res, gacc, rows, gm, b0, b1, b2, b3, b4,
    lsem, osem, send, recv,
):
    at = Plane()
    pairs = [
        (gate_ref, ggate), (up_ref, gup), (wg_ref, wg), (wu_ref, wu),
        (cot_ref, cot), (ao_ref, ao), (gain_ref, gain), (wo_ref, wo),
    ]
    loads = [local(s, d, lsem, i) for i, (s, d) in enumerate(pairs)]
    at.greet()
    R = rows.shape[1]
    for c in loads[:4]:
        c.wait()

    def partial(chip, cols):
        r = pl.ds(pl.multiple_of(chip * 2 * R, 2 * R), 2 * R)
        return nt(ggate[r, :], wg[cols, :]) + nt(gup[r, :], wu[cols, :])

    total = scatter_phase(at, partial, (b0, b1, b2, b3, b4), send, recv, 0)
    for c in loads[4:]:
        c.wait()
    gacc[...] = jnp.zeros_like(gacc)

    def finish(r):
        resid = cot[r, :].astype(f32) + total(r)
        res[r, :] = resid
        out = ao[r, :]
        scale = rms(out)
        hat = out * scale
        gacc[...] += jnp.sum(resid * hat, axis=0, keepdims=True)
        rows[at.f, r, :] = back(resid * gain[...], hat, scale).astype(bf16)

    row_loop(R, finish)
    saves = [local(res, res_ref, lsem, 8), local(gacc, gg_ref, lsem, 9)]
    stores = Stores(osem)

    def on_rows(first, count):
        s = stores.slot()
        m = count * R
        start = pl.multiple_of(first * R, R)
        lhs = rows[pl.ds(first, count)].reshape(m, rows.shape[2])
        gm[s, pl.ds(0, m), :] = nn(lhs, wo[...]).astype(bf16)
        stores.put(
            [
                (gm.at[s, pl.ds(0, m)], gm_ref.at[pl.ds(start, m)]),
                (rows.at[pl.ds(first, count)], all_ref.at[pl.ds(first, count)]),
            ]
        )

    gather_phase(at, rows, send, recv, SCATTER_COPIES, on_rows)
    for s in saves:
        s.wait()
    stores.finish()


def mid_call(F, gate, up, wg, wu, cot, ao, gain, wo):
    R, D = cot.shape
    n, e = wg.shape[1], wo.shape[1]
    T = F * R
    copies = SCATTER_COPIES + GATHER_COPIES
    return pl.pallas_call(
        mid_kernel,
        out_shape=[
            jax.ShapeDtypeStruct((R, D), f32),
            jax.ShapeDtypeStruct((1, D), f32),
            jax.ShapeDtypeStruct((F, R, D), bf16),
            jax.ShapeDtypeStruct((T, e), bf16),
        ],
        in_specs=[ANY] * 8,
        out_specs=[ANY] * 4,
        scratch_shapes=[
            pltpu.VMEM((T, n), bf16),
            pltpu.VMEM((T, n), bf16),
            pltpu.VMEM((D, n), bf16),
            pltpu.VMEM((D, n), bf16),
            pltpu.VMEM((R, D), bf16),
            pltpu.VMEM((R, D), f32),
            pltpu.VMEM((1, D), f32),
            pltpu.VMEM((D, e), bf16),
            pltpu.VMEM((R, D), f32),
            pltpu.VMEM((1, D), f32),
            pltpu.VMEM((F, R, D), bf16),
            pltpu.VMEM((2, 2 * R, e), bf16),
        ]
        + scatter_scratch(R, D)
        + [dma(10), dma(10), dma(copies), dma(copies)],
        compiler_params=params(4),
        cost_estimate=cost(92),
    )(gate, up, wg, wu, cot, ao, gain, wo)


def last_kernel(
    width, q_ref, k_ref, v_ref, proj_ref, st_ref, in_ref, w_ref, res_ref, gain_ref,
    out_ref, gp_ref, gsum_ref,
    q, k, proj, st, ins, gains, gsum, gp, w, res, out, b0, b1, b2, b3, b4,
    lsem, send, recv, ssend, srecv, gsend, grecv,
):
    at = Plane()
    F, T = st.shape[0], st.shape[2]
    e = q.shape[1]
    R = res.shape[0]
    pairs = [
        (in_ref, ins.at[at.f]), (st_ref, st), (q_ref, q), (k_ref, k),
        (v_ref, gp.at[:, pl.ds(2 * e, e)]), (proj_ref.at[:, pl.ds(0, 2 * e)], proj), (w_ref, w), (res_ref, res),
        (gain_ref, gains.at[at.f]),
    ]
    loads = [local(s, d, lsem, i) for i, (s, d) in enumerate(pairs)]
    barrier = pltpu.get_barrier_semaphore()
    for s in range(1, F):
        pl.semaphore_signal(barrier, inc=1, device_id={"fsdp": (at.f + s) % F}, device_id_type=MESH)
    pl.semaphore_wait(barrier, F - 1)
    loads[0].wait()
    share_stats(at, F, ins, ssend, srecv, 0)
    for c in loads[1:6]:
        c.wait()
    step = 256

    @pl.loop(0, T // step)
    def _(t):
        r = pl.ds(pl.multiple_of(t * step, step), step)
        sums = jnp.sum(st[:, :, r], axis=0)
        inner = jnp.sum(ins[:, :, r], axis=0) / width
        for row, grad in ((0, q), (1, k)):
            scale = lax.rsqrt(column(sums[row : row + 1], HEAD_DIM) / width + epsilon)
            mean = column(inner[row : row + 1], HEAD_DIM)
            for h in range(e // HEAD_DIM):
                hat = proj[r, row * e + h * HEAD_DIM : row * e + (h + 1) * HEAD_DIM] * scale
                got = scale * (grad[r, h * HEAD_DIM : (h + 1) * HEAD_DIM] - hat * mean)
                gp[r, row * e + h * HEAD_DIM : row * e + (h + 1) * HEAD_DIM] = got.astype(bf16)

    save = local(gp, gp_ref, lsem, 9)
    loads[6].wait()

    def partial(chip, cols):
        return nt(gp[pl.ds(pl.multiple_of(chip * 2 * R, 2 * R), 2 * R), :], w[cols, :])

    total = scatter_phase(at, partial, (b0, b1, b2, b3, b4), send, recv, 0)
    loads[7].wait()

    def finish(r):
        out[r, :] = (res[r, :] + total(r)).astype(bf16)

    row_loop(R, finish)
    store = local(out, out_ref, lsem, 10)
    loads[8].wait()
    share_stats(at, F, gains, gsend, grecv, 0)
    gsum[...] = jnp.sum(gains[...], axis=0)
    local(gsum, gsum_ref, lsem, 11).wait()
    store.wait()
    save.wait()


def last_call(F, wq, wk, gv, proj, st, ins, w, res, gains):
    R, D = res.shape
    n = w.shape[1]
    T, e = F * R, n // 3
    return pl.pallas_call(
        functools.partial(last_kernel, D),
        out_shape=[
            jax.ShapeDtypeStruct((R, D), bf16),
            jax.ShapeDtypeStruct((T, n), bf16),
            jax.ShapeDtypeStruct((8, D), f32),
        ],
        in_specs=[ANY] * 9,
        out_specs=[ANY] * 3,
        scratch_shapes=[
            pltpu.VMEM((T, e), f32),
            pltpu.VMEM((T, e), f32),
            pltpu.VMEM((T, 2 * e), f32),
            pltpu.VMEM((F, 8, T), f32),
            pltpu.VMEM((F, 8, T), f32),
            pltpu.VMEM((F, 8, D), f32),
            pltpu.VMEM((8, D), f32),
            pltpu.VMEM((T, n), bf16),
            pltpu.VMEM((D, n), bf16),
            pltpu.VMEM((R, D), f32),
            pltpu.VMEM((R, D), bf16),
        ]
        + scatter_scratch(R, D)
        + [dma(12), dma(SCATTER_COPIES), dma(SCATTER_COPIES), dma(F), dma(F), dma(F), dma(F)],
        compiler_params=params(5),
        cost_estimate=cost(55),
    )(wq, wk, gv, proj, st, ins, w, res, gains)


def share_stats(at, F, st, send, recv, base):
    sent = []
    for k in range(1, F):
        to = (at.f + k) % F
        c = remote(st.at[at.f], st.at[at.f], send, recv, base + k, to)
        c.start()
        sent.append(c)
    for k in range(1, F):
        frm = (at.f - k + F) % F
        remote(st.at[frm], st.at[frm], send, recv, base + k, frm).wait_recv()
    for c in sent:
        c.wait_send()


def row_sums(a, b):
    r = lax.broadcasted_iota(jnp.int32, (8, a.shape[1]), 0)
    one, two = (r == 0).astype(f32), (r == 1).astype(f32)

    def half(sel, v):
        return lax.dot_general(
            sel, v, (((1,), (1,)), ((), ())), preferred_element_type=f32, precision=lax.Precision.HIGHEST
        )

    return half(one, a) + half(two, b)


def column(row, lanes):
    return jnp.broadcast_to(row, (lanes, row.shape[1])).T


def turn(v, cos, sin):
    return v * cos + pltpu.roll(v, HEAD_DIM // 2, 1) * sin


def seq_columns(st, c, chips, R):
    return jnp.concatenate([st[:, pl.ds(pl.multiple_of((2 * j + c) * R, R), R)] for j in range(chips)], axis=1)


def attend_kernel(width, q_ref, k_ref, v_ref, st_ref, gq_ref, gk_ref, cos_ref, sin_ref, pos_ref, posc_ref, mix_ref, qr_ref, kr_ref, lse_ref):
    c = pl.program_id(0)
    chips, R = q_ref.shape[0], q_ref.shape[2]
    L = chips * R
    sums = jnp.sum(seq_columns_all(st_ref, c, chips, R), axis=0)
    cos, sin = cos_ref[0], sin_ref[0]

    def norm_turn(ref, row, gain):
        scale = lax.rsqrt(column(sums[row : row + 1], HEAD_DIM) / width + epsilon)
        return turn(ref[...].reshape(L, HEAD_DIM) * scale * gain[...], cos, sin)

    qr = (norm_turn(q_ref, 0, gq_ref) * HEAD_DIM ** (-0.5)).astype(bf16)
    kr = norm_turn(k_ref, 1, gk_ref).astype(bf16)
    v = v_ref[...].reshape(L, HEAD_DIM).astype(bf16)
    qr_ref[...] = qr.reshape(qr_ref.shape)
    kr_ref[...] = kr.reshape(kr_ref.shape)
    pos = pos_ref[0]
    for t in range(chips):
        rows = slice(t * R, (t + 1) * R)
        s = nt(qr[rows], kr)
        s = jnp.where(posc_ref[0, rows, :1] >= pos, s, -1e30)
        top = jnp.max(s, axis=-1, keepdims=True)
        e = jnp.exp(s - top)
        total = jnp.sum(e, axis=-1, keepdims=True)
        p = (e * (1.0 / total)).astype(bf16)
        mix_ref[t, 0] = nn(p, v).astype(bf16)
        lse_ref[0, 0, rows, :] = jnp.broadcast_to(top + jnp.log(total), (R, HEAD_DIM))


def seq_columns_all(st_ref, c, chips, R):
    return jnp.concatenate(
        [st_ref[:, :, pl.ds(pl.multiple_of((2 * j + c) * R, R), R)] for j in range(chips)], axis=2
    )


def attend_specs(chips, R, heads, F, L):
    def at(offset):
        return pl.BlockSpec((chips, 1, R, HEAD_DIM), lambda c, h: (0, c, 0, offset + h))

    gain = pl.BlockSpec((1, HEAD_DIM), lambda c, h: (0, h))
    table = pl.BlockSpec((1, L, HEAD_DIM), lambda c, h: (c, 0, 0))
    stats = pl.BlockSpec((F, 8, F * R), lambda c, h: (0, 0, 0))
    posr = pl.BlockSpec((1, 1, L), lambda c, h: (c, 0, 0))
    lse = pl.BlockSpec((1, 1, L, HEAD_DIM), lambda c, h: (c, h, 0, 0))
    return at, gain, table, stats, posr, lse


def attend_call(F, proj, st, gq, gk, cos, sin, pos, posc):
    R = proj.shape[0] // F
    e = proj.shape[1] // 3
    heads, chips = e // HEAD_DIM, F // 2
    L = chips * R
    at, gain, table, stats, posr, lse = attend_specs(chips, R, heads, F, L)
    view = proj.reshape(chips, 2, R, 3 * e)
    flat = jax.ShapeDtypeStruct((chips, 2, R, e), bf16)
    out = pl.pallas_call(
        functools.partial(attend_kernel, heads * HEAD_DIM * F),
        out_shape=[flat, flat, flat, jax.ShapeDtypeStruct((2, heads, L, HEAD_DIM), f32)],
        grid=(2, heads),
        in_specs=[at(0), at(heads), at(2 * heads), stats, gain, gain, table, table, posr, table],
        out_specs=[at(0), at(0), at(0), lse],
        compiler_params=pltpu.CompilerParams(vmem_limit_bytes=VMEM_LIMIT),
        cost_estimate=cost(15),
    )(view, view, view, st, gq, gk, cos, sin, pos, posc)
    return out


def attend_back_kernel(
    width, q_ref, k_ref, v_ref, qr_ref, kr_ref, gm_ref, lse_ref, st_ref, gq_ref, gk_ref, cos_ref, sin_ref, pos_ref, posc_ref,
    wq_ref, wk_ref, gv_ref, in_ref, gg_ref, dk, dv, dq,
):
    c = pl.program_id(0)
    chips, R = q_ref.shape[0], q_ref.shape[2]
    L = chips * R
    kr = kr_ref[...].reshape(L, HEAD_DIM)
    v = v_ref[...].reshape(L, HEAD_DIM).astype(bf16)
    pos = pos_ref[0]
    dk[...] = jnp.zeros_like(dk)
    dv[...] = jnp.zeros_like(dv)
    for t in range(chips):
        rows = slice(t * R, (t + 1) * R)
        qt, gm = qr_ref[t, 0], gm_ref[t, 0]
        s = nt(qt, kr)
        s = jnp.where(posc_ref[0, rows, :1] >= pos, s, -1e30)
        p = jnp.exp(s - lse_ref[0, 0, rows, :1])
        dp = nt(gm, v)
        dv[...] += lax.dot_general(p.astype(bf16), gm, (((0,), (0,)), ((), ())), preferred_element_type=f32)
        inner = jnp.sum(dp * p, axis=-1, keepdims=True)
        ds = (p * (dp - inner)).astype(bf16)
        dq[rows, :] = nn(ds, kr)
        dk[...] += lax.dot_general(ds, qt, (((0,), (0,)), ((), ())), preferred_element_type=f32)
    gv_ref[...] = dv[...].astype(bf16).reshape(gv_ref.shape)
    sums = jnp.sum(seq_columns_all(st_ref, c, chips, R), axis=0)
    cos, sin = cos_ref[0], sin_ref[0]

    def finish(grad, ref, row, gain, out):
        norm = turn(grad, cos, -sin)
        hat = ref[...].reshape(L, HEAD_DIM) * lax.rsqrt(column(sums[row : row + 1], HEAD_DIM) / width + epsilon)
        gg_ref[0, 0, row : row + 1, :] = jnp.sum(norm * hat, axis=0, keepdims=True)
        weighted = norm * gain[...]
        out[...] = weighted.reshape(out.shape)
        return weighted * hat

    gg_ref[...] = jnp.zeros_like(gg_ref)
    in_ref[0, 0] = row_sums(
        finish(dq[...] * HEAD_DIM ** (-0.5), q_ref, 0, gq_ref, wq_ref), finish(dk[...], k_ref, 1, gk_ref, wk_ref)
    )


def attend_back_call(F, proj, qr, kr, gm, lse_in, st, gq, gk, cos, sin, pos, posc):
    R = proj.shape[0] // F
    e = proj.shape[1] // 3
    heads, chips = e // HEAD_DIM, F // 2
    L = chips * R
    at, gain, table, stats, posr, lse = attend_specs(chips, R, heads, F, L)
    view = proj.reshape(chips, 2, R, 3 * e)
    flat = (chips, 2, R, e)
    small = pl.BlockSpec((1, 1, 8, L), lambda c, h: (c, h, 0, 0))
    tiny = pl.BlockSpec((1, 1, 8, HEAD_DIM), lambda c, h: (c, h, 0, 0))
    wide = jax.ShapeDtypeStruct(flat, f32)
    return pl.pallas_call(
        functools.partial(attend_back_kernel, heads * HEAD_DIM * F),
        out_shape=[
            wide, wide, jax.ShapeDtypeStruct(flat, bf16),
            jax.ShapeDtypeStruct((2, heads, 8, L), f32),
            jax.ShapeDtypeStruct((2, heads, 8, HEAD_DIM), f32),
        ],
        grid=(2, heads),
        in_specs=[
            at(0), at(heads), at(2 * heads), at(0), at(0), at(0), lse, stats, gain, gain, table, table, posr, table,
        ],
        out_specs=[at(0), at(0), at(0), small, tiny],
        scratch_shapes=[pltpu.VMEM((L, HEAD_DIM), f32)] * 3,
        compiler_params=pltpu.CompilerParams(vmem_limit_bytes=VMEM_LIMIT),
        cost_estimate=cost(35),
    )(view, view, view, qr, kr, gm.reshape(flat), lse_in, st, gq, gk, cos, sin, pos, posc)


def newton_kernel(
    C, x_ref, rows_ref, gain_ref, out_ref, home_ref, gsum_ref,
    v, gram, y, yf, stat, stage, gains, gsum,
    lsem, osem, vsend, vrecv, ysend, yrecv, ssend, srecv, tsend, trecv, gsend, grecv,
):
    me = lax.axis_index("fsdp")
    z = lax.axis_index("ctx")
    core, chip = me % 2, me // 2
    peer = me + 1 - 2 * core
    load = local(x_ref, v.at[0], lsem, 0)
    gload = local(gain_ref, gains.at[z], lsem, 1)
    barrier = pltpu.get_barrier_semaphore()
    pl.semaphore_signal(barrier, inc=1, device_id={"fsdp": peer}, device_id_type=MESH)
    for k in range(1, C):
        pl.semaphore_signal(barrier, inc=1, device_id={"ctx": (z + k) % C}, device_id_type=MESH)
        pl.semaphore_signal(
            barrier, inc=1, device_id={"fsdp": 2 * ((chip + k) % C) + core}, device_id_type=MESH
        )
    pl.semaphore_wait(barrier, 2 * (C - 1) + 1)
    piece = rows_ref.shape[1] // C

    def part(j):
        return pl.ds(j * piece, piece)

    sent, keep = [], []
    for a in range(2):
        for k in range(1, C):
            to = (z + k) % C
            c = remote(rows_ref.at[a, part(to)], stage.at[a, z], tsend, trecv, 2 * C * a + k, to, "ctx")
            c.start()
            sent.append(c)
        keep.append(local(rows_ref.at[a, part(z)], stage.at[a, z], lsem, 2 + a))
    gload.wait()
    for k in range(1, C):
        c = remote(gains.at[z], gains.at[z], gsend, grecv, k, (z + k) % C, "ctx")
        c.start()
        sent.append(c)

    def leave_layer():
        for a in range(2):
            for k in range(1, C):
                frm = (z - k + C) % C
                remote(stage.at[a, frm], stage.at[a, frm], tsend, trecv, 2 * C * a + k, frm, "ctx").wait_recv()
            keep[a].wait()
            for k in range(1, C):
                to = (chip + k) % C
                c = remote(
                    stage.at[a, to], home_ref.at[a, part(chip)], tsend, trecv, 2 * C * a + C + k, 2 * to + core
                )
                c.start()
                sent.append(c)
            keep[a] = local(stage.at[a, chip], home_ref.at[a, part(chip)], lsem, 4 + a)

    def arrived_home():
        for a in range(2):
            keep[a].wait()
            for k in range(1, C):
                frm = (chip - k + C) % C
                dst = home_ref.at[a, part(frm)]
                remote(dst, dst, tsend, trecv, 2 * C * a + C + k, 2 * frm + core).wait_recv()
        for k in range(1, C):
            frm = (z - k + C) % C
            remote(gains.at[frm], gains.at[frm], gsend, grecv, k, frm, "ctx").wait_recv()
        gsum[...] = jnp.sum(gains[...], axis=0)
        local(gsum, gsum_ref, lsem, 6).wait()
        for c in sent:
            c.wait_send()

    load.wait()
    M, D = v.shape[1], v.shape[2]
    tile, col = 256, 512
    tiles = M // tile

    def block(i):
        return pl.ds(i * tile, tile)

    def swap(buf, i, sends, recvs):
        return remote(buf.at[0, block(i)], buf.at[1, block(i)], sends, recvs, i, peer)

    pending = [swap(v, i, vsend, vrecv) for i in range(tiles)]
    for c in pending:
        c.start()
    stat[0] = jnp.zeros_like(stat[0])

    def add(r):
        part = v[0, r, :].astype(f32)
        stat[0] += jnp.sum((part * part).reshape(-1, 8, D // 128, 128), axis=(0, 2))

    row_loop(M, add)
    share = remote(stat.at[0], stat.at[1], ssend, srecv, 0, peer)
    share.start()
    share.wait()
    inv = 1.0 / (jnp.sqrt(jnp.sum(stat[0] + stat[1])) + 1e-07)

    for iteration in range(NS_STEPS):
        factor = inv if iteration == 0 else 1.0

        def grams(h, n):
            rhs = pl.ds(pl.multiple_of(n * col, col), col)
            cols = pl.ds(pl.multiple_of(h * M + n * col, col), col)

            @pl.loop(0, tiles)
            def _(i):
                rows = pl.ds(pl.multiple_of(i * tile, tile), tile)
                got = nt(v[0, rows, :], v[h, rhs, :])
                if iteration == 0:
                    got = got * (factor * factor)
                gram[rows, cols] = got.astype(bf16)

        @pl.loop(0, M // col)
        def _(n):
            grams(0, n)

        for c in pending:
            c.wait()

        @pl.loop(0, M // col)
        def _(n):
            grams(1, n)

        def times(src, i, n):
            rows = block(i)
            cols = pl.ds(pl.multiple_of(n * col, col), col)
            return cols, nn(gram[rows, :M], src[0, :, cols]) + nn(gram[rows, M:], src[1, :, cols])

        pending = []
        for i in range(tiles):

            @pl.loop(0, D // col)
            def _(n):
                cols, got = times(v, i, n)
                if iteration == 0:
                    got = got * factor
                yf[block(i), cols] = got
                y[0, block(i), cols] = got.astype(bf16)

            c = swap(y, i, ysend, yrecv)
            c.start()
            pending.append(c)
        for c in pending:
            c.wait()
        if iteration == 0:
            leave_layer()
        pending = []
        for i in range(tiles):

            @pl.loop(0, D // col)
            def _(n):
                cols, got = times(y, i, n)
                old = v[0, block(i), cols].astype(f32)
                if iteration == 0:
                    old = old * factor
                v[0, block(i), cols] = (
                    quintic_one * old + quintic_two * yf[block(i), cols] + quintic_three * got
                ).astype(bf16)

            if iteration < NS_STEPS - 1:
                c = swap(v, i, vsend, vrecv)
            else:
                c = pltpu.make_async_copy(v.at[0, block(i)], out_ref.at[block(i)], osem.at[i])
            c.start()
            pending.append(c)
    arrived_home()
    for c in pending:
        c.wait()


def newton_call(C, x, rows, gains):
    M, D = x.shape
    _, R, _ = rows.shape
    n = M // 256
    return pl.pallas_call(
        functools.partial(newton_kernel, C),
        out_shape=[
            jax.ShapeDtypeStruct((M, D), bf16),
            jax.ShapeDtypeStruct((2, R, D), bf16),
            jax.ShapeDtypeStruct((8, D), f32),
        ],
        in_specs=[ANY] * 3,
        out_specs=[ANY] * 3,
        scratch_shapes=[
            pltpu.VMEM((2, M, D), bf16),
            pltpu.VMEM((M, 2 * M), bf16),
            pltpu.VMEM((2, M, D), bf16),
            pltpu.VMEM((M, D), f32),
            pltpu.VMEM((2, 8, 128), f32),
            pltpu.VMEM((2, C, R // C, D), bf16),
            pltpu.VMEM((C, 8, D), f32),
            pltpu.VMEM((8, D), f32),
            dma(7), dma(n), dma(n), dma(n), dma(n), dma(n), dma(1), dma(1),
            dma(4 * C), dma(4 * C), dma(C), dma(C),
        ],
        compiler_params=params(6),
        cost_estimate=cost(95),
    )(x, rows, gains)


def project(C, F, x, w):
    own = to_layer(C, F, x)
    rows = token_rows(own)
    return own, rows, dot(rows, w, 1, 0)


def attn_out_and_up(C, F, mixed, wo, x, gain, wg, wu):
    if kernels_fit(C, F):
        hidden_in, out, inp = out_call(F, mixed, wo, x, gain)
        return (hidden_in, out, *up_call(F, inp, wg, wu))
    out = token_sums(dot(mixed, wo, 1, 1))
    hidden_in = x.astype(f32) + out * rms(out) * gain
    rows = token_rows(hidden_in.astype(bf16))
    g, u = dot(rows, wg, 1, 0), dot(rows, wu, 1, 0)
    sig = jax.nn.sigmoid(g)
    der = u * (sig * (1.0 + g * (1.0 - sig)))
    act = g * sig
    return hidden_in, out, rows, act.astype(bf16), der.astype(bf16), (act * u).astype(bf16)


def down_and_back(C, F, h, wd, hidden_in, cot, gain, act, der):
    if kernels_fit(C, F):
        return down_call(F, h, wd, hidden_in, cot, gain, act, der)
    out = token_sums(dot(h, wd, 1, 1))
    scale = rms(out)
    hat = out * scale
    g = cot.astype(f32)
    rows = token_rows(back(g * gain, hat, scale).astype(bf16))
    gh = dot(rows, wd, 1, 0)
    return (
        (hidden_in + hat * gain).astype(bf16),
        jnp.sum(g * hat, axis=0, keepdims=True),
        rows,
        (gh * der.astype(f32)).astype(bf16),
        (gh * act.astype(f32)).astype(bf16),
    )


def back_to_attn(C, F, grad_gate, grad_up, wg, wu, cot, out, gain, wo):
    if kernels_fit(C, F):
        return mid_call(F, grad_gate, grad_up, wg, wu, cot, out, gain, wo)
    resid = cot.astype(f32) + token_sums(dot(grad_gate, wg, 1, 1) + dot(grad_up, wu, 1, 1))
    scale = rms(out)
    hat = out * scale
    rows = token_rows(back(resid * gain, hat, scale).astype(bf16))
    return resid, jnp.sum(resid * hat, axis=0, keepdims=True), rows, dot(rows, wo, 1, 0).astype(bf16)


def back_to_input(C, F, grad_projected, w, resid):
    return (resid + token_sums(dot(grad_projected, w, 1, 1))).astype(bf16)


def kernels_fit(C, F):
    return C == 4 and F == 8 and UNITS_ATTN * 4 * 2 == C * F


def to_layer(C, F, x):
    z, chip = lax.axis_index("ctx"), lax.axis_index("fsdp") // 2
    x = x.reshape(C, x.shape[0] // C, x.shape[1])
    got = []
    for k in range(C):
        pairs = [
            (s * F + f, (f // 2) * F + 2 * ((s + k) % C) + f % 2) for s in range(C) for f in range(F)
        ]
        block = lax.dynamic_index_in_dim(x, (z + k) % C, 0, keepdims=False)
        got.append(lax.ppermute(block, BOTH, pairs))
    got = jnp.stack(got)
    got = [lax.dynamic_index_in_dim(got, (chip - s + C) % C, 0, keepdims=False) for s in range(C)]
    return jnp.concatenate(got, axis=0)


def from_layer(C, F, x):
    z, chip = lax.axis_index("ctx"), lax.axis_index("fsdp") // 2
    x = x.reshape(C, x.shape[0] // C, x.shape[1])
    got = []
    for k in range(C):
        pairs = [
            ((f // 2) * F + 2 * ((s + k) % C) + f % 2, s * F + f) for s in range(C) for f in range(F)
        ]
        block = lax.dynamic_index_in_dim(x, (chip - k + C) % C, 0, keepdims=False)
        got.append(lax.ppermute(block, BOTH, pairs))
    got = jnp.stack(got)
    got = [lax.dynamic_index_in_dim(got, (j - z + C) % C, 0, keepdims=False) for j in range(C)]
    return jnp.concatenate(got, axis=0)


def shards(C, F, layer_input, cotangent, positions, w_attn, w_ffn, gains, mom_attn, mom_ffn, gain_mom):
    z = lax.axis_index("ctx")
    f = lax.axis_index("fsdp")
    local_rows, width = layer_input.shape[1], layer_input.shape[2]
    seq_total, seq_length = positions.shape
    dz, head_cols = w_attn.shape[1], w_attn.shape[2]
    local_heads = head_cols // HEAD_DIM
    block_count = w_ffn.shape[2]
    per = seq_total // C
    piece = local_rows // C
    chips = F // per
    tokens = F * local_rows
    hidden_cols = block_count * head_cols
    units = UNITS_ATTN + 3 * block_count
    parts = C * F // units

    def after(a, b):
        return lax.optimization_barrier((a, b))[0]

    def rows_gather(shard):
        return lax.all_gather(shard, "ctx", axis=0, tiled=True)

    def rows_product(lhs, rhs):
        return dot(lhs.reshape(tokens, width), rhs, 0, 0).astype(bf16)

    def rows_scatter(grad):
        return lax.psum_scatter(grad, "ctx", scatter_dimension=0, tiled=True)

    w_qkv = rows_gather(jnp.concatenate([w_attn[0], w_attn[1], w_attn[2]], axis=1))
    w_out = rows_gather(w_attn[3])
    ffn_flat = w_ffn.reshape(3, dz, hidden_cols)
    w_gate = rows_gather(ffn_flat[0])
    w_up = rows_gather(ffn_flat[1])
    w_down = rows_gather(ffn_flat[2])
    gain_query = lax.dynamic_slice_in_dim(gains[0], f * head_cols, head_cols)
    gain_key = lax.dynamic_slice_in_dim(gains[1], f * head_cols, head_cols)
    pos = lax.dynamic_slice_in_dim(positions, z * per, per, 0)
    pos = jnp.transpose(pos.reshape(per, C, chips, piece), (0, 2, 1, 3)).reshape(per, seq_length)
    cosine_table, sine_table = rotary_tables(pos)
    kernels = kernels_fit(C, F)

    def heads(a):
        return jnp.transpose(
            a.reshape(chips, per, local_rows, local_heads, HEAD_DIM), (1, 0, 2, 3, 4)
        ).reshape(per, seq_length, local_heads, HEAD_DIM)

    def unheads(a):
        return jnp.transpose(
            a.reshape(per, chips, local_rows, local_heads, HEAD_DIM), (1, 0, 2, 3, 4)
        ).reshape(tokens, head_cols)

    if kernels:
        sign = jnp.where(jnp.arange(HEAD_DIM) < HEAD_DIM // 2, -1.0, 1.0)
        tables = (
            gain_query[None],
            gain_key[None],
            jnp.broadcast_to(cosine_table[:, :, 0], (per, seq_length, HEAD_DIM)),
            sine_table[:, :, 0] * sign,
            pos.astype(f32)[:, None, :],
            jnp.broadcast_to(pos.astype(f32)[..., None], (per, seq_length, HEAD_DIM)),
        )
        own_input, own_grad, input_all = enter_call(
            C, F, layer_input.reshape(local_rows, width), cotangent.reshape(local_rows, width)
        )
        projected, stats = qkv_call(F, input_all, w_qkv)
        attn_mixed, query_rows, key_rows, log_total = attend_call(F, projected, stats, *tables)
        attn_mixed = attn_mixed.reshape(tokens, head_cols)
    else:
        own_input, input_all, projected = project(C, F, layer_input.reshape(local_rows, width), w_qkv)
        own_grad = to_layer(C, F, after(cotangent.reshape(local_rows, width), own_input))
        query_raw = projected[:, :head_cols]
        key_raw = projected[:, head_cols : 2 * head_cols]
        value_raw = projected[:, 2 * head_cols :]
        query_total, key_total = norm_stats(
            jnp.sum(query_raw * query_raw, axis=-1), jnp.sum(key_raw * key_raw, axis=-1)
        )
        query_scale = lax.rsqrt(query_total / width + epsilon)[..., None]
        key_scale = lax.rsqrt(key_total / width + epsilon)[..., None]
        query_hat = query_raw * query_scale
        key_hat = key_raw * key_scale
        query_rows = (
            rotate(heads(query_hat * gain_query), cosine_table, sine_table) * HEAD_DIM ** (-0.5)
        ).astype(bf16)
        key_rows = rotate(heads(key_hat * gain_key), cosine_table, sine_table).astype(bf16)
        value_rows = heads(value_raw.astype(bf16))
        attn_mixed, log_total = attend(query_rows, key_rows, value_rows, pos)
        attn_mixed = unheads(attn_mixed)
    hidden_in, attn_out, mlp_all, act, der, hidden = attn_out_and_up(
        C, F, attn_mixed, w_out, own_input, gains[2:3], w_gate, w_up
    )
    result, mlp_gain, grad_mlp_all, grad_gate, grad_up = down_and_back(
        C, F, hidden, w_down, hidden_in, own_grad, gains[3:4], act, der
    )
    p_down = rows_product(grad_mlp_all, hidden)
    p_gate = rows_product(mlp_all, grad_gate)
    p_up = rows_product(mlp_all, grad_up)
    g_down = rows_scatter(p_down)
    g_gate = rows_scatter(p_gate)
    g_up = rows_scatter(p_up)
    grad_gate, grad_up, p_down, p_gate, p_up = lax.optimization_barrier(
        (grad_gate, grad_up, p_down, p_gate, p_up)
    )
    grad_resid, attn_gain, grad_attn_all, grad_mixed = back_to_attn(
        C, F, grad_gate, grad_up, w_gate, w_up, own_grad, attn_out, gains[2:3], w_out
    )
    p_out = rows_product(grad_attn_all, attn_mixed)
    grad_mixed, p_out, g_down = lax.optimization_barrier((grad_mixed, p_out, g_down))
    g_out = rows_scatter(p_out)
    if kernels:
        weighted_q, weighted_k, grad_value, inner, gain_cols = attend_back_call(
            F, projected, query_rows, key_rows, grad_mixed, log_total, stats, *tables
        )
        inner = jnp.transpose(
            jnp.sum(inner, axis=1).reshape(per, 8, chips, local_rows), (1, 2, 0, 3)
        ).reshape(8, tokens)
        gain_cols = jnp.sum(gain_cols, axis=0)
        query_gain_cols = gain_cols[:, 0].reshape(head_cols)
        key_gain_cols = gain_cols[:, 1].reshape(head_cols)
        flat = (tokens, head_cols)
        zero = jnp.zeros((width,), f32)
        gain_local = jnp.stack(
            [
                lax.dynamic_update_slice(zero, query_gain_cols, (f * head_cols,)),
                lax.dynamic_update_slice(zero, key_gain_cols, (f * head_cols,)),
                attn_gain[0],
                mlp_gain[0],
                *[zero] * 4,
            ]
        )
        grad_rows, grad_projected, gain_layer = last_call(
            F, weighted_q.reshape(flat), weighted_k.reshape(flat), grad_value.reshape(flat),
            projected, stats, inner, w_qkv, grad_resid, gain_local,
        )
    else:
        grad_query, grad_key, grad_value = attend_back(
            query_rows, key_rows, value_rows, pos, heads(grad_mixed), log_total
        )
        grad_query_norm = unheads(unrotate(grad_query * HEAD_DIM ** (-0.5), cosine_table, sine_table))
        grad_key_norm = unheads(unrotate(grad_key, cosine_table, sine_table))
        query_gain_cols = jnp.sum(grad_query_norm * query_hat, axis=0)
        key_gain_cols = jnp.sum(grad_key_norm * key_hat, axis=0)
        query_weighted = grad_query_norm * gain_query
        key_weighted = grad_key_norm * gain_key
        query_inner, key_inner = norm_stats(
            jnp.sum(query_weighted * query_hat, axis=-1), jnp.sum(key_weighted * key_hat, axis=-1)
        )
        grad_query_raw = query_scale * (query_weighted - query_hat * (query_inner / width)[..., None])
        grad_key_raw = key_scale * (key_weighted - key_hat * (key_inner / width)[..., None])
        grad_projected = jnp.concatenate(
            [grad_query_raw.astype(bf16), grad_key_raw.astype(bf16), unheads(grad_value).astype(bf16)],
            axis=1,
        )
        grad_rows = back_to_input(C, F, grad_projected, w_qkv, grad_resid)
    p_qkv = rows_product(input_all, grad_projected)
    g_qkv = rows_scatter(p_qkv)
    if not kernels:
        grad_input = from_layer(C, F, grad_rows)
        result = from_layer(C, F, result)
        zero = jnp.zeros((width,), f32)
        gain_local = jnp.stack(
            [
                lax.dynamic_update_slice(zero, query_gain_cols, (f * head_cols,)),
                lax.dynamic_update_slice(zero, key_gain_cols, (f * head_cols,)),
                attn_gain[0],
                mlp_gain[0],
            ]
        )
        gain_total = jnp.sum(lax.all_gather(gain_local, BOTH, axis=0, tiled=False), axis=0)

    g_qkv, g_out, g_gate, g_up, g_down, _ = lax.optimization_barrier(
        (g_qkv, g_out, g_gate, g_up, g_down, grad_rows)
    )
    g_qkv, g_out, g_gate, g_up, g_down = (g.astype(f32) for g in (g_qkv, g_out, g_gate, g_up, g_down))
    grad_attn = jnp.stack(
        [g_qkv[:, :head_cols], g_qkv[:, head_cols : 2 * head_cols], g_qkv[:, 2 * head_cols :], g_out]
    )
    grad_ffn = jnp.stack([g_gate, g_up, g_down]).reshape(3, dz, block_count, head_cols)
    new_attn = momentum * mom_attn + grad_attn
    new_ffn = momentum * mom_ffn + grad_ffn
    send = jnp.concatenate(
        [
            new_attn.astype(bf16),
            jnp.transpose(new_ffn.astype(bf16), (0, 2, 1, 3)).reshape(3 * block_count, dz, head_cols),
        ],
        axis=0,
    ).reshape(C * F, dz // parts, head_cols)
    got = lax.all_to_all(send, BOTH, split_axis=0, concat_axis=0, tiled=True)
    own = jnp.transpose(got.reshape(C, F, dz // parts, head_cols), (0, 2, 1, 3)).reshape(
        C * dz // parts, F * head_cols
    )

    def peers(a):
        out = [a]
        for s in range(1, parts):
            pairs = [(i, i - i % parts + (i + parts - s) % parts) for i in range(C * F)]
            out.append(lax.ppermute(a, BOTH, pairs))
        return out

    if kernels:
        own, back_rows, gain_total = newton_call(C, own, jnp.stack([result, grad_rows]), gain_layer)
        result, grad_input, gain_total = back_rows[0], back_rows[1], gain_total[:4]
    else:
        own32 = own.astype(f32)
        square = jnp.sum(own32 * own32)
        total = sum(peers(square.reshape(1, 1)))
        inv = 1.0 / (jnp.sqrt(total) + 1e-07)
        for iteration in range(NS_STEPS):
            factor = inv if iteration == 0 else 1.0
            every = peers(own)
            gram = [(dot(own, b, 1, 1) * (factor * factor)).astype(bf16) for b in every]
            product = sum(dot(g, b, 1, 0) for g, b in zip(gram, every)) * factor
            product_all = peers(product.astype(bf16))
            product_two = sum(dot(g, b, 1, 0) for g, b in zip(gram, product_all))
            own = (
                quintic_one * factor * own.astype(f32) + quintic_two * product + quintic_three * product_two
            ).astype(bf16)
    own, result, grad_input = lax.optimization_barrier((own, result, grad_input))
    home = jnp.transpose(own.reshape(C, dz // parts, F, head_cols), (0, 2, 1, 3)).reshape(
        C * F, dz // parts, head_cols
    )
    steps = lax.all_to_all(home, BOTH, split_axis=0, concat_axis=0, tiled=True)
    steps = -muon_rate * steps.astype(f32).reshape(units, dz, head_cols)
    step_attn = steps[:UNITS_ATTN]
    step_ffn = jnp.transpose(
        steps[UNITS_ATTN:].reshape(3, block_count, dz, head_cols), (0, 2, 1, 3)
    )
    new_gain_mom = momentum * gain_mom + gain_total
    return (
        result.reshape(layer_input.shape),
        grad_input.astype(f32).reshape(layer_input.shape),
        grad_attn,
        grad_ffn,
        gain_total,
        new_attn,
        new_ffn,
        new_gain_mom,
        step_attn,
        step_ffn,
        -gain_rate * new_gain_mom,
    )


def solution(mesh):
    tokens = P("fsdp", "ctx", None)
    attn = P(None, "ctx", "fsdp")
    ffn = P(None, "ctx", None, "fsdp")
    in_specs = (tokens, tokens, P(), attn, ffn, P(), attn, ffn, P())
    out_specs = (tokens, tokens, attn, ffn, P(), attn, ffn, P(), attn, ffn, P())
    body = functools.partial(shards, mesh.shape["ctx"], mesh.shape["fsdp"])
    return jax.shard_map(body, mesh=mesh, in_specs=in_specs, out_specs=out_specs, check_vma=False)
```

time: 1750 us -> 1230 us (0.70); the launches traced: 1720 us -> 1220 us
  Pallas kernels: 0 us -> 642 us
  waiting for transfers between devices: 921 us -> 399 us
  matrix products: 362 us -> 60.8 us
  blocking collectives: 113 us -> 0 us
  starting transfers between devices: 102 us -> 15.5 us
  local copies, waits for them, and re-layouts: 117 us -> 59.8 us
  other arithmetic: 86.1 us -> 30.6 us
    pallas_call x0 -> x10, Pallas kernels: none -> 642 us  [the longest x1 135 us: newton_call(): pl.pallas_call(functools.partial(newton_kernel, C), out_shape=[jax.ShapeD...]
    ppermute x41 -> x0, waiting for transfers between devices: 507 us -> none  [the longest x15 276 us: ring_gather(): held.append(lax.ppermute(held[-1], 'ctx', ring))]
    dot_general x48 -> x5, matrix products: 328 us -> 60.8 us  [dot(): lax.dot_general(a, b, (((ca,), (cb,)), ((), ())), preferred_element_type=...]
    reduce_scatter x4 -> x5, waiting for transfers between devices: 258 us -> 96.1 us  [rows_scatter(): return lax.psum_scatter(grad, 'ctx', scatter_dimension=0, tiled=True)]
    ppermute x41 -> x0, starting transfers between devices: 98.1 us -> none  [the longest x15 84.9 us: ring_gather(): held.append(lax.ppermute(held[-1], 'ctx', ring))]
    all_to_all x1 -> x0, blocking collectives: 95.4 us -> none  [shards(): got = lax.all_to_all(send, BOTH, split_axis=0, concat_axis=0, tiled=True)]
    all_to_all x0 -> x1, waiting for transfers between devices: none -> 90.9 us  [shards(): got = lax.all_to_all(send, BOTH, split_axis=0, concat_axis=0, tiled=True)]
    all_to_all x1, waiting for transfers between devices: 0.01 us -> 77.2 us  [shards(): steps = lax.all_to_all(home, BOTH, split_axis=0, concat_axis=0, tiled=True)]
  transfers between devices with their start and end apart: 51 -> 12, of which waited for: 36 -> 8; matrix products, arithmetic and copies ran while one was open for 13% -> 7% of each run, Pallas kernels for 0% -> 34%
where the time goes in v2:
time: 1230 us; the launch traced here: 1220 us
  Pallas kernels  642 us (52%)
  waiting for transfers between devices  399 us (32%)
  matrix products  60.8 us (5%)
  local copies, waits for them, and re-layouts  59.8 us (5%)
  other arithmetic  30.6 us (2%)
  starting transfers between devices  15.5 us (1%)
  between operations  14.8 us (1%)
    pallas_call x1, Pallas kernels, newton_call(): pl.pallas_call(functools.partial(newton_kernel, C), out_shape=[jax.ShapeD...  135 us
    all_gather x5, waiting for transfers between devices, rows_gather(): return lax.all_gather(shard, 'ctx', axis=0, tiled=True)  134 us
    pallas_call x1, Pallas kernels, mid_call(): pl.pallas_call(mid_kernel, out_shape=[jax.ShapeDtypeStruct((R, D), f32),...  96.3 us
    pallas_call x1, Pallas kernels, enter_call(): pl.pallas_call(functools.partial(enter_kernel, C), out_shape=[one, one, j...  96.2 us
    reduce_scatter x5, waiting for transfers between devices, rows_scatter(): return lax.psum_scatter(grad, 'ctx', scatter_dimension=0, tiled=True)  96.1 us
    pallas_call x1, Pallas kernels, down_call(): pl.pallas_call(down_kernel, out_shape=[jax.ShapeDtypeStruct((R, D), bf16)...  95.3 us
    all_to_all x1, waiting for transfers between devices, shards(): got = lax.all_to_all(send, BOTH, split_axis=0, concat_axis=0, tiled=True)  90.9 us
    all_to_all x1, waiting for transfers between devices, shards(): steps = lax.all_to_all(home, BOTH, split_axis=0, concat_axis=0, tiled=True)  77.2 us
  transfers between devices with their start and end apart: 12, of which 8 were waited for; matrix products, arithmetic and copies ran while one was open for 7% of the time, Pallas kernels for 34%

profile of v2, /device:TPU:0, one launch (start us, length us, event | category | flops | bytes accessed | tf_op | source)
XLA Modules:
  0.0 1222.0 jit_solution(85240483964695485)
XLA Ops:
  20.2 96.2 %shard_map.176 = (bf16[256,2048]{1,0:T(8,128)(2,1)}, bf16[256,2048]{1,0:T(8,128)(2,1)}, bf16[8,256,2048]{2,1,0:T(8,128)(2,1)}) custom-call(bf16[256,2048]{1,0:T(8,128)(2,1)} %bitcast.114, bf16[256,2048]{1,0:T(8,128)(2,1)} %bitcast.115), custom_call_target="tpu_custom_call" | custom-call | flops 74999996416 | bytes 1048576 | tf_op jit(solution)/shard_map/pallas_call | solution.py:406
  122.2 22.3 %shard_map.177 = (f32[2048,768]{1,0:T(8,128)}, f32[8,8,2048]{2,1,0:T(8,128)}) custom-call(bf16[8,256,2048]{2,1,0:T(8,128)(2,1)} %get-tuple-element.60.all_ref, bf16[2048,768]{1,0:T(8,128)(2,1)} %all-gather.7.cloned.1.call-done.w_ref), custom_call_target="tpu_custom_call" | custom-call | flops 22000001024 | bytes 1048576 | tf_op jit(solution)/shard_map/pallas_call | solution.py:470
  145.8 17.7 %shard_map.178 = (bf16[4,2,256,256]{3,2,1,0:T(8,128)(2,1)}, bf16[4,2,256,256]{3,2,1,0:T(8,128)(2,1)}, bf16[4,2,256,256]{3,2,1,0:T(8,128)(2,1)}, f32[2,2,1024,128]{3,2,1,0:T(8,128)}) custom-call(f32[4,2,256,768]{3,2,1,0:T(8,128)} %bitcast.123, f32[4,2,256,768]{3,2,1,0:T(8,128)} %bitcast.124, f32[4,2,256,768]{3,2,1,0:T(8,128)} %bitcast.125, ...), custom_call_target="tpu_custom_call" | custom-call | flops 15000000512 | bytes 1048576 | tf_op jit(solution)/shard_map/pallas_call | solution.py:1006
  163.5 46.4 %shard_map.179 = (f32[256,2048]{1,0:T(8,128)}, f32[256,2048]{1,0:T(8,128)}, bf16[256,2048]{1,0:T(8,128)(2,1)}) custom-call(bf16[2048,256]{1,0:T(8,128)(2,1)} %bitcast.131, bf16[2048,256]{1,0:T(8,128)(2,1)} %bitcast.116, bf16[256,2048]{1,0:T(8,128)(2,1)} %get-tuple-element.66.x_ref, f32[1,2048]{1,0:T(1,128)} %get-tuple-element.156.gain_ref), custom_call_target="tpu_custom_call" | custom-call | flops 46000001024 | bytes 1048576 | tf_op jit(solution)/shard_map/pallas_call | solution.py:524
  209.9 18.0 %all-gather.11.cloned.1.call-done.wu_ref = bf16[2048,1024]{1,0:T(8,128)(2,1)} async-done(((bf16[512,1024]{1,0:T(8,128)(2,1)}), bf16[2048,1024]{1,0:T(8,128)(2,1)}) %all-gather.11.cloned.1.call-update) | async-done | bytes 4194320 | tf_op jit(solution)/shard_map/all_gather | solution.py:1392
  227.9 81.3 %all-gather.9.cloned.1.call-done.wg_ref = bf16[2048,1024]{1,0:T(8,128)(2,1)} async-done(((bf16[512,1024]{1,0:T(8,128)(2,1)}), bf16[2048,1024]{1,0:T(8,128)(2,1)}) %all-gather.9.cloned.1.call-update) | async-done | bytes 4194320 | tf_op jit(solution)/shard_map/all_gather | solution.py:1392
  309.2 47.0 %shard_map.180 = (bf16[8,256,2048]{2,1,0:T(8,128)(2,1)}, bf16[2048,1024]{1,0:T(8,128)(2,1)}, bf16[2048,1024]{1,0:T(8,128)(2,1)}, bf16[2048,1024]{1,0:T(8,128)(2,1)}) custom-call(bf16[256,2048]{1,0:T(8,128)(2,1)} %get-tuple-element.67.in_ref, bf16[2048,1024]{1,0:T(8,128)(2,1)} %all-gather.9.cloned.1.call-done.wg_ref, ...), custom_call_target="tpu_custom_call" | custom-call | flops 46000001024 | bytes 1048576 | tf_op jit(solution)/shard_map/pallas_call | solution.py:600
  356.2 34.3 %all-gather.13.cloned.1.call-done.wd_ref = bf16[2048,1024]{1,0:T(8,128)(2,1)} async-done(((bf16[512,1024]{1,0:T(8,128)(2,1)}), bf16[2048,1024]{1,0:T(8,128)(2,1)}) %all-gather.13.cloned.1.call-update) | async-done | bytes 4194320 | tf_op jit(solution)/shard_map/all_gather | solution.py:1392
  390.6 95.3 %shard_map.181 = (bf16[256,2048]{1,0:T(8,128)(2,1)}, f32[1,2048]{1,0:T(1,128)}, bf16[8,256,2048]{2,1,0:T(8,128)(2,1)}, bf16[2048,1024]{1,0:T(8,128)(2,1)}, bf16[2048,1024]{1,0:T(8,128)(2,1)}) custom-call(bf16[2048,1024]{1,0:T(8,128)(2,1)} %get-tuple-element.68.h_ref, bf16[2048,1024]{1,0:T(8,128)(2,1)} %all-gather.13.cloned.1.call-done.wd_ref, ...), custom_call_target="tpu_custom_call" | custom-call | flops 92000002048 | bytes 1048576 | tf_op jit(solution)/shard_map/pallas_call | solution.py:693
  485.8 14.4 %convolution_convert_fusion.2 = bf16[2048,1024]{1,0:T(8,128)(2,1)} fusion(bf16[2048,2048]{1,0:T(8,128)(2,1)} %bitcast.122, bf16[2048,1024]{1,0:T(8,128)(2,1)} %get-tuple-element.68.h_ref), kind=kOutput, calls=%fused_computation.6 | convolution fusion | flops 8592031744 | bytes 16777216 | tf_op jit(solution)/shard_map/dot_general | solution.py:27
  500.3 14.0 %convolution_convert_fusion = bf16[2048,1024]{1,0:T(8,128)(2,1)} fusion(bf16[2048,2048]{1,0:T(8,128)(2,1)} %bitcast.119, bf16[2048,1024]{1,0:T(8,128)(2,1)} %get-tuple-element.78.up_ref), kind=kOutput, calls=%fused_computation.4 | convolution fusion | flops 8592031744 | bytes 16777216 | tf_op jit(solution)/shard_map/dot_general | solution.py:27
  514.3 14.0 %convolution_convert_fusion.1 = bf16[2048,1024]{1,0:T(8,128)(2,1)} fusion(bf16[2048,2048]{1,0:T(8,128)(2,1)} %bitcast.120, bf16[2048,1024]{1,0:T(8,128)(2,1)} %get-tuple-element.77.gate_ref), kind=kOutput, calls=%fused_computation.5 | convolution fusion | flops 8592031744 | bytes 16777216 | tf_op jit(solution)/shard_map/dot_general | solution.py:27
  528.4 96.3 %shard_map.182 = (f32[256,2048]{1,0:T(8,128)}, f32[1,2048]{1,0:T(1,128)}, bf16[8,256,2048]{2,1,0:T(8,128)(2,1)}, bf16[2048,256]{1,0:T(8,128)(2,1)}) custom-call(bf16[2048,1024]{1,0:T(8,128)(2,1)} %get-tuple-element.77.gate_ref, bf16[2048,1024]{1,0:T(8,128)(2,1)} %get-tuple-element.78.up_ref, bf16[2048,1024]{1,0:T(8,128)(2,1)} %all-gather.9.cloned.1.call-done.wg_ref, ...), custom_call_target="tpu_custom_call" | custom-call | flops 92000002048 | bytes 1048576 | tf_op jit(solution)/shard_map/pallas_call | solution.py:788
  624.8 7.0 convolution_convert_fusion.4
  631.8 25.1 %shard_map.183 = (f32[4,2,256,256]{3,2,1,0:T(8,128)}, f32[4,2,256,256]{3,2,1,0:T(8,128)}, bf16[4,2,256,256]{3,2,1,0:T(8,128)(2,1)}, f32[2,2,8,1024]{3,2,1,0:T(8,128)}, f32[2,2,8,128]{3,2,1,0:T(8,128)}) custom-call(f32[4,2,256,768]{3,2,1,0:T(8,128)} %bitcast.126, f32[4,2,256,768]{3,2,1,0:T(8,128)} %bitcast.127, f32[4,2,256,768]{3,2,1,0:T(8,128)} %bitcast.128, ...), custom_call_target="tpu_custom_call" | custom-call | flops 35000000512 | bytes 1048576 | tf_op jit(solution)/shard_map/pallas_call | solution.py:1071
  660.1 60.9 %shard_map.184 = (bf16[256,2048]{1,0:T(8,128)(2,1)}, bf16[2048,768]{1,0:T(8,128)(2,1)}, f32[8,2048]{1,0:T(8,128)}) custom-call(f32[2048,256]{1,0:T(8,128)} %bitcast.129, f32[2048,256]{1,0:T(8,128)} %bitcast.130, bf16[2048,256]{1,0:T(8,128)(2,1)} %bitcast.133, f32[2048,768]{1,0:T(8,128)} %get-tuple-element.61.proj_ref, ...), custom_call_target="tpu_custom_call" | custom-call | flops 54999998464 | bytes 1048576 | tf_op jit(solution)/shard_map/pallas_call | solution.py:884
  721.0 11.4 convolution_convert_fusion.3
  736.8 30.1 %reduce-scatter.10.cloned.1.call-done = bf16[512,256]{1,0:T(8,128)(2,1)} async-done(((bf16[2048,256]{1,0:T(8,128)(2,1)}), bf16[512,256]{1,0:T(8,128)(2,1)}) %reduce-scatter.10.cloned.1.call-update) | async-done | bytes 262160 | tf_op jit(solution)/shard_map/reduce_scatter | solution.py:1398
  766.8 61.7 %reduce-scatter.8.cloned.1.call-done = bf16[512,768]{1,0:T(8,128)(2,1)} async-done(((bf16[2048,768]{1,0:T(8,128)(2,1)}), bf16[512,768]{1,0:T(8,128)(2,1)}) %reduce-scatter.8.cloned.1.call-update) | async-done | bytes 786448 | tf_op jit(solution)/shard_map/reduce_scatter | solution.py:1398
  857.8 90.9 %all-to-all-done = bf16[32,256,256]{2,1,0:T(8,128)(2,1)} async-done(((bf16[32,256,256]{2,1,0:T(8,128)(2,1)}), bf16[32,256,256]{2,1,0:T(8,128)(2,1)}, u32[]{:S(2)}, u32[]{:S(2)}) %all-to-all-start) | async-done | bytes 4194336 | tf_op jit(solution)/shard_map/all_to_all | solution.py:1558
  956.8 134.8 %shard_map.185 = (bf16[1024,2048]{1,0:T(8,128)(2,1)}, bf16[2,256,2048]{2,1,0:T(8,128)(2,1)}, f32[8,2048]{1,0:T(8,128)}) custom-call(bf16[1024,2048]{1,0:T(8,128)(2,1)} %bitcast.99, bf16[2,256,2048]{2,1,0:T(8,128)(2,1)} %pad_maximum_fusion.2.rows_ref, f32[8,2048]{1,0:T(8,128)} %get-tuple-element.102.gain_ref), custom_call_target="tpu_custom_call" | custom-call | flops 95000002560 | bytes 1048576 | tf_op jit(solution)/shard_map/pallas_call | solution.py:1260
  1099.4 10.0 all-to-all-start.1
  1125.7 77.2 %all-to-all-done.1 = bf16[32,256,256]{2,1,0:T(8,128)(2,1)} async-done(((bf16[32,256,256]{2,1,0:T(8,128)(2,1)}), bf16[32,256,256]{2,1,0:T(8,128)(2,1)}, u32[]{:S(2)}, u32[]{:S(2)}) %all-to-all-start.1) | async-done | bytes 4194336 | tf_op jit(solution)/shard_map/all_to_all | solution.py:1592
  1208.1 6.9 copy.42
  (115 shorter events, 94.1 us)
Async XLA Ops:
  7.2 115.0 %all-gather.7.cloned.1.call-start = ((), (), s32[]{:S(2)}) async-start(), calls=%async_computation.7 | async-start | bytes 3932160 | tf_op jit(solution)/shard_map/all_gather | solution.py:1392
  10.1 153.4 %all-gather.15.cloned.1.call-start = ((), (), s32[]{:S(2)}) async-start(), calls=%async_computation.16 | async-start | bytes 1310720 | tf_op jit(solution)/shard_map/all_gather | solution.py:1392
  10.9 217.0 %all-gather.11.cloned.1.call-start = ((), (), s32[]{:S(2)}) async-start(), calls=%async_computation.9 | async-start | bytes 5242880 | tf_op jit(solution)/shard_map/all_gather | solution.py:1392
  15.1 294.1 %all-gather.9.cloned.1.call-start = ((), (), s32[]{:S(2)}) async-start(), calls=%async_computation.8 | async-start | bytes 5242880 | tf_op jit(solution)/shard_map/all_gather | solution.py:1392
  16.4 374.2 %all-gather.13.cloned.1.call-start = ((), (), s32[]{:S(2)}) async-start(), calls=%async_computation.10 | async-start | bytes 5242880 | tf_op jit(solution)/shard_map/all_gather | solution.py:1392
  17.7 614.1 %reduce-scatter.6.cloned.1.call-start = ((), (), s32[]{:S(2)}) async-start(), calls=%async_computation.11 | async-start | bytes 5242880 | tf_op jit(solution)/shard_map/reduce_scatter | solution.py:1398
  500.2 232.2 %reduce-scatter.14.cloned.1.call-start = ((), (), s32[]{:S(2)}) async-start(), calls=%async_computation.15 | async-start | bytes 5242880 | tf_op jit(solution)/shard_map/reduce_scatter | solution.py:1398
  514.3 222.5 %reduce-scatter.12.cloned.1.call-start = ((), (), s32[]{:S(2)}) async-start(), calls=%async_computation.14 | async-start | bytes 5242880 | tf_op jit(solution)/shard_map/reduce_scatter | solution.py:1398
  528.4 238.4 %reduce-scatter.10.cloned.1.call-start = ((), (), s32[]{:S(2)}) async-start(), calls=%async_computation.13 | async-start | bytes 1310720 | tf_op jit(solution)/shard_map/reduce_scatter | solution.py:1398
  528.4 96.4 %copy-start.14 = (bf16[4,2,256,256]{3,2,1,0:T(8,128)(2,1)S(1)}, bf16[4,2,256,256]{3,2,1,0:T(8,128)(2,1)}, u32[]{:S(2)}) copy-start(bf16[4,2,256,256]{3,2,1,0:T(8,128)(2,1)} %get-tuple-element.65) | copy-start | bytes 3145732
  631.8 27.6 %copy-start.12 = (f32[1,2048]{1,0:T(1,128)S(1)}, f32[1,2048]{1,0:T(1,128)}, u32[]{:S(2)}) copy-start(f32[1,2048]{1,0:T(1,128)} %get-tuple-element.91) | copy-start | bytes 24580
  631.8 27.6 %copy-start.13 = (f32[1,2048]{1,0:T(1,128)S(1)}, f32[1,2048]{1,0:T(1,128)}, u32[]{:S(2)}) copy-start(f32[1,2048]{1,0:T(1,128)} %get-tuple-element.90) | copy-start | bytes 24580
  659.3 169.2 %reduce-scatter.8.cloned.1.call-start = ((), (), s32[]{:S(2)}) async-start(), calls=%async_computation.12 | async-start | bytes 3932160 | tf_op jit(solution)/shard_map/reduce_scatter | solution.py:1398
  736.8 95.0 %copy-start.7 = (bf16[512,1024]{1,0:T(8,128)(2,1)S(1)}, bf16[512,1024]{1,0:T(8,128)(2,1)}, u32[]{:S(2)}) copy-start(bf16[512,1024]{1,0:T(8,128)(2,1)} %reduce-scatter.12.cloned.1.call-done) | copy-start | bytes 3145732
  766.8 64.1 %copy-start.8 = (bf16[512,256]{1,0:T(8,128)(2,1)S(1)}, bf16[512,256]{1,0:T(8,128)(2,1)}, u32[]{:S(2)}) copy-start(bf16[512,256]{1,0:T(8,128)(2,1)} %reduce-scatter.10.cloned.1.call-done) | copy-start | bytes 786436
  838.7 6.3 copy-start.2
  838.7 6.3 copy-start.3
  849.9 98.8 %all-to-all-start = ((bf16[32,256,256]{2,1,0:T(8,128)(2,1)}), bf16[32,256,256]{2,1,0:T(8,128)(2,1)}, u32[]{:S(2)}, u32[]{:S(2)}) async-start(bf16[32,256,256]{2,1,0:T(8,128)(2,1)} %bitcast.94), calls=%async_computation.5 | async-start | bytes 8388608 | tf_op jit(solution)/shard_map/all_to_all | solution.py:1558
  1099.4 103.5 %all-to-all-start.1 = ((bf16[32,256,256]{2,1,0:T(8,128)(2,1)}), bf16[32,256,256]{2,1,0:T(8,128)(2,1)}, u32[]{:S(2)}, u32[]{:S(2)}) async-start(bf16[32,256,256]{2,1,0:T(8,128)(2,1)} %bitcast.93), calls=%async_computation.6 | async-start | bytes 8388608 | tf_op jit(solution)/shard_map/all_to_all | solution.py:1592
  1109.4 7.3 slice-start
  1109.9 6.8 slice-start.1
  1116.7 6.8 copy-start.9
  1116.7 6.8 copy-start.11
  1116.7 7.4 copy-start.1
  (5 other events, 26.5 us)
Sparse Core Ops, SparseCore 0:
  10.3 106.4 all-gather.6
  118.9 26.4 all-gather.14
  147.6 80.2 all-gather.10
  229.9 79.2 all-gather.8
  311.2 79.2 all-gather.12
  500.4 75.8 reduce-scatter.5
  579.2 77.3 reduce-scatter.13
  659.4 77.2 reduce-scatter.11
  739.2 27.6 reduce-scatter.9
  769.5 58.8 reduce-scatter.7

commit v3 on v2

--- a/solution.py
+++ b/solution.py
@@ -211,7 +211,7 @@
     ]
 
 
-def scatter_phase(at, partial, bufs, send, recv, base):
+def scatter_phase(at, partial, bufs, send, recv, base, between=None):
     to_core, from_core, mine, out, inc = bufs
     R, D = to_core.shape[1], to_core.shape[2]
     half = R // 2
@@ -256,6 +256,8 @@
 
     compute(0, at.qd, 0)
     compute(1, at.qx, 1)
+    if between is not None:
+        between()
     chip_sum(0, 0)
     go(4, out.at[0, A], inc.at[0, A], at.fx)
     go(5, out.at[0, B], inc.at[0, B], at.fy)
@@ -334,90 +336,99 @@
                 c.wait()
 
 
-def enter_kernel(C, x_ref, g_ref, own_ref, gown_ref, all_ref, stage, mine, rows, gown, lsem, osem, send, recv, tsend, trecv):
-    at = Plane()
-    z = lax.axis_index("ctx")
-    F, R = rows.shape[0], rows.shape[1]
-    piece = R // C
-    barrier = pltpu.get_barrier_semaphore()
-    for k in range(1, C):
-        pl.semaphore_signal(barrier, inc=1, device_id={"ctx": (z + k) % C}, device_id_type=MESH)
-        pl.semaphore_signal(
-            barrier, inc=1, device_id={"fsdp": 2 * ((at.chip + k) % C) + at.c}, device_id_type=MESH
-        )
-    pl.semaphore_signal(barrier, inc=1, device_id={"fsdp": at.fc}, device_id_type=MESH)
-    loads = [local(x_ref, mine.at[0], lsem, 0), local(g_ref, mine.at[1], lsem, 1)]
-    pl.semaphore_wait(barrier, 2 * (C - 1) + 1)
-    sent = []
-    keep = []
-    for a in range(2):
-        loads[a].wait()
+class Moving:
+    def __init__(self, at, C, mine, stage, landing, lsem, base, send, recv):
+        self.at, self.C, self.mine, self.stage, self.landing = at, C, mine, stage, landing
+        self.lsem, self.base, self.send, self.recv = lsem, base, send, recv
+        self.z = lax.axis_index("ctx")
+        self.piece = mine.shape[0] // C
+        self.sent = []
+
+    def greet(self, barrier):
+        at, C = self.at, self.C
+        for k in range(1, C):
+            pl.semaphore_signal(barrier, inc=1, device_id={"ctx": (self.z + k) % C}, device_id_type=MESH)
+            pl.semaphore_signal(
+                barrier, inc=1, device_id={"fsdp": 2 * ((at.chip + k) % C) + at.c}, device_id_type=MESH
+            )
+
+    def first(self):
+        at, C, piece = self.at, self.C, self.piece
         for k in range(1, C):
             j = (at.chip + k) % C
-            c = remote(
-                mine.at[a, pl.ds(j * piece, piece)], stage.at[a, at.chip], tsend, trecv, 2 * C * a + k, 2 * j + at.c
-            )
+            src = self.mine.at[pl.ds(j * piece, piece)]
+            c = remote(src, self.stage.at[at.chip], self.send, self.recv, k, 2 * j + at.c)
             c.start()
-            sent.append(c)
-        keep.append(local(mine.at[a, pl.ds(at.chip * piece, piece)], stage.at[a, at.chip], lsem, 2 + a))
-
-    def landing(a, layer):
-        r = pl.ds(layer * piece, piece)
-        return rows.at[at.f, r] if a == 0 else gown.at[r]
-
-    for a in range(2):
-        keep[a].wait()
+            self.sent.append(c)
+        src = self.mine.at[pl.ds(at.chip * piece, piece)]
+        self.keep = local(src, self.stage.at[at.chip], self.lsem, self.base)
+
+    def land(self, layer):
+        return self.landing.at[pl.ds(layer * self.piece, self.piece)]
+
+    def second(self):
+        at, C, z = self.at, self.C, self.z
+        self.keep.wait()
         for k in range(1, C):
             frm = (at.chip - k + C) % C
-            remote(stage.at[a, frm], stage.at[a, frm], tsend, trecv, 2 * C * a + k, 2 * frm + at.c).wait_recv()
+            remote(self.stage.at[frm], self.stage.at[frm], self.send, self.recv, k, 2 * frm + at.c).wait_recv()
         for k in range(1, C):
             to = (z + k) % C
-            c = remote(stage.at[a, to], landing(a, z), tsend, trecv, 2 * C * a + C + k, to, "ctx")
+            c = remote(self.stage.at[to], self.land(z), self.send, self.recv, C + k, to, "ctx")
             c.start()
-            sent.append(c)
-        keep[a] = local(stage.at[a, z], landing(a, z), lsem, 4 + a)
-
-    def arrive(a):
-        keep[a].wait()
+            self.sent.append(c)
+        self.keep = local(self.stage.at[z], self.land(z), self.lsem, self.base + 1)
+
+    def finish(self):
+        C, z = self.C, self.z
+        self.keep.wait()
         for k in range(1, C):
             frm = (z - k + C) % C
-            remote(landing(a, frm), landing(a, frm), tsend, trecv, 2 * C * a + C + k, frm, "ctx").wait_recv()
-
-    arrive(0)
-    save = local(rows.at[at.f], own_ref, lsem, 6)
+            remote(self.land(frm), self.land(frm), self.send, self.recv, C + k, frm, "ctx").wait_recv()
+        for c in self.sent:
+            c.wait_send()
+
+
+def enter_kernel(C, x_ref, own_ref, all_ref, stage, mine, rows, lsem, osem, send, recv, tsend, trecv):
+    at = Plane()
+    load = local(x_ref, mine, lsem, 0)
+    moving = Moving(at, C, mine, stage, rows.at[at.f], lsem, 1, tsend, trecv)
+    barrier = pltpu.get_barrier_semaphore()
+    moving.greet(barrier)
+    pl.semaphore_signal(barrier, inc=1, device_id={"fsdp": at.fc}, device_id_type=MESH)
+    pl.semaphore_wait(barrier, 2 * (C - 1) + 1)
+    load.wait()
+    moving.first()
+    moving.second()
+    moving.finish()
+    save = local(rows.at[at.f], own_ref, lsem, 3)
     stores = []
 
     def on_rows(first, count):
         stores.append(local(rows.at[pl.ds(first, count)], all_ref.at[pl.ds(first, count)], osem, len(stores)))
 
     gather_phase(at, rows, send, recv, 0, on_rows)
-    arrive(1)
-    local(gown, gown_ref, lsem, 7).wait()
-    for c in sent:
-        c.wait_send()
     save.wait()
     for c in stores:
         c.wait()
 
 
-def enter_call(C, F, x, g):
+def enter_call(C, F, x):
     R, D = x.shape
-    one = jax.ShapeDtypeStruct((R, D), bf16)
     return pl.pallas_call(
         functools.partial(enter_kernel, C),
-        out_shape=[one, one, jax.ShapeDtypeStruct((F, R, D), bf16)],
-        in_specs=[ANY] * 2,
-        out_specs=[ANY] * 3,
+        out_shape=[jax.ShapeDtypeStruct((R, D), bf16), jax.ShapeDtypeStruct((F, R, D), bf16)],
+        in_specs=[ANY],
+        out_specs=[ANY] * 2,
         scratch_shapes=[
-            pltpu.VMEM((2, C, R // C, D), bf16),
-            pltpu.VMEM((2, R, D), bf16),
+            pltpu.VMEM((C, R // C, D), bf16),
+            pltpu.VMEM((R, D), bf16),
             pltpu.VMEM((F, R, D), bf16),
-            pltpu.VMEM((R, D), bf16),
-            dma(8), dma(5), dma(GATHER_COPIES), dma(GATHER_COPIES), dma(4 * C), dma(4 * C),
+            dma(4), dma(5), dma(GATHER_COPIES), dma(GATHER_COPIES), dma(2 * C), dma(2 * C),
         ],
         compiler_params=params(1),
-        cost_estimate=cost(75),
-    )(x, g)
+        cost_estimate=cost(70),
+    )(x)
 
 
 def qkv_kernel(all_ref, w_ref, proj_ref, st_ref, rows, w, acc, st, lsem, osem, ssend, srecv):
@@ -548,11 +559,13 @@
 
 def up_kernel(
     in_ref, wg_ref, wu_ref, all_ref, act_ref, der_ref, h_ref,
-    wg, wu, rows, act, der, h, lsem, osem, send, recv,
+    w, rows, act, der, h, lsem, osem, send, recv,
 ):
     at = Plane()
     own = local(in_ref, rows.at[at.f], lsem, 0)
-    loads = [local(wg_ref, wg, lsem, 1), local(wu_ref, wu, lsem, 2)]
+    n = act.shape[2]
+    loads = [local(wg_ref, w.at[:, pl.ds(0, n)], lsem, 1), local(wu_ref, w.at[:, pl.ds(n, n)], lsem, 2)]
+    width = 256
     at.greet()
     R = rows.shape[1]
     own.wait()
@@ -567,17 +580,18 @@
                 c.wait()
             waited.append(1)
 
-        def tile(c):
+        @pl.loop(0, n // width)
+        def _(t):
+            c = pl.ds(pl.multiple_of(t * width, width), width)
             lhs = rows[pl.ds(first, count)].reshape(m, rows.shape[2])
-            g = nn(lhs, wg[:, c])
-            u = nn(lhs, wu[:, c])
+            g = nn(lhs, w[:, c])
+            u = nn(lhs, w[:, pl.ds(pl.multiple_of(n + t * width, width), width)])
             sig = jax.nn.sigmoid(g)
             a = g * sig
             act[s, pl.ds(0, m), c] = a.astype(bf16)
             der[s, pl.ds(0, m), c] = (u * (sig * (1.0 + g * (1.0 - sig)))).astype(bf16)
             h[s, pl.ds(0, m), c] = (a * u).astype(bf16)
 
-        pair_loop(m, 256, wg.shape[1], tile)
         start = pl.multiple_of(first * R, R)
         stores.put(
             [
@@ -603,8 +617,7 @@
         in_specs=[ANY] * 3,
         out_specs=[ANY] * 4,
         scratch_shapes=[
-            pltpu.VMEM((D, n), bf16),
-            pltpu.VMEM((D, n), bf16),
+            pltpu.VMEM((D, 2 * n), bf16),
             pltpu.VMEM((F, R, D), bf16),
             pltpu.VMEM((2, 2 * R, n), bf16),
             pltpu.VMEM((2, 2 * R, n), bf16),
@@ -617,29 +630,37 @@
 
 
 def down_kernel(
-    h_ref, wd_ref, hid_ref, cot_ref, gain_ref, act_ref, der_ref,
-    res_ref, gg_ref, all_ref, gate_ref, up_ref,
-    h, wd, hid, cot, gain, act, der, res, gacc, rows, ggate, gup, b0, b1, b2, b3, b4,
-    lsem, osem, asem, send, recv,
+    C, h_ref, wd_ref, hid_ref, cot_ref, gain_ref, act_ref, der_ref,
+    res_ref, gg_ref, all_ref, grad_ref, own_ref,
+    h, wd, hid, mine, gain, act, der, res, gacc, rows, grad, cot, stage, b0, b1, b2, b3, b4,
+    lsem, osem, asem, send, recv, tsend, trecv,
 ):
     at = Plane()
     loads = [
         local(s, d, lsem, i)
         for i, (s, d) in enumerate(
-            [(h_ref, h), (wd_ref, wd), (hid_ref, hid), (cot_ref, cot), (gain_ref, gain)]
+            [(cot_ref, mine), (h_ref, h), (wd_ref, wd), (hid_ref, hid), (gain_ref, gain)]
         )
     ]
-    at.greet()
+    moving = Moving(at, C, mine, stage, cot, lsem, 5, tsend, trecv)
+    barrier = pltpu.get_barrier_semaphore()
+    moving.greet(barrier)
+    pl.semaphore_signal(barrier, inc=1, device_id={"fsdp": at.fc}, device_id_type=MESH)
+    pl.semaphore_wait(barrier, 2 * (C - 1) + 1)
     R = rows.shape[1]
+    n = wd.shape[1]
     loads[0].wait()
+    moving.first()
     loads[1].wait()
+    loads[2].wait()
 
     def partial(chip, cols):
         return nt(h[pl.ds(pl.multiple_of(chip * 2 * R, 2 * R), 2 * R), :], wd[cols, :])
 
-    total = scatter_phase(at, partial, (b0, b1, b2, b3, b4), send, recv, 0)
-    for c in loads[2:]:
+    total = scatter_phase(at, partial, (b0, b1, b2, b3, b4), send, recv, 0, moving.second)
+    for c in loads[3:]:
         c.wait()
+    moving.finish()
     gacc[...] = jnp.zeros_like(gacc)
 
     def finish(r):
@@ -652,7 +673,7 @@
         rows[at.f, r, :] = back(g * gain[...], hat, scale).astype(bf16)
 
     row_loop(R, finish)
-    saves = [local(res, res_ref, lsem, 5), local(gacc, gg_ref, lsem, 6)]
+    saves = [local(res, res_ref, lsem, 7), local(gacc, gg_ref, lsem, 8), local(cot, own_ref, lsem, 9)]
     stores = Stores(osem)
 
     def on_rows(first, count):
@@ -665,16 +686,19 @@
         la.wait()
         ld.wait()
 
-        def tile(c):
+        width = 512
+
+        @pl.loop(0, n // width)
+        def _(t):
+            c = pl.ds(pl.multiple_of(t * width, width), width)
+            up = pl.ds(pl.multiple_of(n + t * width, width), width)
             gh = nn(rows[pl.ds(first, count)].reshape(m, rows.shape[2]), wd[:, c])
-            gup[s, pl.ds(0, m), c] = (gh * act[s, pl.ds(0, m), c].astype(f32)).astype(bf16)
-            ggate[s, pl.ds(0, m), c] = (gh * der[s, pl.ds(0, m), c].astype(f32)).astype(bf16)
-
-        pair_loop(m, 256, wd.shape[1], tile)
+            grad[s, pl.ds(0, m), up] = (gh * act[s, pl.ds(0, m), c].astype(f32)).astype(bf16)
+            grad[s, pl.ds(0, m), c] = (gh * der[s, pl.ds(0, m), c].astype(f32)).astype(bf16)
+
         stores.put(
             [
-                (ggate.at[s, pl.ds(0, m)], gate_ref.at[pl.ds(start, m)]),
-                (gup.at[s, pl.ds(0, m)], up_ref.at[pl.ds(start, m)]),
+                (grad.at[s, pl.ds(0, m)], grad_ref.at[pl.ds(start, m)]),
                 (rows.at[pl.ds(first, count)], all_ref.at[pl.ds(first, count)]),
             ]
         )
@@ -685,19 +709,20 @@
     stores.finish()
 
 
-def down_call(F, h, wd, hid, cot, gain, act, der):
+def down_call(C, F, h, wd, hid, cot, gain, act, der):
     R, D = hid.shape
     n = wd.shape[1]
     T = F * R
     copies = SCATTER_COPIES + GATHER_COPIES
+    one = jax.ShapeDtypeStruct((R, D), bf16)
     return pl.pallas_call(
-        down_kernel,
+        functools.partial(down_kernel, C),
         out_shape=[
-            jax.ShapeDtypeStruct((R, D), bf16),
+            one,
             jax.ShapeDtypeStruct((1, D), f32),
             jax.ShapeDtypeStruct((F, R, D), bf16),
-            jax.ShapeDtypeStruct((T, n), bf16),
-            jax.ShapeDtypeStruct((T, n), bf16),
+            jax.ShapeDtypeStruct((T, 2 * n), bf16),
+            one,
         ],
         in_specs=[ANY] * 7,
         out_specs=[ANY] * 5,
@@ -712,39 +737,40 @@
             pltpu.VMEM((R, D), bf16),
             pltpu.VMEM((1, D), f32),
             pltpu.VMEM((F, R, D), bf16),
-            pltpu.VMEM((2, 2 * R, n), bf16),
-            pltpu.VMEM((2, 2 * R, n), bf16),
+            pltpu.VMEM((2, 2 * R, 2 * n), bf16),
+            pltpu.VMEM((R, D), bf16),
+            pltpu.VMEM((C, R // C, D), bf16),
         ]
         + scatter_scratch(R, D)
-        + [dma(7), dma(15), dma(10), dma(copies), dma(copies)],
+        + [dma(10), dma(15), dma(10), dma(copies), dma(copies), dma(2 * C), dma(2 * C)],
         compiler_params=params(3),
-        cost_estimate=cost(92),
+        cost_estimate=cost(95),
     )(h, wd, hid, cot, gain, act, der)
 
 
 def mid_kernel(
-    gate_ref, up_ref, wg_ref, wu_ref, cot_ref, ao_ref, gain_ref, wo_ref,
+    grad_ref, wg_ref, wu_ref, cot_ref, ao_ref, gain_ref, wo_ref,
     res_ref, gg_ref, all_ref, gm_ref,
-    ggate, gup, wg, wu, cot, ao, gain, wo, res, gacc, rows, gm, b0, b1, b2, b3, b4,
+    grad, w, cot, ao, gain, wo, res, gacc, rows, gm, b0, b1, b2, b3, b4,
     lsem, osem, send, recv,
 ):
     at = Plane()
+    n = w.shape[1] // 2
     pairs = [
-        (gate_ref, ggate), (up_ref, gup), (wg_ref, wg), (wu_ref, wu),
+        (grad_ref, grad), (wg_ref, w.at[:, pl.ds(0, n)]), (wu_ref, w.at[:, pl.ds(n, n)]),
         (cot_ref, cot), (ao_ref, ao), (gain_ref, gain), (wo_ref, wo),
     ]
     loads = [local(s, d, lsem, i) for i, (s, d) in enumerate(pairs)]
     at.greet()
     R = rows.shape[1]
-    for c in loads[:4]:
+    for c in loads[:3]:
         c.wait()
 
     def partial(chip, cols):
-        r = pl.ds(pl.multiple_of(chip * 2 * R, 2 * R), 2 * R)
-        return nt(ggate[r, :], wg[cols, :]) + nt(gup[r, :], wu[cols, :])
+        return nt(grad[pl.ds(pl.multiple_of(chip * 2 * R, 2 * R), 2 * R), :], w[cols, :])
 
     total = scatter_phase(at, partial, (b0, b1, b2, b3, b4), send, recv, 0)
-    for c in loads[4:]:
+    for c in loads[3:]:
         c.wait()
     gacc[...] = jnp.zeros_like(gacc)
 
@@ -780,9 +806,9 @@
     stores.finish()
 
 
-def mid_call(F, gate, up, wg, wu, cot, ao, gain, wo):
+def mid_call(F, grad, wg, wu, cot, ao, gain, wo):
     R, D = cot.shape
-    n, e = wg.shape[1], wo.shape[1]
+    n, e = 2 * wg.shape[1], wo.shape[1]
     T = F * R
     copies = SCATTER_COPIES + GATHER_COPIES
     return pl.pallas_call(
@@ -793,12 +819,10 @@
             jax.ShapeDtypeStruct((F, R, D), bf16),
             jax.ShapeDtypeStruct((T, e), bf16),
         ],
-        in_specs=[ANY] * 8,
+        in_specs=[ANY] * 7,
         out_specs=[ANY] * 4,
         scratch_shapes=[
             pltpu.VMEM((T, n), bf16),
-            pltpu.VMEM((T, n), bf16),
-            pltpu.VMEM((D, n), bf16),
             pltpu.VMEM((D, n), bf16),
             pltpu.VMEM((R, D), bf16),
             pltpu.VMEM((R, D), f32),
@@ -813,7 +837,7 @@
         + [dma(10), dma(10), dma(copies), dma(copies)],
         compiler_params=params(4),
         cost_estimate=cost(92),
-    )(gate, up, wg, wu, cot, ao, gain, wo)
+    )(grad, wg, wu, cot, ao, gain, wo)
 
 
 def last_kernel(
@@ -910,6 +934,42 @@
     )(wq, wk, gv, proj, st, ins, w, res, gains)
 
 
+def tn(a, b):
+    return lax.dot_general(a, b, (((0,), (0,)), ((), ())), preferred_element_type=f32)
+
+
+def grad_kernel(*refs):
+    out = refs[-1]
+    start = 0
+    for x_ref, dy_ref in zip(refs[:-1:2], refs[1:-1:2]):
+        got = tn(x_ref[...], dy_ref[...]).astype(bf16)
+        units = dy_ref.shape[1] // out.shape[-1]
+        for b in range(units):
+            out[(start + b,) + (0,) * (len(out.shape) - 3)] = got[:, b * out.shape[-1] : (b + 1) * out.shape[-1]]
+        start += units
+
+
+def grad_call(pairs, units, cols, groups):
+    T, D = pairs[0][0].shape
+    tile = 512
+    specs, args = [], []
+    for x, dy in pairs:
+        specs += [
+            pl.BlockSpec((T, tile), lambda g, d: (0, d)),
+            pl.BlockSpec((T, dy.shape[1] // groups), lambda g, d: (0, g)),
+        ]
+        args += [x, dy]
+    return pl.pallas_call(
+        grad_kernel,
+        out_shape=jax.ShapeDtypeStruct((units, groups, D, cols), bf16),
+        grid=(groups, D // tile),
+        in_specs=specs,
+        out_specs=pl.BlockSpec((units, 1, tile, cols), lambda g, d: (0, g, d, 0)),
+        compiler_params=pltpu.CompilerParams(vmem_limit_bytes=VMEM_LIMIT),
+        cost_estimate=cost(12 * groups),
+    )(*args)
+
+
 def share_stats(at, F, st, send, recv, base):
     sent = []
     for k in range(1, F):
@@ -1087,24 +1147,36 @@
 
 
 def newton_kernel(
-    C, x_ref, rows_ref, gain_ref, out_ref, home_ref, gsum_ref,
+    C, m_ref, rows_ref, gain_ref, out_ref, home_ref, gsum_ref,
     v, gram, y, yf, stat, stage, gains, gsum,
-    lsem, osem, vsend, vrecv, ysend, yrecv, ssend, srecv, tsend, trecv, gsend, grecv,
+    lsem, osem, vsend, vrecv, ysend, yrecv, ssend, srecv, tsend, trecv, gsend, grecv, usend, urecv, usem,
 ):
     me = lax.axis_index("fsdp")
     z = lax.axis_index("ctx")
     core, chip = me % 2, me // 2
     peer = me + 1 - 2 * core
-    load = local(x_ref, v.at[0], lsem, 0)
+    F = 2 * C
+    cols = m_ref.shape[2]
     gload = local(gain_ref, gains.at[z], lsem, 1)
     barrier = pltpu.get_barrier_semaphore()
-    pl.semaphore_signal(barrier, inc=1, device_id={"fsdp": peer}, device_id_type=MESH)
     for k in range(1, C):
         pl.semaphore_signal(barrier, inc=1, device_id={"ctx": (z + k) % C}, device_id_type=MESH)
-        pl.semaphore_signal(
-            barrier, inc=1, device_id={"fsdp": 2 * ((chip + k) % C) + core}, device_id_type=MESH
-        )
-    pl.semaphore_wait(barrier, 2 * (C - 1) + 1)
+    for k in range(1, F):
+        pl.semaphore_signal(barrier, inc=1, device_id={"fsdp": (me + k) % F}, device_id_type=MESH)
+    pl.semaphore_wait(barrier, C + F - 2)
+    rows_in = v.shape[1] // C
+    units_sent, units_kept = [], []
+    for k in range(F):
+        to = (me + k) % F
+        for b in range(C):
+            src = m_ref.at[to // 2, pl.ds((2 * b + to % 2) * rows_in, rows_in)]
+            dst = v.at[0, pl.ds(b * rows_in, rows_in), pl.ds(me * cols, cols)]
+            if k == 0:
+                units_kept.append(local(src, dst, usem, b))
+            else:
+                c = remote(src, dst, usend, urecv, k * C + b, to)
+                c.start()
+                units_sent.append(c)
     piece = rows_ref.shape[1] // C
 
     def part(j):
@@ -1154,9 +1226,17 @@
         for c in sent:
             c.wait_send()
 
-    load.wait()
+    for k in range(1, F):
+        frm = (me - k + F) % F
+        for b in range(C):
+            dst = v.at[0, pl.ds(b * rows_in, rows_in), pl.ds(frm * cols, cols)]
+            remote(dst, dst, usend, urecv, k * C + b, frm).wait_recv()
+    for c in units_sent:
+        c.wait_send()
+    for c in units_kept:
+        c.wait()
     M, D = v.shape[1], v.shape[2]
-    tile, col = 256, 512
+    tile, col = 512, 1024
     tiles = M // tile
 
     def block(i):
@@ -1254,9 +1334,10 @@
 
 
 def newton_call(C, x, rows, gains):
-    M, D = x.shape
+    _, D, cols = x.shape
+    M = D // 2
     _, R, _ = rows.shape
-    n = M // 256
+    n = M // 512
     return pl.pallas_call(
         functools.partial(newton_kernel, C),
         out_shape=[
@@ -1276,7 +1357,7 @@
             pltpu.VMEM((C, 8, D), f32),
             pltpu.VMEM((8, D), f32),
             dma(7), dma(n), dma(n), dma(n), dma(n), dma(n), dma(1), dma(1),
-            dma(4 * C), dma(4 * C), dma(C), dma(C),
+            dma(4 * C), dma(4 * C), dma(C), dma(C), dma(2 * C * C), dma(2 * C * C), dma(C),
         ],
         compiler_params=params(6),
         cost_estimate=cost(95),
@@ -1305,7 +1386,8 @@
 
 def down_and_back(C, F, h, wd, hidden_in, cot, gain, act, der):
     if kernels_fit(C, F):
-        return down_call(F, h, wd, hidden_in, cot, gain, act, der)
+        return down_call(C, F, h, wd, hidden_in, cot, gain, act, der)
+    cot = to_layer(C, F, cot)
     out = token_sums(dot(h, wd, 1, 1))
     scale = rms(out)
     hat = out * scale
@@ -1316,15 +1398,15 @@
         (hidden_in + hat * gain).astype(bf16),
         jnp.sum(g * hat, axis=0, keepdims=True),
         rows,
-        (gh * der.astype(f32)).astype(bf16),
-        (gh * act.astype(f32)).astype(bf16),
+        jnp.concatenate([(gh * der.astype(f32)).astype(bf16), (gh * act.astype(f32)).astype(bf16)], axis=1),
+        cot,
     )
 
 
-def back_to_attn(C, F, grad_gate, grad_up, wg, wu, cot, out, gain, wo):
+def back_to_attn(C, F, grad, wg, wu, cot, out, gain, wo):
     if kernels_fit(C, F):
-        return mid_call(F, grad_gate, grad_up, wg, wu, cot, out, gain, wo)
-    resid = cot.astype(f32) + token_sums(dot(grad_gate, wg, 1, 1) + dot(grad_up, wu, 1, 1))
+        return mid_call(F, grad, wg, wu, cot, out, gain, wo)
+    resid = cot.astype(f32) + token_sums(dot(grad, jnp.concatenate([wg, wu], axis=1), 1, 1))
     scale = rms(out)
     hat = out * scale
     rows = token_rows(back(resid * gain, hat, scale).astype(bf16))
@@ -1391,24 +1473,31 @@
     def rows_gather(shard):
         return lax.all_gather(shard, "ctx", axis=0, tiled=True)
 
-    def rows_product(lhs, rhs):
-        return dot(lhs.reshape(tokens, width), rhs, 0, 0).astype(bf16)
-
-    def rows_scatter(grad):
-        return lax.psum_scatter(grad, "ctx", scatter_dimension=0, tiled=True)
-
+    def product(units, groups, *pairs):
+        pairs = [(x.reshape(tokens, width), dy) for x, dy in pairs]
+        if kernels:
+            return grad_call(pairs, units, head_cols, groups)
+        grad = jnp.concatenate([dot(x, dy, 0, 0).astype(bf16) for x, dy in pairs], axis=1)
+        return jnp.transpose(grad.reshape(width, groups, units, head_cols), (2, 1, 0, 3))
+
+    def scatter(grad):
+        if kernels:
+            return lax.psum_scatter(grad, "ctx", scatter_dimension=0, tiled=True)[0]
+        return lax.psum_scatter(grad, "ctx", scatter_dimension=2, tiled=True)
+
+    kernels = kernels_fit(C, F)
     w_qkv = rows_gather(jnp.concatenate([w_attn[0], w_attn[1], w_attn[2]], axis=1))
     w_out = rows_gather(w_attn[3])
     ffn_flat = w_ffn.reshape(3, dz, hidden_cols)
     w_gate = rows_gather(ffn_flat[0])
     w_up = rows_gather(ffn_flat[1])
     w_down = rows_gather(ffn_flat[2])
+
     gain_query = lax.dynamic_slice_in_dim(gains[0], f * head_cols, head_cols)
     gain_key = lax.dynamic_slice_in_dim(gains[1], f * head_cols, head_cols)
     pos = lax.dynamic_slice_in_dim(positions, z * per, per, 0)
     pos = jnp.transpose(pos.reshape(per, C, chips, piece), (0, 2, 1, 3)).reshape(per, seq_length)
     cosine_table, sine_table = rotary_tables(pos)
-    kernels = kernels_fit(C, F)
 
     def heads(a):
         return jnp.transpose(
@@ -1430,15 +1519,12 @@
             pos.astype(f32)[:, None, :],
             jnp.broadcast_to(pos.astype(f32)[..., None], (per, seq_length, HEAD_DIM)),
         )
-        own_input, own_grad, input_all = enter_call(
-            C, F, layer_input.reshape(local_rows, width), cotangent.reshape(local_rows, width)
-        )
+        own_input, input_all = enter_call(C, F, layer_input.reshape(local_rows, width))
         projected, stats = qkv_call(F, input_all, w_qkv)
         attn_mixed, query_rows, key_rows, log_total = attend_call(F, projected, stats, *tables)
         attn_mixed = attn_mixed.reshape(tokens, head_cols)
     else:
         own_input, input_all, projected = project(C, F, layer_input.reshape(local_rows, width), w_qkv)
-        own_grad = to_layer(C, F, after(cotangent.reshape(local_rows, width), own_input))
         query_raw = projected[:, :head_cols]
         key_raw = projected[:, head_cols : 2 * head_cols]
         value_raw = projected[:, 2 * head_cols :]
@@ -1459,25 +1545,27 @@
     hidden_in, attn_out, mlp_all, act, der, hidden = attn_out_and_up(
         C, F, attn_mixed, w_out, own_input, gains[2:3], w_gate, w_up
     )
-    result, mlp_gain, grad_mlp_all, grad_gate, grad_up = down_and_back(
-        C, F, hidden, w_down, hidden_in, own_grad, gains[3:4], act, der
+    result, mlp_gain, grad_mlp_all, grad_ffn_in, own_grad = down_and_back(
+        C, F, hidden, w_down, hidden_in, cotangent.reshape(local_rows, width), gains[3:4], act, der
     )
-    p_down = rows_product(grad_mlp_all, hidden)
-    p_gate = rows_product(mlp_all, grad_gate)
-    p_up = rows_product(mlp_all, grad_up)
-    g_down = rows_scatter(p_down)
-    g_gate = rows_scatter(p_gate)
-    g_up = rows_scatter(p_up)
-    grad_gate, grad_up, p_down, p_gate, p_up = lax.optimization_barrier(
-        (grad_gate, grad_up, p_down, p_gate, p_up)
+    if kernels:
+        units_in = jnp.concatenate(
+            [mom_attn[:, None].astype(bf16), jnp.transpose(mom_ffn.astype(bf16), (2, 0, 1, 3))], axis=1
+        )
+        units_in = after(units_in, w_down)
+        mom_own = jnp.swapaxes(lax.all_to_all(units_in, "ctx", split_axis=0, concat_axis=0, tiled=True), 0, 1)
+        grad_mlp_all, mom_own = lax.optimization_barrier((grad_mlp_all, mom_own))
+    p_down = product(block_count, 1, (grad_mlp_all, hidden))
+    g_down = scatter(p_down)
+    p_gate_up = product(block_count, 2, (mlp_all, grad_ffn_in))
+    if kernels:
+        grad_ffn_in, p_gate_up = lax.optimization_barrier((grad_ffn_in, p_gate_up))
+    g_gate_up = scatter(p_gate_up)
+    grad_resid, attn_gain, grad_attn_all, grad_mixed = back_to_attn(
+        C, F, grad_ffn_in, w_gate, w_up, own_grad, attn_out, gains[2:3], w_out
     )
-    grad_resid, attn_gain, grad_attn_all, grad_mixed = back_to_attn(
-        C, F, grad_gate, grad_up, w_gate, w_up, own_grad, attn_out, gains[2:3], w_out
-    )
-    p_out = rows_product(grad_attn_all, attn_mixed)
-    grad_mixed, p_out, g_down = lax.optimization_barrier((grad_mixed, p_out, g_down))
-    g_out = rows_scatter(p_out)
     if kernels:
+        grad_mixed = after(grad_mixed, g_down)
         weighted_q, weighted_k, grad_value, inner, gain_cols = attend_back_call(
             F, projected, query_rows, key_rows, grad_mixed, log_total, stats, *tables
         )
@@ -1522,8 +1610,9 @@
             axis=1,
         )
         grad_rows = back_to_input(C, F, grad_projected, w_qkv, grad_resid)
-    p_qkv = rows_product(input_all, grad_projected)
-    g_qkv = rows_scatter(p_qkv)
+    g_attn = scatter(
+        product(UNITS_ATTN, 1, (input_all, grad_projected), (grad_attn_all, attn_mixed))
+    )
     if not kernels:
         grad_input = from_layer(C, F, grad_rows)
         result = from_layer(C, F, result)
@@ -1538,39 +1627,44 @@
         )
         gain_total = jnp.sum(lax.all_gather(gain_local, BOTH, axis=0, tiled=False), axis=0)
 
-    g_qkv, g_out, g_gate, g_up, g_down, _ = lax.optimization_barrier(
-        (g_qkv, g_out, g_gate, g_up, g_down, grad_rows)
-    )
-    g_qkv, g_out, g_gate, g_up, g_down = (g.astype(f32) for g in (g_qkv, g_out, g_gate, g_up, g_down))
-    grad_attn = jnp.stack(
-        [g_qkv[:, :head_cols], g_qkv[:, head_cols : 2 * head_cols], g_qkv[:, 2 * head_cols :], g_out]
-    )
-    grad_ffn = jnp.stack([g_gate, g_up, g_down]).reshape(3, dz, block_count, head_cols)
+    if kernels:
+        got = jnp.stack([g_attn[0], g_gate_up[0], g_gate_up[1], g_down[0]])
+        mom = mom_own.reshape(got.shape).astype(f32)
+        owned = (momentum * mom + got.astype(f32)).astype(bf16)
+        sent_back = got.reshape(UNITS_ATTN, C, dz, head_cols)
+        sent_back = lax.all_to_all(sent_back, "ctx", split_axis=1, concat_axis=0, tiled=False)
+        sent_back = sent_back.reshape(C, UNITS_ATTN, dz, head_cols).astype(f32)
+        grad_attn = sent_back[:, 0]
+        grad_ffn = jnp.transpose(sent_back[:, 1:], (1, 2, 0, 3))
+        own, back_rows, gain_total = newton_call(C, owned, jnp.stack([result, grad_rows]), gain_layer)
+        result, grad_input, gain_total = back_rows[0], back_rows[1], gain_total[:4]
+    else:
+        grad_attn = g_attn[:, 0].astype(f32)
+        grad_ffn = jnp.transpose(
+            jnp.concatenate([g_gate_up, g_down], axis=1).astype(f32), (1, 2, 0, 3)
+        )
     new_attn = momentum * mom_attn + grad_attn
     new_ffn = momentum * mom_ffn + grad_ffn
-    send = jnp.concatenate(
-        [
-            new_attn.astype(bf16),
-            jnp.transpose(new_ffn.astype(bf16), (0, 2, 1, 3)).reshape(3 * block_count, dz, head_cols),
-        ],
-        axis=0,
-    ).reshape(C * F, dz // parts, head_cols)
-    got = lax.all_to_all(send, BOTH, split_axis=0, concat_axis=0, tiled=True)
-    own = jnp.transpose(got.reshape(C, F, dz // parts, head_cols), (0, 2, 1, 3)).reshape(
-        C * dz // parts, F * head_cols
-    )
-
-    def peers(a):
-        out = [a]
-        for s in range(1, parts):
-            pairs = [(i, i - i % parts + (i + parts - s) % parts) for i in range(C * F)]
-            out.append(lax.ppermute(a, BOTH, pairs))
-        return out
-
-    if kernels:
-        own, back_rows, gain_total = newton_call(C, own, jnp.stack([result, grad_rows]), gain_layer)
-        result, grad_input, gain_total = back_rows[0], back_rows[1], gain_total[:4]
-    else:
+    if not kernels:
+        send = jnp.concatenate(
+            [
+                new_attn.astype(bf16),
+                jnp.transpose(new_ffn.astype(bf16), (0, 2, 1, 3)).reshape(3 * block_count, dz, head_cols),
+            ],
+            axis=0,
+        ).reshape(C * F, dz // parts, head_cols)
+        own = lax.all_to_all(send, BOTH, split_axis=0, concat_axis=0, tiled=True)
+        own = jnp.transpose(own.reshape(C, F, dz // parts, head_cols), (0, 2, 1, 3)).reshape(
+            C * dz // parts, F * head_cols
+        )
+
+        def peers(a):
+            out = [a]
+            for s in range(1, parts):
+                pairs = [(i, i - i % parts + (i + parts - s) % parts) for i in range(C * F)]
+                out.append(lax.ppermute(a, BOTH, pairs))
+            return out
+
         own32 = own.astype(f32)
         square = jnp.sum(own32 * own32)
         total = sum(peers(square.reshape(1, 1)))
@@ -1585,16 +1679,21 @@
             own = (
                 quintic_one * factor * own.astype(f32) + quintic_two * product + quintic_three * product_two
             ).astype(bf16)
-    own, result, grad_input = lax.optimization_barrier((own, result, grad_input))
     home = jnp.transpose(own.reshape(C, dz // parts, F, head_cols), (0, 2, 1, 3)).reshape(
         C * F, dz // parts, head_cols
     )
     steps = lax.all_to_all(home, BOTH, split_axis=0, concat_axis=0, tiled=True)
-    steps = -muon_rate * steps.astype(f32).reshape(units, dz, head_cols)
-    step_attn = steps[:UNITS_ATTN]
-    step_ffn = jnp.transpose(
-        steps[UNITS_ATTN:].reshape(3, block_count, dz, head_cols), (0, 2, 1, 3)
-    )
+    steps = -muon_rate * steps.astype(f32)
+    if kernels:
+        steps = steps.reshape(C, UNITS_ATTN, dz, head_cols)
+        step_attn = steps[:, 0]
+        step_ffn = jnp.transpose(steps[:, 1:], (1, 2, 0, 3))
+    else:
+        steps = steps.reshape(units, dz, head_cols)
+        step_attn = steps[:UNITS_ATTN]
+        step_ffn = jnp.transpose(
+            steps[UNITS_ATTN:].reshape(3, block_count, dz, head_cols), (0, 2, 1, 3)
+        )
     new_gain_mom = momentum * gain_mom + gain_total
     return (
         result.reshape(layer_input.shape),

time: 1230 us -> 1270 us (1.033)
  Pallas kernels: 642 us -> 765 us
  matrix products: 60.8 us -> 0 us
  waiting for transfers between devices: 399 us -> 353 us
  starting transfers between devices: 15.5 us -> 35.3 us
    all_to_all x1 -> x2, waiting for transfers between devices: 90.9 us -> 0.01 us  [the longest x1 0.01 us: shards(): lax.all_to_all(units_in, 'ctx', split_axis=0, concat_axis=0, tiled=True)]
    all_gather x5, waiting for transfers between devices: 134 us -> 216 us  [rows_gather(): return lax.all_gather(shard, 'ctx', axis=0, tiled=True)]
    pallas_call x1, Pallas kernels: 135 us -> 208 us  [newton_call(): pl.pallas_call(functools.partial(newton_kernel, C), out_shape=[jax.ShapeD...]
    dot_general x5 -> x0, matrix products: 60.8 us -> none  [dot(): lax.dot_general(a, b, (((ca,), (cb,)), ((), ())), preferred_element_type=...]
    pallas_call x2 -> x5, Pallas kernels: 191 us -> 241 us  [the longest x1 99.7 us: down_call(): pl.pallas_call(functools.partial(down_kernel, C), out_shape=[one, jax.Sha...]
    reduce_scatter x5 -> x3, waiting for transfers between devices: 96.1 us -> 69.8 us  [scatter(): return lax.psum_scatter(grad, 'ctx', scatter_dimension=0, tiled=True)[0]]
    all_to_all x1 -> x2, starting transfers between devices: 4.92 us -> 25.1 us  [the longest x1 20.2 us: shards(): lax.all_to_all(units_in, 'ctx', split_axis=0, concat_axis=0, tiled=True)]
    unnamed x42 -> x32, local copies, waits for them, and re-layouts: 29.1 us -> 31.5 us
  transfers between devices with their start and end apart: 12 -> 11, of which waited for: 8 -> 4; matrix products, arithmetic and copies ran while one was open for 7% -> 6% of each run, Pallas kernels for 34% -> 59%
where the time goes in v3:
time: 1270 us; the launch traced here: 1260 us
  Pallas kernels  765 us (60%)
  waiting for transfers between devices  353 us (28%)
  local copies, waits for them, and re-layouts  53.9 us (4%)
  other arithmetic  41.8 us (3%)
  starting transfers between devices  35.3 us (3%)
  between operations  14.7 us (1%)
    all_gather x5, waiting for transfers between devices, rows_gather(): return lax.all_gather(shard, 'ctx', axis=0, tiled=True)  216 us
    pallas_call x1, Pallas kernels, newton_call(): pl.pallas_call(functools.partial(newton_kernel, C), out_shape=[jax.ShapeD...  208 us
    pallas_call x1, Pallas kernels, down_call(): pl.pallas_call(functools.partial(down_kernel, C), out_shape=[one, jax.Sha...  99.7 us
    pallas_call x1, Pallas kernels, mid_call(): pl.pallas_call(mid_kernel, out_shape=[jax.ShapeDtypeStruct((R, D), f32),...  96.1 us
    pallas_call x1, Pallas kernels, enter_call(): pl.pallas_call(functools.partial(enter_kernel, C), out_shape=[jax.ShapeDt...  89.8 us
    reduce_scatter x3, waiting for transfers between devices, scatter(): return lax.psum_scatter(grad, 'ctx', scatter_dimension=0, tiled=True)[0]  69.8 us
    all_to_all x1, waiting for transfers between devices, shards(): steps = lax.all_to_all(home, BOTH, split_axis=0, concat_axis=0, tiled=True)  66.9 us
    pallas_call x1, Pallas kernels, last_call(): pl.pallas_call(functools.partial(last_kernel, D), out_shape=[jax.ShapeDty...  60.6 us
  transfers between devices with their start and end apart: 11, of which 4 were waited for; matrix products, arithmetic and copies ran while one was open for 6% of the time, Pallas kernels for 59%

profile of v3, /device:TPU:0, one launch (start us, length us, event | category | flops | bytes accessed | tf_op | source)
XLA Modules:
  0.0 1264.4 jit_solution(2287051501842689292)
XLA Ops:
  20.0 89.8 %shard_map.176 = (bf16[256,2048]{1,0:T(8,128)(2,1)}, bf16[8,256,2048]{2,1,0:T(8,128)(2,1)}) custom-call(bf16[256,2048]{1,0:T(8,128)(2,1)} %bitcast.120), custom_call_target="tpu_custom_call" | custom-call | flops 70000001024 | bytes 1048576 | tf_op jit(solution)/shard_map/pallas_call | solution.py:418
  115.1 4.9 sine_multiply_fusion
  122.9 22.9 %shard_map.177 = (f32[2048,768]{1,0:T(8,128)}, f32[8,8,2048]{2,1,0:T(8,128)}) custom-call(bf16[8,256,2048]{2,1,0:T(8,128)(2,1)} %get-tuple-element.52.all_ref, bf16[2048,768]{1,0:T(8,128)(2,1)} %all-gather.7.cloned.1.call-done.w_ref), custom_call_target="tpu_custom_call" | custom-call | flops 22000001024 | bytes 1048576 | tf_op jit(solution)/shard_map/pallas_call | solution.py:481
  147.2 17.7 %shard_map.178 = (bf16[4,2,256,256]{3,2,1,0:T(8,128)(2,1)}, bf16[4,2,256,256]{3,2,1,0:T(8,128)(2,1)}, bf16[4,2,256,256]{3,2,1,0:T(8,128)(2,1)}, f32[2,2,1024,128]{3,2,1,0:T(8,128)}) custom-call(f32[4,2,256,768]{3,2,1,0:T(8,128)} %bitcast.128, f32[4,2,256,768]{3,2,1,0:T(8,128)} %bitcast.129, f32[4,2,256,768]{3,2,1,0:T(8,128)} %bitcast.130, ...), custom_call_target="tpu_custom_call" | custom-call | flops 15000000512 | bytes 1048576 | tf_op jit(solution)/shard_map/pallas_call | solution.py:1066
  164.9 46.4 %shard_map.179 = (f32[256,2048]{1,0:T(8,128)}, f32[256,2048]{1,0:T(8,128)}, bf16[256,2048]{1,0:T(8,128)(2,1)}) custom-call(bf16[2048,256]{1,0:T(8,128)(2,1)} %bitcast.136, bf16[2048,256]{1,0:T(8,128)(2,1)} %bitcast.122, bf16[256,2048]{1,0:T(8,128)(2,1)} %get-tuple-element.56.x_ref, f32[1,2048]{1,0:T(1,128)} %get-tuple-element.138.gain_ref), custom_call_target="tpu_custom_call" | custom-call | flops 46000001024 | bytes 1048576 | tf_op jit(solution)/shard_map/pallas_call | solution.py:535
  211.4 20.2 %all-to-all-start = ((bf16[4,4,512,256]{3,2,1,0:T(8,128)(2,1)}), bf16[4,4,512,256]{3,2,1,0:T(8,128)(2,1)}, u32[]{:S(2)}, u32[]{:S(2)}) async-start(bf16[4,4,512,256]{3,2,1,0:T(8,128)(2,1)} %pad_maximum_fusion), calls=%async_computation | async-start | bytes 8388608 | tf_op jit(solution)/shard_map/all_to_all | solution.py:1556
  231.6 130.8 %all-gather.11.cloned.1.call-done.wu_ref = bf16[2048,1024]{1,0:T(8,128)(2,1)} async-done(((bf16[512,1024]{1,0:T(8,128)(2,1)}), bf16[2048,1024]{1,0:T(8,128)(2,1)}) %all-gather.11.cloned.1.call-update) | async-done | bytes 4194320 | tf_op jit(solution)/shard_map/all_gather | solution.py:1474
  362.4 85.0 %all-gather.9.cloned.1.call-done.wg_ref = bf16[2048,1024]{1,0:T(8,128)(2,1)} async-done(((bf16[512,1024]{1,0:T(8,128)(2,1)}), bf16[2048,1024]{1,0:T(8,128)(2,1)}) %all-gather.9.cloned.1.call-update) | async-done | bytes 4194320 | tf_op jit(solution)/shard_map/all_gather | solution.py:1474
  447.4 47.0 %shard_map.180 = (bf16[8,256,2048]{2,1,0:T(8,128)(2,1)}, bf16[2048,1024]{1,0:T(8,128)(2,1)}, bf16[2048,1024]{1,0:T(8,128)(2,1)}, bf16[2048,1024]{1,0:T(8,128)(2,1)}) custom-call(bf16[256,2048]{1,0:T(8,128)(2,1)} %get-tuple-element.57.in_ref, bf16[2048,1024]{1,0:T(8,128)(2,1)} %all-gather.9.cloned.1.call-done.wg_ref, ...), custom_call_target="tpu_custom_call" | custom-call | flops 46000001024 | bytes 1048576 | tf_op jit(solution)/shard_map/pallas_call | solution.py:614
  494.4 99.7 %shard_map.181 = (bf16[256,2048]{1,0:T(8,128)(2,1)}, f32[1,2048]{1,0:T(1,128)}, bf16[8,256,2048]{2,1,0:T(8,128)(2,1)}, bf16[2048,2048]{1,0:T(8,128)(2,1)}, bf16[256,2048]{1,0:T(8,128)(2,1)}) custom-call(bf16[2048,1024]{1,0:T(8,128)(2,1)} %get-tuple-element.58.h_ref.refs_1_, bf16[2048,1024]{1,0:T(8,128)(2,1)} %all-gather.13.cloned.1.call-done.wd_ref, ...), custom_call_target="tpu_custom_call" | custom-call | flops 95000002560 | bytes 1048576 | tf_op jit(solution)/shard_map/pallas_call | solution.py:718
  594.1 13.3 %shard_map.184 = bf16[4,1,2048,256]{3,2,1,0:T(8,128)(2,1)} custom-call(bf16[2048,2048]{1,0:T(8,128)(2,1)} %bitcast.127, bf16[2048,1024]{1,0:T(8,128)(2,1)} %get-tuple-element.58.h_ref.refs_1_), custom_call_target="tpu_custom_call" | custom-call | flops 12000000000 | bytes 1048576 | tf_op jit(solution)/shard_map/pallas_call | solution.py:962
  607.5 24.0 %shard_map.182 = bf16[4,2,2048,256]{3,2,1,0:T(8,128)(2,1)} custom-call(bf16[2048,2048]{1,0:T(8,128)(2,1)} %bitcast.126, bf16[2048,2048]{1,0:T(8,128)(2,1)} %get-tuple-element.69.refs_1_.grad_ref), custom_call_target="tpu_custom_call" | custom-call | flops 24000000000 | bytes 1048576 | tf_op jit(solution)/shard_map/pallas_call | solution.py:962
  631.6 96.1 %shard_map.183 = (f32[256,2048]{1,0:T(8,128)}, f32[1,2048]{1,0:T(1,128)}, bf16[8,256,2048]{2,1,0:T(8,128)(2,1)}, bf16[2048,256]{1,0:T(8,128)(2,1)}) custom-call(bf16[2048,2048]{1,0:T(8,128)(2,1)} %get-tuple-element.69.refs_1_.grad_ref, bf16[2048,1024]{1,0:T(8,128)(2,1)} %all-gather.9.cloned.1.call-done.wg_ref, ...), custom_call_target="tpu_custom_call" | custom-call | flops 92000002048 | bytes 1048576 | tf_op jit(solution)/shard_map/pallas_call | solution.py:814
  727.8 25.4 %shard_map.185 = (f32[4,2,256,256]{3,2,1,0:T(8,128)}, f32[4,2,256,256]{3,2,1,0:T(8,128)}, bf16[4,2,256,256]{3,2,1,0:T(8,128)(2,1)}, f32[2,2,8,1024]{3,2,1,0:T(8,128)}, f32[2,2,8,128]{3,2,1,0:T(8,128)}) custom-call(f32[4,2,256,768]{3,2,1,0:T(8,128)} %bitcast.131, f32[4,2,256,768]{3,2,1,0:T(8,128)} %bitcast.132, f32[4,2,256,768]{3,2,1,0:T(8,128)} %bitcast.133, ...), custom_call_target="tpu_custom_call" | custom-call | flops 35000000512 | bytes 1048576 | tf_op jit(solution)/shard_map/pallas_call | solution.py:1131
  756.3 60.6 %shard_map.186 = (bf16[256,2048]{1,0:T(8,128)(2,1)}, bf16[2048,768]{1,0:T(8,128)(2,1)}, f32[8,2048]{1,0:T(8,128)}) custom-call(f32[2048,256]{1,0:T(8,128)} %bitcast.134, f32[2048,256]{1,0:T(8,128)} %bitcast.135, bf16[2048,256]{1,0:T(8,128)(2,1)} %bitcast.138, f32[2048,768]{1,0:T(8,128)} %get-tuple-element.53.proj_ref, ...), custom_call_target="tpu_custom_call" | custom-call | flops 54999998464 | bytes 1048576 | tf_op jit(solution)/shard_map/pallas_call | solution.py:908
  816.9 14.3 %shard_map.187 = bf16[4,1,2048,256]{3,2,1,0:T(8,128)(2,1)} custom-call(bf16[2048,2048]{1,0:T(8,128)(2,1)} %bitcast.124, bf16[2048,768]{1,0:T(8,128)(2,1)} %get-tuple-element.84.refs_1_, bf16[2048,2048]{1,0:T(8,128)(2,1)} %bitcast.125, bf16[2048,256]{1,0:T(8,128)(2,1)} %bitcast.137), custom_call_target="tpu_custom_call" | custom-call | flops 12000000000 | bytes 1048576 | tf_op jit(solution)/shard_map/pallas_call | solution.py:962
  843.0 69.8 %reduce-scatter.6.cloned.1.call-done = bf16[1,1,2048,256]{3,2,1,0:T(8,128)(2,1)} async-done(((bf16[4,1,2048,256]{3,2,1,0:T(8,128)(2,1)}), bf16[1,1,2048,256]{3,2,1,0:T(8,128)(2,1)}) %reduce-scatter.6.cloned.1.call-update) | async-done | bytes 1048592 | tf_op jit(solution)/shard_map/reduce_scatter | solution.py:1485
  921.3 5.5 fusion.m_ref
  926.8 208.2 %shard_map.188 = (bf16[1024,2048]{1,0:T(8,128)(2,1)}, bf16[2,256,2048]{2,1,0:T(8,128)(2,1)}, f32[8,2048]{1,0:T(8,128)}) custom-call(bf16[4,2048,256]{2,1,0:T(8,128)(2,1)} %fusion.m_ref, bf16[2,256,2048]{2,1,0:T(8,128)(2,1)} %pad_maximum_fusion.2.rows_ref, f32[8,2048]{1,0:T(8,128)} %get-tuple-element.89.gain_ref), custom_call_target="tpu_custom_call" | custom-call | flops 95000002560 | bytes 1048576 | tf_op jit(solution)/shard_map/pallas_call | solution.py:1341
  1141.7 9.9 all-to-all-start.2
  1157.8 6.7 copy.47
  1169.0 6.7 copy.48
  1178.2 66.9 %all-to-all-done.2 = bf16[32,256,256]{2,1,0:T(8,128)(2,1)} async-done(((bf16[32,256,256]{2,1,0:T(8,128)(2,1)}), bf16[32,256,256]{2,1,0:T(8,128)(2,1)}, u32[]{:S(2)}, u32[]{:S(2)}) %all-to-all-start.2) | async-done | bytes 4194336 | tf_op jit(solution)/shard_map/all_to_all | solution.py:1685
  1250.7 6.7 copy.49
  (94 shorter events, 71.0 us)
Async XLA Ops:
  7.2 115.8 %all-gather.7.cloned.1.call-start = ((), (), s32[]{:S(2)}) async-start(), calls=%async_computation.6 | async-start | bytes 3932160 | tf_op jit(solution)/shard_map/all_gather | solution.py:1474
  10.2 154.8 %all-gather.15.cloned.1.call-start = ((), (), s32[]{:S(2)}) async-start(), calls=%async_computation.13 | async-start | bytes 1310720 | tf_op jit(solution)/shard_map/all_gather | solution.py:1474
  10.9 200.5 %all-gather.13.cloned.1.call-start = ((), (), s32[]{:S(2)}) async-start(), calls=%async_computation.9 | async-start | bytes 5242880 | tf_op jit(solution)/shard_map/all_gather | solution.py:1474
  15.1 4.3 copy-start.8
  15.2 347.2 %all-gather.11.cloned.1.call-start = ((), (), s32[]{:S(2)}) async-start(), calls=%async_computation.8 | async-start | bytes 5242880 | tf_op jit(solution)/shard_map/all_gather | solution.py:1474
  16.4 430.9 %all-gather.9.cloned.1.call-start = ((), (), s32[]{:S(2)}) async-start(), calls=%async_computation.7 | async-start | bytes 5242880 | tf_op jit(solution)/shard_map/all_gather | solution.py:1474
  109.8 3.9 copy-start
  114.8 5.2 copy-start.3
  211.4 382.8 %all-to-all-start = ((bf16[4,4,512,256]{3,2,1,0:T(8,128)(2,1)}), bf16[4,4,512,256]{3,2,1,0:T(8,128)(2,1)}, u32[]{:S(2)}, u32[]{:S(2)}) async-start(bf16[4,4,512,256]{3,2,1,0:T(8,128)(2,1)} %pad_maximum_fusion), calls=%async_computation | async-start | bytes 8388608 | tf_op jit(solution)/shard_map/all_to_all | solution.py:1556
  231.6 496.1 %reduce-scatter.4.cloned.1.call-start = ((), (), s32[]{:S(2)}) async-start(), calls=%async_computation.10 | async-start | bytes 5242880 | tf_op jit(solution)/shard_map/reduce_scatter | solution.py:1485
  607.5 232.4 %reduce-scatter.8.cloned.1.call-start = ((), (), s32[]{:S(2)}) async-start(), calls=%async_computation.12 | async-start | bytes 10485760 | tf_op jit(solution)/shard_map/reduce_scatter | solution.py:1485
  631.5 281.3 %reduce-scatter.6.cloned.1.call-start = ((), (), s32[]{:S(2)}) async-start(), calls=%async_computation.11 | async-start | bytes 5242880 | tf_op jit(solution)/shard_map/reduce_scatter | solution.py:1485
  727.7 27.8 %copy-start.10 = (f32[1,2048]{1,0:T(1,128)S(1)}, f32[1,2048]{1,0:T(1,128)}, u32[]{:S(2)}) copy-start(f32[1,2048]{1,0:T(1,128)} %get-tuple-element.83) | copy-start | bytes 24580
  727.7 27.8 %copy-start.11 = (f32[1,2048]{1,0:T(1,128)S(1)}, f32[1,2048]{1,0:T(1,128)}, u32[]{:S(2)}) copy-start(f32[1,2048]{1,0:T(1,128)} %get-tuple-element.82) | copy-start | bytes 24580
  834.4 3.9 copy-start.5
  834.4 3.9 copy-start.6
  839.8 73.0 %copy-start.2 = (bf16[1,1,2048,256]{3,2,1,0:T(8,128)(2,1)S(1)}, bf16[1,1,2048,256]{3,2,1,0:T(8,128)(2,1)}, u32[]{:S(2)}) copy-start(bf16[1,1,2048,256]{3,2,1,0:T(8,128)(2,1)} %reduce-scatter.4.cloned.1.call-done) | copy-start | bytes 3145732
  916.5 225.2 %all-to-all-start.1 = ((bf16[1,4,4,512,256]{4,3,1,0,2:T(8,128)(2,1)}), bf16[1,4,4,512,256]{4,3,1,0,2:T(8,128)(2,1)}, u32[]{:S(2)}, u32[]{:S(2)}) async-start(bf16[1,4,4,512,256]{4,3,1,0,2:T(8,128)(2,1)} %pad_maximum_fusion.1), calls=%async_computation.4 | async-start | bytes 8388608 | tf_op jit(solution)/shard_map/all_to_all | solution.py:1635
  1141.7 10.0 copy-start.7
  1141.7 10.0 copy-start.9
  1141.7 10.6 copy-start.4
  1141.7 103.4 %all-to-all-start.2 = ((bf16[32,256,256]{2,1,0:T(8,128)(2,1)}), bf16[32,256,256]{2,1,0:T(8,128)(2,1)}, u32[]{:S(2)}, u32[]{:S(2)}) async-start(bf16[32,256,256]{2,1,0:T(8,128)(2,1)} %bitcast.98), calls=%async_computation.5 | async-start | bytes 8388608 | tf_op jit(solution)/shard_map/all_to_all | solution.py:1685
  1169.0 6.8 copy-start.1
Sparse Core Ops, SparseCore 0:
  10.3 88.2 all-gather.6
  100.2 26.5 all-gather.14
  128.3 80.2 all-gather.12
  210.6 151.7 all-gather.10
  364.4 82.9 all-gather.8
  607.6 77.2 reduce-scatter.3
  687.3 144.9 reduce-scatter.7
  835.3 77.4 reduce-scatter.5

commit v4 on v3

--- a/solution.py
+++ b/solution.py
@@ -436,7 +436,7 @@
     F, R = rows.shape[0], rows.shape[1]
     e = w.shape[1] // 3
     m = 2 * R
-    loads = [local(w_ref, w, lsem, 0)] + [
+    loads = [local(w_ref.at[:, pl.ds(0, 3 * e)], w, lsem, 0)] + [
         local(all_ref.at[pl.ds(2 * p, 2)], rows.at[pl.ds(2 * p, 2)], lsem, 1 + p) for p in range(F // 2)
     ]
     barrier = pltpu.get_barrier_semaphore()
@@ -477,7 +477,7 @@
 
 def qkv_call(F, rows, w):
     _, R, D = rows.shape
-    n = w.shape[1]
+    n = w.shape[1] // 4 * 3
     return pl.pallas_call(
         qkv_kernel,
         out_shape=[
@@ -503,7 +503,8 @@
     mixed, wo, x, gain, hid, ao, inp, b0, b1, b2, b3, b4, lsem, send, recv,
 ):
     at = Plane()
-    pairs = [(mixed_ref, mixed), (wo_ref, wo), (x_ref, x), (gain_ref, gain)]
+    e = wo.shape[1]
+    pairs = [(mixed_ref, mixed), (wo_ref.at[:, pl.ds(3 * e, e)], wo), (x_ref, x), (gain_ref, gain)]
     loads = [local(s, d, lsem, i) for i, (s, d) in enumerate(pairs)]
     at.greet()
     R = x.shape[0]
@@ -531,7 +532,7 @@
 
 def out_call(F, mixed, wo, x, gain):
     R, D = x.shape
-    e = wo.shape[1]
+    e = wo.shape[1] // 4
     return pl.pallas_call(
         out_kernel,
         out_shape=[
@@ -630,10 +631,10 @@
 
 
 def down_kernel(
-    C, h_ref, wd_ref, hid_ref, cot_ref, gain_ref, act_ref, der_ref,
-    res_ref, gg_ref, all_ref, grad_ref, own_ref,
-    h, wd, hid, mine, gain, act, der, res, gacc, rows, grad, cot, stage, b0, b1, b2, b3, b4,
-    lsem, osem, asem, send, recv, tsend, trecv,
+    C, h_ref, wd_ref, hid_ref, cot_ref, gain_ref, act_ref, der_ref, unit_ref,
+    res_ref, gg_ref, all_ref, grad_ref, own_ref, mom_ref, p_ref,
+    h, wd, hid, mine, gain, act, der, res, gacc, rows, grad, cot, stage, prod, b0, b1, b2, b3, b4,
+    lsem, osem, asem, psem, send, recv, tsend, trecv, usend, urecv,
 ):
     at = Plane()
     loads = [
@@ -657,7 +658,19 @@
     def partial(chip, cols):
         return nt(h[pl.ds(pl.multiple_of(chip * 2 * R, 2 * R), 2 * R), :], wd[cols, :])
 
-    total = scatter_phase(at, partial, (b0, b1, b2, b3, b4), send, recv, 0, moving.second)
+    z = moving.z
+    units = []
+
+    def between():
+        moving.second()
+        for k in range(1, C):
+            to = (z + k) % C
+            c = remote(unit_ref.at[to], mom_ref.at[z], usend, urecv, k, to, "ctx")
+            c.start()
+            units.append(c)
+        units.append(local(unit_ref.at[z], mom_ref.at[z], lsem, 10))
+
+    total = scatter_phase(at, partial, (b0, b1, b2, b3, b4), send, recv, 0, between)
     for c in loads[3:]:
         c.wait()
     moving.finish()
@@ -704,12 +717,43 @@
         )
 
     gather_phase(at, rows, send, recv, SCATTER_COPIES, on_rows)
+    F, D = rows.shape[0], rows.shape[2]
+    tile, cols = prod.shape[1], p_ref.shape[3]
+    puts = []
+    for t in range(D // tile):
+        if t >= 2:
+            for c in puts[t - 2]:
+                c.wait()
+        rhs = rows[:, :, t * tile : (t + 1) * tile].reshape(F * R, tile)
+        prod[t % 2] = lax.dot_general(
+            rhs, h[...], (((0,), (0,)), ((), ())), preferred_element_type=f32
+        ).astype(bf16)
+        puts.append(
+            [
+                local(
+                    prod.at[t % 2, :, pl.ds(b * cols, cols)],
+                    p_ref.at[b, 0, pl.ds(t * tile, tile)],
+                    psem,
+                    t * (n // cols) + b,
+                )
+                for b in range(n // cols)
+            ]
+        )
+    for step in puts[-2:]:
+        for c in step:
+            c.wait()
+    for k in range(1, C):
+        frm = (z - k + C) % C
+        remote(mom_ref.at[frm], mom_ref.at[frm], usend, urecv, k, frm, "ctx").wait_recv()
+    for c in units[:-1]:
+        c.wait_send()
+    units[-1].wait()
     for s in saves:
         s.wait()
     stores.finish()
 
 
-def down_call(C, F, h, wd, hid, cot, gain, act, der):
+def down_call(C, F, h, wd, hid, cot, gain, act, der, units):
     R, D = hid.shape
     n = wd.shape[1]
     T = F * R
@@ -723,9 +767,11 @@
             jax.ShapeDtypeStruct((F, R, D), bf16),
             jax.ShapeDtypeStruct((T, 2 * n), bf16),
             one,
+            jax.ShapeDtypeStruct(units.shape, bf16),
+            jax.ShapeDtypeStruct((units.shape[1], 1, D, units.shape[3]), bf16),
         ],
-        in_specs=[ANY] * 7,
-        out_specs=[ANY] * 5,
+        in_specs=[ANY] * 8,
+        out_specs=[ANY] * 7,
         scratch_shapes=[
             pltpu.VMEM((T, n), bf16),
             pltpu.VMEM((D, n), bf16),
@@ -740,12 +786,13 @@
             pltpu.VMEM((2, 2 * R, 2 * n), bf16),
             pltpu.VMEM((R, D), bf16),
             pltpu.VMEM((C, R // C, D), bf16),
+            pltpu.VMEM((2, 512, n), bf16),
         ]
         + scatter_scratch(R, D)
-        + [dma(10), dma(15), dma(10), dma(copies), dma(copies), dma(2 * C), dma(2 * C)],
+        + [dma(11), dma(15), dma(10), dma(16), dma(copies), dma(copies), dma(2 * C), dma(2 * C), dma(C), dma(C)],
         compiler_params=params(3),
-        cost_estimate=cost(95),
-    )(h, wd, hid, cot, gain, act, der)
+        cost_estimate=cost(115),
+    )(h, wd, hid, cot, gain, act, der, units)
 
 
 def mid_kernel(
@@ -755,10 +802,10 @@
     lsem, osem, send, recv,
 ):
     at = Plane()
-    n = w.shape[1] // 2
+    n, e = w.shape[1] // 2, wo.shape[1]
     pairs = [
         (grad_ref, grad), (wg_ref, w.at[:, pl.ds(0, n)]), (wu_ref, w.at[:, pl.ds(n, n)]),
-        (cot_ref, cot), (ao_ref, ao), (gain_ref, gain), (wo_ref, wo),
+        (cot_ref, cot), (ao_ref, ao), (gain_ref, gain), (wo_ref.at[:, pl.ds(3 * e, e)], wo),
     ]
     loads = [local(s, d, lsem, i) for i, (s, d) in enumerate(pairs)]
     at.greet()
@@ -808,7 +855,7 @@
 
 def mid_call(F, grad, wg, wu, cot, ao, gain, wo):
     R, D = cot.shape
-    n, e = 2 * wg.shape[1], wo.shape[1]
+    n, e = 2 * wg.shape[1], wo.shape[1] // 4
     T = F * R
     copies = SCATTER_COPIES + GATHER_COPIES
     return pl.pallas_call(
@@ -852,7 +899,7 @@
     R = res.shape[0]
     pairs = [
         (in_ref, ins.at[at.f]), (st_ref, st), (q_ref, q), (k_ref, k),
-        (v_ref, gp.at[:, pl.ds(2 * e, e)]), (proj_ref.at[:, pl.ds(0, 2 * e)], proj), (w_ref, w), (res_ref, res),
+        (v_ref, gp.at[:, pl.ds(2 * e, e)]), (proj_ref.at[:, pl.ds(0, 2 * e)], proj), (w_ref.at[:, pl.ds(0, 3 * e)], w), (res_ref, res),
         (gain_ref, gains.at[at.f]),
     ]
     loads = [local(s, d, lsem, i) for i, (s, d) in enumerate(pairs)]
@@ -903,7 +950,7 @@
 
 def last_call(F, wq, wk, gv, proj, st, ins, w, res, gains):
     R, D = res.shape
-    n = w.shape[1]
+    n = w.shape[1] // 4 * 3
     T, e = F * R, n // 3
     return pl.pallas_call(
         functools.partial(last_kernel, D),
@@ -1307,7 +1354,7 @@
             pending.append(c)
         for c in pending:
             c.wait()
-        if iteration == 0:
+        if iteration == NS_STEPS - 1:
             leave_layer()
         pending = []
         for i in range(tiles):
@@ -1384,9 +1431,9 @@
     return hidden_in, out, rows, act.astype(bf16), der.astype(bf16), (act * u).astype(bf16)
 
 
-def down_and_back(C, F, h, wd, hidden_in, cot, gain, act, der):
+def down_and_back(C, F, h, wd, hidden_in, cot, gain, act, der, units):
     if kernels_fit(C, F):
-        return down_call(C, F, h, wd, hidden_in, cot, gain, act, der)
+        return down_call(C, F, h, wd, hidden_in, cot, gain, act, der, units)
     cot = to_layer(C, F, cot)
     out = token_sums(dot(h, wd, 1, 1))
     scale = rms(out)
@@ -1400,6 +1447,8 @@
         rows,
         jnp.concatenate([(gh * der.astype(f32)).astype(bf16), (gh * act.astype(f32)).astype(bf16)], axis=1),
         cot,
+        None,
+        None,
     )
 
 
@@ -1486,8 +1535,8 @@
         return lax.psum_scatter(grad, "ctx", scatter_dimension=2, tiled=True)
 
     kernels = kernels_fit(C, F)
-    w_qkv = rows_gather(jnp.concatenate([w_attn[0], w_attn[1], w_attn[2]], axis=1))
-    w_out = rows_gather(w_attn[3])
+    w_heads = rows_gather(jnp.concatenate([w_attn[i] for i in range(UNITS_ATTN)], axis=1))
+    w_qkv, w_out = (w_heads, w_heads) if kernels else (w_heads[:, : 3 * head_cols], w_heads[:, 3 * head_cols :])
     ffn_flat = w_ffn.reshape(3, dz, hidden_cols)
     w_gate = rows_gather(ffn_flat[0])
     w_up = rows_gather(ffn_flat[1])
@@ -1545,17 +1594,18 @@
     hidden_in, attn_out, mlp_all, act, der, hidden = attn_out_and_up(
         C, F, attn_mixed, w_out, own_input, gains[2:3], w_gate, w_up
     )
-    result, mlp_gain, grad_mlp_all, grad_ffn_in, own_grad = down_and_back(
-        C, F, hidden, w_down, hidden_in, cotangent.reshape(local_rows, width), gains[3:4], act, der
+    by_layer = None
+    if kernels:
+        by_layer = jnp.concatenate(
+            [mom_attn[:, None].astype(bf16), jnp.transpose(mom_ffn.astype(bf16), (2, 0, 1, 3))], axis=1
+        )
+    result, mlp_gain, grad_mlp_all, grad_ffn_in, own_grad, mom_own, p_down = down_and_back(
+        C, F, hidden, w_down, hidden_in, cotangent.reshape(local_rows, width), gains[3:4], act, der, by_layer
     )
     if kernels:
-        units_in = jnp.concatenate(
-            [mom_attn[:, None].astype(bf16), jnp.transpose(mom_ffn.astype(bf16), (2, 0, 1, 3))], axis=1
-        )
-        units_in = after(units_in, w_down)
-        mom_own = jnp.swapaxes(lax.all_to_all(units_in, "ctx", split_axis=0, concat_axis=0, tiled=True), 0, 1)
-        grad_mlp_all, mom_own = lax.optimization_barrier((grad_mlp_all, mom_own))
-    p_down = product(block_count, 1, (grad_mlp_all, hidden))
+        mom_own = jnp.swapaxes(mom_own, 0, 1)
+    else:
+        p_down = product(block_count, 1, (grad_mlp_all, hidden))
     g_down = scatter(p_down)
     p_gate_up = product(block_count, 2, (mlp_all, grad_ffn_in))
     if kernels:

time: 1270 us -> 1120 us (0.88)
  waiting for transfers between devices: 353 us -> 251 us
  starting transfers between devices: 35.3 us -> 9.27 us
  Pallas kernels: 765 us -> 746 us
    all_gather x5 -> x4, waiting for transfers between devices: 216 us -> 102 us  [rows_gather(): return lax.all_gather(shard, 'ctx', axis=0, tiled=True)]
    pallas_call x1, Pallas kernels: 208 us -> 173 us  [newton_call(): pl.pallas_call(functools.partial(newton_kernel, C), out_shape=[jax.ShapeD...]
    pallas_call x1, Pallas kernels: 99.7 us -> 129 us  [down_call(): pl.pallas_call(functools.partial(down_kernel, C), out_shape=[one, jax.Sha...]
    all_to_all x1 -> x0, starting transfers between devices: 20.2 us -> none  [shards(): lax.all_to_all(units_in, 'ctx', split_axis=0, concat_axis=0, tiled=True)]
    pallas_call x3 -> x2, Pallas kernels: 51.6 us -> 38.1 us  [grad_call(): pl.pallas_call(grad_kernel, out_shape=jax.ShapeDtypeStruct((units, groups...]
  transfers between devices with their start and end apart: 11 -> 9, of which waited for: 4 -> 5; matrix products, arithmetic and copies ran while one was open for 6% -> 7% of each run, Pallas kernels for 59% -> 55%
where the time goes in v4:
time: 1120 us
  Pallas kernels  746 us (67%)
  waiting for transfers between devices  251 us (22%)
  local copies, waits for them, and re-layouts  53.1 us (5%)
  other arithmetic  41.9 us (4%)
  between operations  14.7 us (1%)
    pallas_call x1, Pallas kernels, newton_call(): pl.pallas_call(functools.partial(newton_kernel, C), out_shape=[jax.ShapeD...  173 us
    pallas_call x1, Pallas kernels, down_call(): pl.pallas_call(functools.partial(down_kernel, C), out_shape=[one, jax.Sha...  129 us
    all_gather x4, waiting for transfers between devices, rows_gather(): return lax.all_gather(shard, 'ctx', axis=0, tiled=True)  102 us
    pallas_call x1, Pallas kernels, mid_call(): pl.pallas_call(mid_kernel, out_shape=[jax.ShapeDtypeStruct((R, D), f32),...  96.6 us
    pallas_call x1, Pallas kernels, enter_call(): pl.pallas_call(functools.partial(enter_kernel, C), out_shape=[jax.ShapeDt...  89.8 us
    reduce_scatter x3, waiting for transfers between devices, scatter(): return lax.psum_scatter(grad, 'ctx', scatter_dimension=0, tiled=True)[0]  82 us
    all_to_all x1, waiting for transfers between devices, shards(): steps = lax.all_to_all(home, BOTH, split_axis=0, concat_axis=0, tiled=True)  66.9 us
    pallas_call x1, Pallas kernels, last_call(): pl.pallas_call(functools.partial(last_kernel, D), out_shape=[jax.ShapeDty...  60.2 us
  transfers between devices with their start and end apart: 9, of which 5 were waited for; matrix products, arithmetic and copies ran while one was open for 7% of the time, Pallas kernels for 55%

profile of v4, /device:TPU:0, one launch (start us, length us, event | category | flops | bytes accessed | tf_op | source)
XLA Modules:
  0.0 1115.6 jit_solution(16060229638729481847)
XLA Ops:
  18.1 89.8 %shard_map.176 = (bf16[256,2048]{1,0:T(8,128)(2,1)}, bf16[8,256,2048]{2,1,0:T(8,128)(2,1)}) custom-call(bf16[256,2048]{1,0:T(8,128)(2,1)} %bitcast.121), custom_call_target="tpu_custom_call" | custom-call | flops 70000001024 | bytes 1048576 | tf_op jit(solution)/shard_map/pallas_call | solution.py:418
  113.9 4.9 sine_multiply_fusion
  121.7 23.1 %shard_map.177 = (f32[2048,768]{1,0:T(8,128)}, f32[8,8,2048]{2,1,0:T(8,128)}) custom-call(bf16[8,256,2048]{2,1,0:T(8,128)(2,1)} %get-tuple-element.50.all_ref, bf16[2048,1024]{1,0:T(8,128)(2,1)} %all-gather.5.cloned.1.call-done.w_ref.wo_ref), custom_call_target="tpu_custom_call" | custom-call | flops 22000001024 | bytes 1048576 | tf_op jit(solution)/shard_map/pallas_call | solution.py:481
  146.1 17.7 %shard_map.178 = (bf16[4,2,256,256]{3,2,1,0:T(8,128)(2,1)}, bf16[4,2,256,256]{3,2,1,0:T(8,128)(2,1)}, bf16[4,2,256,256]{3,2,1,0:T(8,128)(2,1)}, f32[2,2,1024,128]{3,2,1,0:T(8,128)}) custom-call(f32[4,2,256,768]{3,2,1,0:T(8,128)} %bitcast.126, f32[4,2,256,768]{3,2,1,0:T(8,128)} %bitcast.127, f32[4,2,256,768]{3,2,1,0:T(8,128)} %bitcast.128, ...), custom_call_target="tpu_custom_call" | custom-call | flops 15000000512 | bytes 1048576 | tf_op jit(solution)/shard_map/pallas_call | solution.py:1113
  163.8 46.9 %shard_map.179 = (f32[256,2048]{1,0:T(8,128)}, f32[256,2048]{1,0:T(8,128)}, bf16[256,2048]{1,0:T(8,128)(2,1)}) custom-call(bf16[2048,256]{1,0:T(8,128)(2,1)} %bitcast.134, bf16[2048,1024]{1,0:T(8,128)(2,1)} %all-gather.5.cloned.1.call-done.w_ref.wo_ref, bf16[256,2048]{1,0:T(8,128)(2,1)} %get-tuple-element.54.x_ref, f32[1,2048]{1,0:T(1,128)} %get-tuple-element.134.gain_ref), custom_call_target="tpu_custom_call" | custom-call | flops 46000001024 | bytes 1048576 | tf_op jit(solution)/shard_map/pallas_call | solution.py:536
  210.8 67.9 %all-gather.9.cloned.1.call-done.wu_ref = bf16[2048,1024]{1,0:T(8,128)(2,1)} async-done(((bf16[512,1024]{1,0:T(8,128)(2,1)}), bf16[2048,1024]{1,0:T(8,128)(2,1)}) %all-gather.9.cloned.1.call-update) | async-done | bytes 4194320 | tf_op jit(solution)/shard_map/all_gather | solution.py:1523
  278.7 47.1 %shard_map.180 = (bf16[8,256,2048]{2,1,0:T(8,128)(2,1)}, bf16[2048,1024]{1,0:T(8,128)(2,1)}, bf16[2048,1024]{1,0:T(8,128)(2,1)}, bf16[2048,1024]{1,0:T(8,128)(2,1)}) custom-call(bf16[256,2048]{1,0:T(8,128)(2,1)} %get-tuple-element.55.in_ref, bf16[2048,1024]{1,0:T(8,128)(2,1)} %all-gather.7.cloned.1.call-done.wg_ref, ...), custom_call_target="tpu_custom_call" | custom-call | flops 46000001024 | bytes 1048576 | tf_op jit(solution)/shard_map/pallas_call | solution.py:615
  325.8 33.7 %all-gather.11.cloned.1.call-done.wd_ref = bf16[2048,1024]{1,0:T(8,128)(2,1)} async-done(((bf16[512,1024]{1,0:T(8,128)(2,1)}), bf16[2048,1024]{1,0:T(8,128)(2,1)}) %all-gather.11.cloned.1.call-update) | async-done | bytes 4194320 | tf_op jit(solution)/shard_map/all_gather | solution.py:1523
  359.4 128.9 %shard_map.181 = (bf16[256,2048]{1,0:T(8,128)(2,1)}, f32[1,2048]{1,0:T(1,128)}, bf16[8,256,2048]{2,1,0:T(8,128)(2,1)}, bf16[2048,2048]{1,0:T(8,128)(2,1)}, bf16[...) custom-call(bf16[2048,1024]{1,0:T(8,128)(2,1)} %get-tuple-element.56.h_ref, ...), custom_call_target="tpu_custom_call" | custom-call | flops 115000000512 | bytes 1048576 | tf_op jit(solution)/shard_map/pallas_call | solution.py:762
  488.4 23.8 %shard_map.182 = bf16[4,2,2048,256]{3,2,1,0:T(8,128)(2,1)} custom-call(bf16[2048,2048]{1,0:T(8,128)(2,1)} %bitcast.125, bf16[2048,2048]{1,0:T(8,128)(2,1)} %get-tuple-element.65.refs_1_.grad_ref), custom_call_target="tpu_custom_call" | custom-call | flops 24000000000 | bytes 1048576 | tf_op jit(solution)/shard_map/pallas_call | solution.py:1009
  512.2 96.6 %shard_map.183 = (f32[256,2048]{1,0:T(8,128)}, f32[1,2048]{1,0:T(1,128)}, bf16[8,256,2048]{2,1,0:T(8,128)(2,1)}, bf16[2048,256]{1,0:T(8,128)(2,1)}) custom-call(bf16[2048,2048]{1,0:T(8,128)(2,1)} %get-tuple-element.65.refs_1_.grad_ref, bf16[2048,1024]{1,0:T(8,128)(2,1)} %all-gather.7.cloned.1.call-done.wg_ref, ...), custom_call_target="tpu_custom_call" | custom-call | flops 92000002048 | bytes 1048576 | tf_op jit(solution)/shard_map/pallas_call | solution.py:861
  608.9 25.3 %shard_map.184 = (f32[4,2,256,256]{3,2,1,0:T(8,128)}, f32[4,2,256,256]{3,2,1,0:T(8,128)}, bf16[4,2,256,256]{3,2,1,0:T(8,128)(2,1)}, f32[2,2,8,1024]{3,2,1,0:T(8,128)}, f32[2,2,8,128]{3,2,1,0:T(8,128)}) custom-call(f32[4,2,256,768]{3,2,1,0:T(8,128)} %bitcast.129, f32[4,2,256,768]{3,2,1,0:T(8,128)} %bitcast.130, f32[4,2,256,768]{3,2,1,0:T(8,128)} %bitcast.131, ...), custom_call_target="tpu_custom_call" | custom-call | flops 35000000512 | bytes 1048576 | tf_op jit(solution)/shard_map/pallas_call | solution.py:1178
  637.3 60.2 %shard_map.185 = (bf16[256,2048]{1,0:T(8,128)(2,1)}, bf16[2048,768]{1,0:T(8,128)(2,1)}, f32[8,2048]{1,0:T(8,128)}) custom-call(f32[2048,256]{1,0:T(8,128)} %bitcast.132, f32[2048,256]{1,0:T(8,128)} %bitcast.133, bf16[2048,256]{1,0:T(8,128)(2,1)} %bitcast.136, f32[2048,768]{1,0:T(8,128)} %get-tuple-element.51.proj_ref, ...), custom_call_target="tpu_custom_call" | custom-call | flops 54999998464 | bytes 1048576 | tf_op jit(solution)/shard_map/pallas_call | solution.py:955
  697.5 14.3 %shard_map.186 = bf16[4,1,2048,256]{3,2,1,0:T(8,128)(2,1)} custom-call(bf16[2048,2048]{1,0:T(8,128)(2,1)} %bitcast.123, bf16[2048,768]{1,0:T(8,128)(2,1)} %get-tuple-element.80.refs_1_, bf16[2048,2048]{1,0:T(8,128)(2,1)} %bitcast.124, bf16[2048,256]{1,0:T(8,128)(2,1)} %bitcast.135), custom_call_target="tpu_custom_call" | custom-call | flops 12000000000 | bytes 1048576 | tf_op jit(solution)/shard_map/pallas_call | solution.py:1009
  720.4 4.6 reduce-scatter.8.cloned.1.call-done
  728.1 77.4 %reduce-scatter.6.cloned.1.call-done = bf16[1,1,2048,256]{3,2,1,0:T(8,128)(2,1)} async-done(((bf16[4,1,2048,256]{3,2,1,0:T(8,128)(2,1)}), bf16[1,1,2048,256]{3,2,1,0:T(8,128)(2,1)}) %reduce-scatter.6.cloned.1.call-update) | async-done | bytes 1048592 | tf_op jit(solution)/shard_map/reduce_scatter | solution.py:1534
  809.1 4.8 all-to-all-start
  814.0 5.5 fusion.m_ref
  819.5 172.5 %shard_map.187 = (bf16[1024,2048]{1,0:T(8,128)(2,1)}, bf16[2,256,2048]{2,1,0:T(8,128)(2,1)}, f32[8,2048]{1,0:T(8,128)}) custom-call(bf16[4,2048,256]{2,1,0:T(8,128)(2,1)} %fusion.m_ref, bf16[2,256,2048]{2,1,0:T(8,128)(2,1)} %pad_maximum_fusion.2.rows_ref, f32[8,2048]{1,0:T(8,128)} %get-tuple-element.85.gain_ref), custom_call_target="tpu_custom_call" | custom-call | flops 95000002560 | bytes 1048576 | tf_op jit(solution)/shard_map/pallas_call | solution.py:1388
  1009.0 6.7 copy.47
  1015.7 4.4 fusion.1
  1020.2 6.7 copy.48
  1029.4 66.9 %all-to-all-done.1 = bf16[32,256,256]{2,1,0:T(8,128)(2,1)} async-done(((bf16[32,256,256]{2,1,0:T(8,128)(2,1)}), bf16[32,256,256]{2,1,0:T(8,128)(2,1)}, u32[]{:S(2)}, u32[]{:S(2)}) %all-to-all-start.1) | async-done | bytes 4194336 | tf_op jit(solution)/shard_map/all_to_all | solution.py:1735
  1101.9 6.7 copy.49
  (88 shorter events, 64.5 us)
Async XLA Ops:
  7.2 114.5 %all-gather.5.cloned.1.call-start = ((), (), s32[]{:S(2)}) async-start(), calls=%async_computation.5 | async-start | bytes 5242880 | tf_op jit(solution)/shard_map/all_gather | solution.py:1523
  9.6 201.1 %all-gather.7.cloned.1.call-start = ((), (), s32[]{:S(2)}) async-start(), calls=%async_computation.6 | async-start | bytes 5242880 | tf_op jit(solution)/shard_map/all_gather | solution.py:1523
  13.8 264.8 %all-gather.9.cloned.1.call-start = ((), (), s32[]{:S(2)}) async-start(), calls=%async_computation.7 | async-start | bytes 5242880 | tf_op jit(solution)/shard_map/all_gather | solution.py:1523
  15.1 344.3 %all-gather.11.cloned.1.call-start = ((), (), s32[]{:S(2)}) async-start(), calls=%async_computation.8 | async-start | bytes 5242880 | tf_op jit(solution)/shard_map/all_gather | solution.py:1523
  16.4 592.5 %reduce-scatter.4.cloned.1.call-start = ((), (), s32[]{:S(2)}) async-start(), calls=%async_computation.9 | async-start | bytes 5242880 | tf_op jit(solution)/shard_map/reduce_scatter | solution.py:1534
  18.1 89.8 %copy-start.8 = (f32[4,2048]{1,0:T(4,128)S(1)}, f32[4,2048]{1,0:T(4,128)}, u32[]{:S(2)}) copy-start(f32[4,2048]{1,0:T(4,128)} %param.14) | copy-start | bytes 98308
  108.6 3.9 copy-start
  113.5 5.2 copy-start.3
  488.4 236.6 %reduce-scatter.8.cloned.1.call-start = ((), (), s32[]{:S(2)}) async-start(), calls=%async_computation.11 | async-start | bytes 10485760 | tf_op jit(solution)/shard_map/reduce_scatter | solution.py:1534
  512.2 293.3 %reduce-scatter.6.cloned.1.call-start = ((), (), s32[]{:S(2)}) async-start(), calls=%async_computation.10 | async-start | bytes 5242880 | tf_op jit(solution)/shard_map/reduce_scatter | solution.py:1534
  608.9 27.7 %copy-start.10 = (f32[1,2048]{1,0:T(1,128)S(1)}, f32[1,2048]{1,0:T(1,128)}, u32[]{:S(2)}) copy-start(f32[1,2048]{1,0:T(1,128)} %get-tuple-element.79) | copy-start | bytes 24580
  608.9 27.7 %copy-start.11 = (f32[1,2048]{1,0:T(1,128)S(1)}, f32[1,2048]{1,0:T(1,128)}, u32[]{:S(2)}) copy-start(f32[1,2048]{1,0:T(1,128)} %get-tuple-element.78) | copy-start | bytes 24580
  715.0 3.9 copy-start.5
  715.0 3.9 copy-start.6
  720.4 85.1 %copy-start.2 = (bf16[1,1,2048,256]{3,2,1,0:T(8,128)(2,1)S(1)}, bf16[1,1,2048,256]{3,2,1,0:T(8,128)(2,1)}, u32[]{:S(2)}) copy-start(bf16[1,1,2048,256]{3,2,1,0:T(8,128)(2,1)} %reduce-scatter.4.cloned.1.call-done) | copy-start | bytes 3145732
  809.1 189.6 %all-to-all-start = ((bf16[1,4,4,512,256]{4,3,1,0,2:T(8,128)(2,1)}), bf16[1,4,4,512,256]{4,3,1,0,2:T(8,128)(2,1)}, u32[]{:S(2)}, u32[]{:S(2)}) async-start(bf16[1,4,4,512,256]{4,3,1,0,2:T(8,128)(2,1)} %pad_maximum_fusion.1), calls=%async_computation.3 | async-start | bytes 8388608 | tf_op jit(solution)/shard_map/all_to_all | solution.py:1685
  998.7 4.1 copy-start.7
  998.7 4.2 copy-start.9
  998.7 4.8 copy-start.4
  998.7 97.6 %all-to-all-start.1 = ((bf16[32,256,256]{2,1,0:T(8,128)(2,1)}), bf16[32,256,256]{2,1,0:T(8,128)(2,1)}, u32[]{:S(2)}, u32[]{:S(2)}) async-start(bf16[32,256,256]{2,1,0:T(8,128)(2,1)} %bitcast.99), calls=%async_computation.4 | async-start | bytes 8388608 | tf_op jit(solution)/shard_map/all_to_all | solution.py:1735
  1020.2 6.8 copy-start.1
Sparse Core Ops, SparseCore 0:
  10.2 105.5 all-gather.4
  117.9 79.2 all-gather.6
  199.4 79.2 all-gather.8
  280.1 79.2 all-gather.10
  488.5 89.1 reduce-scatter.3
  580.0 144.9 reduce-scatter.7
  728.0 77.4 reduce-scatter.5

commit v5 on v4

--- a/solution.py
+++ b/solution.py
@@ -559,13 +559,13 @@
 
 
 def up_kernel(
-    in_ref, wg_ref, wu_ref, all_ref, act_ref, der_ref, h_ref,
+    in_ref, w_ref, all_ref, act_ref, der_ref, h_ref,
     w, rows, act, der, h, lsem, osem, send, recv,
 ):
     at = Plane()
     own = local(in_ref, rows.at[at.f], lsem, 0)
     n = act.shape[2]
-    loads = [local(wg_ref, w.at[:, pl.ds(0, n)], lsem, 1), local(wu_ref, w.at[:, pl.ds(n, n)], lsem, 2)]
+    loads = [local(w_ref, w, lsem, 1)]
     width = 256
     at.greet()
     R = rows.shape[1]
@@ -607,15 +607,15 @@
     stores.finish()
 
 
-def up_call(F, inp, wg, wu):
+def up_call(F, inp, w):
     R, D = inp.shape
-    n = wg.shape[1]
+    n = w.shape[1] // 2
     T = F * R
     wide = jax.ShapeDtypeStruct((T, n), bf16)
     return pl.pallas_call(
         up_kernel,
         out_shape=[jax.ShapeDtypeStruct((F, R, D), bf16), wide, wide, wide],
-        in_specs=[ANY] * 3,
+        in_specs=[ANY] * 2,
         out_specs=[ANY] * 4,
         scratch_shapes=[
             pltpu.VMEM((D, 2 * n), bf16),
@@ -624,10 +624,10 @@
             pltpu.VMEM((2, 2 * R, n), bf16),
             pltpu.VMEM((2, 2 * R, n), bf16),
         ]
-        + [dma(3), dma(20), dma(GATHER_COPIES), dma(GATHER_COPIES)],
+        + [dma(2), dma(20), dma(GATHER_COPIES), dma(GATHER_COPIES)],
         compiler_params=params(2),
         cost_estimate=cost(46),
-    )(inp, wg, wu)
+    )(inp, w)
 
 
 def down_kernel(
@@ -650,6 +650,16 @@
     pl.semaphore_wait(barrier, 2 * (C - 1) + 1)
     R = rows.shape[1]
     n = wd.shape[1]
+    z = moving.z
+    units = []
+
+    def send_units(k):
+        to = (z + k) % C
+        c = remote(unit_ref.at[to], mom_ref.at[z], usend, urecv, k, to, "ctx")
+        c.start()
+        units.append(c)
+
+    send_units(1)
     loads[0].wait()
     moving.first()
     loads[1].wait()
@@ -658,16 +668,10 @@
     def partial(chip, cols):
         return nt(h[pl.ds(pl.multiple_of(chip * 2 * R, 2 * R), 2 * R), :], wd[cols, :])
 
-    z = moving.z
-    units = []
-
     def between():
         moving.second()
-        for k in range(1, C):
-            to = (z + k) % C
-            c = remote(unit_ref.at[to], mom_ref.at[z], usend, urecv, k, to, "ctx")
-            c.start()
-            units.append(c)
+        for k in range(2, C):
+            send_units(k)
         units.append(local(unit_ref.at[z], mom_ref.at[z], lsem, 10))
 
     total = scatter_phase(at, partial, (b0, b1, b2, b3, b4), send, recv, 0, between)
@@ -796,28 +800,28 @@
 
 
 def mid_kernel(
-    grad_ref, wg_ref, wu_ref, cot_ref, ao_ref, gain_ref, wo_ref,
+    grad_ref, w_ref, cot_ref, ao_ref, gain_ref, wo_ref,
     res_ref, gg_ref, all_ref, gm_ref,
     grad, w, cot, ao, gain, wo, res, gacc, rows, gm, b0, b1, b2, b3, b4,
     lsem, osem, send, recv,
 ):
     at = Plane()
-    n, e = w.shape[1] // 2, wo.shape[1]
+    e = wo.shape[1]
     pairs = [
-        (grad_ref, grad), (wg_ref, w.at[:, pl.ds(0, n)]), (wu_ref, w.at[:, pl.ds(n, n)]),
+        (grad_ref, grad), (w_ref, w),
         (cot_ref, cot), (ao_ref, ao), (gain_ref, gain), (wo_ref.at[:, pl.ds(3 * e, e)], wo),
     ]
     loads = [local(s, d, lsem, i) for i, (s, d) in enumerate(pairs)]
     at.greet()
     R = rows.shape[1]
-    for c in loads[:3]:
+    for c in loads[:2]:
         c.wait()
 
     def partial(chip, cols):
         return nt(grad[pl.ds(pl.multiple_of(chip * 2 * R, 2 * R), 2 * R), :], w[cols, :])
 
     total = scatter_phase(at, partial, (b0, b1, b2, b3, b4), send, recv, 0)
-    for c in loads[3:]:
+    for c in loads[2:]:
         c.wait()
     gacc[...] = jnp.zeros_like(gacc)
 
@@ -853,9 +857,9 @@
     stores.finish()
 
 
-def mid_call(F, grad, wg, wu, cot, ao, gain, wo):
+def mid_call(F, grad, w, cot, ao, gain, wo):
     R, D = cot.shape
-    n, e = 2 * wg.shape[1], wo.shape[1] // 4
+    n, e = w.shape[1], wo.shape[1] // 4
     T = F * R
     copies = SCATTER_COPIES + GATHER_COPIES
     return pl.pallas_call(
@@ -866,7 +870,7 @@
             jax.ShapeDtypeStruct((F, R, D), bf16),
             jax.ShapeDtypeStruct((T, e), bf16),
         ],
-        in_specs=[ANY] * 7,
+        in_specs=[ANY] * 6,
         out_specs=[ANY] * 4,
         scratch_shapes=[
             pltpu.VMEM((T, n), bf16),
@@ -884,7 +888,7 @@
         + [dma(10), dma(10), dma(copies), dma(copies)],
         compiler_params=params(4),
         cost_estimate=cost(92),
-    )(grad, wg, wu, cot, ao, gain, wo)
+    )(grad, w, cot, ao, gain, wo)
 
 
 def last_kernel(
@@ -1194,8 +1198,8 @@
 
 
 def newton_kernel(
-    C, m_ref, rows_ref, gain_ref, out_ref, home_ref, gsum_ref,
-    v, gram, y, yf, stat, stage, gains, gsum,
+    C, m_ref, rows_ref, gain_ref, out_ref, stage_ref, gsum_ref,
+    v, gram, y, yf, stat, gains, gsum,
     lsem, osem, vsend, vrecv, ysend, yrecv, ssend, srecv, tsend, trecv, gsend, grecv, usend, urecv, usem,
 ):
     me = lax.axis_index("fsdp")
@@ -1233,38 +1237,22 @@
     for a in range(2):
         for k in range(1, C):
             to = (z + k) % C
-            c = remote(rows_ref.at[a, part(to)], stage.at[a, z], tsend, trecv, 2 * C * a + k, to, "ctx")
+            c = remote(rows_ref.at[a, part(to)], stage_ref.at[a, z], tsend, trecv, C * a + k, to, "ctx")
             c.start()
             sent.append(c)
-        keep.append(local(rows_ref.at[a, part(z)], stage.at[a, z], lsem, 2 + a))
+        keep.append(local(rows_ref.at[a, part(z)], stage_ref.at[a, z], lsem, 2 + a))
     gload.wait()
     for k in range(1, C):
         c = remote(gains.at[z], gains.at[z], gsend, grecv, k, (z + k) % C, "ctx")
         c.start()
         sent.append(c)
 
-    def leave_layer():
-        for a in range(2):
-            for k in range(1, C):
-                frm = (z - k + C) % C
-                remote(stage.at[a, frm], stage.at[a, frm], tsend, trecv, 2 * C * a + k, frm, "ctx").wait_recv()
-            keep[a].wait()
-            for k in range(1, C):
-                to = (chip + k) % C
-                c = remote(
-                    stage.at[a, to], home_ref.at[a, part(chip)], tsend, trecv, 2 * C * a + C + k, 2 * to + core
-                )
-                c.start()
-                sent.append(c)
-            keep[a] = local(stage.at[a, chip], home_ref.at[a, part(chip)], lsem, 4 + a)
-
-    def arrived_home():
+    def rows_arrived():
         for a in range(2):
             keep[a].wait()
             for k in range(1, C):
-                frm = (chip - k + C) % C
-                dst = home_ref.at[a, part(frm)]
-                remote(dst, dst, tsend, trecv, 2 * C * a + C + k, 2 * frm + core).wait_recv()
+                dst = stage_ref.at[a, (z - k + C) % C]
+                remote(dst, dst, tsend, trecv, C * a + k, (z - k + C) % C, "ctx").wait_recv()
         for k in range(1, C):
             frm = (z - k + C) % C
             remote(gains.at[frm], gains.at[frm], gsend, grecv, k, frm, "ctx").wait_recv()
@@ -1354,8 +1342,6 @@
             pending.append(c)
         for c in pending:
             c.wait()
-        if iteration == NS_STEPS - 1:
-            leave_layer()
         pending = []
         for i in range(tiles):
 
@@ -1375,7 +1361,7 @@
                 c = pltpu.make_async_copy(v.at[0, block(i)], out_ref.at[block(i)], osem.at[i])
             c.start()
             pending.append(c)
-    arrived_home()
+    rows_arrived()
     for c in pending:
         c.wait()
 
@@ -1389,7 +1375,7 @@
         functools.partial(newton_kernel, C),
         out_shape=[
             jax.ShapeDtypeStruct((M, D), bf16),
-            jax.ShapeDtypeStruct((2, R, D), bf16),
+            jax.ShapeDtypeStruct((2, C, R // C, D), bf16),
             jax.ShapeDtypeStruct((8, D), f32),
         ],
         in_specs=[ANY] * 3,
@@ -1400,31 +1386,73 @@
             pltpu.VMEM((2, M, D), bf16),
             pltpu.VMEM((M, D), f32),
             pltpu.VMEM((2, 8, 128), f32),
-            pltpu.VMEM((2, C, R // C, D), bf16),
             pltpu.VMEM((C, 8, D), f32),
             pltpu.VMEM((8, D), f32),
             dma(7), dma(n), dma(n), dma(n), dma(n), dma(n), dma(1), dma(1),
-            dma(4 * C), dma(4 * C), dma(C), dma(C), dma(2 * C * C), dma(2 * C * C), dma(C),
+            dma(2 * C), dma(2 * C), dma(C), dma(C), dma(2 * C * C), dma(2 * C * C), dma(C),
         ],
         compiler_params=params(6),
         cost_estimate=cost(95),
     )(x, rows, gains)
 
 
+def leave_kernel(C, stage_ref, home_ref, lsem, send, recv):
+    at = Plane()
+    piece = stage_ref.shape[2]
+    barrier = pltpu.get_barrier_semaphore()
+    for k in range(1, C):
+        pl.semaphore_signal(
+            barrier, inc=1, device_id={"fsdp": 2 * ((at.chip + k) % C) + at.c}, device_id_type=MESH
+        )
+    pl.semaphore_wait(barrier, C - 1)
+
+    def part(j):
+        return pl.ds(j * piece, piece)
+
+    sent, keep = [], []
+    for a in range(2):
+        for k in range(1, C):
+            to = (at.chip + k) % C
+            c = remote(stage_ref.at[a, to], home_ref.at[a, part(at.chip)], send, recv, C * a + k, 2 * to + at.c)
+            c.start()
+            sent.append(c)
+        keep.append(local(stage_ref.at[a, at.chip], home_ref.at[a, part(at.chip)], lsem, a))
+    for a in range(2):
+        keep[a].wait()
+        for k in range(1, C):
+            frm = (at.chip - k + C) % C
+            dst = home_ref.at[a, part(frm)]
+            remote(dst, dst, send, recv, C * a + k, 2 * frm + at.c).wait_recv()
+    for c in sent:
+        c.wait_send()
+
+
+def leave_call(C, stage):
+    return pl.pallas_call(
+        functools.partial(leave_kernel, C),
+        out_shape=jax.ShapeDtypeStruct((2, C * stage.shape[2], stage.shape[3]), bf16),
+        in_specs=[ANY],
+        out_specs=ANY,
+        scratch_shapes=[dma(2), dma(2 * C), dma(2 * C)],
+        compiler_params=params(9),
+        cost_estimate=cost(30),
+    )(stage)
+
+
 def project(C, F, x, w):
     own = to_layer(C, F, x)
     rows = token_rows(own)
     return own, rows, dot(rows, w, 1, 0)
 
 
-def attn_out_and_up(C, F, mixed, wo, x, gain, wg, wu):
+def attn_out_and_up(C, F, mixed, wo, x, gain, w):
     if kernels_fit(C, F):
         hidden_in, out, inp = out_call(F, mixed, wo, x, gain)
-        return (hidden_in, out, *up_call(F, inp, wg, wu))
+        return (hidden_in, out, *up_call(F, inp, w))
     out = token_sums(dot(mixed, wo, 1, 1))
     hidden_in = x.astype(f32) + out * rms(out) * gain
     rows = token_rows(hidden_in.astype(bf16))
-    g, u = dot(rows, wg, 1, 0), dot(rows, wu, 1, 0)
+    g, u = jnp.split(dot(rows, w, 1, 0), 2, axis=1)
     sig = jax.nn.sigmoid(g)
     der = u * (sig * (1.0 + g * (1.0 - sig)))
     act = g * sig
@@ -1452,10 +1480,10 @@
     )
 
 
-def back_to_attn(C, F, grad, wg, wu, cot, out, gain, wo):
+def back_to_attn(C, F, grad, w, cot, out, gain, wo):
     if kernels_fit(C, F):
-        return mid_call(F, grad, wg, wu, cot, out, gain, wo)
-    resid = cot.astype(f32) + token_sums(dot(grad, jnp.concatenate([wg, wu], axis=1), 1, 1))
+        return mid_call(F, grad, w, cot, out, gain, wo)
+    resid = cot.astype(f32) + token_sums(dot(grad, w, 1, 1))
     scale = rms(out)
     hat = out * scale
     rows = token_rows(back(resid * gain, hat, scale).astype(bf16))
@@ -1538,8 +1566,7 @@
     w_heads = rows_gather(jnp.concatenate([w_attn[i] for i in range(UNITS_ATTN)], axis=1))
     w_qkv, w_out = (w_heads, w_heads) if kernels else (w_heads[:, : 3 * head_cols], w_heads[:, 3 * head_cols :])
     ffn_flat = w_ffn.reshape(3, dz, hidden_cols)
-    w_gate = rows_gather(ffn_flat[0])
-    w_up = rows_gather(ffn_flat[1])
+    w_gate_up = rows_gather(jnp.concatenate([ffn_flat[0], ffn_flat[1]], axis=1))
     w_down = rows_gather(ffn_flat[2])
 
     gain_query = lax.dynamic_slice_in_dim(gains[0], f * head_cols, head_cols)
@@ -1592,7 +1619,7 @@
         attn_mixed, log_total = attend(query_rows, key_rows, value_rows, pos)
         attn_mixed = unheads(attn_mixed)
     hidden_in, attn_out, mlp_all, act, der, hidden = attn_out_and_up(
-        C, F, attn_mixed, w_out, own_input, gains[2:3], w_gate, w_up
+        C, F, attn_mixed, w_out, own_input, gains[2:3], w_gate_up
     )
     by_layer = None
     if kernels:
@@ -1612,7 +1639,7 @@
         grad_ffn_in, p_gate_up = lax.optimization_barrier((grad_ffn_in, p_gate_up))
     g_gate_up = scatter(p_gate_up)
     grad_resid, attn_gain, grad_attn_all, grad_mixed = back_to_attn(
-        C, F, grad_ffn_in, w_gate, w_up, own_grad, attn_out, gains[2:3], w_out
+        C, F, grad_ffn_in, w_gate_up, own_grad, attn_out, gains[2:3], w_out
     )
     if kernels:
         grad_mixed = after(grad_mixed, g_down)
@@ -1678,15 +1705,21 @@
         gain_total = jnp.sum(lax.all_gather(gain_local, BOTH, axis=0, tiled=False), axis=0)
 
     if kernels:
-        got = jnp.stack([g_attn[0], g_gate_up[0], g_gate_up[1], g_down[0]])
-        mom = mom_own.reshape(got.shape).astype(f32)
-        owned = (momentum * mom + got.astype(f32)).astype(bf16)
+        early = jnp.stack([jnp.zeros_like(g_down[0]), g_gate_up[0], g_gate_up[1], g_down[0]])
+        mom = momentum * mom_own.reshape(early.shape).astype(f32)
+        owned = (mom + early.astype(f32)).astype(bf16)
+        mom_first = mom[0]
+        early, owned, mom_first, grad_rows = lax.optimization_barrier((early, owned, mom_first, grad_rows))
+        late = (mom_first + g_attn[0].astype(f32)).astype(bf16)
+        owned = lax.dynamic_update_slice(owned, late[None], (0, 0, 0))
+        got = lax.dynamic_update_slice(early, g_attn, (0, 0, 0))
         sent_back = got.reshape(UNITS_ATTN, C, dz, head_cols)
         sent_back = lax.all_to_all(sent_back, "ctx", split_axis=1, concat_axis=0, tiled=False)
         sent_back = sent_back.reshape(C, UNITS_ATTN, dz, head_cols).astype(f32)
         grad_attn = sent_back[:, 0]
         grad_ffn = jnp.transpose(sent_back[:, 1:], (1, 2, 0, 3))
-        own, back_rows, gain_total = newton_call(C, owned, jnp.stack([result, grad_rows]), gain_layer)
+        own, leaving, gain_total = newton_call(C, owned, jnp.stack([result, grad_rows]), gain_layer)
+        back_rows = leave_call(C, leaving)
         result, grad_input, gain_total = back_rows[0], back_rows[1], gain_total[:4]
     else:
         grad_attn = g_attn[:, 0].astype(f32)

time: 1120 us -> 1110 us (level)
  waiting for transfers between devices: 251 us -> 197 us
  Pallas kernels: 746 us -> 778 us
    pallas_call x0 -> x1, Pallas kernels: none -> 67.2 us  [leave_call(): pl.pallas_call(functools.partial(leave_kernel, C), out_shape=jax.ShapeDty...]
    all_to_all x1, waiting for transfers between devices: 66.9 us -> 0.01 us  [shards(): steps = lax.all_to_all(home, BOTH, split_axis=0, concat_axis=0, tiled=True)]
    reduce_scatter x3, waiting for transfers between devices: 82 us -> 107 us  [scatter(): return lax.psum_scatter(grad, 'ctx', scatter_dimension=0, tiled=True)[0]]
    pallas_call x1, Pallas kernels: 129 us -> 108 us  [down_call(): pl.pallas_call(functools.partial(down_kernel, C), out_shape=[one, jax.Sha...]
    pallas_call x1, Pallas kernels: 173 us -> 158 us  [newton_call(): pl.pallas_call(functools.partial(newton_kernel, C), out_shape=[jax.ShapeD...]
    all_gather x4 -> x3, waiting for transfers between devices: 102 us -> 90.2 us  [rows_gather(): return lax.all_gather(shard, 'ctx', axis=0, tiled=True)]
    unnamed x32 -> x34, local copies, waits for them, and re-layouts: 31.4 us -> 32.4 us
  transfers between devices with their start and end apart: 9 -> 8, of which waited for: 5 -> 5; matrix products, arithmetic and copies ran while one was open for 7% -> 7% of each run, Pallas kernels for 55% -> 61%
where the time goes in v5:
time: 1110 us; the launch traced here: 1100 us
  Pallas kernels  778 us (70%)
  waiting for transfers between devices  197 us (18%)
  local copies, waits for them, and re-layouts  57.6 us (5%)
  other arithmetic  44.2 us (4%)
  between operations  14.7 us (1%)
    pallas_call x1, Pallas kernels, newton_call(): pl.pallas_call(functools.partial(newton_kernel, C), out_shape=[jax.ShapeD...  158 us
    pallas_call x1, Pallas kernels, down_call(): pl.pallas_call(functools.partial(down_kernel, C), out_shape=[one, jax.Sha...  108 us
    reduce_scatter x3, waiting for transfers between devices, scatter(): return lax.psum_scatter(grad, 'ctx', scatter_dimension=0, tiled=True)[0]  107 us
    pallas_call x1, Pallas kernels, mid_call(): pl.pallas_call(mid_kernel, out_shape=[jax.ShapeDtypeStruct((R, D), f32),...  96.6 us
    all_gather x3, waiting for transfers between devices, rows_gather(): return lax.all_gather(shard, 'ctx', axis=0, tiled=True)  90.2 us
    pallas_call x1, Pallas kernels, enter_call(): pl.pallas_call(functools.partial(enter_kernel, C), out_shape=[jax.ShapeDt...  89.8 us
    pallas_call x1, Pallas kernels, leave_call(): pl.pallas_call(functools.partial(leave_kernel, C), out_shape=jax.ShapeDty...  67.2 us
    pallas_call x1, Pallas kernels, last_call(): pl.pallas_call(functools.partial(last_kernel, D), out_shape=[jax.ShapeDty...  61.7 us
  transfers between devices with their start and end apart: 8, of which 5 were waited for; matrix products, arithmetic and copies ran while one was open for 7% of the time, Pallas kernels for 61%

profile of v5, /device:TPU:0, one launch (start us, length us, event | category | flops | bytes accessed | tf_op | source)
XLA Modules:
  0.0 1101.8 jit_solution(1854278554468046879)
XLA Ops:
  17.6 89.8 %shard_map.176 = (bf16[256,2048]{1,0:T(8,128)(2,1)}, bf16[8,256,2048]{2,1,0:T(8,128)(2,1)}) custom-call(bf16[256,2048]{1,0:T(8,128)(2,1)} %bitcast.118), custom_call_target="tpu_custom_call" | custom-call | flops 70000001024 | bytes 1048576 | tf_op jit(solution)/shard_map/pallas_call | solution.py:418
  113.3 4.9 sine_multiply_fusion
  121.1 23.0 %shard_map.177 = (f32[2048,768]{1,0:T(8,128)}, f32[8,8,2048]{2,1,0:T(8,128)}) custom-call(bf16[8,256,2048]{2,1,0:T(8,128)(2,1)} %get-tuple-element.54.all_ref, bf16[2048,1024]{1,0:T(8,128)(2,1)} %all-gather.4.cloned.1.call-done.w_ref.wo_ref), custom_call_target="tpu_custom_call" | custom-call | flops 22000001024 | bytes 1048576 | tf_op jit(solution)/shard_map/pallas_call | solution.py:481
  145.5 17.7 %shard_map.178 = (bf16[4,2,256,256]{3,2,1,0:T(8,128)(2,1)}, bf16[4,2,256,256]{3,2,1,0:T(8,128)(2,1)}, bf16[4,2,256,256]{3,2,1,0:T(8,128)(2,1)}, f32[2,2,1024,128]{3,2,1,0:T(8,128)}) custom-call(f32[4,2,256,768]{3,2,1,0:T(8,128)} %bitcast.123, f32[4,2,256,768]{3,2,1,0:T(8,128)} %bitcast.124, f32[4,2,256,768]{3,2,1,0:T(8,128)} %bitcast.125, ...), custom_call_target="tpu_custom_call" | custom-call | flops 15000000512 | bytes 1048576 | tf_op jit(solution)/shard_map/pallas_call | solution.py:1117
  163.2 46.9 %shard_map.179 = (f32[256,2048]{1,0:T(8,128)}, f32[256,2048]{1,0:T(8,128)}, bf16[256,2048]{1,0:T(8,128)(2,1)}) custom-call(bf16[2048,256]{1,0:T(8,128)(2,1)} %bitcast.131, bf16[2048,1024]{1,0:T(8,128)(2,1)} %all-gather.4.cloned.1.call-done.w_ref.wo_ref, bf16[256,2048]{1,0:T(8,128)(2,1)} %get-tuple-element.58.x_ref, f32[1,2048]{1,0:T(1,128)} %get-tuple-element.142.gain_ref), custom_call_target="tpu_custom_call" | custom-call | flops 46000001024 | bytes 1048576 | tf_op jit(solution)/shard_map/pallas_call | solution.py:536
  210.1 56.0 %all-gather.6.cloned.1.call-done.w_ref = bf16[2048,2048]{1,0:T(8,128)(2,1)} async-done(((bf16[512,2048]{1,0:T(8,128)(2,1)}), bf16[2048,2048]{1,0:T(8,128)(2,1)}) %all-gather.6.cloned.1.call-update) | async-done | bytes 8388624 | tf_op jit(solution)/shard_map/all_gather | solution.py:1551
  266.1 47.0 %shard_map.180 = (bf16[8,256,2048]{2,1,0:T(8,128)(2,1)}, bf16[2048,1024]{1,0:T(8,128)(2,1)}, bf16[2048,1024]{1,0:T(8,128)(2,1)}, bf16[2048,1024]{1,0:T(8,128)(2,1)}) custom-call(bf16[256,2048]{1,0:T(8,128)(2,1)} %get-tuple-element.59.in_ref, bf16[2048,2048]{1,0:T(8,128)(2,1)} %all-gather.6.cloned.1.call-done.w_ref), custom_call_target="tpu_custom_call" | custom-call | flops 46000001024 | bytes 1048576 | tf_op jit(solution)/shard_map/pallas_call | solution.py:615
  313.1 34.2 %all-gather.8.cloned.1.call-done.wd_ref = bf16[2048,1024]{1,0:T(8,128)(2,1)} async-done(((bf16[512,1024]{1,0:T(8,128)(2,1)}), bf16[2048,1024]{1,0:T(8,128)(2,1)}) %all-gather.8.cloned.1.call-update) | async-done | bytes 4194320 | tf_op jit(solution)/shard_map/all_gather | solution.py:1551
  347.3 107.7 %shard_map.181 = (bf16[256,2048]{1,0:T(8,128)(2,1)}, f32[1,2048]{1,0:T(1,128)}, bf16[8,256,2048]{2,1,0:T(8,128)(2,1)}, bf16[2048,2048]{1,0:T(8,128)(2,1)}, bf16[...) custom-call(bf16[2048,1024]{1,0:T(8,128)(2,1)} %get-tuple-element.60.h_ref, ...), custom_call_target="tpu_custom_call" | custom-call | flops 115000000512 | bytes 1048576 | tf_op jit(solution)/shard_map/pallas_call | solution.py:766
  455.1 23.8 %shard_map.182 = bf16[4,2,2048,256]{3,2,1,0:T(8,128)(2,1)} custom-call(bf16[2048,2048]{1,0:T(8,128)(2,1)} %bitcast.122, bf16[2048,2048]{1,0:T(8,128)(2,1)} %get-tuple-element.71.refs_1_.grad_ref), custom_call_target="tpu_custom_call" | custom-call | flops 24000000000 | bytes 1048576 | tf_op jit(solution)/shard_map/pallas_call | solution.py:1013
  478.9 96.6 %shard_map.183 = (f32[256,2048]{1,0:T(8,128)}, f32[1,2048]{1,0:T(1,128)}, bf16[8,256,2048]{2,1,0:T(8,128)(2,1)}, bf16[2048,256]{1,0:T(8,128)(2,1)}) custom-call(bf16[2048,2048]{1,0:T(8,128)(2,1)} %get-tuple-element.71.refs_1_.grad_ref, bf16[2048,2048]{1,0:T(8,128)(2,1)} %all-gather.6.cloned.1.call-done.w_ref, bf16[256,2048]{1,0:T(8,128)(2,1)} %get-tuple-element.72.cot_ref, ...), custom_call_target="tpu_custom_call" | custom-call | flops 92000002048 | bytes 1048576 | tf_op jit(solution)/shard_map/pallas_call | solution.py:865
  576.4 25.1 %shard_map.184 = (f32[4,2,256,256]{3,2,1,0:T(8,128)}, f32[4,2,256,256]{3,2,1,0:T(8,128)}, bf16[4,2,256,256]{3,2,1,0:T(8,128)(2,1)}, f32[2,2,8,1024]{3,2,1,0:T(8,128)}, f32[2,2,8,128]{3,2,1,0:T(8,128)}) custom-call(f32[4,2,256,768]{3,2,1,0:T(8,128)} %bitcast.126, f32[4,2,256,768]{3,2,1,0:T(8,128)} %bitcast.127, f32[4,2,256,768]{3,2,1,0:T(8,128)} %bitcast.128, ...), custom_call_target="tpu_custom_call" | custom-call | flops 35000000512 | bytes 1048576 | tf_op jit(solution)/shard_map/pallas_call | solution.py:1182
  604.6 61.7 %shard_map.185 = (bf16[256,2048]{1,0:T(8,128)(2,1)}, bf16[2048,768]{1,0:T(8,128)(2,1)}, f32[8,2048]{1,0:T(8,128)}) custom-call(f32[2048,256]{1,0:T(8,128)} %bitcast.129, f32[2048,256]{1,0:T(8,128)} %bitcast.130, bf16[2048,256]{1,0:T(8,128)(2,1)} %bitcast.133, f32[2048,768]{1,0:T(8,128)} %get-tuple-element.55.proj_ref, ...), custom_call_target="tpu_custom_call" | custom-call | flops 54999998464 | bytes 1048576 | tf_op jit(solution)/shard_map/pallas_call | solution.py:959
  666.3 14.3 %shard_map.186 = bf16[4,1,2048,256]{3,2,1,0:T(8,128)(2,1)} custom-call(bf16[2048,2048]{1,0:T(8,128)(2,1)} %bitcast.120, bf16[2048,768]{1,0:T(8,128)(2,1)} %get-tuple-element.88.refs_1_, bf16[2048,2048]{1,0:T(8,128)(2,1)} %bitcast.121, bf16[2048,256]{1,0:T(8,128)(2,1)} %bitcast.132), custom_call_target="tpu_custom_call" | custom-call | flops 12000000000 | bytes 1048576 | tf_op jit(solution)/shard_map/pallas_call | solution.py:1013
  689.6 34.1 %reduce-scatter.4.cloned.1.call-done = bf16[1,2,2048,256]{3,2,1,0:T(8,128)(2,1)} async-done(((bf16[4,2,2048,256]{3,2,1,0:T(8,128)(2,1)}), bf16[1,2,2048,256]{3,2,1,0:T(8,128)(2,1)}) %reduce-scatter.4.cloned.1.call-update) | async-done | bytes 2097168 | tf_op jit(solution)/shard_map/reduce_scatter | solution.py:1562
  732.3 71.7 %reduce-scatter.8.cloned.1.call-done = bf16[1,1,2048,256]{3,2,1,0:T(8,128)(2,1)} async-done(((bf16[4,1,2048,256]{3,2,1,0:T(8,128)(2,1)}), bf16[1,1,2048,256]{3,2,1,0:T(8,128)(2,1)}) %reduce-scatter.8.cloned.1.call-update) | async-done | bytes 1048592 | tf_op jit(solution)/shard_map/reduce_scatter | solution.py:1562
  806.9 4.6 copy.37
  811.5 5.2 all-to-all-start
  818.2 157.6 %shard_map.187 = (bf16[1024,2048]{1,0:T(8,128)(2,1)}, bf16[2,4,64,2048]{3,2,1,0:T(8,128)(2,1)}, f32[8,2048]{1,0:T(8,128)}) custom-call(bf16[4,2048,256]{2,1,0:T(8,128)(2,1)} %get-tuple-element.132.m_ref, bf16[2,256,2048]{2,1,0:T(8,128)(2,1)} %pad_maximum_fusion.3.rows_ref, f32[8,2048]{1,0:T(8,128)} %get-tuple-element.92.gain_ref), custom_call_target="tpu_custom_call" | custom-call | flops 95000002560 | bytes 1048576 | tf_op jit(solution)/shard_map/pallas_call | solution.py:1374
  987.6 67.2 %shard_map.188 = bf16[2,256,2048]{2,1,0:T(8,128)(2,1)} custom-call(bf16[2,4,64,2048]{3,2,1,0:T(8,128)(2,1)} %get-tuple-element.93.stage_ref), custom_call_target="tpu_custom_call" | custom-call | flops 30000001024 | bytes 1048576 | tf_op jit(solution)/shard_map/pallas_call | solution.py:1431
  1061.8 6.7 copy.41
  1068.6 4.4 fusion.1
  1073.0 6.7 copy.42
  1087.9 6.7 copy.43
  (94 shorter events, 73.3 us)
Async XLA Ops:
  7.2 114.0 %all-gather.4.cloned.1.call-start = ((), (), s32[]{:S(2)}) async-start(), calls=%async_computation.5 | async-start | bytes 5242880 | tf_op jit(solution)/shard_map/all_gather | solution.py:1551
  9.6 256.5 %all-gather.6.cloned.1.call-start = ((), (), s32[]{:S(2)}) async-start(), calls=%async_computation.6 | async-start | bytes 10485760 | tf_op jit(solution)/shard_map/all_gather | solution.py:1551
  14.6 332.7 %all-gather.8.cloned.1.call-start = ((), (), s32[]{:S(2)}) async-start(), calls=%async_computation.7 | async-start | bytes 5242880 | tf_op jit(solution)/shard_map/all_gather | solution.py:1551
  15.9 560.5 %reduce-scatter.6.cloned.1.call-start = ((), (), s32[]{:S(2)}) async-start(), calls=%async_computation.9 | async-start | bytes 5242880 | tf_op jit(solution)/shard_map/reduce_scatter | solution.py:1562
  17.6 89.8 %copy-start.9 = (f32[4,2048]{1,0:T(4,128)S(1)}, f32[4,2048]{1,0:T(4,128)}, u32[]{:S(2)}) copy-start(f32[4,2048]{1,0:T(4,128)} %param.14) | copy-start | bytes 98308
  108.1 3.9 copy-start.2
  113.0 5.2 copy-start.5
  455.0 268.7 %reduce-scatter.4.cloned.1.call-start = ((), (), s32[]{:S(2)}) async-start(), calls=%async_computation.8 | async-start | bytes 10485760 | tf_op jit(solution)/shard_map/reduce_scatter | solution.py:1562
  478.9 325.2 %reduce-scatter.8.cloned.1.call-start = ((), (), s32[]{:S(2)}) async-start(), calls=%async_computation.10 | async-start | bytes 5242880 | tf_op jit(solution)/shard_map/reduce_scatter | solution.py:1562
  576.4 27.5 %copy-start.11 = (f32[1,2048]{1,0:T(1,128)S(1)}, f32[1,2048]{1,0:T(1,128)}, u32[]{:S(2)}) copy-start(f32[1,2048]{1,0:T(1,128)} %get-tuple-element.84) | copy-start | bytes 24580
  576.4 27.5 %copy-start.12 = (f32[1,2048]{1,0:T(1,128)S(1)}, f32[1,2048]{1,0:T(1,128)}, u32[]{:S(2)}) copy-start(f32[1,2048]{1,0:T(1,128)} %get-tuple-element.83) | copy-start | bytes 24580
  683.8 5.8 copy-start
  689.6 35.9 %copy-start.4 = (bf16[1,1,2048,256]{3,2,1,0:T(8,128)(2,1)S(1)}, bf16[1,1,2048,256]{3,2,1,0:T(8,128)(2,1)}, u32[]{:S(2)}) copy-start(bf16[1,1,2048,256]{3,2,1,0:T(8,128)(2,1)} %reduce-scatter.6.cloned.1.call-done) | copy-start | bytes 3145732
  723.7 5.5 copy-start.1
  729.3 74.8 %slice-start = ((f32[4,4,512,256]{3,2,0,1:T(8,128)}), f32[1,4,512,256]{3,2,0,1:T(8,128)S(1)}, s32[]{:S(2)}) async-start(f32[4,4,512,256]{3,2,0,1:T(8,128)} %copy-done), calls=%async_computation.11 | async-start | bytes 4194304 | tf_op jit(solution)/shard_map/slice | solution.py:1711
  811.5 5.2 copy-start.6
  811.5 5.2 copy-start.7
  811.5 171.1 %all-to-all-start = ((bf16[1,4,4,512,256]{4,3,1,0,2:T(8,128)(2,1)}), bf16[1,4,4,512,256]{4,3,1,0,2:T(8,128)(2,1)}, u32[]{:S(2)}, u32[]{:S(2)}) async-start(bf16[1,4,4,512,256]{4,3,1,0,2:T(8,128)(2,1)} %copy.37), calls=%async_computation.3 | async-start | bytes 8388608 | tf_op jit(solution)/shard_map/all_to_all | solution.py:1717
  982.6 4.4 copy-start.8
  982.6 4.4 copy-start.10
  982.6 99.7 %all-to-all-start.1 = ((bf16[32,256,256]{2,1,0:T(8,128)(2,1)}), bf16[32,256,256]{2,1,0:T(8,128)(2,1)}, u32[]{:S(2)}, u32[]{:S(2)}) async-start(bf16[32,256,256]{2,1,0:T(8,128)(2,1)} %bitcast.99), calls=%async_computation.4 | async-start | bytes 8388608 | tf_op jit(solution)/shard_map/all_to_all | solution.py:1768
  1073.0 6.8 copy-start.3
Sparse Core Ops, SparseCore 0:
  10.2 105.5 all-gather.3
  117.9 148.1 all-gather.5
  268.3 78.9 all-gather.7
  455.2 121.1 reduce-scatter.5
  578.7 144.9 reduce-scatter.3
  726.6 77.4 reduce-scatter.7

commit v6 on v5

--- a/solution.py
+++ b/solution.py
@@ -120,6 +120,17 @@
         for to in (self.fc, self.fx, self.fy):
             pl.semaphore_signal(barrier, inc=1, device_id={"fsdp": to}, device_id_type=MESH)
         pl.semaphore_wait(barrier, 3)
+
+
+def partner(i, k):
+    if k == 3:
+        return 3 - i
+    if k == 2:
+        return (i + 2) % 4
+    return i + 1 - 2 * (i % 2)
+
+
+FAR_FIRST = (3, 2, 1)
 
 
 def remote(src, dst, send, recv, i, to, axis="fsdp"):
@@ -354,8 +365,8 @@
 
     def first(self):
         at, C, piece = self.at, self.C, self.piece
-        for k in range(1, C):
-            j = (at.chip + k) % C
+        for k in FAR_FIRST:
+            j = partner(at.chip, k)
             src = self.mine.at[pl.ds(j * piece, piece)]
             c = remote(src, self.stage.at[at.chip], self.send, self.recv, k, 2 * j + at.c)
             c.start()
@@ -369,11 +380,11 @@
     def second(self):
         at, C, z = self.at, self.C, self.z
         self.keep.wait()
-        for k in range(1, C):
-            frm = (at.chip - k + C) % C
+        for k in FAR_FIRST:
+            frm = partner(at.chip, k)
             remote(self.stage.at[frm], self.stage.at[frm], self.send, self.recv, k, 2 * frm + at.c).wait_recv()
-        for k in range(1, C):
-            to = (z + k) % C
+        for k in FAR_FIRST:
+            to = partner(z, k)
             c = remote(self.stage.at[to], self.land(z), self.send, self.recv, C + k, to, "ctx")
             c.start()
             self.sent.append(c)
@@ -382,8 +393,8 @@
     def finish(self):
         C, z = self.C, self.z
         self.keep.wait()
-        for k in range(1, C):
-            frm = (z - k + C) % C
+        for k in FAR_FIRST:
+            frm = partner(z, k)
             remote(self.land(frm), self.land(frm), self.send, self.recv, C + k, frm, "ctx").wait_recv()
         for c in self.sent:
             c.wait_send()
@@ -654,12 +665,12 @@
     units = []
 
     def send_units(k):
-        to = (z + k) % C
+        to = partner(z, k)
         c = remote(unit_ref.at[to], mom_ref.at[z], usend, urecv, k, to, "ctx")
         c.start()
         units.append(c)
 
-    send_units(1)
+    send_units(FAR_FIRST[0])
     loads[0].wait()
     moving.first()
     loads[1].wait()
@@ -670,7 +681,7 @@
 
     def between():
         moving.second()
-        for k in range(2, C):
+        for k in FAR_FIRST[1:]:
             send_units(k)
         units.append(local(unit_ref.at[z], mom_ref.at[z], lsem, 10))
 
@@ -746,8 +757,8 @@
     for step in puts[-2:]:
         for c in step:
             c.wait()
-    for k in range(1, C):
-        frm = (z - k + C) % C
+    for k in FAR_FIRST:
+        frm = partner(z, k)
         remote(mom_ref.at[frm], mom_ref.at[frm], usend, urecv, k, frm, "ctx").wait_recv()
     for c in units[:-1]:
         c.wait_send()
@@ -1235,8 +1246,8 @@
 
     sent, keep = [], []
     for a in range(2):
-        for k in range(1, C):
-            to = (z + k) % C
+        for k in FAR_FIRST:
+            to = partner(z, k)
             c = remote(rows_ref.at[a, part(to)], stage_ref.at[a, z], tsend, trecv, C * a + k, to, "ctx")
             c.start()
             sent.append(c)
@@ -1250,9 +1261,9 @@
     def rows_arrived():
         for a in range(2):
             keep[a].wait()
-            for k in range(1, C):
-                dst = stage_ref.at[a, (z - k + C) % C]
-                remote(dst, dst, tsend, trecv, C * a + k, (z - k + C) % C, "ctx").wait_recv()
+            for k in FAR_FIRST:
+                dst = stage_ref.at[a, partner(z, k)]
+                remote(dst, dst, tsend, trecv, C * a + k, partner(z, k), "ctx").wait_recv()
         for k in range(1, C):
             frm = (z - k + C) % C
             remote(gains.at[frm], gains.at[frm], gsend, grecv, k, frm, "ctx").wait_recv()
@@ -1396,49 +1407,6 @@
     )(x, rows, gains)
 
 
-def leave_kernel(C, stage_ref, home_ref, lsem, send, recv):
-    at = Plane()
-    piece = stage_ref.shape[2]
-    barrier = pltpu.get_barrier_semaphore()
-    for k in range(1, C):
-        pl.semaphore_signal(
-            barrier, inc=1, device_id={"fsdp": 2 * ((at.chip + k) % C) + at.c}, device_id_type=MESH
-        )
-    pl.semaphore_wait(barrier, C - 1)
-
-    def part(j):
-        return pl.ds(j * piece, piece)
-
-    sent, keep = [], []
-    for a in range(2):
-        for k in range(1, C):
-            to = (at.chip + k) % C
-            c = remote(stage_ref.at[a, to], home_ref.at[a, part(at.chip)], send, recv, C * a + k, 2 * to + at.c)
-            c.start()
-            sent.append(c)
-        keep.append(local(stage_ref.at[a, at.chip], home_ref.at[a, part(at.chip)], lsem, a))
-    for a in range(2):
-        keep[a].wait()
-        for k in range(1, C):
-            frm = (at.chip - k + C) % C
-            dst = home_ref.at[a, part(frm)]
-            remote(dst, dst, send, recv, C * a + k, 2 * frm + at.c).wait_recv()
-    for c in sent:
-        c.wait_send()
-
-
-def leave_call(C, stage):
-    return pl.pallas_call(
-        functools.partial(leave_kernel, C),
-        out_shape=jax.ShapeDtypeStruct((2, C * stage.shape[2], stage.shape[3]), bf16),
-        in_specs=[ANY],
-        out_specs=ANY,
-        scratch_shapes=[dma(2), dma(2 * C), dma(2 * C)],
-        compiler_params=params(9),
-        cost_estimate=cost(30),
-    )(stage)
-
-
 def project(C, F, x, w):
     own = to_layer(C, F, x)
     rows = token_rows(own)
@@ -1513,6 +1481,23 @@
     return jnp.concatenate(got, axis=0)
 
 
+def go_home(C, F, stage):
+    chip = lax.axis_index("fsdp") // 2
+    got = [lax.dynamic_index_in_dim(stage, chip, 1, keepdims=False)]
+    for k in range(1, C):
+        pairs = [(f, 2 * ((f // 2 + k) % C) + f % 2) for f in range(F)]
+        block = lax.dynamic_index_in_dim(stage, (chip + k) % C, 1, keepdims=False)
+        got.append(lax.ppermute(block, "fsdp", pairs))
+    return got
+
+
+def at_home(C, got):
+    chip = lax.axis_index("fsdp") // 2
+    got = jnp.stack(got)
+    got = [lax.dynamic_index_in_dim(got, (chip - j + C) % C, 0, keepdims=False) for j in range(C)]
+    return jnp.concatenate(got, axis=1)
+
+
 def from_layer(C, F, x):
     z, chip = lax.axis_index("ctx"), lax.axis_index("fsdp") // 2
     x = x.reshape(C, x.shape[0] // C, x.shape[1])
@@ -1709,18 +1694,17 @@
         mom = momentum * mom_own.reshape(early.shape).astype(f32)
         owned = (mom + early.astype(f32)).astype(bf16)
         mom_first = mom[0]
+        early = jnp.swapaxes(early.reshape(UNITS_ATTN, C, dz, head_cols), 0, 1)
         early, owned, mom_first, grad_rows = lax.optimization_barrier((early, owned, mom_first, grad_rows))
         late = (mom_first + g_attn[0].astype(f32)).astype(bf16)
         owned = lax.dynamic_update_slice(owned, late[None], (0, 0, 0))
-        got = lax.dynamic_update_slice(early, g_attn, (0, 0, 0))
-        sent_back = got.reshape(UNITS_ATTN, C, dz, head_cols)
-        sent_back = lax.all_to_all(sent_back, "ctx", split_axis=1, concat_axis=0, tiled=False)
-        sent_back = sent_back.reshape(C, UNITS_ATTN, dz, head_cols).astype(f32)
+        got = lax.dynamic_update_slice(early, g_attn.reshape(C, 1, dz, head_cols), (0, 0, 0, 0))
+        sent_back = lax.all_to_all(got, "ctx", split_axis=0, concat_axis=0, tiled=True).astype(f32)
         grad_attn = sent_back[:, 0]
         grad_ffn = jnp.transpose(sent_back[:, 1:], (1, 2, 0, 3))
         own, leaving, gain_total = newton_call(C, owned, jnp.stack([result, grad_rows]), gain_layer)
-        back_rows = leave_call(C, leaving)
-        result, grad_input, gain_total = back_rows[0], back_rows[1], gain_total[:4]
+        homing = go_home(C, F, leaving)
+        gain_total = gain_total[:4]
     else:
         grad_attn = g_attn[:, 0].astype(f32)
         grad_ffn = jnp.transpose(
@@ -1728,6 +1712,12 @@
         )
     new_attn = momentum * mom_attn + grad_attn
     new_ffn = momentum * mom_ffn + grad_ffn
+    if kernels:
+        homing, new_attn, new_ffn, grad_attn, grad_ffn = lax.optimization_barrier(
+            (homing, new_attn, new_ffn, grad_attn, grad_ffn)
+        )
+        back_rows = at_home(C, homing)
+        result, grad_input = back_rows[0], back_rows[1]
     if not kernels:
         send = jnp.concatenate(
             [

time: 1110 us -> 1100 us (level)
    pallas_call x1 -> x0, Pallas kernels: 67.2 us -> none  [leave_call(): pl.pallas_call(functools.partial(leave_kernel, C), out_shape=jax.ShapeDty...]
    ppermute x0 -> x3, waiting for transfers between devices: none -> 49.6 us  [go_home(): got.append(lax.ppermute(block, 'fsdp', pairs))]
    reduce_scatter x3, waiting for transfers between devices: 107 us -> 62 us  [scatter(): return lax.psum_scatter(grad, 'ctx', scatter_dimension=0, tiled=True)[0]]
    pallas_call x1, Pallas kernels: 108 us -> 152 us  [down_call(): pl.pallas_call(functools.partial(down_kernel, C), out_shape=[one, jax.Sha...]
    pallas_call x1, Pallas kernels: 89.8 us -> 109 us  [enter_call(): pl.pallas_call(functools.partial(enter_kernel, C), out_shape=[jax.ShapeDt...]
    all_gather x3, waiting for transfers between devices: 90.2 us -> 70.9 us  [rows_gather(): return lax.all_gather(shard, 'ctx', axis=0, tiled=True)]
    unnamed x34 -> x46, local copies, waits for them, and re-layouts: 32.4 us -> 34.2 us
  transfers between devices with their start and end apart: 8 -> 11, of which waited for: 5 -> 7; matrix products, arithmetic and copies ran while one was open for 7% -> 7% of each run, Pallas kernels for 61% -> 57%
where the time goes in v6:
time: 1100 us
  Pallas kernels  773 us (70%)
  waiting for transfers between devices  193 us (18%)
  local copies, waits for them, and re-layouts  61.3 us (6%)
  other arithmetic  40.9 us (4%)
  between operations  14.9 us (1%)
  starting transfers between devices  14.5 us (1%)
    pallas_call x1, Pallas kernels, newton_call(): pl.pallas_call(functools.partial(newton_kernel, C), out_shape=[jax.ShapeD...  158 us
    pallas_call x1, Pallas kernels, down_call(): pl.pallas_call(functools.partial(down_kernel, C), out_shape=[one, jax.Sha...  152 us
    pallas_call x1, Pallas kernels, enter_call(): pl.pallas_call(functools.partial(enter_kernel, C), out_shape=[jax.ShapeDt...  109 us
    pallas_call x1, Pallas kernels, mid_call(): pl.pallas_call(mid_kernel, out_shape=[jax.ShapeDtypeStruct((R, D), f32),...  96.5 us
    all_gather x3, waiting for transfers between devices, rows_gather(): return lax.all_gather(shard, 'ctx', axis=0, tiled=True)  70.9 us
    reduce_scatter x3, waiting for transfers between devices, scatter(): return lax.psum_scatter(grad, 'ctx', scatter_dimension=0, tiled=True)[0]  62 us
    pallas_call x1, Pallas kernels, last_call(): pl.pallas_call(functools.partial(last_kernel, D), out_shape=[jax.ShapeDty...  60.9 us
    ppermute x3, waiting for transfers between devices, go_home(): got.append(lax.ppermute(block, 'fsdp', pairs))  49.6 us
  transfers between devices with their start and end apart: 11, of which 7 were waited for; matrix products, arithmetic and copies ran while one was open for 7% of the time, Pallas kernels for 57%

profile of v6, /device:TPU:0, one launch (start us, length us, event | category | flops | bytes accessed | tf_op | source)
XLA Modules:
  0.0 1098.4 jit_solution(11258492390729305060)
XLA Ops:
  18.2 109.4 %shard_map.176 = (bf16[256,2048]{1,0:T(8,128)(2,1)}, bf16[8,256,2048]{2,1,0:T(8,128)(2,1)}) custom-call(bf16[256,2048]{1,0:T(8,128)(2,1)} %bitcast.154), custom_call_target="tpu_custom_call" | custom-call | flops 70000001024 | bytes 1048576 | tf_op jit(solution)/shard_map/pallas_call | solution.py:429
  133.4 4.9 sine_multiply_fusion
  141.2 22.7 %shard_map.177 = (f32[2048,768]{1,0:T(8,128)}, f32[8,8,2048]{2,1,0:T(8,128)}) custom-call(bf16[8,256,2048]{2,1,0:T(8,128)(2,1)} %get-tuple-element.62.all_ref, bf16[2048,1024]{1,0:T(8,128)(2,1)} %all-gather.4.cloned.1.call-done.w_ref.wo_ref), custom_call_target="tpu_custom_call" | custom-call | flops 22000001024 | bytes 1048576 | tf_op jit(solution)/shard_map/pallas_call | solution.py:492
  165.2 17.7 %shard_map.178 = (bf16[4,2,256,256]{3,2,1,0:T(8,128)(2,1)}, bf16[4,2,256,256]{3,2,1,0:T(8,128)(2,1)}, bf16[4,2,256,256]{3,2,1,0:T(8,128)(2,1)}, f32[2,2,1024,128]{3,2,1,0:T(8,128)}) custom-call(f32[4,2,256,768]{3,2,1,0:T(8,128)} %bitcast.159, f32[4,2,256,768]{3,2,1,0:T(8,128)} %bitcast.160, f32[4,2,256,768]{3,2,1,0:T(8,128)} %bitcast.161, ...), custom_call_target="tpu_custom_call" | custom-call | flops 15000000512 | bytes 1048576 | tf_op jit(solution)/shard_map/pallas_call | solution.py:1128
  182.9 46.6 %shard_map.179 = (f32[256,2048]{1,0:T(8,128)}, f32[256,2048]{1,0:T(8,128)}, bf16[256,2048]{1,0:T(8,128)(2,1)}) custom-call(bf16[2048,256]{1,0:T(8,128)(2,1)} %bitcast.167, bf16[2048,1024]{1,0:T(8,128)(2,1)} %all-gather.4.cloned.1.call-done.w_ref.wo_ref, bf16[256,2048]{1,0:T(8,128)(2,1)} %get-tuple-element.66.x_ref, f32[1,2048]{1,0:T(1,128)} %get-tuple-element.164.gain_ref), custom_call_target="tpu_custom_call" | custom-call | flops 46000001024 | bytes 1048576 | tf_op jit(solution)/shard_map/pallas_call | solution.py:547
  229.5 36.6 %all-gather.6.cloned.1.call-done.w_ref = bf16[2048,2048]{1,0:T(8,128)(2,1)} async-done(((bf16[512,2048]{1,0:T(8,128)(2,1)}), bf16[2048,2048]{1,0:T(8,128)(2,1)}) %all-gather.6.cloned.1.call-update) | async-done | bytes 8388624 | tf_op jit(solution)/shard_map/all_gather | solution.py:1536
  266.1 46.9 %shard_map.180 = (bf16[8,256,2048]{2,1,0:T(8,128)(2,1)}, bf16[2048,1024]{1,0:T(8,128)(2,1)}, bf16[2048,1024]{1,0:T(8,128)(2,1)}, bf16[2048,1024]{1,0:T(8,128)(2,1)}) custom-call(bf16[256,2048]{1,0:T(8,128)(2,1)} %get-tuple-element.67.in_ref, bf16[2048,2048]{1,0:T(8,128)(2,1)} %all-gather.6.cloned.1.call-done.w_ref), custom_call_target="tpu_custom_call" | custom-call | flops 46000001024 | bytes 1048576 | tf_op jit(solution)/shard_map/pallas_call | solution.py:626
  313.0 34.3 %all-gather.8.cloned.1.call-done.wd_ref = bf16[2048,1024]{1,0:T(8,128)(2,1)} async-done(((bf16[512,1024]{1,0:T(8,128)(2,1)}), bf16[2048,1024]{1,0:T(8,128)(2,1)}) %all-gather.8.cloned.1.call-update) | async-done | bytes 4194320 | tf_op jit(solution)/shard_map/all_gather | solution.py:1536
  347.3 152.2 %shard_map.181 = (bf16[256,2048]{1,0:T(8,128)(2,1)}, f32[1,2048]{1,0:T(1,128)}, bf16[8,256,2048]{2,1,0:T(8,128)(2,1)}, bf16[2048,2048]{1,0:T(8,128)(2,1)}, bf16[...) custom-call(bf16[2048,1024]{1,0:T(8,128)(2,1)} %get-tuple-element.68.h_ref, ...), custom_call_target="tpu_custom_call" | custom-call | flops 115000000512 | bytes 1048576 | tf_op jit(solution)/shard_map/pallas_call | solution.py:777
  499.5 23.8 %shard_map.182 = bf16[4,2,2048,256]{3,2,1,0:T(8,128)(2,1)} custom-call(bf16[2048,2048]{1,0:T(8,128)(2,1)} %bitcast.158, bf16[2048,2048]{1,0:T(8,128)(2,1)} %get-tuple-element.79.refs_1_.grad_ref), custom_call_target="tpu_custom_call" | custom-call | flops 24000000000 | bytes 1048576 | tf_op jit(solution)/shard_map/pallas_call | solution.py:1024
  523.4 96.5 %shard_map.183 = (f32[256,2048]{1,0:T(8,128)}, f32[1,2048]{1,0:T(1,128)}, bf16[8,256,2048]{2,1,0:T(8,128)(2,1)}, bf16[2048,256]{1,0:T(8,128)(2,1)}) custom-call(bf16[2048,2048]{1,0:T(8,128)(2,1)} %get-tuple-element.79.refs_1_.grad_ref, bf16[2048,2048]{1,0:T(8,128)(2,1)} %all-gather.6.cloned.1.call-done.w_ref, bf16[256,2048]{1,0:T(8,128)(2,1)} %get-tuple-element.80.cot_ref, ...), custom_call_target="tpu_custom_call" | custom-call | flops 92000002048 | bytes 1048576 | tf_op jit(solution)/shard_map/pallas_call | solution.py:876
  620.0 25.1 %shard_map.184 = (f32[4,2,256,256]{3,2,1,0:T(8,128)}, f32[4,2,256,256]{3,2,1,0:T(8,128)}, bf16[4,2,256,256]{3,2,1,0:T(8,128)(2,1)}, f32[2,2,8,1024]{3,2,1,0:T(8,128)}, f32[2,2,8,128]{3,2,1,0:T(8,128)}) custom-call(f32[4,2,256,768]{3,2,1,0:T(8,128)} %bitcast.162, f32[4,2,256,768]{3,2,1,0:T(8,128)} %bitcast.163, f32[4,2,256,768]{3,2,1,0:T(8,128)} %bitcast.164, ...), custom_call_target="tpu_custom_call" | custom-call | flops 35000000512 | bytes 1048576 | tf_op jit(solution)/shard_map/pallas_call | solution.py:1193
  648.2 60.9 %shard_map.185 = (bf16[256,2048]{1,0:T(8,128)(2,1)}, bf16[2048,768]{1,0:T(8,128)(2,1)}, f32[8,2048]{1,0:T(8,128)}) custom-call(f32[2048,256]{1,0:T(8,128)} %bitcast.165, f32[2048,256]{1,0:T(8,128)} %bitcast.166, bf16[2048,256]{1,0:T(8,128)(2,1)} %bitcast.169, f32[2048,768]{1,0:T(8,128)} %get-tuple-element.63.proj_ref, ...), custom_call_target="tpu_custom_call" | custom-call | flops 54999998464 | bytes 1048576 | tf_op jit(solution)/shard_map/pallas_call | solution.py:970
  709.1 14.2 %shard_map.186 = bf16[4,1,2048,256]{3,2,1,0:T(8,128)(2,1)} custom-call(bf16[2048,2048]{1,0:T(8,128)(2,1)} %bitcast.156, bf16[2048,768]{1,0:T(8,128)(2,1)} %get-tuple-element.96.refs_1_, bf16[2048,2048]{1,0:T(8,128)(2,1)} %bitcast.157, bf16[2048,256]{1,0:T(8,128)(2,1)} %bitcast.168), custom_call_target="tpu_custom_call" | custom-call | flops 12000000000 | bytes 1048576 | tf_op jit(solution)/shard_map/pallas_call | solution.py:1024
  741.8 62.0 %reduce-scatter.8.cloned.1.call-done = bf16[1,1,2048,256]{3,2,1,0:T(8,128)(2,1)} async-done(((bf16[4,1,2048,256]{3,2,1,0:T(8,128)(2,1)}), bf16[1,1,2048,256]{3,2,1,0:T(8,128)(2,1)}) %reduce-scatter.8.cloned.1.call-update) | async-done | bytes 1048592 | tf_op jit(solution)/shard_map/reduce_scatter | solution.py:1547
  806.1 5.2 all-to-all-start
  815.2 157.5 %shard_map.187 = (bf16[1024,2048]{1,0:T(8,128)(2,1)}, bf16[2,4,64,2048]{3,2,1,0:T(8,128)(2,1)}, f32[8,2048]{1,0:T(8,128)}) custom-call(bf16[4,2048,256]{2,1,0:T(8,128)(2,1)} %fusion.5.m_ref, bf16[2,256,2048]{2,1,0:T(8,128)(2,1)} %pad_maximum_fusion.2.rows_ref, f32[8,2048]{1,0:T(8,128)} %get-tuple-element.100.gain_ref), custom_call_target="tpu_custom_call" | custom-call | flops 95000002560 | bytes 1048576 | tf_op jit(solution)/shard_map/pallas_call | solution.py:1385
  1002.3 36.9 %collective-permute-done = bf16[2,64,2048]{2,1,0:T(8,128)(2,1)S(1)} collective-permute-done((bf16[2,64,2048]{2,1,0:T(8,128)(2,1)}, bf16[2,64,2048]{2,1,0:T(8,128)(2,1)S(1)}, u32[]{:S(2)}, u32[]{:S(2)}) %collective-permute-start) | collective-permute-done | bytes 524320 | tf_op jit(solution)/shard_map/ppermute | solution.py:1490
  1039.2 7.5 collective-permute-done.1
  1046.7 5.2 collective-permute-done.2
  1051.9 6.7 copy.47
  1058.7 6.7 copy.48
  1068.3 10.9 all-to-all-done.1
  1084.6 6.7 copy.49
  (118 shorter events, 86.5 us)
Async XLA Ops:
  7.2 134.0 %all-gather.4.cloned.1.call-start = ((), (), s32[]{:S(2)}) async-start(), calls=%async_computation.5 | async-start | bytes 5242880 | tf_op jit(solution)/shard_map/all_gather | solution.py:1536
  9.6 256.5 %all-gather.6.cloned.1.call-start = ((), (), s32[]{:S(2)}) async-start(), calls=%async_computation.6 | async-start | bytes 10485760 | tf_op jit(solution)/shard_map/all_gather | solution.py:1536
  14.6 332.6 %all-gather.8.cloned.1.call-start = ((), (), s32[]{:S(2)}) async-start(), calls=%async_computation.7 | async-start | bytes 5242880 | tf_op jit(solution)/shard_map/all_gather | solution.py:1536
  15.9 604.1 %reduce-scatter.6.cloned.1.call-start = ((), (), s32[]{:S(2)}) async-start(), calls=%async_computation.9 | async-start | bytes 5242880 | tf_op jit(solution)/shard_map/reduce_scatter | solution.py:1547
  133.0 5.2 copy-start.6
  499.5 232.8 %reduce-scatter.4.cloned.1.call-start = ((), (), s32[]{:S(2)}) async-start(), calls=%async_computation.8 | async-start | bytes 10485760 | tf_op jit(solution)/shard_map/reduce_scatter | solution.py:1547
  523.4 280.5 %reduce-scatter.8.cloned.1.call-start = ((), (), s32[]{:S(2)}) async-start(), calls=%async_computation.10 | async-start | bytes 5242880 | tf_op jit(solution)/shard_map/reduce_scatter | solution.py:1547
  620.0 27.5 %copy-start.13 = (f32[1,2048]{1,0:T(1,128)S(1)}, f32[1,2048]{1,0:T(1,128)}, u32[]{:S(2)}) copy-start(f32[1,2048]{1,0:T(1,128)} %get-tuple-element.92) | copy-start | bytes 24580
  620.0 27.5 %copy-start.14 = (f32[1,2048]{1,0:T(1,128)S(1)}, f32[1,2048]{1,0:T(1,128)}, u32[]{:S(2)}) copy-start(f32[1,2048]{1,0:T(1,128)} %get-tuple-element.91) | copy-start | bytes 24580
  726.5 5.8 copy-start
  732.3 6.5 copy-start.1
  806.1 5.2 copy-start.8
  806.1 5.2 copy-start.9
  806.1 173.3 %all-to-all-start = ((bf16[4,4,512,256]{3,2,1,0:T(8,128)(2,1)}), bf16[4,4,512,256]{3,2,1,0:T(8,128)(2,1)}, u32[]{:S(2)}, u32[]{:S(2)}) async-start(bf16[4,4,512,256]{3,2,1,0:T(8,128)(2,1)} %constant_dynamic-update-slice_fusion), calls=%async_computation.3 | async-start | bytes 8388608 | tf_op jit(solution)/shard_map/all_to_all | solution.py:1702
  979.4 99.8 %all-to-all-start.1 = ((bf16[32,256,256]{2,1,0:T(8,128)(2,1)}), bf16[32,256,256]{2,1,0:T(8,128)(2,1)}, u32[]{:S(2)}, u32[]{:S(2)}) async-start(bf16[32,256,256]{2,1,0:T(8,128)(2,1)} %bitcast.129), calls=%async_computation.4 | async-start | bytes 8388608 | tf_op jit(solution)/shard_map/all_to_all | solution.py:1758
  983.6 5.9 copy-start.10
  983.6 5.9 copy-start.12
  984.8 54.4 %collective-permute-start = (bf16[2,64,2048]{2,1,0:T(8,128)(2,1)}, bf16[2,64,2048]{2,1,0:T(8,128)(2,1)S(1)}, u32[]{:S(2)}, u32[]{:S(2)}) collective-permute-start(bf16[2,64,2048]{2,1,0:T(8,128)(2,1)} %get-tuple-element.149), channel_id=1, source_target_pairs={{0,2},{1,3},{2,4},{3,5},{4,6},{5,7},{6,0},{7,1},{8,10},{9,11},{10,... | collective-permute-start | bytes 1572872 | tf_op jit(solution)/shard_map/ppermute | solution.py:1490
  986.4 60.2 %collective-permute-start.1 = (bf16[2,64,2048]{2,1,0:T(8,128)(2,1)S(1)}, bf16[2,64,2048]{2,1,0:T(8,128)(2,1)S(1)}, u32[]{:S(2)}, u32[]{:S(2)}) collective-permute-start(bf16[2,64,2048]{2,1,0:T(8,128)(2,1)S(1)} %get-tuple-element.148), channel_id=1, source_target_pairs={{0,4},{1,5},{2,6},{3,7},{4,0},{5,1},{6,2},{7,3},{8,12},{9,13},{10,... | collective-permute-start | bytes 1572872 | tf_op jit(solution)/shard_map/ppermute | solution.py:1490
  987.9 64.0 %collective-permute-start.2 = (bf16[2,64,2048]{2,1,0:T(8,128)(2,1)S(1)}, bf16[2,64,2048]{2,1,0:T(8,128)(2,1)S(1)}, u32[]{:S(2)}, u32[]{:S(2)}) collective-permute-start(bf16[2,64,2048]{2,1,0:T(8,128)(2,1)S(1)} %get-tuple-element.147), channel_id=1, source_target_pairs={{0,6},{1,7},{2,0},{3,1},{4,2},{5,3},{6,4},{7,5},{8,14},{9,15},{10,... | collective-permute-start | bytes 1572872 | tf_op jit(solution)/shard_map/ppermute | solution.py:1490
  989.6 8.1 slice-start.1
  990.2 7.4 slice-start.2
  1051.9 6.8 slice-start.3
  1051.9 6.8 slice-start.4
  (7 other events, 23.1 us)
Sparse Core Ops, SparseCore 0:
  10.2 105.7 all-gather.3
  118.0 147.9 all-gather.5
  268.2 78.9 all-gather.7
  499.6 76.4 reduce-scatter.5
  578.5 144.9 reduce-scatter.3
  726.3 77.4 reduce-scatter.7

commit v7 on v6

--- a/solution.py
+++ b/solution.py
@@ -442,6 +442,38 @@
     )(x)
 
 
+def move_kernel(C, x_ref, own_ref, stage, mine, own, lsem, send, recv):
+    at = Plane()
+    load = local(x_ref, mine, lsem, 0)
+    moving = Moving(at, C, mine, stage, own, lsem, 1, send, recv)
+    barrier = pltpu.get_barrier_semaphore()
+    moving.greet(barrier)
+    pl.semaphore_wait(barrier, 2 * (C - 1))
+    load.wait()
+    moving.first()
+    moving.second()
+    moving.finish()
+    local(own, own_ref, lsem, 3).wait()
+
+
+def move_call(C, x):
+    R, D = x.shape
+    return pl.pallas_call(
+        functools.partial(move_kernel, C),
+        out_shape=jax.ShapeDtypeStruct((R, D), bf16),
+        in_specs=[ANY],
+        out_specs=ANY,
+        scratch_shapes=[
+            pltpu.VMEM((C, R // C, D), bf16),
+            pltpu.VMEM((R, D), bf16),
+            pltpu.VMEM((R, D), bf16),
+            dma(4), dma(2 * C), dma(2 * C),
+        ],
+        compiler_params=params(9),
+        cost_estimate=cost(50),
+    )(x)
+
+
 def qkv_kernel(all_ref, w_ref, proj_ref, st_ref, rows, w, acc, st, lsem, osem, ssend, srecv):
     at = Plane()
     F, R = rows.shape[0], rows.shape[1]
@@ -643,25 +675,26 @@
 
 def down_kernel(
     C, h_ref, wd_ref, hid_ref, cot_ref, gain_ref, act_ref, der_ref, unit_ref,
-    res_ref, gg_ref, all_ref, grad_ref, own_ref, mom_ref, p_ref,
-    h, wd, hid, mine, gain, act, der, res, gacc, rows, grad, cot, stage, prod, b0, b1, b2, b3, b4,
-    lsem, osem, asem, psem, send, recv, tsend, trecv, usend, urecv,
+    res_ref, gg_ref, all_ref, grad_ref, mom_ref, p_ref,
+    h, wd, hid, cot, gain, act, der, res, gacc, rows, grad, prod, b0, b1, b2, b3, b4,
+    lsem, osem, asem, psem, send, recv, usend, urecv,
 ):
     at = Plane()
     loads = [
         local(s, d, lsem, i)
         for i, (s, d) in enumerate(
-            [(cot_ref, mine), (h_ref, h), (wd_ref, wd), (hid_ref, hid), (gain_ref, gain)]
+            [(h_ref, h), (wd_ref, wd), (hid_ref, hid), (gain_ref, gain), (cot_ref, cot)]
         )
     ]
-    moving = Moving(at, C, mine, stage, cot, lsem, 5, tsend, trecv)
+    z = lax.axis_index("ctx")
     barrier = pltpu.get_barrier_semaphore()
-    moving.greet(barrier)
-    pl.semaphore_signal(barrier, inc=1, device_id={"fsdp": at.fc}, device_id_type=MESH)
-    pl.semaphore_wait(barrier, 2 * (C - 1) + 1)
+    for to in (at.fc, at.fx, at.fy):
+        pl.semaphore_signal(barrier, inc=1, device_id={"fsdp": to}, device_id_type=MESH)
+    for k in FAR_FIRST:
+        pl.semaphore_signal(barrier, inc=1, device_id={"ctx": partner(z, k)}, device_id_type=MESH)
+    pl.semaphore_wait(barrier, C + 2)
     R = rows.shape[1]
     n = wd.shape[1]
-    z = moving.z
     units = []
 
     def send_units(k):
@@ -670,25 +703,18 @@
         c.start()
         units.append(c)
 
-    send_units(FAR_FIRST[0])
+    for k in FAR_FIRST:
+        send_units(k)
+    units.append(local(unit_ref.at[z], mom_ref.at[z], lsem, 5))
     loads[0].wait()
-    moving.first()
     loads[1].wait()
-    loads[2].wait()
 
     def partial(chip, cols):
         return nt(h[pl.ds(pl.multiple_of(chip * 2 * R, 2 * R), 2 * R), :], wd[cols, :])
 
-    def between():
-        moving.second()
-        for k in FAR_FIRST[1:]:
-            send_units(k)
-        units.append(local(unit_ref.at[z], mom_ref.at[z], lsem, 10))
-
-    total = scatter_phase(at, partial, (b0, b1, b2, b3, b4), send, recv, 0, between)
-    for c in loads[3:]:
+    total = scatter_phase(at, partial, (b0, b1, b2, b3, b4), send, recv, 0)
+    for c in loads[2:]:
         c.wait()
-    moving.finish()
     gacc[...] = jnp.zeros_like(gacc)
 
     def finish(r):
@@ -701,7 +727,7 @@
         rows[at.f, r, :] = back(g * gain[...], hat, scale).astype(bf16)
 
     row_loop(R, finish)
-    saves = [local(res, res_ref, lsem, 7), local(gacc, gg_ref, lsem, 8), local(cot, own_ref, lsem, 9)]
+    saves = [local(res, res_ref, lsem, 6), local(gacc, gg_ref, lsem, 7)]
     stores = Stores(osem)
 
     def on_rows(first, count):
@@ -781,12 +807,11 @@
             jax.ShapeDtypeStruct((1, D), f32),
             jax.ShapeDtypeStruct((F, R, D), bf16),
             jax.ShapeDtypeStruct((T, 2 * n), bf16),
-            one,
             jax.ShapeDtypeStruct(units.shape, bf16),
             jax.ShapeDtypeStruct((units.shape[1], 1, D, units.shape[3]), bf16),
         ],
         in_specs=[ANY] * 8,
-        out_specs=[ANY] * 7,
+        out_specs=[ANY] * 6,
         scratch_shapes=[
             pltpu.VMEM((T, n), bf16),
             pltpu.VMEM((D, n), bf16),
@@ -799,14 +824,12 @@
             pltpu.VMEM((1, D), f32),
             pltpu.VMEM((F, R, D), bf16),
             pltpu.VMEM((2, 2 * R, 2 * n), bf16),
-            pltpu.VMEM((R, D), bf16),
-            pltpu.VMEM((C, R // C, D), bf16),
             pltpu.VMEM((2, 512, n), bf16),
         ]
         + scatter_scratch(R, D)
-        + [dma(11), dma(15), dma(10), dma(16), dma(copies), dma(copies), dma(2 * C), dma(2 * C), dma(C), dma(C)],
+        + [dma(8), dma(15), dma(10), dma(16), dma(copies), dma(copies), dma(C), dma(C)],
         compiler_params=params(3),
-        cost_estimate=cost(115),
+        cost_estimate=cost(108),
     )(h, wd, hid, cot, gain, act, der, units)
 
 
@@ -1286,12 +1309,15 @@
     tiles = M // tile
 
     def block(i):
-        return pl.ds(i * tile, tile)
-
-    def swap(buf, i, sends, recvs):
-        return remote(buf.at[0, block(i)], buf.at[1, block(i)], sends, recvs, i, peer)
-
-    pending = [swap(v, i, vsend, vrecv) for i in range(tiles)]
+        return pl.ds(pl.multiple_of(i * tile, tile), tile)
+
+    halves = D // col
+
+    def swap(buf, n, i, sends, recvs):
+        part = (block(i), pl.ds(n * col, col))
+        return remote(buf.at[(0, *part)], buf.at[(1, *part)], sends, recvs, n * tiles + i, peer)
+
+    pending = [swap(v, n, i, vsend, vrecv) for n in range(halves) for i in range(tiles)]
     for c in pending:
         c.start()
     stat[0] = jnp.zeros_like(stat[0])
@@ -1333,45 +1359,46 @@
             grams(1, n)
 
         def times(src, i, n):
-            rows = block(i)
-            cols = pl.ds(pl.multiple_of(n * col, col), col)
-            return cols, nn(gram[rows, :M], src[0, :, cols]) + nn(gram[rows, M:], src[1, :, cols])
-
-        pending = []
-        for i in range(tiles):
-
-            @pl.loop(0, D // col)
-            def _(n):
-                cols, got = times(v, i, n)
+            rows, c = block(i), pl.ds(n * col, col)
+            return nn(gram[rows, :M], src[0, :, c]) + nn(gram[rows, M:], src[1, :, c])
+
+        swaps = []
+        for n in range(halves):
+
+            @pl.loop(0, tiles)
+            def _(i):
+                at = (block(i), pl.ds(n * col, col))
+                got = times(v, i, n)
                 if iteration == 0:
                     got = got * factor
-                yf[block(i), cols] = got
-                y[0, block(i), cols] = got.astype(bf16)
-
-            c = swap(y, i, ysend, yrecv)
-            c.start()
-            pending.append(c)
-        for c in pending:
-            c.wait()
+                yf[at] = got
+                y[(0, *at)] = got.astype(bf16)
+                swap(y, n, i, ysend, yrecv).start()
+
+            swaps += [swap(y, n, i, ysend, yrecv) for i in range(tiles)]
         pending = []
-        for i in range(tiles):
-
-            @pl.loop(0, D // col)
-            def _(n):
-                cols, got = times(y, i, n)
-                old = v[0, block(i), cols].astype(f32)
+        for n in range(halves):
+            for c in swaps[n * tiles : (n + 1) * tiles]:
+                c.wait()
+
+            @pl.loop(0, tiles)
+            def _(i):
+                at = (block(i), pl.ds(n * col, col))
+                got = times(y, i, n)
+                old = v[(0, *at)].astype(f32)
                 if iteration == 0:
                     old = old * factor
-                v[0, block(i), cols] = (
-                    quintic_one * old + quintic_two * yf[block(i), cols] + quintic_three * got
-                ).astype(bf16)
+                v[(0, *at)] = (quintic_one * old + quintic_two * yf[at] + quintic_three * got).astype(bf16)
+                if iteration < NS_STEPS - 1:
+                    swap(v, n, i, vsend, vrecv).start()
 
             if iteration < NS_STEPS - 1:
-                c = swap(v, i, vsend, vrecv)
+                pending += [swap(v, n, i, vsend, vrecv) for i in range(tiles)]
             else:
-                c = pltpu.make_async_copy(v.at[0, block(i)], out_ref.at[block(i)], osem.at[i])
-            c.start()
-            pending.append(c)
+                for b in range(C):
+                    for g in range(n * col // cols, (n + 1) * col // cols):
+                        src = v.at[0, pl.ds(b * rows_in, rows_in), pl.ds(g * cols, cols)]
+                        pending.append(local(src, out_ref.at[b * F + g], osem, b * F + g))
     rows_arrived()
     for c in pending:
         c.wait()
@@ -1381,11 +1408,11 @@
     _, D, cols = x.shape
     M = D // 2
     _, R, _ = rows.shape
-    n = M // 512
+    n = 4
     return pl.pallas_call(
         functools.partial(newton_kernel, C),
         out_shape=[
-            jax.ShapeDtypeStruct((M, D), bf16),
+            jax.ShapeDtypeStruct((2 * C * C, M // C, cols), bf16),
             jax.ShapeDtypeStruct((2, C, R // C, D), bf16),
             jax.ShapeDtypeStruct((8, D), f32),
         ],
@@ -1399,7 +1426,7 @@
             pltpu.VMEM((2, 8, 128), f32),
             pltpu.VMEM((C, 8, D), f32),
             pltpu.VMEM((8, D), f32),
-            dma(7), dma(n), dma(n), dma(n), dma(n), dma(n), dma(1), dma(1),
+            dma(7), dma(2 * C * C), dma(n), dma(n), dma(n), dma(n), dma(1), dma(1),
             dma(2 * C), dma(2 * C), dma(C), dma(C), dma(2 * C * C), dma(2 * C * C), dma(C),
         ],
         compiler_params=params(6),
@@ -1413,10 +1440,12 @@
     return own, rows, dot(rows, w, 1, 0)
 
 
-def attn_out_and_up(C, F, mixed, wo, x, gain, w):
+def attn_out_and_up(C, F, mixed, wo, x, gain, w, cot):
     if kernels_fit(C, F):
         hidden_in, out, inp = out_call(F, mixed, wo, x, gain)
-        return (hidden_in, out, *up_call(F, inp, w))
+        cot, inp = lax.optimization_barrier((cot, inp))
+        cot, inp = lax.optimization_barrier((move_call(C, cot), inp))
+        return (cot, hidden_in, out, *up_call(F, inp, w))
     out = token_sums(dot(mixed, wo, 1, 1))
     hidden_in = x.astype(f32) + out * rms(out) * gain
     rows = token_rows(hidden_in.astype(bf16))
@@ -1424,13 +1453,13 @@
     sig = jax.nn.sigmoid(g)
     der = u * (sig * (1.0 + g * (1.0 - sig)))
     act = g * sig
-    return hidden_in, out, rows, act.astype(bf16), der.astype(bf16), (act * u).astype(bf16)
+    cot = to_layer(C, F, cot)
+    return cot, hidden_in, out, rows, act.astype(bf16), der.astype(bf16), (act * u).astype(bf16)
 
 
 def down_and_back(C, F, h, wd, hidden_in, cot, gain, act, der, units):
     if kernels_fit(C, F):
         return down_call(C, F, h, wd, hidden_in, cot, gain, act, der, units)
-    cot = to_layer(C, F, cot)
     out = token_sums(dot(h, wd, 1, 1))
     scale = rms(out)
     hat = out * scale
@@ -1442,7 +1471,6 @@
         jnp.sum(g * hat, axis=0, keepdims=True),
         rows,
         jnp.concatenate([(gh * der.astype(f32)).astype(bf16), (gh * act.astype(f32)).astype(bf16)], axis=1),
-        cot,
         None,
         None,
     )
@@ -1603,16 +1631,17 @@
         value_rows = heads(value_raw.astype(bf16))
         attn_mixed, log_total = attend(query_rows, key_rows, value_rows, pos)
         attn_mixed = unheads(attn_mixed)
-    hidden_in, attn_out, mlp_all, act, der, hidden = attn_out_and_up(
-        C, F, attn_mixed, w_out, own_input, gains[2:3], w_gate_up
+    own_grad, hidden_in, attn_out, mlp_all, act, der, hidden = attn_out_and_up(
+        C, F, attn_mixed, w_out, own_input, gains[2:3], w_gate_up,
+        cotangent.reshape(local_rows, width),
     )
     by_layer = None
     if kernels:
         by_layer = jnp.concatenate(
             [mom_attn[:, None].astype(bf16), jnp.transpose(mom_ffn.astype(bf16), (2, 0, 1, 3))], axis=1
         )
-    result, mlp_gain, grad_mlp_all, grad_ffn_in, own_grad, mom_own, p_down = down_and_back(
-        C, F, hidden, w_down, hidden_in, cotangent.reshape(local_rows, width), gains[3:4], act, der, by_layer
+    result, mlp_gain, grad_mlp_all, grad_ffn_in, mom_own, p_down = down_and_back(
+        C, F, hidden, w_down, hidden_in, own_grad, gains[3:4], act, der, by_layer
     )
     if kernels:
         mom_own = jnp.swapaxes(mom_own, 0, 1)
@@ -1752,9 +1781,12 @@
             own = (
                 quintic_one * factor * own.astype(f32) + quintic_two * product + quintic_three * product_two
             ).astype(bf16)
-    home = jnp.transpose(own.reshape(C, dz // parts, F, head_cols), (0, 2, 1, 3)).reshape(
-        C * F, dz // parts, head_cols
-    )
+    if kernels:
+        home = own
+    else:
+        home = jnp.transpose(own.reshape(C, dz // parts, F, head_cols), (0, 2, 1, 3)).reshape(
+            C * F, dz // parts, head_cols
+        )
     steps = lax.all_to_all(home, BOTH, split_axis=0, concat_axis=0, tiled=True)
     steps = -muon_rate * steps.astype(f32)
     if kernels:

time: 1100 us -> 1060 us (0.964)
  waiting for transfers between devices: 193 us -> 156 us
    pallas_call x0 -> x1, Pallas kernels: none -> 59.8 us  [move_call(): pl.pallas_call(functools.partial(move_kernel, C), out_shape=jax.ShapeDtyp...]
    pallas_call x1, Pallas kernels: 152 us -> 103 us  [down_call(): pl.pallas_call(functools.partial(down_kernel, C), out_shape=[one, jax.Sha...]
    all_gather x3, waiting for transfers between devices: 70.9 us -> 33.3 us  [rows_gather(): return lax.all_gather(shard, 'ctx', axis=0, tiled=True)]
    pallas_call x1, Pallas kernels: 158 us -> 146 us  [newton_call(): pl.pallas_call(functools.partial(newton_kernel, C), out_shape=[jax.ShapeD...]
    unnamed x46 -> x45, local copies, waits for them, and re-layouts: 34.2 us -> 30.6 us
  transfers between devices with their start and end apart: 11 -> 11, of which waited for: 7 -> 6; matrix products, arithmetic and copies ran while one was open for 7% -> 7% of each run, Pallas kernels for 57% -> 64%
where the time goes in v7:
time: 1060 us; the launch traced here: 1050 us
  Pallas kernels  773 us (73%)
  waiting for transfers between devices  156 us (15%)
  local copies, waits for them, and re-layouts  54.4 us (5%)
  other arithmetic  40.9 us (4%)
  between operations  14.9 us (1%)
  starting transfers between devices  14.3 us (1%)
    pallas_call x1, Pallas kernels, newton_call(): pl.pallas_call(functools.partial(newton_kernel, C), out_shape=[jax.ShapeD...  146 us
    pallas_call x1, Pallas kernels, enter_call(): pl.pallas_call(functools.partial(enter_kernel, C), out_shape=[jax.ShapeDt...  109 us
    pallas_call x1, Pallas kernels, down_call(): pl.pallas_call(functools.partial(down_kernel, C), out_shape=[one, jax.Sha...  103 us
    pallas_call x1, Pallas kernels, mid_call(): pl.pallas_call(mid_kernel, out_shape=[jax.ShapeDtypeStruct((R, D), f32),...  96.6 us
    reduce_scatter x3, waiting for transfers between devices, scatter(): return lax.psum_scatter(grad, 'ctx', scatter_dimension=0, tiled=True)[0]  61.7 us
    pallas_call x1, Pallas kernels, last_call(): pl.pallas_call(functools.partial(last_kernel, D), out_shape=[jax.ShapeDty...  60.8 us
    pallas_call x1, Pallas kernels, move_call(): pl.pallas_call(functools.partial(move_kernel, C), out_shape=jax.ShapeDtyp...  59.8 us
    ppermute x3, waiting for transfers between devices, go_home(): got.append(lax.ppermute(block, 'fsdp', pairs))  49.6 us
  transfers between devices with their start and end apart: 11, of which 6 were waited for; matrix products, arithmetic and copies ran while one was open for 7% of the time, Pallas kernels for 64%

profile of v7, /device:TPU:0, one launch (start us, length us, event | category | flops | bytes accessed | tf_op | source)
XLA Modules:
  0.0 1053.2 jit_solution(11386925374239914551)
XLA Ops:
  18.2 109.4 %shard_map.176 = (bf16[256,2048]{1,0:T(8,128)(2,1)}, bf16[8,256,2048]{2,1,0:T(8,128)(2,1)}) custom-call(bf16[256,2048]{1,0:T(8,128)(2,1)} %bitcast.149), custom_call_target="tpu_custom_call" | custom-call | flops 70000001024 | bytes 1048576 | tf_op jit(solution)/shard_map/pallas_call | solution.py:429
  133.4 4.9 sine_multiply_fusion
  141.2 22.7 %shard_map.177 = (f32[2048,768]{1,0:T(8,128)}, f32[8,8,2048]{2,1,0:T(8,128)}) custom-call(bf16[8,256,2048]{2,1,0:T(8,128)(2,1)} %get-tuple-element.65.all_ref, bf16[2048,1024]{1,0:T(8,128)(2,1)} %all-gather.4.cloned.1.call-done.w_ref.wo_ref), custom_call_target="tpu_custom_call" | custom-call | flops 22000001024 | bytes 1048576 | tf_op jit(solution)/shard_map/pallas_call | solution.py:524
  165.2 17.7 %shard_map.178 = (bf16[4,2,256,256]{3,2,1,0:T(8,128)(2,1)}, bf16[4,2,256,256]{3,2,1,0:T(8,128)(2,1)}, bf16[4,2,256,256]{3,2,1,0:T(8,128)(2,1)}, f32[2,2,1024,128]{3,2,1,0:T(8,128)}) custom-call(f32[4,2,256,768]{3,2,1,0:T(8,128)} %bitcast.154, f32[4,2,256,768]{3,2,1,0:T(8,128)} %bitcast.155, f32[4,2,256,768]{3,2,1,0:T(8,128)} %bitcast.156, ...), custom_call_target="tpu_custom_call" | custom-call | flops 15000000512 | bytes 1048576 | tf_op jit(solution)/shard_map/pallas_call | solution.py:1151
  182.9 46.6 %shard_map.179 = (f32[256,2048]{1,0:T(8,128)}, f32[256,2048]{1,0:T(8,128)}, bf16[256,2048]{1,0:T(8,128)(2,1)}) custom-call(bf16[2048,256]{1,0:T(8,128)(2,1)} %bitcast.162, bf16[2048,1024]{1,0:T(8,128)(2,1)} %all-gather.4.cloned.1.call-done.w_ref.wo_ref, bf16[256,2048]{1,0:T(8,128)(2,1)} %get-tuple-element.69.x_ref, f32[1,2048]{1,0:T(1,128)} %get-tuple-element.170.gain_ref), custom_call_target="tpu_custom_call" | custom-call | flops 46000001024 | bytes 1048576 | tf_op jit(solution)/shard_map/pallas_call | solution.py:579
  229.5 59.8 %shard_map.180.cot_ref = bf16[256,2048]{1,0:T(8,128)(2,1)} custom-call(bf16[256,2048]{1,0:T(8,128)(2,1)} %bitcast.150), custom_call_target="tpu_custom_call" | custom-call | flops 49999998976 | bytes 1048576 | tf_op jit(solution)/shard_map/pallas_call | solution.py:461
  289.4 46.9 %shard_map.181 = (bf16[8,256,2048]{2,1,0:T(8,128)(2,1)}, bf16[2048,1024]{1,0:T(8,128)(2,1)}, bf16[2048,1024]{1,0:T(8,128)(2,1)}, bf16[2048,1024]{1,0:T(8,128)(2,1)}) custom-call(bf16[256,2048]{1,0:T(8,128)(2,1)} %get-tuple-element.73.in_ref, bf16[2048,2048]{1,0:T(8,128)(2,1)} %all-gather.6.cloned.1.call-done.w_ref), custom_call_target="tpu_custom_call" | custom-call | flops 46000001024 | bytes 1048576 | tf_op jit(solution)/shard_map/pallas_call | solution.py:658
  336.3 33.3 %all-gather.8.cloned.1.call-done.wd_ref = bf16[2048,1024]{1,0:T(8,128)(2,1)} async-done(((bf16[512,1024]{1,0:T(8,128)(2,1)}), bf16[2048,1024]{1,0:T(8,128)(2,1)}) %all-gather.8.cloned.1.call-update) | async-done | bytes 4194320 | tf_op jit(solution)/shard_map/all_gather | solution.py:1564
  369.5 103.1 %shard_map.182 = (bf16[256,2048]{1,0:T(8,128)(2,1)}, f32[1,2048]{1,0:T(1,128)}, bf16[8,256,2048]{2,1,0:T(8,128)(2,1)}, bf16[2048,2048]{1,0:T(8,128)(2,1)}, bf16[...) custom-call(bf16[2048,1024]{1,0:T(8,128)(2,1)} %get-tuple-element.74.h_ref, ...), custom_call_target="tpu_custom_call" | custom-call | flops 108000002048 | bytes 1048576 | tf_op jit(solution)/shard_map/pallas_call | solution.py:803
  472.7 23.8 %shard_map.183 = bf16[4,2,2048,256]{3,2,1,0:T(8,128)(2,1)} custom-call(bf16[2048,2048]{1,0:T(8,128)(2,1)} %bitcast.153, bf16[2048,2048]{1,0:T(8,128)(2,1)} %get-tuple-element.86.refs_1_.grad_ref), custom_call_target="tpu_custom_call" | custom-call | flops 24000000000 | bytes 1048576 | tf_op jit(solution)/shard_map/pallas_call | solution.py:1047
  496.6 96.6 %shard_map.184 = (f32[256,2048]{1,0:T(8,128)}, f32[1,2048]{1,0:T(1,128)}, bf16[8,256,2048]{2,1,0:T(8,128)(2,1)}, bf16[2048,256]{1,0:T(8,128)(2,1)}) custom-call(bf16[2048,2048]{1,0:T(8,128)(2,1)} %get-tuple-element.86.refs_1_.grad_ref, bf16[2048,2048]{1,0:T(8,128)(2,1)} %all-gather.6.cloned.1.call-done.w_ref, bf16[256,2048]{1,0:T(8,128)(2,1)} %shard_map.180.cot_ref, ...), custom_call_target="tpu_custom_call" | custom-call | flops 92000002048 | bytes 1048576 | tf_op jit(solution)/shard_map/pallas_call | solution.py:899
  593.2 25.1 %shard_map.185 = (f32[4,2,256,256]{3,2,1,0:T(8,128)}, f32[4,2,256,256]{3,2,1,0:T(8,128)}, bf16[4,2,256,256]{3,2,1,0:T(8,128)(2,1)}, f32[2,2,8,1024]{3,2,1,0:T(8,128)}, f32[2,2,8,128]{3,2,1,0:T(8,128)}) custom-call(f32[4,2,256,768]{3,2,1,0:T(8,128)} %bitcast.157, f32[4,2,256,768]{3,2,1,0:T(8,128)} %bitcast.158, f32[4,2,256,768]{3,2,1,0:T(8,128)} %bitcast.159, ...), custom_call_target="tpu_custom_call" | custom-call | flops 35000000512 | bytes 1048576 | tf_op jit(solution)/shard_map/pallas_call | solution.py:1216
  621.5 60.8 %shard_map.186 = (bf16[256,2048]{1,0:T(8,128)(2,1)}, bf16[2048,768]{1,0:T(8,128)(2,1)}, f32[8,2048]{1,0:T(8,128)}) custom-call(f32[2048,256]{1,0:T(8,128)} %bitcast.160, f32[2048,256]{1,0:T(8,128)} %bitcast.161, bf16[2048,256]{1,0:T(8,128)(2,1)} %bitcast.164, f32[2048,768]{1,0:T(8,128)} %get-tuple-element.66.proj_ref, ...), custom_call_target="tpu_custom_call" | custom-call | flops 54999998464 | bytes 1048576 | tf_op jit(solution)/shard_map/pallas_call | solution.py:993
  682.3 14.3 %shard_map.187 = bf16[4,1,2048,256]{3,2,1,0:T(8,128)(2,1)} custom-call(bf16[2048,2048]{1,0:T(8,128)(2,1)} %bitcast.151, bf16[2048,768]{1,0:T(8,128)(2,1)} %get-tuple-element.102.refs_1_, bf16[2048,2048]{1,0:T(8,128)(2,1)} %bitcast.152, bf16[2048,256]{1,0:T(8,128)(2,1)} %bitcast.163), custom_call_target="tpu_custom_call" | custom-call | flops 12000000000 | bytes 1048576 | tf_op jit(solution)/shard_map/pallas_call | solution.py:1047
  714.9 61.7 %reduce-scatter.8.cloned.1.call-done = bf16[1,1,2048,256]{3,2,1,0:T(8,128)(2,1)} async-done(((bf16[4,1,2048,256]{3,2,1,0:T(8,128)(2,1)}), bf16[1,1,2048,256]{3,2,1,0:T(8,128)(2,1)}) %reduce-scatter.8.cloned.1.call-update) | async-done | bytes 1048592 | tf_op jit(solution)/shard_map/reduce_scatter | solution.py:1575
  778.8 5.2 all-to-all-start
  787.9 146.4 %shard_map.188 = (bf16[32,256,256]{2,1,0:T(8,128)(2,1)}, bf16[2,4,64,2048]{3,2,1,0:T(8,128)(2,1)}, f32[8,2048]{1,0:T(8,128)}) custom-call(bf16[4,2048,256]{2,1,0:T(8,128)(2,1)} %fusion.5.m_ref, bf16[2,256,2048]{2,1,0:T(8,128)(2,1)} %pad_maximum_fusion.2.rows_ref, f32[8,2048]{1,0:T(8,128)} %get-tuple-element.106.gain_ref), custom_call_target="tpu_custom_call" | custom-call | flops 95000002560 | bytes 1048576 | tf_op jit(solution)/shard_map/pallas_call | solution.py:1412
  957.1 36.9 %collective-permute-done = bf16[2,64,2048]{2,1,0:T(8,128)(2,1)S(1)} collective-permute-done((bf16[2,64,2048]{2,1,0:T(8,128)(2,1)}, bf16[2,64,2048]{2,1,0:T(8,128)(2,1)S(1)}, u32[]{:S(2)}, u32[]{:S(2)}) %collective-permute-start) | collective-permute-done | bytes 524320 | tf_op jit(solution)/shard_map/ppermute | solution.py:1518
  994.0 7.5 collective-permute-done.1
  1001.5 5.2 collective-permute-done.2
  1006.7 6.7 copy.50
  1013.5 6.7 copy.51
  1023.1 10.9 %all-to-all-done.1 = bf16[32,256,256]{2,1,0:T(8,128)(2,1)} async-done(((bf16[32,256,256]{2,1,0:T(8,128)(2,1)}), bf16[32,256,256]{2,1,0:T(8,128)(2,1)}, u32[]{:S(2)}, u32[]{:S(2)}) %all-to-all-start.1) | async-done | bytes 4194336 | tf_op jit(solution)/shard_map/all_to_all | solution.py:1790
  1039.4 6.7 copy.66
  (117 shorter events, 79.4 us)
Async XLA Ops:
  7.2 134.0 %all-gather.4.cloned.1.call-start = ((), (), s32[]{:S(2)}) async-start(), calls=%async_computation.5 | async-start | bytes 5242880 | tf_op jit(solution)/shard_map/all_gather | solution.py:1564
  9.6 279.7 %all-gather.6.cloned.1.call-start = ((), (), s32[]{:S(2)}) async-start(), calls=%async_computation.6 | async-start | bytes 10485760 | tf_op jit(solution)/shard_map/all_gather | solution.py:1564
  14.6 354.9 %all-gather.8.cloned.1.call-start = ((), (), s32[]{:S(2)}) async-start(), calls=%async_computation.7 | async-start | bytes 5242880 | tf_op jit(solution)/shard_map/all_gather | solution.py:1564
  15.9 577.3 %reduce-scatter.6.cloned.1.call-start = ((), (), s32[]{:S(2)}) async-start(), calls=%async_computation.9 | async-start | bytes 5242880 | tf_op jit(solution)/shard_map/reduce_scatter | solution.py:1575
  133.0 5.2 copy-start.6
  472.7 232.9 %reduce-scatter.4.cloned.1.call-start = ((), (), s32[]{:S(2)}) async-start(), calls=%async_computation.8 | async-start | bytes 10485760 | tf_op jit(solution)/shard_map/reduce_scatter | solution.py:1575
  496.5 280.0 %reduce-scatter.8.cloned.1.call-start = ((), (), s32[]{:S(2)}) async-start(), calls=%async_computation.10 | async-start | bytes 5242880 | tf_op jit(solution)/shard_map/reduce_scatter | solution.py:1575
  593.2 27.5 %copy-start.13 = (f32[1,2048]{1,0:T(1,128)S(1)}, f32[1,2048]{1,0:T(1,128)}, u32[]{:S(2)}) copy-start(f32[1,2048]{1,0:T(1,128)} %get-tuple-element.98) | copy-start | bytes 24580
  593.2 27.5 %copy-start.14 = (f32[1,2048]{1,0:T(1,128)S(1)}, f32[1,2048]{1,0:T(1,128)}, u32[]{:S(2)}) copy-start(f32[1,2048]{1,0:T(1,128)} %get-tuple-element.97) | copy-start | bytes 24580
  699.7 5.8 copy-start
  705.6 6.2 copy-start.1
  778.8 5.2 copy-start.8
  778.8 5.2 copy-start.9
  778.8 155.5 %all-to-all-start = ((bf16[4,4,512,256]{3,2,1,0:T(8,128)(2,1)}), bf16[4,4,512,256]{3,2,1,0:T(8,128)(2,1)}, u32[]{:S(2)}, u32[]{:S(2)}) async-start(bf16[4,4,512,256]{3,2,1,0:T(8,128)(2,1)} %constant_dynamic-update-slice_fusion), calls=%async_computation.3 | async-start | bytes 8388608 | tf_op jit(solution)/shard_map/all_to_all | solution.py:1731
  934.3 99.6 %all-to-all-start.1 = ((bf16[32,256,256]{2,1,0:T(8,128)(2,1)}), bf16[32,256,256]{2,1,0:T(8,128)(2,1)}, u32[]{:S(2)}, u32[]{:S(2)}) async-start(bf16[32,256,256]{2,1,0:T(8,128)(2,1)} %get-tuple-element.118), calls=%async_computation.4 | async-start | bytes 8388608 | tf_op jit(solution)/shard_map/all_to_all | solution.py:1790
  938.4 5.9 copy-start.10
  938.4 5.9 copy-start.12
  939.5 54.4 %collective-permute-start = (bf16[2,64,2048]{2,1,0:T(8,128)(2,1)}, bf16[2,64,2048]{2,1,0:T(8,128)(2,1)S(1)}, u32[]{:S(2)}, u32[]{:S(2)}) collective-permute-start(bf16[2,64,2048]{2,1,0:T(8,128)(2,1)} %get-tuple-element.155), channel_id=1, source_target_pairs={{0,2},{1,3},{2,4},{3,5},{4,6},{5,7},{6,0},{7,1},{8,10},{9,11},{10,... | collective-permute-start | bytes 1572872 | tf_op jit(solution)/shard_map/ppermute | solution.py:1518
  941.2 60.2 %collective-permute-start.1 = (bf16[2,64,2048]{2,1,0:T(8,128)(2,1)S(1)}, bf16[2,64,2048]{2,1,0:T(8,128)(2,1)S(1)}, u32[]{:S(2)}, u32[]{:S(2)}) collective-permute-start(bf16[2,64,2048]{2,1,0:T(8,128)(2,1)S(1)} %get-tuple-element.154), channel_id=1, source_target_pairs={{0,4},{1,5},{2,6},{3,7},{4,0},{5,1},{6,2},{7,3},{8,12},{9,13},{10,... | collective-permute-start | bytes 1572872 | tf_op jit(solution)/shard_map/ppermute | solution.py:1518
  942.7 64.0 %collective-permute-start.2 = (bf16[2,64,2048]{2,1,0:T(8,128)(2,1)S(1)}, bf16[2,64,2048]{2,1,0:T(8,128)(2,1)S(1)}, u32[]{:S(2)}, u32[]{:S(2)}) collective-permute-start(bf16[2,64,2048]{2,1,0:T(8,128)(2,1)S(1)} %get-tuple-element.153), channel_id=1, source_target_pairs={{0,6},{1,7},{2,0},{3,1},{4,2},{5,3},{6,4},{7,5},{8,14},{9,15},{10,... | collective-permute-start | bytes 1572872 | tf_op jit(solution)/shard_map/ppermute | solution.py:1518
  944.4 8.1 slice-start.1
  945.0 7.4 slice-start.2
  1006.7 6.8 slice-start.3
  1006.7 6.8 slice-start.4
  (7 other events, 22.7 us)
Sparse Core Ops, SparseCore 0:
  10.2 105.7 all-gather.3
  118.0 170.3 all-gather.5
  290.6 78.8 all-gather.7
  472.8 76.0 reduce-scatter.5
  551.2 144.9 reduce-scatter.3
  699.0 77.4 reduce-scatter.7

commit v8 on v7

--- a/solution.py
+++ b/solution.py
@@ -1232,9 +1232,9 @@
 
 
 def newton_kernel(
-    C, m_ref, rows_ref, gain_ref, out_ref, stage_ref, gsum_ref,
+    C, m_ref, rows_ref, gain_ref, grad_ref, out_ref, stage_ref, gsum_ref, back_ref,
     v, gram, y, yf, stat, gains, gsum,
-    lsem, osem, vsend, vrecv, ysend, yrecv, ssend, srecv, tsend, trecv, gsend, grecv, usend, urecv, usem,
+    lsem, osem, vsend, vrecv, ysend, yrecv, ssend, srecv, tsend, trecv, gsend, grecv, usend, urecv, usem, bsend, brecv,
 ):
     me = lax.axis_index("fsdp")
     z = lax.axis_index("ctx")
@@ -1267,7 +1267,12 @@
     def part(j):
         return pl.ds(j * piece, piece)
 
-    sent, keep = [], []
+    sent, keep = [], [local(grad_ref.at[z], back_ref.at[z], lsem, 4)]
+    for k in FAR_FIRST:
+        to = partner(z, k)
+        c = remote(grad_ref.at[to], back_ref.at[z], bsend, brecv, k, to, "ctx")
+        c.start()
+        sent.append(c)
     for a in range(2):
         for k in FAR_FIRST:
             to = partner(z, k)
@@ -1282,8 +1287,12 @@
         sent.append(c)
 
     def rows_arrived():
+        for c in keep:
+            c.wait()
+        for k in FAR_FIRST:
+            dst = back_ref.at[partner(z, k)]
+            remote(dst, dst, bsend, brecv, k, partner(z, k), "ctx").wait_recv()
         for a in range(2):
-            keep[a].wait()
             for k in FAR_FIRST:
                 dst = stage_ref.at[a, partner(z, k)]
                 remote(dst, dst, tsend, trecv, C * a + k, partner(z, k), "ctx").wait_recv()
@@ -1404,7 +1413,7 @@
         c.wait()
 
 
-def newton_call(C, x, rows, gains):
+def newton_call(C, x, rows, gains, grads):
     _, D, cols = x.shape
     M = D // 2
     _, R, _ = rows.shape
@@ -1415,9 +1424,10 @@
             jax.ShapeDtypeStruct((2 * C * C, M // C, cols), bf16),
             jax.ShapeDtypeStruct((2, C, R // C, D), bf16),
             jax.ShapeDtypeStruct((8, D), f32),
+            jax.ShapeDtypeStruct(grads.shape, bf16),
         ],
-        in_specs=[ANY] * 3,
-        out_specs=[ANY] * 3,
+        in_specs=[ANY] * 4,
+        out_specs=[ANY] * 4,
         scratch_shapes=[
             pltpu.VMEM((2, M, D), bf16),
             pltpu.VMEM((M, 2 * M), bf16),
@@ -1427,11 +1437,11 @@
             pltpu.VMEM((C, 8, D), f32),
             pltpu.VMEM((8, D), f32),
             dma(7), dma(2 * C * C), dma(n), dma(n), dma(n), dma(n), dma(1), dma(1),
-            dma(2 * C), dma(2 * C), dma(C), dma(C), dma(2 * C * C), dma(2 * C * C), dma(C),
+            dma(2 * C), dma(2 * C), dma(C), dma(C), dma(2 * C * C), dma(2 * C * C), dma(C), dma(C), dma(C),
         ],
         compiler_params=params(6),
         cost_estimate=cost(95),
-    )(x, rows, gains)
+    )(x, rows, gains, grads)
 
 
 def project(C, F, x, w):
@@ -1728,10 +1738,12 @@
         late = (mom_first + g_attn[0].astype(f32)).astype(bf16)
         owned = lax.dynamic_update_slice(owned, late[None], (0, 0, 0))
         got = lax.dynamic_update_slice(early, g_attn.reshape(C, 1, dz, head_cols), (0, 0, 0, 0))
-        sent_back = lax.all_to_all(got, "ctx", split_axis=0, concat_axis=0, tiled=True).astype(f32)
+        own, leaving, gain_total, sent_back = newton_call(
+            C, owned, jnp.stack([result, grad_rows]), gain_layer, got
+        )
+        sent_back = sent_back.astype(f32)
         grad_attn = sent_back[:, 0]
         grad_ffn = jnp.transpose(sent_back[:, 1:], (1, 2, 0, 3))
-        own, leaving, gain_total = newton_call(C, owned, jnp.stack([result, grad_rows]), gain_layer)
         homing = go_home(C, F, leaving)
         gain_total = gain_total[:4]
     else:
@@ -1788,12 +1800,13 @@
             C * F, dz // parts, head_cols
         )
     steps = lax.all_to_all(home, BOTH, split_axis=0, concat_axis=0, tiled=True)
-    steps = -muon_rate * steps.astype(f32)
     if kernels:
         steps = steps.reshape(C, UNITS_ATTN, dz, head_cols)
-        step_attn = steps[:, 0]
-        step_ffn = jnp.transpose(steps[:, 1:], (1, 2, 0, 3))
+        arranged = lax.optimization_barrier(jnp.transpose(steps[:, 1:], (1, 2, 0, 3)))
+        step_attn = -muon_rate * steps[:, 0].astype(f32)
+        step_ffn = -muon_rate * arranged.astype(f32)
     else:
+        steps = -muon_rate * steps.astype(f32)
         steps = steps.reshape(units, dz, head_cols)
         step_attn = steps[:UNITS_ATTN]
         step_ffn = jnp.transpose(

time: 1060 us -> 1050 us (level)
    unnamed x45 -> x43, local copies, waits for them, and re-layouts: 30.6 us -> 25.1 us
  transfers between devices with their start and end apart: 11 -> 10, of which waited for: 6 -> 6; matrix products, arithmetic and copies ran while one was open for 7% -> 7% of each run, Pallas kernels for 64% -> 50%
where the time goes in v8:
time: 1050 us
  Pallas kernels  775 us (74%)
  waiting for transfers between devices  157 us (15%)
  local copies, waits for them, and re-layouts  47.3 us (5%)
  other arithmetic  45.7 us (4%)
  between operations  14.9 us (1%)
    pallas_call x1, Pallas kernels, newton_call(): pl.pallas_call(functools.partial(newton_kernel, C), out_shape=[jax.ShapeD...  148 us
    pallas_call x1, Pallas kernels, enter_call(): pl.pallas_call(functools.partial(enter_kernel, C), out_shape=[jax.ShapeDt...  109 us
    pallas_call x1, Pallas kernels, down_call(): pl.pallas_call(functools.partial(down_kernel, C), out_shape=[one, jax.Sha...  103 us
    pallas_call x1, Pallas kernels, mid_call(): pl.pallas_call(mid_kernel, out_shape=[jax.ShapeDtypeStruct((R, D), f32),...  96.4 us
    reduce_scatter x3, waiting for transfers between devices, scatter(): return lax.psum_scatter(grad, 'ctx', scatter_dimension=0, tiled=True)[0]  61.8 us
    pallas_call x1, Pallas kernels, last_call(): pl.pallas_call(functools.partial(last_kernel, D), out_shape=[jax.ShapeDty...  60.8 us
    pallas_call x1, Pallas kernels, move_call(): pl.pallas_call(functools.partial(move_kernel, C), out_shape=jax.ShapeDtyp...  59.8 us
    ppermute x3, waiting for transfers between devices, go_home(): got.append(lax.ppermute(block, 'fsdp', pairs))  51.3 us
  transfers between devices with their start and end apart: 10, of which 6 were waited for; matrix products, arithmetic and copies ran while one was open for 7% of the time, Pallas kernels for 50%

profile of v8, /device:TPU:0, one launch (start us, length us, event | category | flops | bytes accessed | tf_op | source)
XLA Modules:
  0.0 1048.6 jit_solution(13219945002687442383)
XLA Ops:
  18.2 109.4 %shard_map.176 = (bf16[256,2048]{1,0:T(8,128)(2,1)}, bf16[8,256,2048]{2,1,0:T(8,128)(2,1)}) custom-call(bf16[256,2048]{1,0:T(8,128)(2,1)} %bitcast.141), custom_call_target="tpu_custom_call" | custom-call | flops 70000001024 | bytes 1048576 | tf_op jit(solution)/shard_map/pallas_call | solution.py:429
  127.6 4.3 copy.57
  133.4 4.9 sine_multiply_fusion
  141.2 22.7 %shard_map.177 = (f32[2048,768]{1,0:T(8,128)}, f32[8,8,2048]{2,1,0:T(8,128)}) custom-call(bf16[8,256,2048]{2,1,0:T(8,128)(2,1)} %get-tuple-element.66.all_ref, bf16[2048,1024]{1,0:T(8,128)(2,1)} %all-gather.4.cloned.1.call-done.w_ref.wo_ref), custom_call_target="tpu_custom_call" | custom-call | flops 22000001024 | bytes 1048576 | tf_op jit(solution)/shard_map/pallas_call | solution.py:524
  165.2 17.7 %shard_map.178 = (bf16[4,2,256,256]{3,2,1,0:T(8,128)(2,1)}, bf16[4,2,256,256]{3,2,1,0:T(8,128)(2,1)}, bf16[4,2,256,256]{3,2,1,0:T(8,128)(2,1)}, f32[2,2,1024,128]{3,2,1,0:T(8,128)}) custom-call(f32[4,2,256,768]{3,2,1,0:T(8,128)} %bitcast.146, f32[4,2,256,768]{3,2,1,0:T(8,128)} %bitcast.147, f32[4,2,256,768]{3,2,1,0:T(8,128)} %bitcast.148, ...), custom_call_target="tpu_custom_call" | custom-call | flops 15000000512 | bytes 1048576 | tf_op jit(solution)/shard_map/pallas_call | solution.py:1151
  182.9 46.6 %shard_map.179 = (f32[256,2048]{1,0:T(8,128)}, f32[256,2048]{1,0:T(8,128)}, bf16[256,2048]{1,0:T(8,128)(2,1)}) custom-call(bf16[2048,256]{1,0:T(8,128)(2,1)} %bitcast.154, bf16[2048,1024]{1,0:T(8,128)(2,1)} %all-gather.4.cloned.1.call-done.w_ref.wo_ref, bf16[256,2048]{1,0:T(8,128)(2,1)} %get-tuple-element.70.x_ref, f32[1,2048]{1,0:T(1,128)} %get-tuple-element.183.gain_ref), custom_call_target="tpu_custom_call" | custom-call | flops 46000001024 | bytes 1048576 | tf_op jit(solution)/shard_map/pallas_call | solution.py:579
  229.5 59.8 %shard_map.180.cot_ref = bf16[256,2048]{1,0:T(8,128)(2,1)} custom-call(bf16[256,2048]{1,0:T(8,128)(2,1)} %bitcast.142), custom_call_target="tpu_custom_call" | custom-call | flops 49999998976 | bytes 1048576 | tf_op jit(solution)/shard_map/pallas_call | solution.py:461
  289.4 46.9 %shard_map.181 = (bf16[8,256,2048]{2,1,0:T(8,128)(2,1)}, bf16[2048,1024]{1,0:T(8,128)(2,1)}, bf16[2048,1024]{1,0:T(8,128)(2,1)}, bf16[2048,1024]{1,0:T(8,128)(2,1)}) custom-call(bf16[256,2048]{1,0:T(8,128)(2,1)} %get-tuple-element.74.in_ref, bf16[2048,2048]{1,0:T(8,128)(2,1)} %all-gather.6.cloned.1.call-done.w_ref), custom_call_target="tpu_custom_call" | custom-call | flops 46000001024 | bytes 1048576 | tf_op jit(solution)/shard_map/pallas_call | solution.py:658
  336.3 33.2 %all-gather.8.cloned.1.call-done.wd_ref = bf16[2048,1024]{1,0:T(8,128)(2,1)} async-done(((bf16[512,1024]{1,0:T(8,128)(2,1)}), bf16[2048,1024]{1,0:T(8,128)(2,1)}) %all-gather.8.cloned.1.call-update) | async-done | bytes 4194320 | tf_op jit(solution)/shard_map/all_gather | solution.py:1574
  369.5 103.3 %shard_map.182 = (bf16[256,2048]{1,0:T(8,128)(2,1)}, f32[1,2048]{1,0:T(1,128)}, bf16[8,256,2048]{2,1,0:T(8,128)(2,1)}, bf16[2048,2048]{1,0:T(8,128)(2,1)}, bf16[...) custom-call(bf16[2048,1024]{1,0:T(8,128)(2,1)} %get-tuple-element.75.h_ref, ...), custom_call_target="tpu_custom_call" | custom-call | flops 108000002048 | bytes 1048576 | tf_op jit(solution)/shard_map/pallas_call | solution.py:803
  472.9 23.8 %shard_map.183 = bf16[4,2,2048,256]{3,2,1,0:T(8,128)(2,1)} custom-call(bf16[2048,2048]{1,0:T(8,128)(2,1)} %bitcast.145, bf16[2048,2048]{1,0:T(8,128)(2,1)} %get-tuple-element.87.refs_1_.grad_ref), custom_call_target="tpu_custom_call" | custom-call | flops 24000000000 | bytes 1048576 | tf_op jit(solution)/shard_map/pallas_call | solution.py:1047
  496.8 96.4 %shard_map.184 = (f32[256,2048]{1,0:T(8,128)}, f32[1,2048]{1,0:T(1,128)}, bf16[8,256,2048]{2,1,0:T(8,128)(2,1)}, bf16[2048,256]{1,0:T(8,128)(2,1)}) custom-call(bf16[2048,2048]{1,0:T(8,128)(2,1)} %get-tuple-element.87.refs_1_.grad_ref, bf16[2048,2048]{1,0:T(8,128)(2,1)} %all-gather.6.cloned.1.call-done.w_ref, bf16[256,2048]{1,0:T(8,128)(2,1)} %shard_map.180.cot_ref, ...), custom_call_target="tpu_custom_call" | custom-call | flops 92000002048 | bytes 1048576 | tf_op jit(solution)/shard_map/pallas_call | solution.py:899
  593.3 25.1 %shard_map.185 = (f32[4,2,256,256]{3,2,1,0:T(8,128)}, f32[4,2,256,256]{3,2,1,0:T(8,128)}, bf16[4,2,256,256]{3,2,1,0:T(8,128)(2,1)}, f32[2,2,8,1024]{3,2,1,0:T(8,128)}, f32[2,2,8,128]{3,2,1,0:T(8,128)}) custom-call(f32[4,2,256,768]{3,2,1,0:T(8,128)} %bitcast.149, f32[4,2,256,768]{3,2,1,0:T(8,128)} %bitcast.150, f32[4,2,256,768]{3,2,1,0:T(8,128)} %bitcast.151, ...), custom_call_target="tpu_custom_call" | custom-call | flops 35000000512 | bytes 1048576 | tf_op jit(solution)/shard_map/pallas_call | solution.py:1216
  621.5 60.8 %shard_map.186 = (bf16[256,2048]{1,0:T(8,128)(2,1)}, bf16[2048,768]{1,0:T(8,128)(2,1)}, f32[8,2048]{1,0:T(8,128)}) custom-call(f32[2048,256]{1,0:T(8,128)} %bitcast.152, f32[2048,256]{1,0:T(8,128)} %bitcast.153, bf16[2048,256]{1,0:T(8,128)(2,1)} %bitcast.156, f32[2048,768]{1,0:T(8,128)} %get-tuple-element.67.proj_ref, ...), custom_call_target="tpu_custom_call" | custom-call | flops 54999998464 | bytes 1048576 | tf_op jit(solution)/shard_map/pallas_call | solution.py:993
  682.4 14.3 %shard_map.187 = bf16[4,1,2048,256]{3,2,1,0:T(8,128)(2,1)} custom-call(bf16[2048,2048]{1,0:T(8,128)(2,1)} %bitcast.143, bf16[2048,768]{1,0:T(8,128)(2,1)} %get-tuple-element.103.refs_1_, bf16[2048,2048]{1,0:T(8,128)(2,1)} %bitcast.144, bf16[2048,256]{1,0:T(8,128)(2,1)} %bitcast.155), custom_call_target="tpu_custom_call" | custom-call | flops 12000000000 | bytes 1048576 | tf_op jit(solution)/shard_map/pallas_call | solution.py:1047
  715.0 61.7 %reduce-scatter.8.cloned.1.call-done = bf16[1,1,2048,256]{3,2,1,0:T(8,128)(2,1)} async-done(((bf16[4,1,2048,256]{3,2,1,0:T(8,128)(2,1)}), bf16[1,1,2048,256]{3,2,1,0:T(8,128)(2,1)}) %reduce-scatter.8.cloned.1.call-update) | async-done | bytes 1048592 | tf_op jit(solution)/shard_map/reduce_scatter | solution.py:1585
  783.2 147.7 %shard_map.188 = (bf16[32,256,256]{2,1,0:T(8,128)(2,1)}, bf16[2,4,64,2048]{3,2,1,0:T(8,128)(2,1)}, f32[8,2048]{1,0:T(8,128)}, bf16[4,4,512,256]{3,2,1,0:T(8,128)(2,1)}) custom-call(bf16[4,2048,256]{2,1,0:T(8,128)(2,1)} %fusion.4.m_ref, bf16[2,256,2048]{2,1,0:T(8,128)(2,1)} %pad_maximum_fusion.2.rows_ref, f32[8,2048]{1,0:T(8,128)} %get-tuple-element.107.gain_ref, ...), custom_call_target="tpu_custom_call" | custom-call | flops 95000002560 | bytes 1048576 | tf_op jit(solution)/shard_map/pallas_call | solution.py:1421
  946.8 4.3 multiply_add_fusion
  951.5 38.6 %collective-permute-done = bf16[2,64,2048]{2,1,0:T(8,128)(2,1)S(1)} collective-permute-done((bf16[2,64,2048]{2,1,0:T(8,128)(2,1)S(1)}, bf16[2,64,2048]{2,1,0:T(8,128)(2,1)S(1)}, u32[]{:S(2)}, u32[]{:S(2)}) %collective-permute-start) | collective-permute-done | bytes 524320 | tf_op jit(solution)/shard_map/ppermute | solution.py:1528
  990.2 7.5 collective-permute-done.1
  997.7 5.2 collective-permute-done.2
  1002.9 6.7 copy.44
  1009.7 6.7 copy.45
  1019.3 10.9 %all-to-all-done = bf16[32,256,256]{2,1,0:T(8,128)(2,1)} async-done(((bf16[32,256,256]{2,1,0:T(8,128)(2,1)}), bf16[32,256,256]{2,1,0:T(8,128)(2,1)}, u32[]{:S(2)}, u32[]{:S(2)}) %all-to-all-start) | async-done | bytes 4194336 | tf_op jit(solution)/shard_map/all_to_all | solution.py:1802
  (113 shorter events, 74.9 us)
Async XLA Ops:
  7.2 134.0 %all-gather.4.cloned.1.call-start = ((), (), s32[]{:S(2)}) async-start(), calls=%async_computation.4 | async-start | bytes 5242880 | tf_op jit(solution)/shard_map/all_gather | solution.py:1574
  9.6 279.7 %all-gather.6.cloned.1.call-start = ((), (), s32[]{:S(2)}) async-start(), calls=%async_computation.5 | async-start | bytes 10485760 | tf_op jit(solution)/shard_map/all_gather | solution.py:1574
  13.1 4.6 copy-start.10
  14.6 354.9 %all-gather.8.cloned.1.call-start = ((), (), s32[]{:S(2)}) async-start(), calls=%async_computation.6 | async-start | bytes 5242880 | tf_op jit(solution)/shard_map/all_gather | solution.py:1574
  15.9 577.4 %reduce-scatter.6.cloned.1.call-start = ((), (), s32[]{:S(2)}) async-start(), calls=%async_computation.8 | async-start | bytes 5242880 | tf_op jit(solution)/shard_map/reduce_scatter | solution.py:1585
  133.0 5.2 copy-start.6
  472.9 232.7 %reduce-scatter.4.cloned.1.call-start = ((), (), s32[]{:S(2)}) async-start(), calls=%async_computation.7 | async-start | bytes 10485760 | tf_op jit(solution)/shard_map/reduce_scatter | solution.py:1585
  496.8 279.9 %reduce-scatter.8.cloned.1.call-start = ((), (), s32[]{:S(2)}) async-start(), calls=%async_computation.9 | async-start | bytes 5242880 | tf_op jit(solution)/shard_map/reduce_scatter | solution.py:1585
  593.2 27.6 %copy-start.12 = (f32[1,2048]{1,0:T(1,128)S(1)}, f32[1,2048]{1,0:T(1,128)}, u32[]{:S(2)}) copy-start(f32[1,2048]{1,0:T(1,128)} %get-tuple-element.99) | copy-start | bytes 24580
  593.3 27.6 %copy-start.13 = (f32[1,2048]{1,0:T(1,128)S(1)}, f32[1,2048]{1,0:T(1,128)}, u32[]{:S(2)}) copy-start(f32[1,2048]{1,0:T(1,128)} %get-tuple-element.98) | copy-start | bytes 24580
  699.8 5.8 copy-start
  705.6 6.3 copy-start.1
  711.9 67.2 %copy-start.8 = (bf16[256,2048]{1,0:T(8,128)(2,1)S(1)}, bf16[256,2048]{1,0:T(8,128)(2,1)}, u32[]{:S(2)}) copy-start(bf16[256,2048]{1,0:T(8,128)(2,1)} %get-tuple-element.105) | copy-start | bytes 3145732
  715.0 66.8 %slice-start = ((f32[4,4,512,256]{3,2,0,1:T(8,128)}), f32[1,4,512,256]{3,2,0,1:T(8,128)S(1)}, s32[]{:S(2)}) async-start(f32[4,4,512,256]{3,2,0,1:T(8,128)} %copy-done), calls=%async_computation.10 | async-start | bytes 4194304 | tf_op jit(solution)/shard_map/slice | solution.py:1735
  776.7 5.1 copy-start.4
  930.9 99.3 %all-to-all-start = ((bf16[32,256,256]{2,1,0:T(8,128)(2,1)}), bf16[32,256,256]{2,1,0:T(8,128)(2,1)}, u32[]{:S(2)}, u32[]{:S(2)}) async-start(bf16[32,256,256]{2,1,0:T(8,128)(2,1)} %get-tuple-element.120), calls=%async_computation.3 | async-start | bytes 8388608 | tf_op jit(solution)/shard_map/all_to_all | solution.py:1802
  934.7 12.1 %slice-start.1 = ((s8[6291456]{0:T(1024)(128)(4,1)}), s8[4194304]{0:T(1024)(128)(4,1)S(1)}, s32[]{:S(2)}) async-start(s8[6291456]{0:T(1024)(128)(4,1)} %bitcast.114), calls=%async_computation.11 | async-start | bytes 8388608
  938.0 6.5 copy-start.3
  938.0 8.8 slice-start.2
  938.2 52.0 %collective-permute-start = (bf16[2,64,2048]{2,1,0:T(8,128)(2,1)S(1)}, bf16[2,64,2048]{2,1,0:T(8,128)(2,1)S(1)}, u32[]{:S(2)}, u32[]{:S(2)}) collective-permute-start(bf16[2,64,2048]{2,1,0:T(8,128)(2,1)S(1)} %get-tuple-element.168), channel_id=1, source_target_pairs={{0,2},{1,3},{2,4},{3,5},{4,6},{5,7},{6,0},{7,1},{8,10},{9,11},{10,... | collective-permute-start | bytes 1572872 | tf_op jit(solution)/shard_map/ppermute | solution.py:1528
  939.9 57.7 %collective-permute-start.1 = (bf16[2,64,2048]{2,1,0:T(8,128)(2,1)S(1)}, bf16[2,64,2048]{2,1,0:T(8,128)(2,1)S(1)}, u32[]{:S(2)}, u32[]{:S(2)}) collective-permute-start(bf16[2,64,2048]{2,1,0:T(8,128)(2,1)S(1)} %get-tuple-element.167), channel_id=1, source_target_pairs={{0,4},{1,5},{2,6},{3,7},{4,0},{5,1},{6,2},{7,3},{8,12},{9,13},{10,... | collective-permute-start | bytes 1572872 | tf_op jit(solution)/shard_map/ppermute | solution.py:1528
  941.4 61.5 %collective-permute-start.2 = (bf16[2,64,2048]{2,1,0:T(8,128)(2,1)S(1)}, bf16[2,64,2048]{2,1,0:T(8,128)(2,1)S(1)}, u32[]{:S(2)}, u32[]{:S(2)}) collective-permute-start(bf16[2,64,2048]{2,1,0:T(8,128)(2,1)S(1)} %get-tuple-element.166), channel_id=1, source_target_pairs={{0,6},{1,7},{2,0},{3,1},{4,2},{5,3},{6,4},{7,5},{8,14},{9,15},{10,... | collective-permute-start | bytes 1572872 | tf_op jit(solution)/shard_map/ppermute | solution.py:1528
  1002.9 6.8 slice-start.3
  1002.9 6.8 slice-start.4
  (5 other events, 13.1 us)
Sparse Core Ops, SparseCore 0:
  10.2 105.7 all-gather.3
  118.0 170.3 all-gather.5
  290.6 78.8 all-gather.7
  473.0 75.9 reduce-scatter.5
  551.4 144.9 reduce-scatter.3
  699.2 77.4 reduce-scatter.7

commit v9 on v8

--- a/solution.py
+++ b/solution.py
@@ -442,38 +442,6 @@
     )(x)
 
 
-def move_kernel(C, x_ref, own_ref, stage, mine, own, lsem, send, recv):
-    at = Plane()
-    load = local(x_ref, mine, lsem, 0)
-    moving = Moving(at, C, mine, stage, own, lsem, 1, send, recv)
-    barrier = pltpu.get_barrier_semaphore()
-    moving.greet(barrier)
-    pl.semaphore_wait(barrier, 2 * (C - 1))
-    load.wait()
-    moving.first()
-    moving.second()
-    moving.finish()
-    local(own, own_ref, lsem, 3).wait()
-
-
-def move_call(C, x):
-    R, D = x.shape
-    return pl.pallas_call(
-        functools.partial(move_kernel, C),
-        out_shape=jax.ShapeDtypeStruct((R, D), bf16),
-        in_specs=[ANY],
-        out_specs=ANY,
-        scratch_shapes=[
-            pltpu.VMEM((C, R // C, D), bf16),
-            pltpu.VMEM((R, D), bf16),
-            pltpu.VMEM((R, D), bf16),
-            dma(4), dma(2 * C), dma(2 * C),
-        ],
-        compiler_params=params(9),
-        cost_estimate=cost(50),
-    )(x)
-
-
 def qkv_kernel(all_ref, w_ref, proj_ref, st_ref, rows, w, acc, st, lsem, osem, ssend, srecv):
     at = Plane()
     F, R = rows.shape[0], rows.shape[1]
@@ -602,16 +570,23 @@
 
 
 def up_kernel(
-    in_ref, w_ref, all_ref, act_ref, der_ref, h_ref,
-    w, rows, act, der, h, lsem, osem, send, recv,
+    C, in_ref, w_ref, cot_ref, all_ref, act_ref, der_ref, h_ref, moved_ref,
+    w, rows, act, der, h, mine, moved, stage, lsem, osem, send, recv, tsend, trecv,
 ):
     at = Plane()
+    cot = local(cot_ref, mine, lsem, 2)
+    moving = Moving(at, C, mine, stage, moved, lsem, 3, tsend, trecv)
     own = local(in_ref, rows.at[at.f], lsem, 0)
     n = act.shape[2]
     loads = [local(w_ref, w, lsem, 1)]
     width = 256
-    at.greet()
+    barrier = pltpu.get_barrier_semaphore()
+    moving.greet(barrier)
+    pl.semaphore_signal(barrier, inc=1, device_id={"fsdp": at.fc}, device_id_type=MESH)
+    pl.semaphore_wait(barrier, 2 * (C - 1) + 1)
     R = rows.shape[1]
+    cot.wait()
+    moving.first()
     own.wait()
     waited = []
     stores = Stores(osem)
@@ -622,6 +597,7 @@
         if not waited:
             for c in loads:
                 c.wait()
+            moving.second()
             waited.append(1)
 
         @pl.loop(0, n // width)
@@ -647,30 +623,37 @@
         )
 
     gather_phase(at, rows, send, recv, 0, on_rows)
+    moving.finish()
+    local(moved, moved_ref, lsem, 5).wait()
     stores.finish()
 
 
-def up_call(F, inp, w):
+def up_call(C, F, inp, w, cot):
     R, D = inp.shape
     n = w.shape[1] // 2
     T = F * R
     wide = jax.ShapeDtypeStruct((T, n), bf16)
     return pl.pallas_call(
-        up_kernel,
-        out_shape=[jax.ShapeDtypeStruct((F, R, D), bf16), wide, wide, wide],
-        in_specs=[ANY] * 2,
-        out_specs=[ANY] * 4,
+        functools.partial(up_kernel, C),
+        out_shape=[
+            jax.ShapeDtypeStruct((F, R, D), bf16), wide, wide, wide, jax.ShapeDtypeStruct((R, D), bf16),
+        ],
+        in_specs=[ANY] * 3,
+        out_specs=[ANY] * 5,
         scratch_shapes=[
             pltpu.VMEM((D, 2 * n), bf16),
             pltpu.VMEM((F, R, D), bf16),
             pltpu.VMEM((2, 2 * R, n), bf16),
             pltpu.VMEM((2, 2 * R, n), bf16),
             pltpu.VMEM((2, 2 * R, n), bf16),
+            pltpu.VMEM((R, D), bf16),
+            pltpu.VMEM((R, D), bf16),
+            pltpu.VMEM((C, R // C, D), bf16),
         ]
-        + [dma(2), dma(20), dma(GATHER_COPIES), dma(GATHER_COPIES)],
+        + [dma(6), dma(20), dma(GATHER_COPIES), dma(GATHER_COPIES), dma(2 * C), dma(2 * C)],
         compiler_params=params(2),
-        cost_estimate=cost(46),
-    )(inp, w)
+        cost_estimate=cost(56),
+    )(inp, w, cot)
 
 
 def down_kernel(
@@ -1453,9 +1436,8 @@
 def attn_out_and_up(C, F, mixed, wo, x, gain, w, cot):
     if kernels_fit(C, F):
         hidden_in, out, inp = out_call(F, mixed, wo, x, gain)
-        cot, inp = lax.optimization_barrier((cot, inp))
-        cot, inp = lax.optimization_barrier((move_call(C, cot), inp))
-        return (cot, hidden_in, out, *up_call(F, inp, w))
+        rows, act, der, h, cot = up_call(C, F, inp, w, cot)
+        return cot, hidden_in, out, rows, act, der, h
     out = token_sums(dot(mixed, wo, 1, 1))
     hidden_in = x.astype(f32) + out * rms(out) * gain
     rows = token_rows(hidden_in.astype(bf16))

time: 1050 us -> 1050 us (level)
  Pallas kernels: 775 us -> 738 us
  waiting for transfers between devices: 157 us -> 194 us
    pallas_call x2 -> x1, Pallas kernels: 107 us -> 70 us  [up_call(): pl.pallas_call(functools.partial(up_kernel, C), out_shape=[jax.ShapeDtype...]
    all_gather x3, waiting for transfers between devices: 33.3 us -> 69.9 us  [rows_gather(): return lax.all_gather(shard, 'ctx', axis=0, tiled=True)]
  transfers between devices with their start and end apart: 10 -> 10, of which waited for: 6 -> 7; matrix products, arithmetic and copies ran while one was open for 7% -> 7% of each run, Pallas kernels for 50% -> 46%
where the time goes in v9:
time: 1050 us
  Pallas kernels  738 us (70%)
  waiting for transfers between devices  194 us (18%)
  local copies, waits for them, and re-layouts  47.3 us (5%)
  other arithmetic  45.7 us (4%)
  between operations  14.9 us (1%)
    pallas_call x1, Pallas kernels, newton_call(): pl.pallas_call(functools.partial(newton_kernel, C), out_shape=[jax.ShapeD...  148 us
    pallas_call x1, Pallas kernels, enter_call(): pl.pallas_call(functools.partial(enter_kernel, C), out_shape=[jax.ShapeDt...  109 us
    pallas_call x1, Pallas kernels, down_call(): pl.pallas_call(functools.partial(down_kernel, C), out_shape=[one, jax.Sha...  103 us
    pallas_call x1, Pallas kernels, mid_call(): pl.pallas_call(mid_kernel, out_shape=[jax.ShapeDtypeStruct((R, D), f32),...  96.4 us
    pallas_call x1, Pallas kernels, up_call(): pl.pallas_call(functools.partial(up_kernel, C), out_shape=[jax.ShapeDtype...  70 us
    all_gather x3, waiting for transfers between devices, rows_gather(): return lax.all_gather(shard, 'ctx', axis=0, tiled=True)  69.9 us
    reduce_scatter x3, waiting for transfers between devices, scatter(): return lax.psum_scatter(grad, 'ctx', scatter_dimension=0, tiled=True)[0]  61.8 us
    pallas_call x1, Pallas kernels, last_call(): pl.pallas_call(functools.partial(last_kernel, D), out_shape=[jax.ShapeDty...  60.8 us
  transfers between devices with their start and end apart: 10, of which 7 were waited for; matrix products, arithmetic and copies ran while one was open for 7% of the time, Pallas kernels for 46%

profile of v9, /device:TPU:0, one launch (start us, length us, event | category | flops | bytes accessed | tf_op | source)
XLA Modules:
  0.0 1048.7 jit_solution(10311224671911469077)
XLA Ops:
  18.2 109.4 %shard_map.176 = (bf16[256,2048]{1,0:T(8,128)(2,1)}, bf16[8,256,2048]{2,1,0:T(8,128)(2,1)}) custom-call(bf16[256,2048]{1,0:T(8,128)(2,1)} %bitcast.141), custom_call_target="tpu_custom_call" | custom-call | flops 70000001024 | bytes 1048576 | tf_op jit(solution)/shard_map/pallas_call | solution.py:429
  127.6 4.3 copy.57
  133.4 4.9 sine_multiply_fusion
  141.2 22.7 %shard_map.177 = (f32[2048,768]{1,0:T(8,128)}, f32[8,8,2048]{2,1,0:T(8,128)}) custom-call(bf16[8,256,2048]{2,1,0:T(8,128)(2,1)} %get-tuple-element.63.all_ref, bf16[2048,1024]{1,0:T(8,128)(2,1)} %all-gather.4.cloned.1.call-done.w_ref.wo_ref), custom_call_target="tpu_custom_call" | custom-call | flops 22000001024 | bytes 1048576 | tf_op jit(solution)/shard_map/pallas_call | solution.py:492
  165.2 17.7 %shard_map.178 = (bf16[4,2,256,256]{3,2,1,0:T(8,128)(2,1)}, bf16[4,2,256,256]{3,2,1,0:T(8,128)(2,1)}, bf16[4,2,256,256]{3,2,1,0:T(8,128)(2,1)}, f32[2,2,1024,128]{3,2,1,0:T(8,128)}) custom-call(f32[4,2,256,768]{3,2,1,0:T(8,128)} %bitcast.146, f32[4,2,256,768]{3,2,1,0:T(8,128)} %bitcast.147, f32[4,2,256,768]{3,2,1,0:T(8,128)} %bitcast.148, ...), custom_call_target="tpu_custom_call" | custom-call | flops 15000000512 | bytes 1048576 | tf_op jit(solution)/shard_map/pallas_call | solution.py:1134
  182.9 46.6 %shard_map.179 = (f32[256,2048]{1,0:T(8,128)}, f32[256,2048]{1,0:T(8,128)}, bf16[256,2048]{1,0:T(8,128)(2,1)}) custom-call(bf16[2048,256]{1,0:T(8,128)(2,1)} %bitcast.154, bf16[2048,1024]{1,0:T(8,128)(2,1)} %all-gather.4.cloned.1.call-done.w_ref.wo_ref, bf16[256,2048]{1,0:T(8,128)(2,1)} %get-tuple-element.67.x_ref, f32[1,2048]{1,0:T(1,128)} %get-tuple-element.177.gain_ref), custom_call_target="tpu_custom_call" | custom-call | flops 46000001024 | bytes 1048576 | tf_op jit(solution)/shard_map/pallas_call | solution.py:547
  229.5 36.5 %all-gather.6.cloned.1.call-done.w_ref = bf16[2048,2048]{1,0:T(8,128)(2,1)} async-done(((bf16[512,2048]{1,0:T(8,128)(2,1)}), bf16[2048,2048]{1,0:T(8,128)(2,1)}) %all-gather.6.cloned.1.call-update) | async-done | bytes 8388624 | tf_op jit(solution)/shard_map/all_gather | solution.py:1556
  266.1 70.0 %shard_map.180 = (bf16[8,256,2048]{2,1,0:T(8,128)(2,1)}, bf16[2048,1024]{1,0:T(8,128)(2,1)}, bf16[2048,1024]{1,0:T(8,128)(2,1)}, bf16[2048,1024]{1,0:T(8,128)(2,1)}, bf16[256,2048]{1,0:T(8,128)(2,1)}) custom-call(bf16[256,2048]{1,0:T(8,128)(2,1)} %get-tuple-element.68.in_ref, bf16[2048,2048]{1,0:T(8,128)(2,1)} %all-gather.6.cloned.1.call-done.w_ref, ...), custom_call_target="tpu_custom_call" | custom-call | flops 56000000000 | bytes 1048576 | tf_op jit(solution)/shard_map/pallas_call | solution.py:636
  336.1 33.4 %all-gather.8.cloned.1.call-done.wd_ref = bf16[2048,1024]{1,0:T(8,128)(2,1)} async-done(((bf16[512,1024]{1,0:T(8,128)(2,1)}), bf16[2048,1024]{1,0:T(8,128)(2,1)}) %all-gather.8.cloned.1.call-update) | async-done | bytes 4194320 | tf_op jit(solution)/shard_map/all_gather | solution.py:1556
  369.5 103.3 %shard_map.181 = (bf16[256,2048]{1,0:T(8,128)(2,1)}, f32[1,2048]{1,0:T(1,128)}, bf16[8,256,2048]{2,1,0:T(8,128)(2,1)}, bf16[2048,2048]{1,0:T(8,128)(2,1)}, bf16[...) custom-call(bf16[2048,1024]{1,0:T(8,128)(2,1)} %get-tuple-element.69.h_ref, ...), custom_call_target="tpu_custom_call" | custom-call | flops 108000002048 | bytes 1048576 | tf_op jit(solution)/shard_map/pallas_call | solution.py:786
  472.9 23.8 %shard_map.182 = bf16[4,2,2048,256]{3,2,1,0:T(8,128)(2,1)} custom-call(bf16[2048,2048]{1,0:T(8,128)(2,1)} %bitcast.145, bf16[2048,2048]{1,0:T(8,128)(2,1)} %get-tuple-element.81.refs_1_.grad_ref), custom_call_target="tpu_custom_call" | custom-call | flops 24000000000 | bytes 1048576 | tf_op jit(solution)/shard_map/pallas_call | solution.py:1030
  496.8 96.4 %shard_map.183 = (f32[256,2048]{1,0:T(8,128)}, f32[1,2048]{1,0:T(1,128)}, bf16[8,256,2048]{2,1,0:T(8,128)(2,1)}, bf16[2048,256]{1,0:T(8,128)(2,1)}) custom-call(bf16[2048,2048]{1,0:T(8,128)(2,1)} %get-tuple-element.81.refs_1_.grad_ref, bf16[2048,2048]{1,0:T(8,128)(2,1)} %all-gather.6.cloned.1.call-done.w_ref, bf16[256,2048]{1,0:T(8,128)(2,1)} %get-tuple-element.71.cot_ref, ...), custom_call_target="tpu_custom_call" | custom-call | flops 92000002048 | bytes 1048576 | tf_op jit(solution)/shard_map/pallas_call | solution.py:882
  593.2 25.1 %shard_map.184 = (f32[4,2,256,256]{3,2,1,0:T(8,128)}, f32[4,2,256,256]{3,2,1,0:T(8,128)}, bf16[4,2,256,256]{3,2,1,0:T(8,128)(2,1)}, f32[2,2,8,1024]{3,2,1,0:T(8,128)}, f32[2,2,8,128]{3,2,1,0:T(8,128)}) custom-call(f32[4,2,256,768]{3,2,1,0:T(8,128)} %bitcast.149, f32[4,2,256,768]{3,2,1,0:T(8,128)} %bitcast.150, f32[4,2,256,768]{3,2,1,0:T(8,128)} %bitcast.151, ...), custom_call_target="tpu_custom_call" | custom-call | flops 35000000512 | bytes 1048576 | tf_op jit(solution)/shard_map/pallas_call | solution.py:1199
  621.5 60.8 %shard_map.185 = (bf16[256,2048]{1,0:T(8,128)(2,1)}, bf16[2048,768]{1,0:T(8,128)(2,1)}, f32[8,2048]{1,0:T(8,128)}) custom-call(f32[2048,256]{1,0:T(8,128)} %bitcast.152, f32[2048,256]{1,0:T(8,128)} %bitcast.153, bf16[2048,256]{1,0:T(8,128)(2,1)} %bitcast.156, f32[2048,768]{1,0:T(8,128)} %get-tuple-element.64.proj_ref, ...), custom_call_target="tpu_custom_call" | custom-call | flops 54999998464 | bytes 1048576 | tf_op jit(solution)/shard_map/pallas_call | solution.py:976
  682.3 14.3 %shard_map.186 = bf16[4,1,2048,256]{3,2,1,0:T(8,128)(2,1)} custom-call(bf16[2048,2048]{1,0:T(8,128)(2,1)} %bitcast.143, bf16[2048,768]{1,0:T(8,128)(2,1)} %get-tuple-element.97.refs_1_, bf16[2048,2048]{1,0:T(8,128)(2,1)} %bitcast.144, bf16[2048,256]{1,0:T(8,128)(2,1)} %bitcast.155), custom_call_target="tpu_custom_call" | custom-call | flops 12000000000 | bytes 1048576 | tf_op jit(solution)/shard_map/pallas_call | solution.py:1030
  714.9 61.8 %reduce-scatter.8.cloned.1.call-done = bf16[1,1,2048,256]{3,2,1,0:T(8,128)(2,1)} async-done(((bf16[4,1,2048,256]{3,2,1,0:T(8,128)(2,1)}), bf16[1,1,2048,256]{3,2,1,0:T(8,128)(2,1)}) %reduce-scatter.8.cloned.1.call-update) | async-done | bytes 1048592 | tf_op jit(solution)/shard_map/reduce_scatter | solution.py:1567
  783.1 147.7 %shard_map.187 = (bf16[32,256,256]{2,1,0:T(8,128)(2,1)}, bf16[2,4,64,2048]{3,2,1,0:T(8,128)(2,1)}, f32[8,2048]{1,0:T(8,128)}, bf16[4,4,512,256]{3,2,1,0:T(8,128)(2,1)}) custom-call(bf16[4,2048,256]{2,1,0:T(8,128)(2,1)} %fusion.4.m_ref, bf16[2,256,2048]{2,1,0:T(8,128)(2,1)} %pad_maximum_fusion.2.rows_ref, f32[8,2048]{1,0:T(8,128)} %get-tuple-element.101.gain_ref, ...), custom_call_target="tpu_custom_call" | custom-call | flops 95000002560 | bytes 1048576 | tf_op jit(solution)/shard_map/pallas_call | solution.py:1404
  946.9 4.3 multiply_add_fusion
  951.6 38.6 %collective-permute-done = bf16[2,64,2048]{2,1,0:T(8,128)(2,1)S(1)} collective-permute-done((bf16[2,64,2048]{2,1,0:T(8,128)(2,1)S(1)}, bf16[2,64,2048]{2,1,0:T(8,128)(2,1)S(1)}, u32[]{:S(2)}, u32[]{:S(2)}) %collective-permute-start) | collective-permute-done | bytes 524320 | tf_op jit(solution)/shard_map/ppermute | solution.py:1510
  990.3 7.5 collective-permute-done.1
  997.7 5.2 collective-permute-done.2
  1003.0 6.7 copy.44
  1009.7 6.7 copy.45
  1019.4 10.9 %all-to-all-done = bf16[32,256,256]{2,1,0:T(8,128)(2,1)} async-done(((bf16[32,256,256]{2,1,0:T(8,128)(2,1)}), bf16[32,256,256]{2,1,0:T(8,128)(2,1)}, u32[]{:S(2)}, u32[]{:S(2)}) %all-to-all-start) | async-done | bytes 4194336 | tf_op jit(solution)/shard_map/all_to_all | solution.py:1784
  (112 shorter events, 75.0 us)
Async XLA Ops:
  7.2 134.0 %all-gather.4.cloned.1.call-start = ((), (), s32[]{:S(2)}) async-start(), calls=%async_computation.4 | async-start | bytes 5242880 | tf_op jit(solution)/shard_map/all_gather | solution.py:1556
  9.6 256.5 %all-gather.6.cloned.1.call-start = ((), (), s32[]{:S(2)}) async-start(), calls=%async_computation.5 | async-start | bytes 10485760 | tf_op jit(solution)/shard_map/all_gather | solution.py:1556
  13.1 4.6 copy-start.10
  14.6 354.8 %all-gather.8.cloned.1.call-start = ((), (), s32[]{:S(2)}) async-start(), calls=%async_computation.6 | async-start | bytes 5242880 | tf_op jit(solution)/shard_map/all_gather | solution.py:1556
  15.9 577.3 %reduce-scatter.6.cloned.1.call-start = ((), (), s32[]{:S(2)}) async-start(), calls=%async_computation.8 | async-start | bytes 5242880 | tf_op jit(solution)/shard_map/reduce_scatter | solution.py:1567
  133.0 5.2 copy-start.6
  472.8 232.7 %reduce-scatter.4.cloned.1.call-start = ((), (), s32[]{:S(2)}) async-start(), calls=%async_computation.7 | async-start | bytes 10485760 | tf_op jit(solution)/shard_map/reduce_scatter | solution.py:1567
  496.7 280.0 %reduce-scatter.8.cloned.1.call-start = ((), (), s32[]{:S(2)}) async-start(), calls=%async_computation.9 | async-start | bytes 5242880 | tf_op jit(solution)/shard_map/reduce_scatter | solution.py:1567
  593.2 27.6 %copy-start.12 = (f32[1,2048]{1,0:T(1,128)S(1)}, f32[1,2048]{1,0:T(1,128)}, u32[]{:S(2)}) copy-start(f32[1,2048]{1,0:T(1,128)} %get-tuple-element.93) | copy-start | bytes 24580
  593.2 27.6 %copy-start.13 = (f32[1,2048]{1,0:T(1,128)S(1)}, f32[1,2048]{1,0:T(1,128)}, u32[]{:S(2)}) copy-start(f32[1,2048]{1,0:T(1,128)} %get-tuple-element.92) | copy-start | bytes 24580
  699.7 5.8 copy-start
  705.5 6.3 copy-start.1
  711.8 67.2 %copy-start.8 = (bf16[256,2048]{1,0:T(8,128)(2,1)S(1)}, bf16[256,2048]{1,0:T(8,128)(2,1)}, u32[]{:S(2)}) copy-start(bf16[256,2048]{1,0:T(8,128)(2,1)} %get-tuple-element.99) | copy-start | bytes 3145732
  714.9 66.9 %slice-start = ((f32[4,4,512,256]{3,2,0,1:T(8,128)}), f32[1,4,512,256]{3,2,0,1:T(8,128)S(1)}, s32[]{:S(2)}) async-start(f32[4,4,512,256]{3,2,0,1:T(8,128)} %copy-done), calls=%async_computation.10 | async-start | bytes 4194304 | tf_op jit(solution)/shard_map/slice | solution.py:1717
  776.7 5.1 copy-start.4
  930.9 99.4 %all-to-all-start = ((bf16[32,256,256]{2,1,0:T(8,128)(2,1)}), bf16[32,256,256]{2,1,0:T(8,128)(2,1)}, u32[]{:S(2)}, u32[]{:S(2)}) async-start(bf16[32,256,256]{2,1,0:T(8,128)(2,1)} %get-tuple-element.114), calls=%async_computation.3 | async-start | bytes 8388608 | tf_op jit(solution)/shard_map/all_to_all | solution.py:1784
  934.8 12.1 %slice-start.1 = ((s8[6291456]{0:T(1024)(128)(4,1)}), s8[4194304]{0:T(1024)(128)(4,1)S(1)}, s32[]{:S(2)}) async-start(s8[6291456]{0:T(1024)(128)(4,1)} %bitcast.114), calls=%async_computation.11 | async-start | bytes 8388608
  938.1 6.5 copy-start.3
  938.1 8.8 slice-start.2
  938.3 52.0 %collective-permute-start = (bf16[2,64,2048]{2,1,0:T(8,128)(2,1)S(1)}, bf16[2,64,2048]{2,1,0:T(8,128)(2,1)S(1)}, u32[]{:S(2)}, u32[]{:S(2)}) collective-permute-start(bf16[2,64,2048]{2,1,0:T(8,128)(2,1)S(1)} %get-tuple-element.162), channel_id=1, source_target_pairs={{0,2},{1,3},{2,4},{3,5},{4,6},{5,7},{6,0},{7,1},{8,10},{9,11},{10,... | collective-permute-start | bytes 1572872 | tf_op jit(solution)/shard_map/ppermute | solution.py:1510
  940.0 57.7 %collective-permute-start.1 = (bf16[2,64,2048]{2,1,0:T(8,128)(2,1)S(1)}, bf16[2,64,2048]{2,1,0:T(8,128)(2,1)S(1)}, u32[]{:S(2)}, u32[]{:S(2)}) collective-permute-start(bf16[2,64,2048]{2,1,0:T(8,128)(2,1)S(1)} %get-tuple-element.161), channel_id=1, source_target_pairs={{0,4},{1,5},{2,6},{3,7},{4,0},{5,1},{6,2},{7,3},{8,12},{9,13},{10,... | collective-permute-start | bytes 1572872 | tf_op jit(solution)/shard_map/ppermute | solution.py:1510
  941.5 61.5 %collective-permute-start.2 = (bf16[2,64,2048]{2,1,0:T(8,128)(2,1)S(1)}, bf16[2,64,2048]{2,1,0:T(8,128)(2,1)S(1)}, u32[]{:S(2)}, u32[]{:S(2)}) collective-permute-start(bf16[2,64,2048]{2,1,0:T(8,128)(2,1)S(1)} %get-tuple-element.160), channel_id=1, source_target_pairs={{0,6},{1,7},{2,0},{3,1},{4,2},{5,3},{6,4},{7,5},{8,14},{9,15},{10,... | collective-permute-start | bytes 1572872 | tf_op jit(solution)/shard_map/ppermute | solution.py:1510
  1003.0 6.8 slice-start.3
  1003.0 6.8 slice-start.4
  (5 other events, 13.1 us)
Sparse Core Ops, SparseCore 0:
  10.2 105.7 all-gather.3
  118.0 147.9 all-gather.5
  268.2 101.1 all-gather.7
  472.9 76.0 reduce-scatter.5
  551.4 144.9 reduce-scatter.3
  699.2 77.4 reduce-scatter.7

commit v10 on v9

--- a/solution.py
+++ b/solution.py
@@ -1214,10 +1214,19 @@
     )(view, view, view, qr, kr, gm.reshape(flat), lse_in, st, gq, gk, cos, sin, pos, posc)
 
 
+class Sides:
+    def __init__(self, out, into):
+        self.out, self.into = out, into
+
+    def wait(self):
+        self.out.wait_send()
+        self.into.wait_recv()
+
+
 def newton_kernel(
-    C, m_ref, rows_ref, gain_ref, grad_ref, out_ref, stage_ref, gsum_ref, back_ref,
+    C, m_ref, res_ref, gin_ref, gain_ref, grad_ref, late_ref, out_ref, stage_ref, gsum_ref, back_ref,
     v, gram, y, yf, stat, gains, gsum,
-    lsem, osem, vsend, vrecv, ysend, yrecv, ssend, srecv, tsend, trecv, gsend, grecv, usend, urecv, usem, bsend, brecv,
+    lsem, osem, vsend, vrecv, ysend, yrecv, ssend, srecv, tsend, trecv, gsend, grecv, usend, urecv, usem, bsend, brecv, isend, irecv,
 ):
     me = lax.axis_index("fsdp")
     z = lax.axis_index("ctx")
@@ -1233,36 +1242,53 @@
         pl.semaphore_signal(barrier, inc=1, device_id={"fsdp": (me + k) % F}, device_id_type=MESH)
     pl.semaphore_wait(barrier, C + F - 2)
     rows_in = v.shape[1] // C
+    def fellow(a, other):
+        to = partner(chip, a) if a else chip
+        return 2 * to + (1 - core if other else core)
+
     units_sent, units_kept = [], []
-    for k in range(F):
-        to = (me + k) % F
-        for b in range(C):
-            src = m_ref.at[to // 2, pl.ds((2 * b + to % 2) * rows_in, rows_in)]
-            dst = v.at[0, pl.ds(b * rows_in, rows_in), pl.ds(me * cols, cols)]
-            if k == 0:
-                units_kept.append(local(src, dst, usem, b))
-            else:
-                c = remote(src, dst, usend, urecv, k * C + b, to)
-                c.start()
-                units_sent.append(c)
-    piece = rows_ref.shape[1] // C
+    for a in (3, 1, 2, 0):
+        for other in range(2):
+            to = fellow(a, other)
+            for b in range(C):
+                src = m_ref.at[to // 2, pl.ds((2 * b + to % 2) * rows_in, rows_in)]
+                dst = v.at[0, pl.ds(b * rows_in, rows_in), pl.ds(me * cols, cols)]
+                if a == 0 and other == 0:
+                    units_kept.append(local(src, dst, usem, b))
+                else:
+                    c = remote(src, dst, usend, urecv, (2 * a + other) * C + b, to)
+                    c.start()
+                    units_sent.append(c)
+    piece = res_ref.shape[0] // C
 
     def part(j):
         return pl.ds(j * piece, piece)
 
-    sent, keep = [], [local(grad_ref.at[z], back_ref.at[z], lsem, 4)]
-    for k in FAR_FIRST:
-        to = partner(z, k)
-        c = remote(grad_ref.at[to], back_ref.at[z], bsend, brecv, k, to, "ctx")
-        c.start()
-        sent.append(c)
-    for a in range(2):
+    late = grad_ref.shape[2]
+
+    def back_to(layer, frm, k, kind):
+        if kind == 0:
+            src = late_ref.at[pl.ds(pl.multiple_of(layer * late, late), late)]
+            return src, back_ref.at[frm, 0], k
+        return grad_ref.at[layer], back_ref.at[frm, pl.ds(1, grad_ref.shape[1])], C + k
+
+    sent, keep = [], []
+    for kind in range(2):
+        src, dst, _ = back_to(z, z, 0, kind)
+        keep.append(local(src, dst, lsem, (0, 4)[kind]))
         for k in FAR_FIRST:
             to = partner(z, k)
-            c = remote(rows_ref.at[a, part(to)], stage_ref.at[a, z], tsend, trecv, C * a + k, to, "ctx")
+            src, dst, i = back_to(to, z, k, kind)
+            c = remote(src, dst, bsend, brecv, i, to, "ctx")
             c.start()
             sent.append(c)
-        keep.append(local(rows_ref.at[a, part(z)], stage_ref.at[a, z], lsem, 2 + a))
+    for a, rows_ref in enumerate((res_ref, gin_ref)):
+        for k in FAR_FIRST:
+            to = partner(z, k)
+            c = remote(rows_ref.at[part(to)], stage_ref.at[a, z], tsend, trecv, C * a + k, to, "ctx")
+            c.start()
+            sent.append(c)
+        keep.append(local(rows_ref.at[part(z)], stage_ref.at[a, z], lsem, 2 + a))
     gload.wait()
     for k in range(1, C):
         c = remote(gains.at[z], gains.at[z], gsend, grecv, k, (z + k) % C, "ctx")
@@ -1272,9 +1298,10 @@
     def rows_arrived():
         for c in keep:
             c.wait()
-        for k in FAR_FIRST:
-            dst = back_ref.at[partner(z, k)]
-            remote(dst, dst, bsend, brecv, k, partner(z, k), "ctx").wait_recv()
+        for kind in range(2):
+            for k in FAR_FIRST:
+                _, dst, i = back_to(z, partner(z, k), k, kind)
+                remote(dst, dst, bsend, brecv, i, partner(z, k), "ctx").wait_recv()
         for a in range(2):
             for k in FAR_FIRST:
                 dst = stage_ref.at[a, partner(z, k)]
@@ -1287,15 +1314,38 @@
         for c in sent:
             c.wait_send()
 
-    for k in range(1, F):
-        frm = (me - k + F) % F
-        for b in range(C):
-            dst = v.at[0, pl.ds(b * rows_in, rows_in), pl.ds(frm * cols, cols)]
-            remote(dst, dst, usend, urecv, k * C + b, frm).wait_recv()
+    stat[0] = jnp.zeros_like(stat[0])
+
+    def columns(owner):
+        return pl.ds(pl.multiple_of(owner * cols, cols), cols)
+
+    def pass_on(a, other, owner=None):
+        i = 2 * a + other
+        c = columns(fellow(a, other if owner is None else owner))
+        return remote(v.at[0, :, c], v.at[1, :, c], isend, irecv, i, peer)
+
+    pending = []
+    for a in range(C):
+        for other in range(2):
+            frm = fellow(a, other)
+            if a == 0 and other == 0:
+                for c in units_kept:
+                    c.wait()
+            else:
+                for b in range(C):
+                    dst = v.at[0, pl.ds(b * rows_in, rows_in), columns(frm)]
+                    remote(dst, dst, usend, urecv, (2 * a + other) * C + b, frm).wait_recv()
+            c = pass_on(a, other)
+            c.start()
+            pending.append(Sides(c, pass_on(a, other, 1 - other)))
+
+            @pl.loop(0, v.shape[1] // 128)
+            def _(r):
+                block = v[0, pl.ds(pl.multiple_of(r * 128, 128), 128), columns(frm)].astype(f32)
+                stat[0] += jnp.sum((block * block).reshape(-1, 8, cols // 128, 128), axis=(0, 2))
+
     for c in units_sent:
         c.wait_send()
-    for c in units_kept:
-        c.wait()
     M, D = v.shape[1], v.shape[2]
     tile, col = 512, 1024
     tiles = M // tile
@@ -1309,16 +1359,6 @@
         part = (block(i), pl.ds(n * col, col))
         return remote(buf.at[(0, *part)], buf.at[(1, *part)], sends, recvs, n * tiles + i, peer)
 
-    pending = [swap(v, n, i, vsend, vrecv) for n in range(halves) for i in range(tiles)]
-    for c in pending:
-        c.start()
-    stat[0] = jnp.zeros_like(stat[0])
-
-    def add(r):
-        part = v[0, r, :].astype(f32)
-        stat[0] += jnp.sum((part * part).reshape(-1, 8, D // 128, 128), axis=(0, 2))
-
-    row_loop(M, add)
     share = remote(stat.at[0], stat.at[1], ssend, srecv, 0, peer)
     share.start()
     share.wait()
@@ -1396,10 +1436,10 @@
         c.wait()
 
 
-def newton_call(C, x, rows, gains, grads):
+def newton_call(C, x, result, grad_rows, gains, grads, late):
     _, D, cols = x.shape
     M = D // 2
-    _, R, _ = rows.shape
+    R = result.shape[0]
     n = 4
     return pl.pallas_call(
         functools.partial(newton_kernel, C),
@@ -1407,9 +1447,9 @@
             jax.ShapeDtypeStruct((2 * C * C, M // C, cols), bf16),
             jax.ShapeDtypeStruct((2, C, R // C, D), bf16),
             jax.ShapeDtypeStruct((8, D), f32),
-            jax.ShapeDtypeStruct(grads.shape, bf16),
+            jax.ShapeDtypeStruct((C, C, *grads.shape[2:]), bf16),
         ],
-        in_specs=[ANY] * 4,
+        in_specs=[ANY] * 6,
         out_specs=[ANY] * 4,
         scratch_shapes=[
             pltpu.VMEM((2, M, D), bf16),
@@ -1420,11 +1460,11 @@
             pltpu.VMEM((C, 8, D), f32),
             pltpu.VMEM((8, D), f32),
             dma(7), dma(2 * C * C), dma(n), dma(n), dma(n), dma(n), dma(1), dma(1),
-            dma(2 * C), dma(2 * C), dma(C), dma(C), dma(2 * C * C), dma(2 * C * C), dma(C), dma(C), dma(C),
+            dma(2 * C), dma(2 * C), dma(C), dma(C), dma(2 * C * C), dma(2 * C * C), dma(C), dma(2 * C), dma(2 * C), dma(2 * C), dma(2 * C),
         ],
         compiler_params=params(6),
         cost_estimate=cost(95),
-    )(x, rows, gains, grads)
+    )(x, result, grad_rows, gains, grads, late)
 
 
 def project(C, F, x, w):
@@ -1711,17 +1751,16 @@
         gain_total = jnp.sum(lax.all_gather(gain_local, BOTH, axis=0, tiled=False), axis=0)
 
     if kernels:
-        early = jnp.stack([jnp.zeros_like(g_down[0]), g_gate_up[0], g_gate_up[1], g_down[0]])
-        mom = momentum * mom_own.reshape(early.shape).astype(f32)
-        owned = (mom + early.astype(f32)).astype(bf16)
+        early = jnp.stack([g_gate_up[0], g_gate_up[1], g_down[0]])
+        mom = momentum * mom_own.reshape(UNITS_ATTN, width, head_cols).astype(f32)
+        owned = jnp.concatenate([jnp.zeros_like(early[:1]), (mom[1:] + early.astype(f32)).astype(bf16)], axis=0)
         mom_first = mom[0]
-        early = jnp.swapaxes(early.reshape(UNITS_ATTN, C, dz, head_cols), 0, 1)
+        early = jnp.swapaxes(early.reshape(3, C, dz, head_cols), 0, 1)
         early, owned, mom_first, grad_rows = lax.optimization_barrier((early, owned, mom_first, grad_rows))
         late = (mom_first + g_attn[0].astype(f32)).astype(bf16)
         owned = lax.dynamic_update_slice(owned, late[None], (0, 0, 0))
-        got = lax.dynamic_update_slice(early, g_attn.reshape(C, 1, dz, head_cols), (0, 0, 0, 0))
         own, leaving, gain_total, sent_back = newton_call(
-            C, owned, jnp.stack([result, grad_rows]), gain_layer, got
+            C, owned, result, grad_rows, gain_layer, early, g_attn[0]
         )
         sent_back = sent_back.astype(f32)
         grad_attn = sent_back[:, 0]

time: 1050 us -> 1050 us (level)
    unnamed x43 -> x37, local copies, waits for them, and re-layouts: 25.1 us -> 26.2 us
  transfers between devices with their start and end apart: 10 -> 10, of which waited for: 7 -> 7; matrix products, arithmetic and copies ran while one was open for 7% -> 7% of each run, Pallas kernels for 46% -> 47%
where the time goes in v10:
time: 1050 us
  Pallas kernels  738 us (70%)
  waiting for transfers between devices  193 us (18%)
  local copies, waits for them, and re-layouts  47.9 us (5%)
  other arithmetic  41.8 us (4%)
  between operations  15 us (1%)
    pallas_call x1, Pallas kernels, newton_call(): pl.pallas_call(functools.partial(newton_kernel, C), out_shape=[jax.ShapeD...  148 us
    pallas_call x1, Pallas kernels, enter_call(): pl.pallas_call(functools.partial(enter_kernel, C), out_shape=[jax.ShapeDt...  109 us
    pallas_call x1, Pallas kernels, down_call(): pl.pallas_call(functools.partial(down_kernel, C), out_shape=[one, jax.Sha...  103 us
    pallas_call x1, Pallas kernels, mid_call(): pl.pallas_call(mid_kernel, out_shape=[jax.ShapeDtypeStruct((R, D), f32),...  96.4 us
    pallas_call x1, Pallas kernels, up_call(): pl.pallas_call(functools.partial(up_kernel, C), out_shape=[jax.ShapeDtype...  70 us
    all_gather x3, waiting for transfers between devices, rows_gather(): return lax.all_gather(shard, 'ctx', axis=0, tiled=True)  69.9 us
    reduce_scatter x3, waiting for transfers between devices, scatter(): return lax.psum_scatter(grad, 'ctx', scatter_dimension=0, tiled=True)[0]  61.1 us
    pallas_call x1, Pallas kernels, last_call(): pl.pallas_call(functools.partial(last_kernel, D), out_shape=[jax.ShapeDty...  60.8 us
  transfers between devices with their start and end apart: 10, of which 7 were waited for; matrix products, arithmetic and copies ran while one was open for 7% of the time, Pallas kernels for 47%

profile of v10, /device:TPU:0, one launch (start us, length us, event | category | flops | bytes accessed | tf_op | source)
XLA Modules:
  0.0 1045.1 jit_solution(9803278801439444361)
XLA Ops:
  18.2 109.4 %shard_map.176 = (bf16[256,2048]{1,0:T(8,128)(2,1)}, bf16[8,256,2048]{2,1,0:T(8,128)(2,1)}) custom-call(bf16[256,2048]{1,0:T(8,128)(2,1)} %bitcast.131), custom_call_target="tpu_custom_call" | custom-call | flops 70000001024 | bytes 1048576 | tf_op jit(solution)/shard_map/pallas_call | solution.py:429
  127.6 4.3 copy.57
  133.4 4.9 sine_multiply_fusion
  141.2 22.6 %shard_map.177 = (f32[2048,768]{1,0:T(8,128)}, f32[8,8,2048]{2,1,0:T(8,128)}) custom-call(bf16[8,256,2048]{2,1,0:T(8,128)(2,1)} %get-tuple-element.63.all_ref, bf16[2048,1024]{1,0:T(8,128)(2,1)} %all-gather.4.cloned.1.call-done.w_ref.wo_ref), custom_call_target="tpu_custom_call" | custom-call | flops 22000001024 | bytes 1048576 | tf_op jit(solution)/shard_map/pallas_call | solution.py:492
  165.2 17.7 %shard_map.178 = (bf16[4,2,256,256]{3,2,1,0:T(8,128)(2,1)}, bf16[4,2,256,256]{3,2,1,0:T(8,128)(2,1)}, bf16[4,2,256,256]{3,2,1,0:T(8,128)(2,1)}, f32[2,2,1024,128]{3,2,1,0:T(8,128)}) custom-call(f32[4,2,256,768]{3,2,1,0:T(8,128)} %bitcast.136, f32[4,2,256,768]{3,2,1,0:T(8,128)} %bitcast.137, f32[4,2,256,768]{3,2,1,0:T(8,128)} %bitcast.138, ...), custom_call_target="tpu_custom_call" | custom-call | flops 15000000512 | bytes 1048576 | tf_op jit(solution)/shard_map/pallas_call | solution.py:1134
  182.9 46.6 %shard_map.179 = (f32[256,2048]{1,0:T(8,128)}, f32[256,2048]{1,0:T(8,128)}, bf16[256,2048]{1,0:T(8,128)(2,1)}) custom-call(bf16[2048,256]{1,0:T(8,128)(2,1)} %bitcast.144, bf16[2048,1024]{1,0:T(8,128)(2,1)} %all-gather.4.cloned.1.call-done.w_ref.wo_ref, bf16[256,2048]{1,0:T(8,128)(2,1)} %get-tuple-element.67.x_ref, f32[1,2048]{1,0:T(1,128)} %get-tuple-element.177.gain_ref), custom_call_target="tpu_custom_call" | custom-call | flops 46000001024 | bytes 1048576 | tf_op jit(solution)/shard_map/pallas_call | solution.py:547
  229.5 36.5 %all-gather.6.cloned.1.call-done.w_ref = bf16[2048,2048]{1,0:T(8,128)(2,1)} async-done(((bf16[512,2048]{1,0:T(8,128)(2,1)}), bf16[2048,2048]{1,0:T(8,128)(2,1)}) %all-gather.6.cloned.1.call-update) | async-done | bytes 8388624 | tf_op jit(solution)/shard_map/all_gather | solution.py:1596
  266.1 70.0 %shard_map.180 = (bf16[8,256,2048]{2,1,0:T(8,128)(2,1)}, bf16[2048,1024]{1,0:T(8,128)(2,1)}, bf16[2048,1024]{1,0:T(8,128)(2,1)}, bf16[2048,1024]{1,0:T(8,128)(2,1)}, bf16[256,2048]{1,0:T(8,128)(2,1)}) custom-call(bf16[256,2048]{1,0:T(8,128)(2,1)} %get-tuple-element.68.in_ref, bf16[2048,2048]{1,0:T(8,128)(2,1)} %all-gather.6.cloned.1.call-done.w_ref, ...), custom_call_target="tpu_custom_call" | custom-call | flops 56000000000 | bytes 1048576 | tf_op jit(solution)/shard_map/pallas_call | solution.py:636
  336.1 33.4 %all-gather.8.cloned.1.call-done.wd_ref = bf16[2048,1024]{1,0:T(8,128)(2,1)} async-done(((bf16[512,1024]{1,0:T(8,128)(2,1)}), bf16[2048,1024]{1,0:T(8,128)(2,1)}) %all-gather.8.cloned.1.call-update) | async-done | bytes 4194320 | tf_op jit(solution)/shard_map/all_gather | solution.py:1596
  369.5 103.4 %shard_map.181 = (bf16[256,2048]{1,0:T(8,128)(2,1)}, f32[1,2048]{1,0:T(1,128)}, bf16[8,256,2048]{2,1,0:T(8,128)(2,1)}, bf16[2048,2048]{1,0:T(8,128)(2,1)}, bf16[...) custom-call(bf16[2048,1024]{1,0:T(8,128)(2,1)} %get-tuple-element.69.h_ref, ...), custom_call_target="tpu_custom_call" | custom-call | flops 108000002048 | bytes 1048576 | tf_op jit(solution)/shard_map/pallas_call | solution.py:786
  472.9 23.8 %shard_map.182 = bf16[4,2,2048,256]{3,2,1,0:T(8,128)(2,1)} custom-call(bf16[2048,2048]{1,0:T(8,128)(2,1)} %bitcast.135, bf16[2048,2048]{1,0:T(8,128)(2,1)} %get-tuple-element.81.refs_1_.grad_ref), custom_call_target="tpu_custom_call" | custom-call | flops 24000000000 | bytes 1048576 | tf_op jit(solution)/shard_map/pallas_call | solution.py:1030
  496.8 96.4 %shard_map.183 = (f32[256,2048]{1,0:T(8,128)}, f32[1,2048]{1,0:T(1,128)}, bf16[8,256,2048]{2,1,0:T(8,128)(2,1)}, bf16[2048,256]{1,0:T(8,128)(2,1)}) custom-call(bf16[2048,2048]{1,0:T(8,128)(2,1)} %get-tuple-element.81.refs_1_.grad_ref, bf16[2048,2048]{1,0:T(8,128)(2,1)} %all-gather.6.cloned.1.call-done.w_ref, bf16[256,2048]{1,0:T(8,128)(2,1)} %get-tuple-element.71.cot_ref, ...), custom_call_target="tpu_custom_call" | custom-call | flops 92000002048 | bytes 1048576 | tf_op jit(solution)/shard_map/pallas_call | solution.py:882
  593.3 25.1 %shard_map.184 = (f32[4,2,256,256]{3,2,1,0:T(8,128)}, f32[4,2,256,256]{3,2,1,0:T(8,128)}, bf16[4,2,256,256]{3,2,1,0:T(8,128)(2,1)}, f32[2,2,8,1024]{3,2,1,0:T(8,128)}, f32[2,2,8,128]{3,2,1,0:T(8,128)}) custom-call(f32[4,2,256,768]{3,2,1,0:T(8,128)} %bitcast.139, f32[4,2,256,768]{3,2,1,0:T(8,128)} %bitcast.140, f32[4,2,256,768]{3,2,1,0:T(8,128)} %bitcast.141, ...), custom_call_target="tpu_custom_call" | custom-call | flops 35000000512 | bytes 1048576 | tf_op jit(solution)/shard_map/pallas_call | solution.py:1199
  621.5 60.8 %shard_map.185 = (bf16[256,2048]{1,0:T(8,128)(2,1)}, bf16[2048,768]{1,0:T(8,128)(2,1)}, f32[8,2048]{1,0:T(8,128)}) custom-call(f32[2048,256]{1,0:T(8,128)} %bitcast.142, f32[2048,256]{1,0:T(8,128)} %bitcast.143, bf16[2048,256]{1,0:T(8,128)(2,1)} %bitcast.146, f32[2048,768]{1,0:T(8,128)} %get-tuple-element.64.proj_ref, ...), custom_call_target="tpu_custom_call" | custom-call | flops 54999998464 | bytes 1048576 | tf_op jit(solution)/shard_map/pallas_call | solution.py:976
  682.3 14.3 %shard_map.186 = bf16[4,1,2048,256]{3,2,1,0:T(8,128)(2,1)} custom-call(bf16[2048,2048]{1,0:T(8,128)(2,1)} %bitcast.133, bf16[2048,768]{1,0:T(8,128)(2,1)} %get-tuple-element.97.refs_1_, bf16[2048,2048]{1,0:T(8,128)(2,1)} %bitcast.134, bf16[2048,256]{1,0:T(8,128)(2,1)} %bitcast.145), custom_call_target="tpu_custom_call" | custom-call | flops 12000000000 | bytes 1048576 | tf_op jit(solution)/shard_map/pallas_call | solution.py:1030
  715.7 61.1 %reduce-scatter.8.cloned.1.call-done = bf16[1,1,2048,256]{3,2,1,0:T(8,128)(2,1)} async-done(((bf16[4,1,2048,256]{3,2,1,0:T(8,128)(2,1)}), bf16[1,1,2048,256]{3,2,1,0:T(8,128)(2,1)}) %reduce-scatter.8.cloned.1.call-update) | async-done | bytes 1048592 | tf_op jit(solution)/shard_map/reduce_scatter | solution.py:1607
  779.2 147.9 %shard_map.187 = (bf16[32,256,256]{2,1,0:T(8,128)(2,1)}, bf16[2,4,64,2048]{3,2,1,0:T(8,128)(2,1)}, f32[8,2048]{1,0:T(8,128)}, bf16[4,4,512,256]{3,2,1,0:T(8,128)(2,1)}) custom-call(bf16[4,2048,256]{2,1,0:T(8,128)(2,1)} %fusion.3.m_ref, bf16[256,2048]{1,0:T(8,128)(2,1)} %get-tuple-element.99.res_ref, bf16[256,2048]{1,0:T(8,128)(2,1)} %get-tuple-element.100.gin_ref, ...), custom_call_target="tpu_custom_call" | custom-call | flops 95000002560 | bytes 1048576 | tf_op jit(solution)/shard_map/pallas_call | solution.py:1444
  943.1 4.3 multiply_add_fusion
  947.9 38.6 %collective-permute-done = bf16[2,64,2048]{2,1,0:T(8,128)(2,1)S(1)} collective-permute-done((bf16[2,64,2048]{2,1,0:T(8,128)(2,1)S(1)}, bf16[2,64,2048]{2,1,0:T(8,128)(2,1)S(1)}, u32[]{:S(2)}, u32[]{:S(2)}) %collective-permute-start) | collective-permute-done | bytes 524320 | tf_op jit(solution)/shard_map/ppermute | solution.py:1550
  986.5 7.5 collective-permute-done.1
  994.0 5.2 collective-permute-done.2
  999.2 6.7 copy.44
  1006.0 6.7 copy.45
  1015.6 10.9 %all-to-all-done = bf16[32,256,256]{2,1,0:T(8,128)(2,1)} async-done(((bf16[32,256,256]{2,1,0:T(8,128)(2,1)}), bf16[32,256,256]{2,1,0:T(8,128)(2,1)}, u32[]{:S(2)}, u32[]{:S(2)}) %all-to-all-start) | async-done | bytes 4194336 | tf_op jit(solution)/shard_map/all_to_all | solution.py:1823
  (104 shorter events, 71.7 us)
Async XLA Ops:
  7.2 134.0 %all-gather.4.cloned.1.call-start = ((), (), s32[]{:S(2)}) async-start(), calls=%async_computation.4 | async-start | bytes 5242880 | tf_op jit(solution)/shard_map/all_gather | solution.py:1596
  9.6 256.5 %all-gather.6.cloned.1.call-start = ((), (), s32[]{:S(2)}) async-start(), calls=%async_computation.5 | async-start | bytes 10485760 | tf_op jit(solution)/shard_map/all_gather | solution.py:1596
  14.6 3.0 copy-start.9
  14.6 354.9 %all-gather.8.cloned.1.call-start = ((), (), s32[]{:S(2)}) async-start(), calls=%async_computation.6 | async-start | bytes 5242880 | tf_op jit(solution)/shard_map/all_gather | solution.py:1596
  15.9 577.4 %reduce-scatter.6.cloned.1.call-start = ((), (), s32[]{:S(2)}) async-start(), calls=%async_computation.8 | async-start | bytes 5242880 | tf_op jit(solution)/shard_map/reduce_scatter | solution.py:1607
  127.6 4.3 copy-start.3
  133.0 5.2 copy-start.6
  472.9 233.8 %reduce-scatter.4.cloned.1.call-start = ((), (), s32[]{:S(2)}) async-start(), calls=%async_computation.7 | async-start | bytes 10485760 | tf_op jit(solution)/shard_map/reduce_scatter | solution.py:1607
  496.7 280.0 %reduce-scatter.8.cloned.1.call-start = ((), (), s32[]{:S(2)}) async-start(), calls=%async_computation.9 | async-start | bytes 5242880 | tf_op jit(solution)/shard_map/reduce_scatter | solution.py:1607
  593.3 27.6 %copy-start.11 = (f32[1,2048]{1,0:T(1,128)S(1)}, f32[1,2048]{1,0:T(1,128)}, u32[]{:S(2)}) copy-start(f32[1,2048]{1,0:T(1,128)} %get-tuple-element.93) | copy-start | bytes 24580
  593.3 27.6 %copy-start.12 = (f32[1,2048]{1,0:T(1,128)S(1)}, f32[1,2048]{1,0:T(1,128)}, u32[]{:S(2)}) copy-start(f32[1,2048]{1,0:T(1,128)} %get-tuple-element.92) | copy-start | bytes 24580
  699.7 3.3 copy-start
  703.0 5.6 copy-start.5
  706.7 3.4 copy-start.1
  713.7 63.1 %slice-start = ((f32[4,4,512,256]{3,2,0,1:T(8,128)}), f32[1,4,512,256]{3,2,0,1:T(8,128)S(1)}, s32[]{:S(2)}) async-start(f32[4,4,512,256]{3,2,0,1:T(8,128)} %copy-done), calls=%async_computation.10 | async-start | bytes 4194304 | tf_op jit(solution)/shard_map/slice | solution.py:1757
  927.2 99.4 %all-to-all-start = ((bf16[32,256,256]{2,1,0:T(8,128)(2,1)}), bf16[32,256,256]{2,1,0:T(8,128)(2,1)}, u32[]{:S(2)}, u32[]{:S(2)}) async-start(bf16[32,256,256]{2,1,0:T(8,128)(2,1)} %get-tuple-element.114), calls=%async_computation.3 | async-start | bytes 8388608 | tf_op jit(solution)/shard_map/all_to_all | solution.py:1823
  931.1 3.3 copy-start.7
  931.1 12.1 %slice-start.1 = ((s8[6291456]{0:T(1024)(128)(4,1)}), s8[4194304]{0:T(1024)(128)(4,1)S(1)}, s32[]{:S(2)}) async-start(s8[6291456]{0:T(1024)(128)(4,1)} %bitcast.108), calls=%async_computation.11 | async-start | bytes 8388608
  934.3 8.8 slice-start.2
  934.5 6.4 copy-start.4
  934.5 52.0 %collective-permute-start = (bf16[2,64,2048]{2,1,0:T(8,128)(2,1)S(1)}, bf16[2,64,2048]{2,1,0:T(8,128)(2,1)S(1)}, u32[]{:S(2)}, u32[]{:S(2)}) collective-permute-start(bf16[2,64,2048]{2,1,0:T(8,128)(2,1)S(1)} %get-tuple-element.162), channel_id=1, source_target_pairs={{0,2},{1,3},{2,4},{3,5},{4,6},{5,7},{6,0},{7,1},{8,10},{9,11},{10,... | collective-permute-start | bytes 1572872 | tf_op jit(solution)/shard_map/ppermute | solution.py:1550
  936.3 57.7 %collective-permute-start.1 = (bf16[2,64,2048]{2,1,0:T(8,128)(2,1)S(1)}, bf16[2,64,2048]{2,1,0:T(8,128)(2,1)S(1)}, u32[]{:S(2)}, u32[]{:S(2)}) collective-permute-start(bf16[2,64,2048]{2,1,0:T(8,128)(2,1)S(1)} %get-tuple-element.161), channel_id=1, source_target_pairs={{0,4},{1,5},{2,6},{3,7},{4,0},{5,1},{6,2},{7,3},{8,12},{9,13},{10,... | collective-permute-start | bytes 1572872 | tf_op jit(solution)/shard_map/ppermute | solution.py:1550
  937.7 61.5 %collective-permute-start.2 = (bf16[2,64,2048]{2,1,0:T(8,128)(2,1)S(1)}, bf16[2,64,2048]{2,1,0:T(8,128)(2,1)S(1)}, u32[]{:S(2)}, u32[]{:S(2)}) collective-permute-start(bf16[2,64,2048]{2,1,0:T(8,128)(2,1)S(1)} %get-tuple-element.160), channel_id=1, source_target_pairs={{0,6},{1,7},{2,0},{3,1},{4,2},{5,3},{6,4},{7,5},{8,14},{9,15},{10,... | collective-permute-start | bytes 1572872 | tf_op jit(solution)/shard_map/ppermute | solution.py:1550
  999.2 6.8 copy-start.2
  (2 other events, 3.2 us)
Sparse Core Ops, SparseCore 0:
  10.2 105.7 all-gather.3
  118.0 147.9 all-gather.5
  268.2 101.1 all-gather.7
  473.0 76.0 reduce-scatter.5
  551.4 144.9 reduce-scatter.3
  699.3 77.4 reduce-scatter.7

commit v11 on v10

--- a/solution.py
+++ b/solution.py
@@ -659,7 +659,7 @@
 def down_kernel(
     C, h_ref, wd_ref, hid_ref, cot_ref, gain_ref, act_ref, der_ref, unit_ref,
     res_ref, gg_ref, all_ref, grad_ref, mom_ref, p_ref,
-    h, wd, hid, cot, gain, act, der, res, gacc, rows, grad, prod, b0, b1, b2, b3, b4,
+    h, wd, hid, cot, gain, act, der, res, gacc, rows, grad, prod, acc, b0, b1, b2, b3, b4,
     lsem, osem, asem, psem, send, recv, usend, urecv,
 ):
     at = Plane()
@@ -733,6 +733,18 @@
             grad[s, pl.ds(0, m), up] = (gh * act[s, pl.ds(0, m), c].astype(f32)).astype(bf16)
             grad[s, pl.ds(0, m), c] = (gh * der[s, pl.ds(0, m), c].astype(f32)).astype(bf16)
 
+        begun = len(stores.steps) > 0
+        part = prod.shape[1]
+
+        @pl.loop(0, rows.shape[2] // part)
+        def _(t):
+            c = pl.ds(pl.multiple_of(t * part, part), part)
+            got = lax.dot_general(
+                rows[pl.ds(first, count), :, c].reshape(m, part), h[pl.ds(start, m), :],
+                (((0,), (0,)), ((), ())), preferred_element_type=f32,
+            )
+            acc[c, :] = acc[c, :] + got if begun else got
+
         stores.put(
             [
                 (grad.at[s, pl.ds(0, m)], grad_ref.at[pl.ds(start, m)]),
@@ -741,17 +753,14 @@
         )
 
     gather_phase(at, rows, send, recv, SCATTER_COPIES, on_rows)
-    F, D = rows.shape[0], rows.shape[2]
+    D = rows.shape[2]
     tile, cols = prod.shape[1], p_ref.shape[3]
     puts = []
     for t in range(D // tile):
         if t >= 2:
             for c in puts[t - 2]:
                 c.wait()
-        rhs = rows[:, :, t * tile : (t + 1) * tile].reshape(F * R, tile)
-        prod[t % 2] = lax.dot_general(
-            rhs, h[...], (((0,), (0,)), ((), ())), preferred_element_type=f32
-        ).astype(bf16)
+        prod[t % 2] = acc[pl.ds(t * tile, tile), :].astype(bf16)
         puts.append(
             [
                 local(
@@ -808,6 +817,7 @@
             pltpu.VMEM((F, R, D), bf16),
             pltpu.VMEM((2, 2 * R, 2 * n), bf16),
             pltpu.VMEM((2, 512, n), bf16),
+            pltpu.VMEM((D, n), f32),
         ]
         + scatter_scratch(R, D)
         + [dma(8), dma(15), dma(10), dma(16), dma(copies), dma(copies), dma(C), dma(C)],

time: 1050 us -> 1050 us (level)
  no operation moved by 1% of the time
where the time goes in v11:
time: 1050 us
  Pallas kernels  739 us (70%)
  waiting for transfers between devices  193 us (18%)
  local copies, waits for them, and re-layouts  47.9 us (5%)
  other arithmetic  41.8 us (4%)
  between operations  15 us (1%)
    pallas_call x1, Pallas kernels, newton_call(): pl.pallas_call(functools.partial(newton_kernel, C), out_shape=[jax.ShapeD...  148 us
    pallas_call x1, Pallas kernels, enter_call(): pl.pallas_call(functools.partial(enter_kernel, C), out_shape=[jax.ShapeDt...  109 us
    pallas_call x1, Pallas kernels, down_call(): pl.pallas_call(functools.partial(down_kernel, C), out_shape=[one, jax.Sha...  104 us
    pallas_call x1, Pallas kernels, mid_call(): pl.pallas_call(mid_kernel, out_shape=[jax.ShapeDtypeStruct((R, D), f32),...  96.3 us
    pallas_call x1, Pallas kernels, up_call(): pl.pallas_call(functools.partial(up_kernel, C), out_shape=[jax.ShapeDtype...  70 us
    all_gather x3, waiting for transfers between devices, rows_gather(): return lax.all_gather(shard, 'ctx', axis=0, tiled=True)  69.9 us
    pallas_call x1, Pallas kernels, last_call(): pl.pallas_call(functools.partial(last_kernel, D), out_shape=[jax.ShapeDty...  61 us
    reduce_scatter x3, waiting for transfers between devices, scatter(): return lax.psum_scatter(grad, 'ctx', scatter_dimension=0, tiled=True)[0]  60.9 us
  transfers between devices with their start and end apart: 10, of which 7 were waited for; matrix products, arithmetic and copies ran while one was open for 7% of the time, Pallas kernels for 47%

profile of v11, /device:TPU:0, one launch (start us, length us, event | category | flops | bytes accessed | tf_op | source)
XLA Modules:
  0.0 1045.5 jit_solution(12207938223195153035)
XLA Ops:
  18.2 109.4 %shard_map.176 = (bf16[256,2048]{1,0:T(8,128)(2,1)}, bf16[8,256,2048]{2,1,0:T(8,128)(2,1)}) custom-call(bf16[256,2048]{1,0:T(8,128)(2,1)} %bitcast.131), custom_call_target="tpu_custom_call" | custom-call | flops 70000001024 | bytes 1048576 | tf_op jit(solution)/shard_map/pallas_call | solution.py:429
  127.6 4.3 copy.57
  133.4 4.9 sine_multiply_fusion
  141.2 22.6 %shard_map.177 = (f32[2048,768]{1,0:T(8,128)}, f32[8,8,2048]{2,1,0:T(8,128)}) custom-call(bf16[8,256,2048]{2,1,0:T(8,128)(2,1)} %get-tuple-element.63.all_ref, bf16[2048,1024]{1,0:T(8,128)(2,1)} %all-gather.4.cloned.1.call-done.w_ref.wo_ref), custom_call_target="tpu_custom_call" | custom-call | flops 22000001024 | bytes 1048576 | tf_op jit(solution)/shard_map/pallas_call | solution.py:492
  165.2 17.7 %shard_map.178 = (bf16[4,2,256,256]{3,2,1,0:T(8,128)(2,1)}, bf16[4,2,256,256]{3,2,1,0:T(8,128)(2,1)}, bf16[4,2,256,256]{3,2,1,0:T(8,128)(2,1)}, f32[2,2,1024,128]{3,2,1,0:T(8,128)}) custom-call(f32[4,2,256,768]{3,2,1,0:T(8,128)} %bitcast.136, f32[4,2,256,768]{3,2,1,0:T(8,128)} %bitcast.137, f32[4,2,256,768]{3,2,1,0:T(8,128)} %bitcast.138, ...), custom_call_target="tpu_custom_call" | custom-call | flops 15000000512 | bytes 1048576 | tf_op jit(solution)/shard_map/pallas_call | solution.py:1144
  182.9 46.6 %shard_map.179 = (f32[256,2048]{1,0:T(8,128)}, f32[256,2048]{1,0:T(8,128)}, bf16[256,2048]{1,0:T(8,128)(2,1)}) custom-call(bf16[2048,256]{1,0:T(8,128)(2,1)} %bitcast.144, bf16[2048,1024]{1,0:T(8,128)(2,1)} %all-gather.4.cloned.1.call-done.w_ref.wo_ref, bf16[256,2048]{1,0:T(8,128)(2,1)} %get-tuple-element.67.x_ref, f32[1,2048]{1,0:T(1,128)} %get-tuple-element.177.gain_ref), custom_call_target="tpu_custom_call" | custom-call | flops 46000001024 | bytes 1048576 | tf_op jit(solution)/shard_map/pallas_call | solution.py:547
  229.5 36.5 %all-gather.6.cloned.1.call-done.w_ref = bf16[2048,2048]{1,0:T(8,128)(2,1)} async-done(((bf16[512,2048]{1,0:T(8,128)(2,1)}), bf16[2048,2048]{1,0:T(8,128)(2,1)}) %all-gather.6.cloned.1.call-update) | async-done | bytes 8388624 | tf_op jit(solution)/shard_map/all_gather | solution.py:1606
  266.1 70.0 %shard_map.180 = (bf16[8,256,2048]{2,1,0:T(8,128)(2,1)}, bf16[2048,1024]{1,0:T(8,128)(2,1)}, bf16[2048,1024]{1,0:T(8,128)(2,1)}, bf16[2048,1024]{1,0:T(8,128)(2,1)}, bf16[256,2048]{1,0:T(8,128)(2,1)}) custom-call(bf16[256,2048]{1,0:T(8,128)(2,1)} %get-tuple-element.68.in_ref, bf16[2048,2048]{1,0:T(8,128)(2,1)} %all-gather.6.cloned.1.call-done.w_ref, ...), custom_call_target="tpu_custom_call" | custom-call | flops 56000000000 | bytes 1048576 | tf_op jit(solution)/shard_map/pallas_call | solution.py:636
  336.1 33.4 %all-gather.8.cloned.1.call-done.wd_ref = bf16[2048,1024]{1,0:T(8,128)(2,1)} async-done(((bf16[512,1024]{1,0:T(8,128)(2,1)}), bf16[2048,1024]{1,0:T(8,128)(2,1)}) %all-gather.8.cloned.1.call-update) | async-done | bytes 4194320 | tf_op jit(solution)/shard_map/all_gather | solution.py:1606
  369.5 104.0 %shard_map.181 = (bf16[256,2048]{1,0:T(8,128)(2,1)}, f32[1,2048]{1,0:T(1,128)}, bf16[8,256,2048]{2,1,0:T(8,128)(2,1)}, bf16[2048,2048]{1,0:T(8,128)(2,1)}, bf16[...) custom-call(bf16[2048,1024]{1,0:T(8,128)(2,1)} %get-tuple-element.69.h_ref, ...), custom_call_target="tpu_custom_call" | custom-call | flops 108000002048 | bytes 1048576 | tf_op jit(solution)/shard_map/pallas_call | solution.py:795
  473.5 23.8 %shard_map.182 = bf16[4,2,2048,256]{3,2,1,0:T(8,128)(2,1)} custom-call(bf16[2048,2048]{1,0:T(8,128)(2,1)} %bitcast.135, bf16[2048,2048]{1,0:T(8,128)(2,1)} %get-tuple-element.81.refs_1_.grad_ref), custom_call_target="tpu_custom_call" | custom-call | flops 24000000000 | bytes 1048576 | tf_op jit(solution)/shard_map/pallas_call | solution.py:1040
  497.3 96.3 %shard_map.183 = (f32[256,2048]{1,0:T(8,128)}, f32[1,2048]{1,0:T(1,128)}, bf16[8,256,2048]{2,1,0:T(8,128)(2,1)}, bf16[2048,256]{1,0:T(8,128)(2,1)}) custom-call(bf16[2048,2048]{1,0:T(8,128)(2,1)} %get-tuple-element.81.refs_1_.grad_ref, bf16[2048,2048]{1,0:T(8,128)(2,1)} %all-gather.6.cloned.1.call-done.w_ref, bf16[256,2048]{1,0:T(8,128)(2,1)} %get-tuple-element.71.cot_ref, ...), custom_call_target="tpu_custom_call" | custom-call | flops 92000002048 | bytes 1048576 | tf_op jit(solution)/shard_map/pallas_call | solution.py:892
  593.7 25.1 %shard_map.184 = (f32[4,2,256,256]{3,2,1,0:T(8,128)}, f32[4,2,256,256]{3,2,1,0:T(8,128)}, bf16[4,2,256,256]{3,2,1,0:T(8,128)(2,1)}, f32[2,2,8,1024]{3,2,1,0:T(8,128)}, f32[2,2,8,128]{3,2,1,0:T(8,128)}) custom-call(f32[4,2,256,768]{3,2,1,0:T(8,128)} %bitcast.139, f32[4,2,256,768]{3,2,1,0:T(8,128)} %bitcast.140, f32[4,2,256,768]{3,2,1,0:T(8,128)} %bitcast.141, ...), custom_call_target="tpu_custom_call" | custom-call | flops 35000000512 | bytes 1048576 | tf_op jit(solution)/shard_map/pallas_call | solution.py:1209
  621.9 61.0 %shard_map.185 = (bf16[256,2048]{1,0:T(8,128)(2,1)}, bf16[2048,768]{1,0:T(8,128)(2,1)}, f32[8,2048]{1,0:T(8,128)}) custom-call(f32[2048,256]{1,0:T(8,128)} %bitcast.142, f32[2048,256]{1,0:T(8,128)} %bitcast.143, bf16[2048,256]{1,0:T(8,128)(2,1)} %bitcast.146, f32[2048,768]{1,0:T(8,128)} %get-tuple-element.64.proj_ref, ...), custom_call_target="tpu_custom_call" | custom-call | flops 54999998464 | bytes 1048576 | tf_op jit(solution)/shard_map/pallas_call | solution.py:986
  682.9 14.3 %shard_map.186 = bf16[4,1,2048,256]{3,2,1,0:T(8,128)(2,1)} custom-call(bf16[2048,2048]{1,0:T(8,128)(2,1)} %bitcast.133, bf16[2048,768]{1,0:T(8,128)(2,1)} %get-tuple-element.97.refs_1_, bf16[2048,2048]{1,0:T(8,128)(2,1)} %bitcast.134, bf16[2048,256]{1,0:T(8,128)(2,1)} %bitcast.145), custom_call_target="tpu_custom_call" | custom-call | flops 12000000000 | bytes 1048576 | tf_op jit(solution)/shard_map/pallas_call | solution.py:1040
  716.3 60.9 %reduce-scatter.8.cloned.1.call-done = bf16[1,1,2048,256]{3,2,1,0:T(8,128)(2,1)} async-done(((bf16[4,1,2048,256]{3,2,1,0:T(8,128)(2,1)}), bf16[1,1,2048,256]{3,2,1,0:T(8,128)(2,1)}) %reduce-scatter.8.cloned.1.call-update) | async-done | bytes 1048592 | tf_op jit(solution)/shard_map/reduce_scatter | solution.py:1617
  779.6 147.9 %shard_map.187 = (bf16[32,256,256]{2,1,0:T(8,128)(2,1)}, bf16[2,4,64,2048]{3,2,1,0:T(8,128)(2,1)}, f32[8,2048]{1,0:T(8,128)}, bf16[4,4,512,256]{3,2,1,0:T(8,128)(2,1)}) custom-call(bf16[4,2048,256]{2,1,0:T(8,128)(2,1)} %fusion.3.m_ref, bf16[256,2048]{1,0:T(8,128)(2,1)} %get-tuple-element.99.res_ref, bf16[256,2048]{1,0:T(8,128)(2,1)} %get-tuple-element.100.gin_ref, ...), custom_call_target="tpu_custom_call" | custom-call | flops 95000002560 | bytes 1048576 | tf_op jit(solution)/shard_map/pallas_call | solution.py:1454
  943.6 4.3 multiply_add_fusion
  948.3 38.6 %collective-permute-done = bf16[2,64,2048]{2,1,0:T(8,128)(2,1)S(1)} collective-permute-done((bf16[2,64,2048]{2,1,0:T(8,128)(2,1)S(1)}, bf16[2,64,2048]{2,1,0:T(8,128)(2,1)S(1)}, u32[]{:S(2)}, u32[]{:S(2)}) %collective-permute-start) | collective-permute-done | bytes 524320 | tf_op jit(solution)/shard_map/ppermute | solution.py:1560
  987.0 7.5 collective-permute-done.1
  994.4 5.2 collective-permute-done.2
  999.7 6.7 copy.44
  1006.4 6.7 copy.45
  1016.0 10.9 %all-to-all-done = bf16[32,256,256]{2,1,0:T(8,128)(2,1)} async-done(((bf16[32,256,256]{2,1,0:T(8,128)(2,1)}), bf16[32,256,256]{2,1,0:T(8,128)(2,1)}, u32[]{:S(2)}, u32[]{:S(2)}) %all-to-all-start) | async-done | bytes 4194336 | tf_op jit(solution)/shard_map/all_to_all | solution.py:1833
  (104 shorter events, 71.7 us)
Async XLA Ops:
  7.2 134.0 %all-gather.4.cloned.1.call-start = ((), (), s32[]{:S(2)}) async-start(), calls=%async_computation.4 | async-start | bytes 5242880 | tf_op jit(solution)/shard_map/all_gather | solution.py:1606
  9.6 256.5 %all-gather.6.cloned.1.call-start = ((), (), s32[]{:S(2)}) async-start(), calls=%async_computation.5 | async-start | bytes 10485760 | tf_op jit(solution)/shard_map/all_gather | solution.py:1606
  14.6 3.0 copy-start.9
  14.6 354.9 %all-gather.8.cloned.1.call-start = ((), (), s32[]{:S(2)}) async-start(), calls=%async_computation.6 | async-start | bytes 5242880 | tf_op jit(solution)/shard_map/all_gather | solution.py:1606
  15.9 577.8 %reduce-scatter.6.cloned.1.call-start = ((), (), s32[]{:S(2)}) async-start(), calls=%async_computation.8 | async-start | bytes 5242880 | tf_op jit(solution)/shard_map/reduce_scatter | solution.py:1617
  127.6 4.3 copy-start.3
  133.0 5.2 copy-start.6
  473.4 233.8 %reduce-scatter.4.cloned.1.call-start = ((), (), s32[]{:S(2)}) async-start(), calls=%async_computation.7 | async-start | bytes 10485760 | tf_op jit(solution)/shard_map/reduce_scatter | solution.py:1617
  497.3 279.9 %reduce-scatter.8.cloned.1.call-start = ((), (), s32[]{:S(2)}) async-start(), calls=%async_computation.9 | async-start | bytes 5242880 | tf_op jit(solution)/shard_map/reduce_scatter | solution.py:1617
  593.6 27.6 %copy-start.11 = (f32[1,2048]{1,0:T(1,128)S(1)}, f32[1,2048]{1,0:T(1,128)}, u32[]{:S(2)}) copy-start(f32[1,2048]{1,0:T(1,128)} %get-tuple-element.93) | copy-start | bytes 24580
  593.7 27.6 %copy-start.12 = (f32[1,2048]{1,0:T(1,128)S(1)}, f32[1,2048]{1,0:T(1,128)}, u32[]{:S(2)}) copy-start(f32[1,2048]{1,0:T(1,128)} %get-tuple-element.92) | copy-start | bytes 24580
  700.3 3.3 copy-start
  703.6 5.6 copy-start.5
  707.3 3.4 copy-start.1
  714.3 62.9 %slice-start = ((f32[4,4,512,256]{3,2,0,1:T(8,128)}), f32[1,4,512,256]{3,2,0,1:T(8,128)S(1)}, s32[]{:S(2)}) async-start(f32[4,4,512,256]{3,2,0,1:T(8,128)} %copy-done), calls=%async_computation.10 | async-start | bytes 4194304 | tf_op jit(solution)/shard_map/slice | solution.py:1767
  927.6 99.4 %all-to-all-start = ((bf16[32,256,256]{2,1,0:T(8,128)(2,1)}), bf16[32,256,256]{2,1,0:T(8,128)(2,1)}, u32[]{:S(2)}, u32[]{:S(2)}) async-start(bf16[32,256,256]{2,1,0:T(8,128)(2,1)} %get-tuple-element.114), calls=%async_computation.3 | async-start | bytes 8388608 | tf_op jit(solution)/shard_map/all_to_all | solution.py:1833
  931.5 3.3 copy-start.7
  931.5 12.1 %slice-start.1 = ((s8[6291456]{0:T(1024)(128)(4,1)}), s8[4194304]{0:T(1024)(128)(4,1)S(1)}, s32[]{:S(2)}) async-start(s8[6291456]{0:T(1024)(128)(4,1)} %bitcast.108), calls=%async_computation.11 | async-start | bytes 8388608
  934.8 8.8 slice-start.2
  934.9 6.4 copy-start.4
  935.0 52.0 %collective-permute-start = (bf16[2,64,2048]{2,1,0:T(8,128)(2,1)S(1)}, bf16[2,64,2048]{2,1,0:T(8,128)(2,1)S(1)}, u32[]{:S(2)}, u32[]{:S(2)}) collective-permute-start(bf16[2,64,2048]{2,1,0:T(8,128)(2,1)S(1)} %get-tuple-element.162), channel_id=1, source_target_pairs={{0,2},{1,3},{2,4},{3,5},{4,6},{5,7},{6,0},{7,1},{8,10},{9,11},{10,... | collective-permute-start | bytes 1572872 | tf_op jit(solution)/shard_map/ppermute | solution.py:1560
  936.7 57.7 %collective-permute-start.1 = (bf16[2,64,2048]{2,1,0:T(8,128)(2,1)S(1)}, bf16[2,64,2048]{2,1,0:T(8,128)(2,1)S(1)}, u32[]{:S(2)}, u32[]{:S(2)}) collective-permute-start(bf16[2,64,2048]{2,1,0:T(8,128)(2,1)S(1)} %get-tuple-element.161), channel_id=1, source_target_pairs={{0,4},{1,5},{2,6},{3,7},{4,0},{5,1},{6,2},{7,3},{8,12},{9,13},{10,... | collective-permute-start | bytes 1572872 | tf_op jit(solution)/shard_map/ppermute | solution.py:1560
  938.2 61.5 %collective-permute-start.2 = (bf16[2,64,2048]{2,1,0:T(8,128)(2,1)S(1)}, bf16[2,64,2048]{2,1,0:T(8,128)(2,1)S(1)}, u32[]{:S(2)}, u32[]{:S(2)}) collective-permute-start(bf16[2,64,2048]{2,1,0:T(8,128)(2,1)S(1)} %get-tuple-element.160), channel_id=1, source_target_pairs={{0,6},{1,7},{2,0},{3,1},{4,2},{5,3},{6,4},{7,5},{8,14},{9,15},{10,... | collective-permute-start | bytes 1572872 | tf_op jit(solution)/shard_map/ppermute | solution.py:1560
  999.7 6.8 copy-start.2
  (2 other events, 3.2 us)
Sparse Core Ops, SparseCore 0:
  10.2 105.7 all-gather.3
  118.0 147.9 all-gather.5
  268.2 101.1 all-gather.7
  473.6 75.9 reduce-scatter.5
  551.8 144.9 reduce-scatter.3
  699.7 77.4 reduce-scatter.7
